TPU v7x, 128 devices: a whole 4x4x4 slice. The times are simulated.
128 devices in a mesh: seq: 16 (over x, z), mp: 8 (over y, core).
Axes of the slice: x: 4, y: 4, z: 4, core: 2. Of those that a mesh axis runs over, the one named last changes fastest.
Arguments:
- context: bfloat16 [16, 256, 8192], P(None, 'mp', 'seq'), may hold values from -6 to 6
- blocks: bfloat16 [8, 8, 34, 128, 128], P('mp'), may hold values from -0.09375 to 0.09375
- row_blocks: int32 [8, 8, 34], replicated, may hold values from 0 to 63, as said below
- col_blocks: int32 [8, 8, 34], replicated, may hold values from 0 to 63, as said below
- live_counts: int32 [8, 8], replicated, may hold values from 30 to 34, as said below
- cotangent: bfloat16 [4096, 8192], P('seq', 'mp'), may hold values from -6 to 6
Outputs:
- outputs: bfloat16 [4096, 8192], P('seq', 'mp')
- context_grad: bfloat16 [16, 256, 8192], P(None, 'mp', 'seq')
- weight_grad: bfloat16 [8, 8, 34, 128, 128], P('mp', None, None, 'seq')
Inputs may be any that keep to these rules, and one draw needn't show every extreme that they name: Owner o holds block columns o * 8 to o * 8 + 7 and owner j block rows j * 8 to j * 8 + 7; the slots of pair (o, j) name blocks in those ranges, with the block at row_blocks[o, j, k] and col_blocks[o, j, k], all slots of a pair naming distinct blocks. Only the first live_counts[o, j] slots are kept; the others are padding. `col_blocks`: see row_blocks. In every draw there is an owner j with live_counts[o, j] = 34 for every o.
All inputs are finite; a program needn't handle non-finite values.
Results may differ from a plain program's by a relative error of at most 0.001.
Values may be sent and summed in bfloat16 or wider, within the bound.
No kernel may reach another device: no remote copies, remote signals or barrier semaphores. Data moves between devices by JAX's collectives and lax.ppermute only.
A program may use at most 192 MiB of HBM per device.

v0:
```python
import math

import jax
import jax.numpy as jnp
from jax import lax
from jax.sharding import PartitionSpec as P


def row_steps(row_count):
    step_rows = math.gcd(row_count, 128)
    return (step_rows, row_count // step_rows)


def select_owner(table, owner_index, along):
    return lax.dynamic_index_in_dim(table, owner_index, along, keepdims=False)


def on_device(context, blocks, row_blocks, col_blocks, live_counts, cotangent):
    owner_index = lax.axis_index("mp")
    mp_count = lax.axis_size("mp")
    seq_count = lax.axis_size("seq")
    slot_count = blocks.shape[2]
    block_size = blocks.shape[3]
    model_width = context.shape[2] * seq_count
    block_total = model_width // block_size
    owned_blocks = block_total // mp_count
    owned_width = owned_blocks * block_size
    token_count = cotangent.shape[0]
    sub_rows = token_count // mp_count
    slot_total = mp_count * slot_count
    slot_ids = jnp.arange(slot_count, dtype=jnp.int32)
    own_rows = select_owner(row_blocks, owner_index, 0)
    own_cols = select_owner(col_blocks, owner_index, 0)
    own_live = (slot_ids[None, :] < select_owner(live_counts, owner_index, 0)[:, None]).astype(
        jnp.float32
    )
    row_flat = own_rows.reshape(slot_total)
    col_local = (own_cols - owner_index * owned_blocks).reshape(slot_total)
    live_flat = own_live.reshape(slot_total)
    weight_flat = blocks.reshape(slot_total, block_size, block_size)
    live_blocks = weight_flat * live_flat.astype(jnp.bfloat16)[:, None, None]
    column_panel = jnp.zeros((block_total, block_size, owned_blocks, block_size), jnp.bfloat16)
    column_panel = column_panel.at[row_flat, :, col_local, :].set(live_blocks)
    column_panel = column_panel.reshape(model_width, owned_width)
    tokens_view = lax.all_to_all(context, "seq", split_axis=0, concat_axis=2, tiled=True)
    zero_grad = jnp.zeros((slot_total, block_size, block_size), jnp.float32)
    portion = lax.all_gather(tokens_view, "mp", axis=1, tiled=True)
    grad_sum = zero_grad
    row_count = portion.shape[1]
    portion_rows = portion.reshape(row_count, model_width)
    produced = jnp.dot(portion_rows, column_panel, preferred_element_type=jnp.float32)
    out_sum = produced
    step_rows, step_total = row_steps(row_count)
    input_steps = portion_rows.reshape(step_total, step_rows, block_total, block_size)
    cot_steps = cotangent.reshape(step_total, step_rows, owned_blocks, block_size)

    def advance(grad_part, paired):
        input_step, cot_step = paired
        picked = jnp.take(input_step, row_flat, axis=1)
        cot_picked = jnp.take(cot_step, col_local, axis=1)
        grad_part = grad_part + jnp.einsum(
            "bsi,bsj->sij", picked, cot_picked, preferred_element_type=jnp.float32
        )
        return (grad_part, None)

    grad_sum, unused = lax.scan(advance, grad_sum, (input_steps, cot_steps))
    out_sum, grad_sum = (out_sum, grad_sum)
    outputs = out_sum.astype(jnp.bfloat16)
    grad_terms = (grad_sum * live_flat[:, None, None]).reshape(
        1, mp_count, slot_count, block_size, block_size
    )
    grad_total = lax.psum_scatter(grad_terms, "seq", scatter_dimension=3, tiled=True)
    weight_grad = (grad_total * (1.0 / math.sqrt(token_count * seq_count))).astype(jnp.bfloat16)
    moved = lax.all_to_all(blocks, "mp", split_axis=1, concat_axis=0, tiled=True)
    moved_flat = moved.reshape(slot_total, block_size, block_size)
    source_rows = select_owner(row_blocks, owner_index, 1)
    source_cols = select_owner(col_blocks, owner_index, 1)
    source_live = (slot_ids[None, :] < select_owner(live_counts, owner_index, 1)[:, None]).astype(
        jnp.bfloat16
    )
    row_local = (source_rows - owner_index * owned_blocks).reshape(slot_total)
    col_index = source_cols.reshape(slot_total)
    moved_live = moved_flat * source_live.reshape(slot_total)[:, None, None]
    row_panel = jnp.zeros((owned_blocks, block_size, block_total, block_size), jnp.bfloat16)
    row_panel = row_panel.at[row_local, :, col_index, :].set(moved_live)
    row_panel = row_panel.reshape(owned_width, model_width)
    full_cot = lax.all_gather(cotangent, "mp", axis=1, tiled=True)
    row_grads = lax.dot_general(
        full_cot, row_panel, (((1,), (1,)), ((), ())), preferred_element_type=jnp.float32
    )
    slab_grad = lax.all_to_all(
        row_grads.astype(jnp.bfloat16), "mp", split_axis=0, concat_axis=1, tiled=True
    )
    context_grad = lax.all_to_all(
        slab_grad.reshape(1, sub_rows, model_width), "seq", split_axis=2, concat_axis=0, tiled=True
    )
    return (outputs, context_grad, weight_grad)


def solution(mesh):
    in_specs = (
        P(None, "mp", "seq"),
        P("mp", None, None, None, None),
        P(),
        P(),
        P(),
        P("seq", "mp"),
    )
    out_specs = (P("seq", "mp"), P(None, "mp", "seq"), P("mp", None, None, "seq", None))
    return jax.shard_map(
        on_device, mesh=mesh, in_specs=in_specs, out_specs=out_specs, check_vma=False
    )
```

profile of v0, /device:TPU:1, one launch (start us, length us, event | category | flops | bytes accessed | tf_op | source)
XLA Modules:
  0.0 548.7 jit_solution(13938105927486576886)
XLA Ops:
  7.2 18.7 %all_to_all.61 = bf16[16,32,512]{2,1,0:T(8,128)(2,1)S(1)} all-to-all(bf16[16,32,512]{2,1,0:T(8,128)(2,1)} %param.8), channel_id=1, replica_groups=mesh['seq'=16,'mp'=8] {'seq'}, dimensions={0} | all-to-all | bytes 1048576 | tf_op jit(solution)/shard_map/all_to_all | solution.py:45
  26.0 0.8 copy.43
  26.9 0.7 all-gather.5.cloned.1.call-update
  27.7 0.6 reshape.249
  28.4 0.7 dynamic-slice_subtract_fusion
  29.2 1.1 copy.48
  30.4 28.6 %all-gather.3.cloned.1.call-done = bf16[1,256,8192]{2,1,0:T(8,128)(2,1)} async-done(((bf16[1,32,8192]{2,1,0:T(8,128)(2,1)}), bf16[1,256,8192]{2,1,0:T(8,128)(2,1)}) %all-gather.3.cloned.1.call-update) | async-done | bytes 4194320 | tf_op jit(solution)/shard_map/all_gather | solution.py:47
  59.0 5.3 copy.47
  64.4 83.6 %while.11 = (s32[]{:T(128)}, f32[272,128,128]{2,1,0:T(8,128)}, s32[272]{0:T(512)S(1)}, bf16[2,128,64,128]{3,2,1,0:T(8,128)(2,1)}, s32[272]{0:T(512)S(1)}, /*inde...) while((s32[]{:T(128)}, f32[272,128,128]{2,1,0:T(8,128)}, s32[272]{0:T(512)S(1)}, ...), condition=%wide.region_3.4_spmd.clone, body=%wide.region_2.3_spmd.clone.sunk | while | flops 1158683392 | bytes 98586408 | solution.py:66
  64.4 1.8 constant_dynamic-slice_fusion.7
  66.2 1.4 copy.70
  67.5 10.2 %gather_fusion.1 = bf16[272,128,128]{2,1,0:T(8,128)(2,1)} fusion(bf16[128,64,128]{2,0,1:T(8,128)(2,1)S(1)} %bitcast.87, s32[1024]{0:T(1024)S(1)} %pad_clamp_fusion.5), kind=kCustom, calls=%fused_computation.clone.clone.1 | custom fusion | bytes 17826880 | tf_op jit(solution)/shard_map/while/body/eval_jaxpr/jit(_take)/gather | solution.py:59
  77.8 10.2 %gather_fusion = bf16[272,128,128]{2,1,0:T(8,128)(2,1)} fusion(bf16[128,8,128]{2,0,1:T(8,128)(2,1)S(1)} %bitcast.86, s32[1024]{0:T(1024)S(1)} %pad_clamp_fusion.4), kind=kCustom, calls=%fused_computation.1.clone.clone.1 | custom fusion | bytes 17826880 | tf_op jit(solution)/shard_map/while/body/eval_jaxpr/jit(_take)/gather | solution.py:60
  88.0 16.2 %select_add_fusion.2 = f32[272,128,128]{2,1,0:T(8,128)} fusion(f32[272,128,128]{2,1,0:T(8,128)} %get-tuple-element.161, pred[]{:T(512)S(6)} %compare.23, bf16[272,128,128]{2,1,0:T(8,128)(2,1)} %gather_fusion, pred[272]{0:T(512)(128)(4,1)S(1)} %get-tuple-element.149, bf16[272,128,128]{2,1,0:T(8,128)(2,1)} %gather_fusion.1, ...), kind=kOutput, calls=%fused_computation.4.clone.1 | convolution fusion | flops 1158676480 | bytes 53477920 | tf_op jit(solution)/shard_map/while/body/eval_jaxpr/bsi,bsj->sij/dot_general | solution.py:61
  104.3 1.8 constant_dynamic-slice_fusion.7
  106.0 1.4 copy.70
  107.4 10.2 %gather_fusion.1 = bf16[272,128,128]{2,1,0:T(8,128)(2,1)} fusion(bf16[128,64,128]{2,0,1:T(8,128)(2,1)S(1)} %bitcast.87, s32[1024]{0:T(1024)S(1)} %pad_clamp_fusion.5), kind=kCustom, calls=%fused_computation.clone.clone.1 | custom fusion | bytes 17826880 | tf_op jit(solution)/shard_map/while/body/eval_jaxpr/jit(_take)/gather | solution.py:59
  117.7 10.1 %gather_fusion = bf16[272,128,128]{2,1,0:T(8,128)(2,1)} fusion(bf16[128,8,128]{2,0,1:T(8,128)(2,1)S(1)} %bitcast.86, s32[1024]{0:T(1024)S(1)} %pad_clamp_fusion.4), kind=kCustom, calls=%fused_computation.1.clone.clone.1 | custom fusion | bytes 17826880 | tf_op jit(solution)/shard_map/while/body/eval_jaxpr/jit(_take)/gather | solution.py:60
  127.8 20.2 %select_add_fusion.2 = f32[272,128,128]{2,1,0:T(8,128)} fusion(f32[272,128,128]{2,1,0:T(8,128)} %get-tuple-element.161, pred[]{:T(512)S(6)} %compare.23, bf16[272,128,128]{2,1,0:T(8,128)(2,1)} %gather_fusion, pred[272]{0:T(512)(128)(4,1)S(1)} %get-tuple-element.149, bf16[272,128,128]{2,1,0:T(8,128)(2,1)} %gather_fusion.1, ...), kind=kOutput, calls=%fused_computation.4.clone.1 | convolution fusion | flops 1158676480 | bytes 53477920 | tf_op jit(solution)/shard_map/while/body/eval_jaxpr/bsi,bsj->sij/dot_general | solution.py:61
  148.0 12.2 %broadcast_multiply_fusion = f32[272,128,128]{2,1,0:T(8,128)} fusion(f32[272,128,128]{2,1,0:T(8,128)} %get-tuple-element.35, f32[272]{0:T(512)S(1)} %copy-done.5), kind=kLoop, calls=%fused_computation.36 | loop fusion | flops 4456448 | bytes 35652672 | tf_op jit(solution)/shard_map/mul | solution.py:69
  160.2 5.3 all-to-all-start.1
  165.5 0.2 dynamic-slice_reduce_fusion
  165.7 0.8 dynamic-slice_reduce_fusion.1
  166.9 98.1 %all-to-all-done.1 = bf16[1,8,34,128,128]{4,3,2,0,1:T(8,128)(2,1)} async-done(((bf16[1,8,34,128,128]{4,3,2,0,1:T(8,128)(2,1)}), bf16[1,8,34,128,128]{4,3,2,0,1:T(8,128)(2,1)}, u32[]{:S(2)}, u32[]{:S(2)}) %all-to-all-start.1) | async-done | bytes 8912928 | tf_op jit(solution)/shard_map/all_to_all | solution.py:74
  264.9 7.8 %bitcast_multiply_fusion = bf16[272,128,128]{2,1,0:T(8,128)(2,1)} fusion(bf16[1,8,34,128,128]{4,3,2,0,1:T(8,128)(2,1)} %all-to-all-done.1, bf16[272]{0:T(512)(128)(2,1)S(1)} %reshape.250), kind=kLoop, calls=%fused_computation.34 | loop fusion | flops 4456448 | bytes 17826336 | tf_op jit(solution)/shard_map/mul | solution.py:83
  272.7 6.4 %broadcast_in_dim.37 = bf16[8,128,64,128]{3,1,2,0:T(8,128)(2,1)} broadcast(bf16[]{:T(256)} %constant.70.clone.1), dimensions={} | broadcast | bytes 16777218 | tf_op jit(solution)/shard_map/broadcast_in_dim | solution.py:84
  279.1 43.4 %scatter_fusion.1 = bf16[8,128,64,128]{3,1,2,0:T(8,128)(2,1)} fusion(bf16[8,128,64,128]{3,1,2,0:T(8,128)(2,1)} %broadcast_in_dim.37, s32[272]{0:T(512)S(1)} %fusion.40, bf16[272,128,128]{2,1,0:T(8,128)(2,1)} %bitcast_multiply_fusion), kind=kCustom, calls=%fused_computation.3 | custom fusion | bytes 26740864 | tf_op jit(solution)/shard_map/scatter | solution.py:85
  322.6 18.5 %copy.32 = bf16[8,128,64,128]{3,2,1,0:T(8,128)(2,1)} copy(bf16[8,128,64,128]{3,1,2,0:T(8,128)(2,1)} %scatter_fusion.1) | data formatting | bytes 33554432 | tf_op jit(solution)/shard_map/scatter | solution.py:85
  341.1 25.8 %fusion.22 = bf16[1024,256]{0,1:T(8,128)(2,1)} fusion(bf16[256,8192]{1,0:T(8,128)(2,1)} %all-gather.5.cloned.1.call-done, bf16[128,8,64,128]{3,2,1,0:T(8,128)(2,1)} %bitcast.94), kind=kOutput, calls=%fused_computation.38 | convolution fusion | flops 4295229440 | bytes 21495808 | tf_op jit(solution)/shard_map/dot_general | solution.py:88
  366.9 4.3 all-to-all-start.2
  371.2 7.7 %bitcast_multiply_fusion.1 = bf16[272,128,128]{2,1,0:T(8,128)(2,1)} fusion(bf16[1,8,34,128,128]{4,3,2,1,0:T(8,128)(2,1)} %param.9, bf16[272]{0:T(512)(128)(2,1)S(1)} %convert_element_type.48), kind=kLoop, calls=%fused_computation.35 | loop fusion | flops 4456448 | bytes 17826336 | tf_op jit(solution)/shard_map/mul | solution.py:41
  379.1 6.4 %broadcast_in_dim.36 = bf16[64,128,8,128]{3,1,2,0:T(8,128)(2,1)} broadcast(bf16[]{:T(256)} %constant.70.clone.1), dimensions={} | broadcast | bytes 16777218 | tf_op jit(solution)/shard_map/broadcast_in_dim | solution.py:42
  385.5 43.4 %scatter_fusion = bf16[64,128,8,128]{3,1,2,0:T(8,128)(2,1)} fusion(bf16[64,128,8,128]{3,1,2,0:T(8,128)(2,1)} %broadcast_in_dim.36, s32[272]{0:T(512)S(1)} %fusion.39, bf16[272,128,128]{2,1,0:T(8,128)(2,1)} %bitcast_multiply_fusion.1), kind=kCustom, calls=%fused_computation.2 | custom fusion | bytes 26740864 | tf_op jit(solution)/shard_map/scatter | solution.py:43
  428.9 19.3 %copy.29 = bf16[64,128,8,128]{3,2,1,0:T(8,128)(2,1)} copy(bf16[64,128,8,128]{3,1,2,0:T(8,128)(2,1)} %scatter_fusion) | data formatting | bytes 33554432 | tf_op jit(solution)/shard_map/scatter | solution.py:43
  448.2 0.3 copy.33
  448.5 0.2 reshape.245
  448.7 6.8 %copy.34 = bf16[1,32,8192]{1,0,2:T(2,128)(2,1)} copy(bf16[1,32,8192]{2,1,0:T(8,128)(2,1)S(1)} %reshape.245) | data formatting | bytes 1048576 | tf_op jit(solution)/shard_map/reshape | solution.py:95
  455.5 0.5 broadcast.244
  456.0 45.2 %reduce.18 = bf16[8192,32]{1,0:T(8,128)(2,1)S(1)} reduce(bf16[8192,1,32]{2,1,0:T(2,128)(2,1)} %bitcast.91, bf16[]{:T(256)} %broadcast.244), dimensions={1}, to_apply=%bitcast.72.reduce_sub_computation | reduce | bytes 1048578
  501.2 2.7 reshape.306
  504.0 6.7 %all-to-all-start.3 = ((bf16[16,2,8192]{2,1,0:T(2,128)(2,1)}), bf16[16,2,8192]{2,1,0:T(2,128)(2,1)S(1)}, u32[]{:S(2)}, u32[]{:S(2)}) async-start(bf16[16,2,8192]{2,1,0:T(2,128)(2,1)} %reshape.306), calls=%async_computation.3 | async-start | bytes 1048576 | tf_op jit(solution)/shard_map/all_to_all | solution.py:94
  510.7 11.7 %fusion.30 = bf16[256,1024]{0,1:T(8,128)(2,1)S(1)} fusion(bf16[1,256,8192]{2,1,0:T(8,128)(2,1)} %all-gather.3.cloned.1.call-done, bf16[1024,8,8,128]{3,2,1,0:T(8,128)(2,1)} %bitcast.93), kind=kOutput, calls=%fused_computation.40 | convolution fusion | flops 4295229440 | bytes 21495808 | tf_op jit(solution)/shard_map/dot_general | solution.py:51
  522.4 1.0 copy.38
  523.4 7.2 %reshape.307 = bf16[8192,1,32]{2,1,0:T(2,128)(2,1)} reshape(bf16[16,2,8192]{2,1,0:T(2,128)(2,1)S(1)} %all-to-all-done.3) | data formatting | bytes 1048576
  530.6 8.0 %copy.35 = bf16[1,32,8192]{2,1,0:T(8,128)(2,1)S(1)} copy(bf16[1,32,8192]{1,0,2:T(2,128)(2,1)} %bitcast.92) | data formatting | bytes 1048576 | tf_op jit(solution)/shard_map/all_to_all | solution.py:94
  538.6 0.2 copy.46
  538.8 1.1 copy.39
  539.9 2.1 multiply_convert_fusion
  (48 shorter events, 1.2 us)
Async XLA Ops:
  7.2 20.5 %copy-start = (s32[8,8]{1,0:T(8,128)S(1)}, s32[8,8]{1,0:T(8,128)}, u32[]{:S(2)}) copy-start(s32[8,8]{1,0:T(8,128)} %param.12) | copy-start | bytes 772
  7.2 51.8 %all-gather.3.cloned.1.call-start = ((), (), s32[]{:S(2)}) async-start(), calls=%async_computation.5 | async-start | bytes 4718592 | tf_op jit(solution)/shard_map/all_gather | solution.py:47
  26.8 314.3 %all-gather.5.cloned.1.call-start = ((), (), s32[]{:S(2)}) async-start(), calls=%async_computation.6 | async-start | bytes 4718592 | tf_op jit(solution)/shard_map/all_gather | solution.py:87
  27.6 512.3 %reduce-scatter.2.cloned.1.call-start = ((), (), s32[]{:S(2)}) async-start(), calls=%async_computation.7 | async-start | bytes 18939904 | tf_op jit(solution)/shard_map/reduce_scatter | solution.py:72
  29.1 35.3 %copy-start.1 = (s32[1,8,34]{2,1,0:T(8,128)}, s32[1,8,34]{2,1,0:T(8,128)S(1)}, u32[]{:S(2)}) copy-start(s32[1,8,34]{2,1,0:T(8,128)S(1)} %get-tuple-element.105) | copy-start | bytes 3268
  29.1 35.3 %copy-start.3 = (s32[1,8,34]{2,1,0:T(8,128)}, s32[1,8,34]{2,1,0:T(8,128)S(1)}, u32[]{:S(2)}) copy-start(s32[1,8,34]{2,1,0:T(8,128)S(1)} %get-tuple-element.106) | copy-start | bytes 3268
  64.3 83.6 %copy-start.5 = (f32[272]{0:T(512)S(1)}, f32[272]{0:T(512)}, u32[]{:S(2)}) copy-start(f32[272]{0:T(512)} %reshape.249) | copy-start | bytes 3268
  160.2 104.7 %all-to-all-start.1 = ((bf16[1,8,34,128,128]{4,3,2,0,1:T(8,128)(2,1)}), bf16[1,8,34,128,128]{4,3,2,0,1:T(8,128)(2,1)}, u32[]{:S(2)}, u32[]{:S(2)}) async-start(bf16[1,8,34,128,128]{4,3,2,0,1:T(8,128)(2,1)} %bitcast.90), calls=%async_computation.1 | async-start | bytes 17825792 | tf_op jit(solution)/shard_map/all_to_all | solution.py:74
  366.9 81.3 %all-to-all-start.2 = ((bf16[8,32,1024]{2,1,0:T(8,128)(2,1)}), bf16[8,32,1024]{2,1,0:T(8,128)(2,1)S(1)}, u32[]{:S(2)}, u32[]{:S(2)}) async-start(bf16[8,32,1024]{2,1,0:T(8,128)(2,1)} %bitcast.9), calls=%async_computation.2 | async-start | bytes 1048576 | tf_op jit(solution)/shard_map/all_to_all | solution.py:91
  371.2 7.7 %copy-start.4 = (s32[1,8,34]{2,1,0:T(8,128)S(1)}, s32[1,8,34]{2,1,0:T(8,128)}, u32[]{:S(2)}) copy-start(s32[1,8,34]{2,1,0:T(8,128)} %copy-done.3) | copy-start | bytes 3268
  371.2 7.8 %copy-start.2 = (s32[1,8,34]{2,1,0:T(8,128)S(1)}, s32[1,8,34]{2,1,0:T(8,128)}, u32[]{:S(2)}) copy-start(s32[1,8,34]{2,1,0:T(8,128)} %copy-done.1) | copy-start | bytes 3268
  504.0 19.5 %all-to-all-start.3 = ((bf16[16,2,8192]{2,1,0:T(2,128)(2,1)}), bf16[16,2,8192]{2,1,0:T(2,128)(2,1)S(1)}, u32[]{:S(2)}, u32[]{:S(2)}) async-start(bf16[16,2,8192]{2,1,0:T(2,128)(2,1)} %reshape.306), calls=%async_computation.3 | async-start | bytes 1048576 | tf_op jit(solution)/shard_map/all_to_all | solution.py:94
Sparse Core Ops, SparseCore 0:
  26.9 32.0 all-gather.2
  60.7 32.0 all-gather.4
  160.3 115.1 reduce-scatter.1
where the time goes:
time: 559 us; the launch traced here: 549 us
  local copies, waits for them, and re-layouts  221 us (40%)
  waiting for transfers between devices  127 us (23%)
  other arithmetic  76.9 us (14%)
  matrix products  73.9 us (13%)
  blocking collectives  18.7 us (3%)
  starting transfers between devices  16.4 us (3%)
  between operations  14.1 us (3%)
    all_to_all x1, waiting for transfers between devices, on_device(): lax.all_to_all(blocks, 'mp', split_axis=1, concat_axis=0, tiled=True)  98.1 us
    scatter x2, local copies, waits for them, and re-layouts, on_device(): column_panel = column_panel.at[row_flat, :, col_local, :].set(live_blocks)  62.7 us
    scatter x2, local copies, waits for them, and re-layouts, on_device(): row_panel = row_panel.at[row_local, :, col_index, :].set(moved_live)  62 us
    unnamed x2, other arithmetic  45.2 us
    dot_general x2, matrix products, advance(): jnp.einsum('bsi,bsj->sij', picked, cot_picked, preferred_element_type=jnp...  36.4 us
    all_gather x1, waiting for transfers between devices, on_device(): portion = lax.all_gather(tokens_view, 'mp', axis=1, tiled=True)  28.6 us
    dot_general x1, matrix products, on_device(): lax.dot_general(full_cot, row_panel, (((1,), (1,)), ((), ())), preferred_...  25.8 us
    gather x2, local copies, waits for them, and re-layouts, advance(): picked = jnp.take(input_step, row_flat, axis=1)  20.4 us
  transfers between devices with their start and end apart: 6, of which 2 were waited for; matrix products, arithmetic and copies ran while one was open for 67% of the time, Pallas kernels for 0%

commit v1 on v0

v1 whole, which is shorter than its diff:
```python
import functools
import math

import jax
import jax.numpy as jnp
from jax import lax
from jax.experimental import pallas as pl
from jax.experimental.pallas import tpu as pltpu
from jax.sharding import PartitionSpec as P

F32 = jnp.float32
BF16 = jnp.bfloat16
VMEM_LIMIT = 56 * 1024 * 1024


def build_panel(panel, blk_ref, rows_ref, cols_ref, live_ref, owner, j):
    panel[...] = jnp.zeros_like(panel)

    def place(k, carry):
        r = pl.multiple_of((rows_ref[owner, j, k] - 8 * j) * 128, 128)
        c = pl.multiple_of((cols_ref[owner, j, k] - 8 * owner) * 128, 128)
        panel[pl.ds(r, 128), pl.ds(c, 128)] = blk_ref[0, 0, k]
        return carry

    lax.fori_loop(0, live_ref[owner, j], place, 0)


def transpose_kernel(x_ref, o_ref):
    x = x_ref[...].reshape(512, 512).astype(F32)
    t = x.T.reshape(4, 16, 8, 512)
    for cls in range(16):
        o_ref[cls] = t[:, cls].reshape(32, 512).astype(BF16)


def partial_kernel(pos, rows, cols, live, cot_ref, blk_ref, keep, send0, send1, send2, send3, lhs, panel):
    j = pl.program_id(0)
    owner = pos[0]
    y = owner // 2
    core = owner % 2
    sends = (send0, send1, send2, send3)

    @pl.when(j == 0)
    def _():
        for d in range(4):
            group = (y + d) % 4
            lhs[pl.ds(d * 32, 32)] = cot_ref[group, core]
            lhs[pl.ds(128 + d * 32, 32)] = cot_ref[group, 1 - core]

    build_panel(panel, blk_ref, rows, cols, live, owner, j)
    for n in range(4):
        res = lax.dot_general(
            lhs[...], panel[pl.ds(n * 256, 256)], (((1,), (1,)), ((), ())), preferred_element_type=F32
        )
        half, lane = n // 2, (n % 2) * 256
        for d in range(4):
            keep[d, half, :, pl.ds(lane, 256)] = res[d * 32 : d * 32 + 32]
            sends[d][half, :, pl.ds(lane, 256)] = res[128 + d * 32 : 128 + d * 32 + 32]


def place_chunks(lhs, group, core, x, halves):
    start = pl.multiple_of((group * 2 + core) * 32, 32)
    for h in range(halves):
        lhs[pl.ds(start, 32), pl.ds(h * 512, 512)] = x[h]


def out_kernel(pos, rows, cols, live, a0, am, ap, a2a, a2b, b0, bm, bp, b2a, b2b, blk_ref, out_ref, lhs, panel, acc):
    j = pl.program_id(0)
    owner = pos[0]
    y = owner // 2
    core = owner % 2
    for who, (x0, xm, xp, x2a, x2b) in ((core, (a0, am, ap, a2a, a2b)), (1 - core, (b0, bm, bp, b2a, b2b))):
        place_chunks(lhs, y, who, x0, 2)
        place_chunks(lhs, (y + 3) % 4, who, xm, 2)
        place_chunks(lhs, (y + 1) % 4, who, xp, 2)

        @pl.when(j < 4)
        def _():
            place_chunks(lhs, (y + 2) % 4, who, x2a, 2)

        @pl.when(j >= 4)
        def _():
            place_chunks(lhs, (y + 2) % 4, who, x2b, 2)

    build_panel(panel, blk_ref, rows, cols, live, owner, j)
    for n in range(4):
        lanes = pl.ds(n * 256, 256)
        res = jnp.dot(lhs[...], panel[:, lanes], preferred_element_type=F32)

        @pl.when(j == 0)
        def _():
            acc[:, lanes] = res

        @pl.when((j > 0) & (j < 7))
        def _():
            acc[:, lanes] += res

        @pl.when(j == 7)
        def _():
            out_ref[:, lanes] = (acc[:, lanes] + res).astype(BF16)


def grad_kernel(scale, pos, rows, cols, live, a0, am, ap, a2a, a2b, b0, bm, bp, b2a, b2b, g_ref, out_ref, lhs, acc):
    i = pl.program_id(0)
    owner = pos[0]
    full = (a0, am, ap, None, b0, bm, bp, None)
    for at in range(8):

        @pl.when(i == at)
        def _():
            if full[at] is not None:
                lhs[...] = full[at][...].reshape(512, 512)
            else:
                first, second = (a2a, a2b) if at == 3 else (b2a, b2b)
                lhs[pl.ds(0, 256)] = first[...].reshape(256, 512)
                lhs[pl.ds(256, 256)] = second[...].reshape(256, 512)

    g = g_ref[...].reshape(512, 1024)
    for n in range(4):
        lanes = pl.ds(n * 256, 256)
        res = jnp.dot(lhs[...], g[:, n * 256 : n * 256 + 256], preferred_element_type=F32).reshape(64, 8, 256)

        @pl.when(i == 0)
        def _():
            acc[:, :, lanes] = res

        @pl.when(i > 0)
        def _():
            acc[:, :, lanes] += res

    @pl.when(i == 7)
    def _():
        def pick(j, carry):
            count = live[owner, j]

            def one(k, carry):
                r = rows[owner, j, k]
                c = pl.multiple_of((cols[owner, j, k] - 8 * owner) * 128, 128)
                tile = acc[r, :, pl.ds(c, 128)] * scale
                out_ref[0, j, k] = jnp.where(k < count, tile, 0.0).astype(BF16)
                return carry

            return lax.fori_loop(0, 34, one, carry, unroll=2)

        lax.fori_loop(0, 8, pick, 0)


def on_device(context, blocks, row_blocks, col_blocks, live_counts, cotangent):
    owner = lax.axis_index("mp")
    pos = owner.astype(jnp.int32).reshape(1)
    tables = (pos, row_blocks, col_blocks, live_counts)
    params = pltpu.CompilerParams(vmem_limit_bytes=VMEM_LIMIT)

    def along_y(x, step):
        return lax.ppermute(x, "mp", [(i, (i + 2 * step) % 8) for i in range(8)])

    def other_core(x):
        return lax.ppermute(x, "mp", [(i, i ^ 1) for i in range(8)])

    def exchange(x):
        return lax.all_to_all(x, "seq", split_axis=0, concat_axis=0, tiled=True)

    def gather_pieces(x):
        xm = along_y(x, 1)
        xp = along_y(x, -1)
        x2a = along_y(xm[:8], 1)
        x2b = along_y(xp[8:], -1)
        own = (x, xm, xp, x2a, x2b)
        return own + tuple(other_core(piece) for piece in own)

    blk_spec = pl.BlockSpec((1, 1, 34, 128, 128), lambda j, *_: (0, j, 0, 0, 0))
    part = jax.ShapeDtypeStruct((16, 32, 512), F32)
    part_spec = pl.BlockSpec((2, 32, 512), lambda j, *_: (j, 0, 0))
    keep, *sends = pl.pallas_call(
        partial_kernel,
        grid_spec=pltpu.PrefetchScalarGridSpec(
            num_scalar_prefetch=4,
            grid=(8,),
            in_specs=[pl.BlockSpec((4, 2, 32, 1024), lambda j, *_: (0, 0, 0, 0)), blk_spec],
            out_specs=[pl.BlockSpec((4, 2, 32, 512), lambda j, *_: (0, j, 0, 0))] + [part_spec] * 4,
            scratch_shapes=[pltpu.VMEM((256, 1024), BF16), pltpu.VMEM((1024, 1024), BF16)],
        ),
        out_shape=[jax.ShapeDtypeStruct((4, 16, 32, 512), F32)] + [part] * 4,
        compiler_params=params,
        cost_estimate=pl.CostEstimate(flops=4_300_000_000, bytes_accessed=18_000_000, transcendentals=0),
        name="partial_context_grad",
    )(*tables, cotangent.reshape(4, 2, 32, 1024), blocks)

    r2, r1, r3, r0 = (other_core(sends[d]) for d in (2, 1, 3, 0))
    from_a = along_y(keep[2, :8] + r2[:8], 1)
    from_b = along_y(keep[2, 8:] + r2[8:], -1)
    near_b = along_y(keep[1, 8:] + r1[8:], 1)
    near_a = along_y(keep[3, :8] + r3[:8], -1)
    far_a = along_y(keep[1, :8] + r1[:8] + from_a, 1)
    far_b = along_y(keep[3, 8:] + r3[8:] + from_b, -1)
    sum_a = keep[0, :8] + r0[:8] + near_a + far_a
    sum_b = keep[0, 8:] + r0[8:] + near_b + far_b
    context_grad = exchange(jnp.concatenate([sum_a, sum_b], axis=0).astype(BF16))

    x_pieces = gather_pieces(exchange(context))
    whole = pl.BlockSpec((2, 32, 512), lambda j, *_: (j, 0, 0))
    low = pl.BlockSpec((2, 32, 512), lambda j, *_: (jnp.minimum(j, 3), 0, 0))
    high = pl.BlockSpec((2, 32, 512), lambda j, *_: (jnp.maximum(j - 4, 0), 0, 0))
    outputs = pl.pallas_call(
        out_kernel,
        grid_spec=pltpu.PrefetchScalarGridSpec(
            num_scalar_prefetch=4,
            grid=(8,),
            in_specs=[whole, whole, whole, low, high] * 2 + [blk_spec],
            out_specs=pl.BlockSpec((256, 1024), lambda j, *_: (0, 0)),
            scratch_shapes=[
                pltpu.VMEM((256, 1024), BF16),
                pltpu.VMEM((1024, 1024), BF16),
                pltpu.VMEM((256, 1024), F32),
            ],
        ),
        out_shape=jax.ShapeDtypeStruct((256, 1024), BF16),
        compiler_params=params,
        cost_estimate=pl.CostEstimate(flops=4_300_000_000, bytes_accessed=14_000_000, transcendentals=0),
        name="outputs",
    )(*tables, *x_pieces, blocks)

    by_class = pl.pallas_call(
        transpose_kernel,
        out_shape=jax.ShapeDtypeStruct((16, 32, 512), BF16),
        compiler_params=params,
        name="feature_rows",
    )(context)
    t_pieces = gather_pieces(exchange(by_class))
    cot_all = lax.all_gather(cotangent, "seq", axis=0, tiled=True)
    full = pl.BlockSpec((16, 32, 512), lambda i, *_: (0, 0, 0))
    part8 = pl.BlockSpec((8, 32, 512), lambda i, *_: (0, 0, 0))

    def group_of(i, pos, *_):
        owner = pos[0]
        step = lax.rem(i, 4)
        shift = jnp.where(step == 1, 3, jnp.where(step == 2, 1, jnp.where(step == 3, 2, 0)))
        chip = lax.rem(lax.div(owner, 2) + shift, 4)
        core = lax.rem(owner + lax.div(i, 4), 2)
        return (0, chip * 2 + core, 0, 0)

    weight_grad = pl.pallas_call(
        functools.partial(grad_kernel, 1.0 / math.sqrt(4096)),
        grid_spec=pltpu.PrefetchScalarGridSpec(
            num_scalar_prefetch=4,
            grid=(8,),
            in_specs=[full, full, full, part8, part8] * 2 + [pl.BlockSpec((16, 1, 32, 1024), group_of)],
            out_specs=pl.BlockSpec((1, 8, 34, 8, 128), lambda i, *_: (0, 0, 0, 0, 0)),
            scratch_shapes=[pltpu.VMEM((512, 512), BF16), pltpu.VMEM((64, 8, 1024), F32)],
        ),
        out_shape=jax.ShapeDtypeStruct((1, 8, 34, 8, 128), BF16),
        compiler_params=params,
        cost_estimate=pl.CostEstimate(flops=4_300_000_000, bytes_accessed=14_000_000, transcendentals=0),
        name="weight_grad",
    )(*tables, *t_pieces, cot_all.reshape(16, 8, 32, 1024))
    return (outputs, context_grad, weight_grad)


def solution(mesh):
    in_specs = (
        P(None, "mp", "seq"),
        P("mp", None, None, None, None),
        P(),
        P(),
        P(),
        P("seq", "mp"),
    )
    out_specs = (P("seq", "mp"), P(None, "mp", "seq"), P("mp", None, None, "seq", None))
    return jax.shard_map(
        on_device, mesh=mesh, in_specs=in_specs, out_specs=out_specs, check_vma=False
    )
```

time: 559 us -> 200 us (0.36); the launches traced: 549 us -> 198 us
  local copies, waits for them, and re-layouts: 221 us -> 4.14 us
  matrix products: 73.9 us -> 0 us
  other arithmetic: 76.9 us -> 3.44 us
  waiting for transfers between devices: 127 us -> 59.2 us
  Pallas kernels: 0 us -> 67.4 us
  starting transfers between devices: 16.4 us -> 49.8 us
  blocking collectives: 18.7 us -> 0 us
    scatter x4 -> x0, local copies, waits for them, and re-layouts: 125 us -> none  [the longest x2 62.7 us: on_device(): column_panel = column_panel.at[row_flat, :, col_local, :].set(live_blocks)]
    all_to_all x3, waiting for transfers between devices: 98.1 us -> 10.6 us  [exchange(): return lax.all_to_all(x, 'seq', split_axis=0, concat_axis=0, tiled=True)]
    dot_general x4 -> x0, matrix products: 73.9 us -> none  [the longest x2 36.4 us: advance(): jnp.einsum('bsi,bsj->sij', picked, cot_picked, preferred_element_type=jnp...]
    pallas_call x0 -> x4, Pallas kernels: none -> 67.4 us  [the longest x1 24.6 us: on_device(): pl.pallas_call(functools.partial(grad_kernel, 1.0 / math.sqrt(4096)), gri...]
    ppermute x0 -> x28, waiting for transfers between devices: none -> 47.8 us  [the longest x14 47.8 us: along_y(): return lax.ppermute(x, 'mp', [(i, (i + 2 * step) % 8) for i in range(8)])]
    unnamed x2 -> x0, other arithmetic: 45.2 us -> none
    gather x4 -> x0, local copies, waits for them, and re-layouts: 40.6 us -> none  [the longest x2 20.4 us: advance(): picked = jnp.take(input_step, row_flat, axis=1)]
    ppermute x0 -> x28, starting transfers between devices: none -> 29.3 us  [the longest x14 16.4 us: other_core(): return lax.ppermute(x, 'mp', [(i, i ^ 1) for i in range(8)])]
  transfers between devices with their start and end apart: 6 -> 32, of which waited for: 2 -> 7; matrix products, arithmetic and copies ran while one was open for 67% -> 3% of each run, Pallas kernels for 0% -> 22%
where the time goes in v1:
time: 200 us; the launch traced here: 198 us
  Pallas kernels  67.4 us (34%)
  waiting for transfers between devices  59.2 us (30%)
  starting transfers between devices  49.8 us (25%)
  between operations  14.2 us (7%)
  local copies, waits for them, and re-layouts  4.14 us (2%)
  other arithmetic  3.44 us (2%)
    ppermute x14, waiting for transfers between devices, along_y(): return lax.ppermute(x, 'mp', [(i, (i + 2 * step) % 8) for i in range(8)])  47.8 us
    pallas_call x1, Pallas kernels, on_device(): pl.pallas_call(functools.partial(grad_kernel, 1.0 / math.sqrt(4096)), gri...  24.6 us
    pallas_call x1, Pallas kernels, on_device(): pl.pallas_call(out_kernel, grid_spec=pltpu.PrefetchScalarGridSpec(num_sca...  24.1 us
    all_to_all x3, starting transfers between devices, exchange(): return lax.all_to_all(x, 'seq', split_axis=0, concat_axis=0, tiled=True)  20.5 us
    pallas_call x1, Pallas kernels, on_device(): pl.pallas_call(partial_kernel, grid_spec=pltpu.PrefetchScalarGridSpec(num...  16.6 us
    ppermute x14, starting transfers between devices, other_core(): return lax.ppermute(x, 'mp', [(i, i ^ 1) for i in range(8)])  16.4 us
    ppermute x14, starting transfers between devices, along_y(): return lax.ppermute(x, 'mp', [(i, (i + 2 * step) % 8) for i in range(8)])  12.9 us
    all_to_all x3, waiting for transfers between devices, exchange(): return lax.all_to_all(x, 'seq', split_axis=0, concat_axis=0, tiled=True)  10.6 us
  transfers between devices with their start and end apart: 32, of which 7 were waited for; matrix products, arithmetic and copies ran while one was open for 3% of the time, Pallas kernels for 22%

profile of v1, /device:TPU:1, one launch (start us, length us, event | category | flops | bytes accessed | tf_op | source)
XLA Modules:
  0.0 198.2 jit_solution(3171277867744380146)
XLA Ops:
  7.2 0.7 all-gather.2.cloned.1.call-update
  7.9 2.0 %feature_rows.1 = bf16[16,32,512]{2,1,0:T(8,128)(2,1)} custom-call(bf16[16,32,512]{2,1,0:T(8,128)(2,1)} %x_ref.1), custom_call_target="tpu_custom_call" | custom-call | tf_op jit(solution)/shard_map/feature_rows/pallas_call | solution.py:222
  9.9 8.5 %all-to-all-start.2 = ((bf16[16,32,512]{2,1,0:T(8,128)(2,1)}), bf16[16,32,512]{2,1,0:T(8,128)(2,1)}, u32[]{:S(2)}, u32[]{:S(2)}) async-start(bf16[16,32,512]{2,1,0:T(8,128)(2,1)} %feature_rows.1), calls=%async_computation.2 | async-start | bytes 1048576 | tf_op jit(solution)/shard_map/all_to_all | solution.py:160
  18.4 16.6 %partial_context_grad.1 = (f32[4,16,32,512]{3,2,1,0:T(8,128)}, f32[16,32,512]{2,1,0:T(8,128)}, f32[16,32,512]{2,1,0:T(8,128)}, f32[16,32,512]{2,1,0:T(8,128)}, f32[16,32,512]{2,1,0:T(8,128)}) custom-call(s32[1]{0:T(128)} %bitcast.pos, s32[8,8,34]{2,1,0:T(8,128)} %rows.5, s32[8,8,34]{2,1,0:T(8,128)} %cols.5, s32[8,8]{1,0:T(8,128)} %live.5, ...), custom_call_target="tpu_custom_call" | custom-call | flops 4300000256 | bytes 18000000 | tf_op jit(solution)/shard_map/partial_context_grad/pallas_call | solution.py:173
  35.0 1.0 collective-permute-start.13
  36.0 2.7 %collective-permute-start.20 = (bf16[16,32,512]{2,1,0:T(8,128)(2,1)}, bf16[16,32,512]{2,1,0:T(8,128)(2,1)}, u32[]{:S(2)}, u32[]{:S(2)}) collective-permute-start(bf16[16,32,512]{2,1,0:T(8,128)(2,1)} %all-to-all-done.2.a0), channel_id=1, source_target_pairs={{0,6},{1,7},{2,0},{3,1},{4,2},{5,3},{6,4},{7,5},{8,14},{9,15},{10,... | collective-permute-start | bytes 1572872 | tf_op jit(solution)/shard_map/ppermute | solution.py:154
  38.7 6.9 %all-to-all-start = ((bf16[16,32,512]{2,1,0:T(8,128)(2,1)}), bf16[16,32,512]{2,1,0:T(8,128)(2,1)}, u32[]{:S(2)}, u32[]{:S(2)}) async-start(bf16[16,32,512]{2,1,0:T(8,128)(2,1)} %x_ref.1), calls=%async_computation | async-start | bytes 1048576 | tf_op jit(solution)/shard_map/all_to_all | solution.py:160
  45.6 0.7 collective-permute-start.10
  46.3 0.1 collective-permute-start.12
  46.4 10.6 %all-to-all-done.a0 = bf16[16,32,512]{2,1,0:T(8,128)(2,1)} async-done(((bf16[16,32,512]{2,1,0:T(8,128)(2,1)}), bf16[16,32,512]{2,1,0:T(8,128)(2,1)}, u32[]{:S(2)}, u32[]{:S(2)}) %all-to-all-start) | async-done | bytes 524320 | tf_op jit(solution)/shard_map/all_to_all | solution.py:160
  57.1 4.4 %collective-permute-start.9 = (f32[16,32,512]{2,1,0:T(8,128)}, f32[16,32,512]{2,1,0:T(8,128)S(1)}, u32[]{:S(2)}, u32[]{:S(2)}) collective-permute-start(f32[16,32,512]{2,1,0:T(8,128)} %get-tuple-element.9), channel_id=1, source_target_pairs={{0,1},{1,0},{2,3},{3,2},{4,5},{5,4},{6,7},{7,6},{8,9},{9,8},{10,11... | collective-permute-start | bytes 3145736 | tf_op jit(solution)/shard_map/ppermute | solution.py:157
  61.5 1.4 slice_add_fusion.4
  63.0 1.7 collective-permute-start.14
  64.7 1.8 collective-permute-done.1.ap
  66.4 1.5 collective-permute-start.17
  67.9 5.8 %collective-permute-start.4 = (bf16[16,32,512]{2,1,0:T(8,128)(2,1)}, bf16[16,32,512]{2,1,0:T(8,128)(2,1)S(1)}, u32[]{:S(2)}, u32[]{:S(2)}) collective-permute-start(bf16[16,32,512]{2,1,0:T(8,128)(2,1)} %all-to-all-done.a0), channel_id=1, source_target_pairs={{0,1},{1,0},{2,3},{3,2},{4,5},{5,4},{6,7},{7,6},{8,9},{9,8},{10,11... | collective-permute-start | bytes 1572872 | tf_op jit(solution)/shard_map/ppermute | solution.py:157
  73.7 1.7 collective-permute-start
  75.4 1.0 slice.91
  76.4 1.4 collective-permute-done.14
  77.7 1.4 collective-permute-start.3
  79.1 0.6 slice_add_fusion.6
  79.8 1.3 collective-permute-start.11
  81.1 8.1 %collective-permute-done.am = bf16[16,32,512]{2,1,0:T(8,128)(2,1)S(1)} collective-permute-done((bf16[16,32,512]{2,1,0:T(8,128)(2,1)}, bf16[16,32,512]{2,1,0:T(8,128)(2,1)S(1)}, u32[]{:S(2)}, u32[]{:S(2)}) %collective-permute-start) | collective-permute-done | bytes 524320 | tf_op jit(solution)/shard_map/ppermute | solution.py:154
  89.3 1.5 collective-permute-start.16
  90.7 0.3 collective-permute-start.15
  91.1 0.7 collective-permute-done.3.a2b
  91.7 0.6 collective-permute-start.2
  92.3 28.1 %collective-permute-done.2.a2a = bf16[8,32,512]{2,1,0:T(8,128)(2,1)} collective-permute-done((bf16[8,32,512]{2,1,0:T(8,128)(2,1)S(1)}, bf16[8,32,512]{2,1,0:T(8,128)(2,1)}, u32[]{:S(2)}, u32[]{:S(2)}) %collective-permute-start.2) | collective-permute-done | bytes 262176 | tf_op jit(solution)/shard_map/ppermute | solution.py:154
  120.4 1.4 collective-permute-start.6
  121.8 1.0 slice.90
  122.8 0.3 collective-permute-start.21
  123.1 0.3 collective-permute-start.5
  123.4 0.2 collective-permute-start.8
  123.6 0.3 collective-permute-start.7
  123.9 0.5 fusion.7
  124.4 7.7 %collective-permute-done.21.a2a = bf16[8,32,512]{2,1,0:T(8,128)(2,1)} collective-permute-done((bf16[8,32,512]{2,1,0:T(8,128)(2,1)S(1)}, bf16[8,32,512]{2,1,0:T(8,128)(2,1)}, u32[]{:S(2)}, u32[]{:S(2)}) %collective-permute-start.21) | collective-permute-done | bytes 262176 | tf_op jit(solution)/shard_map/ppermute | solution.py:154
  132.2 0.8 collective-permute-start.23
  132.9 0.1 collective-permute-start.25
  133.0 0.7 collective-permute-start.24
  133.7 0.8 pad_maximum_fusion
  134.6 5.2 %all-to-all-start.1 = ((bf16[16,32,512]{2,1,0:T(8,128)(2,1)}), bf16[16,32,512]{2,1,0:T(8,128)(2,1)S(1)}, u32[]{:S(2)}, u32[]{:S(2)}) async-start(bf16[16,32,512]{2,1,0:T(8,128)(2,1)} %pad_maximum_fusion), calls=%async_computation.1 | async-start | bytes 1048576 | tf_op jit(solution)/shard_map/all_to_all | solution.py:160
  139.8 0.4 collective-permute-start.27
  140.2 0.2 collective-permute-start.26
  140.4 0.6 copy-done.6
  141.0 24.1 %outputs.1 = bf16[256,1024]{1,0:T(8,128)(2,1)} custom-call(s32[1]{0:T(128)} %bitcast.pos, s32[8,8,34]{2,1,0:T(8,128)} %rows.5, s32[8,8,34]{2,1,0:T(8,128)} %cols.5, s32[8,8]{1,0:T(8,128)} %live.5, bf16[16,32,512]{2,1,0:T(8,128)(2,1)} %all-to-all-done.a0, bf16[16,32,512]{2,1,0:T(8,128)(2,1)} %copy-done.2, bf16[16,32,512]{2,1,0:T(8,128)(2,1)} %copy-done.1, ...), custom_call_target="tpu_custom_call" | custom-call | flops 4300000256 | bytes 14000000 | tf_op jit(solution)/shard_map/outputs/pallas_call | solution.py:203
  165.2 0.7 copy-done.5
  166.0 24.6 %weight_grad.1 = bf16[1,8,34,8,128]{4,3,2,1,0:T(8,128)(2,1)} custom-call(s32[1]{0:T(128)} %bitcast.pos, s32[8,8,34]{2,1,0:T(8,128)} %rows.5, s32[8,8,34]{2,1,0:T(8,128)} %cols.5, s32[8,8]{1,0:T(8,128)} %live.5, bf16[16,32,512]{2,1,0:T(8,128)(2,1)} %all-to-all-done.2.a0, bf16[16,32,512]{2,1,0:T(8,128)(2,1)} %collective-permute-done.19.am, ...), custom_call_target="tpu_custom_call" | custom-call | flops 4300000256 | bytes 14000000 | tf_op jit(solution)/shard_map/weight_grad/pallas_call | solution.py:241
  190.6 0.8 copy.10
  (50 shorter events, 0.2 us)
Async XLA Ops:
  7.2 158.1 %all-gather.2.cloned.1.call-start = ((), (), s32[]{:S(2)}) async-start(), calls=%async_computation.3 | async-start | bytes 8912896 | tf_op jit(solution)/shard_map/all_gather | solution.py:229
  9.9 26.1 %all-to-all-start.2 = ((bf16[16,32,512]{2,1,0:T(8,128)(2,1)}), bf16[16,32,512]{2,1,0:T(8,128)(2,1)}, u32[]{:S(2)}, u32[]{:S(2)}) async-start(bf16[16,32,512]{2,1,0:T(8,128)(2,1)} %feature_rows.1), calls=%async_computation.2 | async-start | bytes 1048576 | tf_op jit(solution)/shard_map/all_to_all | solution.py:160
  35.0 22.0 %collective-permute-start.13 = (f32[16,32,512]{2,1,0:T(8,128)}, f32[16,32,512]{2,1,0:T(8,128)S(1)}, u32[]{:S(2)}, u32[]{:S(2)}) collective-permute-start(f32[16,32,512]{2,1,0:T(8,128)} %get-tuple-element.12), channel_id=1, source_target_pairs={{0,1},{1,0},{2,3},{3,2},{4,5},{5,4},{6,7},{7,6},{8,9},{9,8},{10,11... | collective-permute-start | bytes 3145736 | tf_op jit(solution)/shard_map/ppermute | solution.py:157
  36.0 21.0 %collective-permute-start.20 = (bf16[16,32,512]{2,1,0:T(8,128)(2,1)}, bf16[16,32,512]{2,1,0:T(8,128)(2,1)}, u32[]{:S(2)}, u32[]{:S(2)}) collective-permute-start(bf16[16,32,512]{2,1,0:T(8,128)(2,1)} %all-to-all-done.2.a0), channel_id=1, source_target_pairs={{0,6},{1,7},{2,0},{3,1},{4,2},{5,3},{6,4},{7,5},{8,14},{9,15},{10,... | collective-permute-start | bytes 1572872 | tf_op jit(solution)/shard_map/ppermute | solution.py:154
  38.7 18.3 %all-to-all-start = ((bf16[16,32,512]{2,1,0:T(8,128)(2,1)}), bf16[16,32,512]{2,1,0:T(8,128)(2,1)}, u32[]{:S(2)}, u32[]{:S(2)}) async-start(bf16[16,32,512]{2,1,0:T(8,128)(2,1)} %x_ref.1), calls=%async_computation | async-start | bytes 1048576 | tf_op jit(solution)/shard_map/all_to_all | solution.py:160
  45.6 22.3 %collective-permute-start.10 = (f32[16,32,512]{2,1,0:T(8,128)}, f32[16,32,512]{2,1,0:T(8,128)S(1)}, u32[]{:S(2)}, u32[]{:S(2)}) collective-permute-start(f32[16,32,512]{2,1,0:T(8,128)} %get-tuple-element.10), channel_id=1, source_target_pairs={{0,1},{1,0},{2,3},{3,2},{4,5},{5,4},{6,7},{7,6},{8,9},{9,8},{10,11... | collective-permute-start | bytes 3145736 | tf_op jit(solution)/shard_map/ppermute | solution.py:157
  46.3 27.4 %collective-permute-start.12 = (f32[16,32,512]{2,1,0:T(8,128)}, f32[16,32,512]{2,1,0:T(8,128)S(1)}, u32[]{:S(2)}, u32[]{:S(2)}) collective-permute-start(f32[16,32,512]{2,1,0:T(8,128)} %get-tuple-element.11), channel_id=1, source_target_pairs={{0,1},{1,0},{2,3},{3,2},{4,5},{5,4},{6,7},{7,6},{8,9},{9,8},{10,11... | collective-permute-start | bytes 3145736 | tf_op jit(solution)/shard_map/ppermute | solution.py:157
  46.4 16.6 %collective-permute-start.19 = (bf16[16,32,512]{2,1,0:T(8,128)(2,1)}, bf16[16,32,512]{2,1,0:T(8,128)(2,1)}, u32[]{:S(2)}, u32[]{:S(2)}) collective-permute-start(bf16[16,32,512]{2,1,0:T(8,128)(2,1)} %all-to-all-done.2.a0), channel_id=1, source_target_pairs={{0,2},{1,3},{2,4},{3,5},{4,6},{5,7},{6,0},{7,1},{8,10},{9,11},{10,... | collective-permute-start | bytes 1572872 | tf_op jit(solution)/shard_map/ppermute | solution.py:154
  57.1 22.1 %copy-start = (f32[4,16,32,512]{3,2,1,0:T(8,128)S(1)}, f32[4,16,32,512]{3,2,1,0:T(8,128)}, u32[]{:S(2)}) copy-start(f32[4,16,32,512]{3,2,1,0:T(8,128)} %get-tuple-element.8) | copy-start | bytes 12582916
  57.1 9.4 %collective-permute-start.1 = (bf16[16,32,512]{2,1,0:T(8,128)(2,1)}, bf16[16,32,512]{2,1,0:T(8,128)(2,1)S(1)}, u32[]{:S(2)}, u32[]{:S(2)}) collective-permute-start(bf16[16,32,512]{2,1,0:T(8,128)(2,1)} %all-to-all-done.a0), channel_id=1, source_target_pairs={{0,6},{1,7},{2,0},{3,1},{4,2},{5,3},{6,4},{7,5},{8,14},{9,15},{10,... | collective-permute-start | bytes 1572872 | tf_op jit(solution)/shard_map/ppermute | solution.py:154
  57.1 32.2 %collective-permute-start.9 = (f32[16,32,512]{2,1,0:T(8,128)}, f32[16,32,512]{2,1,0:T(8,128)S(1)}, u32[]{:S(2)}, u32[]{:S(2)}) collective-permute-start(f32[16,32,512]{2,1,0:T(8,128)} %get-tuple-element.9), channel_id=1, source_target_pairs={{0,1},{1,0},{2,3},{3,2},{4,5},{5,4},{6,7},{7,6},{8,9},{9,8},{10,11... | collective-permute-start | bytes 3145736 | tf_op jit(solution)/shard_map/ppermute | solution.py:157
  63.0 14.8 %collective-permute-start.14 = (f32[8,32,512]{2,1,0:T(8,128)S(1)}, f32[8,32,512]{2,1,0:T(8,128)S(1)}, u32[]{:S(2)}, u32[]{:S(2)}) collective-permute-start(f32[8,32,512]{2,1,0:T(8,128)S(1)} %get-tuple-element.19), channel_id=1, source_target_pairs={{0,2},{1,3},{2,4},{3,5},{4,6},{5,7},{6,0},{7,1},{8,10},{9,11},{10,... | collective-permute-start | bytes 1572872 | tf_op jit(solution)/shard_map/ppermute | solution.py:154
  66.4 54.0 %copy-start.1 = (bf16[16,32,512]{2,1,0:T(8,128)(2,1)}, bf16[16,32,512]{2,1,0:T(8,128)(2,1)S(1)}, u32[]{:S(2)}) copy-start(bf16[16,32,512]{2,1,0:T(8,128)(2,1)S(1)} %collective-permute-done.1.ap) | copy-start | bytes 1572868
  66.4 11.3 %collective-permute-start.17 = (f32[8,32,512]{2,1,0:T(8,128)S(1)}, f32[8,32,512]{2,1,0:T(8,128)S(1)}, u32[]{:S(2)}, u32[]{:S(2)}) collective-permute-start(f32[8,32,512]{2,1,0:T(8,128)S(1)} %get-tuple-element.20), channel_id=1, source_target_pairs={{0,6},{1,7},{2,0},{3,1},{4,2},{5,3},{6,4},{7,5},{8,14},{9,15},{10,... | collective-permute-start | bytes 1572872 | tf_op jit(solution)/shard_map/ppermute | solution.py:154
  67.9 11.8 %collective-permute-start.4 = (bf16[16,32,512]{2,1,0:T(8,128)(2,1)}, bf16[16,32,512]{2,1,0:T(8,128)(2,1)S(1)}, u32[]{:S(2)}, u32[]{:S(2)}) collective-permute-start(bf16[16,32,512]{2,1,0:T(8,128)(2,1)} %all-to-all-done.a0), channel_id=1, source_target_pairs={{0,1},{1,0},{2,3},{3,2},{4,5},{5,4},{6,7},{7,6},{8,9},{9,8},{10,11... | collective-permute-start | bytes 1572872 | tf_op jit(solution)/shard_map/ppermute | solution.py:157
  73.7 15.5 %collective-permute-start = (bf16[16,32,512]{2,1,0:T(8,128)(2,1)}, bf16[16,32,512]{2,1,0:T(8,128)(2,1)S(1)}, u32[]{:S(2)}, u32[]{:S(2)}) collective-permute-start(bf16[16,32,512]{2,1,0:T(8,128)(2,1)} %all-to-all-done.a0), channel_id=1, source_target_pairs={{0,2},{1,3},{2,4},{3,5},{4,6},{5,7},{6,0},{7,1},{8,10},{9,11},{10,... | collective-permute-start | bytes 1572872 | tf_op jit(solution)/shard_map/ppermute | solution.py:154
  77.7 13.0 %collective-permute-start.22 = (bf16[8,32,512]{2,1,0:T(8,128)(2,1)S(1)}, bf16[8,32,512]{2,1,0:T(8,128)(2,1)S(1)}, u32[]{:S(2)}, u32[]{:S(2)}) collective-permute-start(bf16[8,32,512]{2,1,0:T(8,128)(2,1)S(1)} %slice.91), channel_id=1, source_target_pairs={{0,6},{1,7},{2,0},{3,1},{4,2},{5,3},{6,4},{7,5},{8,14},{9,15},{10,... | collective-permute-start | bytes 786440 | tf_op jit(solution)/shard_map/ppermute | solution.py:154
  77.7 14.0 %collective-permute-start.3 = (bf16[8,32,512]{2,1,0:T(8,128)(2,1)S(1)}, bf16[8,32,512]{2,1,0:T(8,128)(2,1)S(1)}, u32[]{:S(2)}, u32[]{:S(2)}) collective-permute-start(bf16[8,32,512]{2,1,0:T(8,128)(2,1)S(1)} %slice.81), channel_id=1, source_target_pairs={{0,6},{1,7},{2,0},{3,1},{4,2},{5,3},{6,4},{7,5},{8,14},{9,15},{10,... | collective-permute-start | bytes 786440 | tf_op jit(solution)/shard_map/ppermute | solution.py:154
  79.8 60.6 %copy-start.3 = (bf16[16,32,512]{2,1,0:T(8,128)(2,1)}, bf16[16,32,512]{2,1,0:T(8,128)(2,1)S(1)}, u32[]{:S(2)}) copy-start(bf16[16,32,512]{2,1,0:T(8,128)(2,1)S(1)} %collective-permute-done.4.b0) | copy-start | bytes 1572868
  79.8 43.0 %collective-permute-start.11 = (f32[8,32,512]{2,1,0:T(8,128)S(1)}, f32[8,32,512]{2,1,0:T(8,128)S(1)}, u32[]{:S(2)}, u32[]{:S(2)}) collective-permute-start(f32[8,32,512]{2,1,0:T(8,128)S(1)} %get-tuple-element.15), channel_id=1, source_target_pairs={{0,6},{1,7},{2,0},{3,1},{4,2},{5,3},{6,4},{7,5},{8,14},{9,15},{10,... | collective-permute-start | bytes 1572872 | tf_op jit(solution)/shard_map/ppermute | solution.py:154
  89.3 51.1 %copy-start.2 = (bf16[16,32,512]{2,1,0:T(8,128)(2,1)}, bf16[16,32,512]{2,1,0:T(8,128)(2,1)S(1)}, u32[]{:S(2)}) copy-start(bf16[16,32,512]{2,1,0:T(8,128)(2,1)S(1)} %collective-permute-done.am) | copy-start | bytes 1572868
  89.3 33.8 %collective-permute-start.18 = (f32[8,32,512]{2,1,0:T(8,128)S(1)}, f32[8,32,512]{2,1,0:T(8,128)S(1)}, u32[]{:S(2)}, u32[]{:S(2)}) collective-permute-start(f32[8,32,512]{2,1,0:T(8,128)S(1)} %get-tuple-element.16), channel_id=1, source_target_pairs={{0,6},{1,7},{2,0},{3,1},{4,2},{5,3},{6,4},{7,5},{8,14},{9,15},{10,... | collective-permute-start | bytes 1572872 | tf_op jit(solution)/shard_map/ppermute | solution.py:154
  89.3 34.1 %collective-permute-start.16 = (f32[8,32,512]{2,1,0:T(8,128)S(1)}, f32[8,32,512]{2,1,0:T(8,128)S(1)}, u32[]{:S(2)}, u32[]{:S(2)}) collective-permute-start(f32[8,32,512]{2,1,0:T(8,128)S(1)} %get-tuple-element.21), channel_id=1, source_target_pairs={{0,2},{1,3},{2,4},{3,5},{4,6},{5,7},{6,0},{7,1},{8,10},{9,11},{10,... | collective-permute-start | bytes 1572872 | tf_op jit(solution)/shard_map/ppermute | solution.py:154
  90.7 74.4 %copy-start.7 = (bf16[8,32,512]{2,1,0:T(8,128)(2,1)}, bf16[8,32,512]{2,1,0:T(8,128)(2,1)S(1)}, u32[]{:S(2)}) copy-start(bf16[8,32,512]{2,1,0:T(8,128)(2,1)S(1)} %collective-permute-done.22.a2b) | copy-start | bytes 786436
  90.7 32.9 %collective-permute-start.15 = (f32[8,32,512]{2,1,0:T(8,128)S(1)}, f32[8,32,512]{2,1,0:T(8,128)S(1)}, u32[]{:S(2)}, u32[]{:S(2)}) collective-permute-start(f32[8,32,512]{2,1,0:T(8,128)S(1)} %get-tuple-element.22), channel_id=1, source_target_pairs={{0,2},{1,3},{2,4},{3,5},{4,6},{5,7},{6,0},{7,1},{8,10},{9,11},{10,... | collective-permute-start | bytes 1572872 | tf_op jit(solution)/shard_map/ppermute | solution.py:154
  91.7 41.3 %copy-start.8 = (bf16[8,32,512]{2,1,0:T(8,128)(2,1)}, bf16[8,32,512]{2,1,0:T(8,128)(2,1)S(1)}, u32[]{:S(2)}) copy-start(bf16[8,32,512]{2,1,0:T(8,128)(2,1)S(1)} %collective-permute-done.3.a2b) | copy-start | bytes 786436
  91.7 28.7 %collective-permute-start.2 = (bf16[8,32,512]{2,1,0:T(8,128)(2,1)S(1)}, bf16[8,32,512]{2,1,0:T(8,128)(2,1)}, u32[]{:S(2)}, u32[]{:S(2)}) collective-permute-start(bf16[8,32,512]{2,1,0:T(8,128)(2,1)S(1)} %slice.80), channel_id=1, source_target_pairs={{0,2},{1,3},{2,4},{3,5},{4,6},{5,7},{6,0},{7,1},{8,10},{9,11},{10,... | collective-permute-start | bytes 786440 | tf_op jit(solution)/shard_map/ppermute | solution.py:154
  120.4 12.6 %collective-permute-start.6 = (bf16[16,32,512]{2,1,0:T(8,128)(2,1)S(1)}, bf16[16,32,512]{2,1,0:T(8,128)(2,1)S(1)}, u32[]{:S(2)}, u32[]{:S(2)}) collective-permute-start(bf16[16,32,512]{2,1,0:T(8,128)(2,1)S(1)} %collective-permute-done.1.ap), channel_id=1, source_target_pairs={{0,1},{1,0},{2,3},{3,2},{4,5},{5,4},{6,7},{7,6},{8,9},{9,8},{10,11... | collective-permute-start | bytes 1572872 | tf_op jit(solution)/shard_map/ppermute | solution.py:157
  122.8 9.3 %collective-permute-start.21 = (bf16[8,32,512]{2,1,0:T(8,128)(2,1)S(1)}, bf16[8,32,512]{2,1,0:T(8,128)(2,1)}, u32[]{:S(2)}, u32[]{:S(2)}) collective-permute-start(bf16[8,32,512]{2,1,0:T(8,128)(2,1)S(1)} %slice.90), channel_id=1, source_target_pairs={{0,2},{1,3},{2,4},{3,5},{4,6},{5,7},{6,0},{7,1},{8,10},{9,11},{10,... | collective-permute-start | bytes 786440 | tf_op jit(solution)/shard_map/ppermute | solution.py:154
  123.1 17.1 %collective-permute-start.5 = (bf16[16,32,512]{2,1,0:T(8,128)(2,1)S(1)}, bf16[16,32,512]{2,1,0:T(8,128)(2,1)S(1)}, u32[]{:S(2)}, u32[]{:S(2)}) collective-permute-start(bf16[16,32,512]{2,1,0:T(8,128)(2,1)S(1)} %collective-permute-done.am), channel_id=1, source_target_pairs={{0,1},{1,0},{2,3},{3,2},{4,5},{5,4},{6,7},{7,6},{8,9},{9,8},{10,11... | collective-permute-start | bytes 1572872 | tf_op jit(solution)/shard_map/ppermute | solution.py:157
  123.4 9.6 %collective-permute-start.8 = (bf16[8,32,512]{2,1,0:T(8,128)(2,1)S(1)}, bf16[8,32,512]{2,1,0:T(8,128)(2,1)S(1)}, u32[]{:S(2)}, u32[]{:S(2)}) collective-permute-start(bf16[8,32,512]{2,1,0:T(8,128)(2,1)S(1)} %collective-permute-done.3.a2b), channel_id=1, source_target_pairs={{0,1},{1,0},{2,3},{3,2},{4,5},{5,4},{6,7},{7,6},{8,9},{9,8},{10,11... | collective-permute-start | bytes 786440 | tf_op jit(solution)/shard_map/ppermute | solution.py:157
  123.6 16.1 %collective-permute-start.7 = (bf16[8,32,512]{2,1,0:T(8,128)(2,1)}, bf16[8,32,512]{2,1,0:T(8,128)(2,1)}, u32[]{:S(2)}, u32[]{:S(2)}) collective-permute-start(bf16[8,32,512]{2,1,0:T(8,128)(2,1)} %collective-permute-done.2.a2a), channel_id=1, source_target_pairs={{0,1},{1,0},{2,3},{3,2},{4,5},{5,4},{6,7},{7,6},{8,9},{9,8},{10,11... | collective-permute-start | bytes 786440 | tf_op jit(solution)/shard_map/ppermute | solution.py:157
  132.2 33.0 %collective-permute-start.23 = (bf16[16,32,512]{2,1,0:T(8,128)(2,1)}, bf16[16,32,512]{2,1,0:T(8,128)(2,1)S(1)}, u32[]{:S(2)}, u32[]{:S(2)}) collective-permute-start(bf16[16,32,512]{2,1,0:T(8,128)(2,1)} %all-to-all-done.2.a0), channel_id=1, source_target_pairs={{0,1},{1,0},{2,3},{3,2},{4,5},{5,4},{6,7},{7,6},{8,9},{9,8},{10,11... | collective-permute-start | bytes 1572872 | tf_op jit(solution)/shard_map/ppermute | solution.py:157
  132.9 0.8 copy-start.9
  132.9 32.2 %collective-permute-start.25 = (bf16[16,32,512]{2,1,0:T(8,128)(2,1)}, bf16[16,32,512]{2,1,0:T(8,128)(2,1)}, u32[]{:S(2)}, u32[]{:S(2)}) collective-permute-start(bf16[16,32,512]{2,1,0:T(8,128)(2,1)} %collective-permute-done.20.ap), channel_id=1, source_target_pairs={{0,1},{1,0},{2,3},{3,2},{4,5},{5,4},{6,7},{7,6},{8,9},{9,8},{10,11... | collective-permute-start | bytes 1572872 | tf_op jit(solution)/shard_map/ppermute | solution.py:157
  133.0 7.3 %copy-start.4 = (bf16[16,32,512]{2,1,0:T(8,128)(2,1)}, bf16[16,32,512]{2,1,0:T(8,128)(2,1)S(1)}, u32[]{:S(2)}) copy-start(bf16[16,32,512]{2,1,0:T(8,128)(2,1)S(1)} %collective-permute-done.6.bp) | copy-start | bytes 1572868
  133.0 32.2 %collective-permute-start.24 = (bf16[16,32,512]{2,1,0:T(8,128)(2,1)}, bf16[16,32,512]{2,1,0:T(8,128)(2,1)}, u32[]{:S(2)}, u32[]{:S(2)}) collective-permute-start(bf16[16,32,512]{2,1,0:T(8,128)(2,1)} %collective-permute-done.19.am), channel_id=1, source_target_pairs={{0,1},{1,0},{2,3},{3,2},{4,5},{5,4},{6,7},{7,6},{8,9},{9,8},{10,11... | collective-permute-start | bytes 1572872 | tf_op jit(solution)/shard_map/ppermute | solution.py:157
  134.6 30.6 %all-to-all-start.1 = ((bf16[16,32,512]{2,1,0:T(8,128)(2,1)}), bf16[16,32,512]{2,1,0:T(8,128)(2,1)S(1)}, u32[]{:S(2)}, u32[]{:S(2)}) async-start(bf16[16,32,512]{2,1,0:T(8,128)(2,1)} %pad_maximum_fusion), calls=%async_computation.1 | async-start | bytes 1048576 | tf_op jit(solution)/shard_map/all_to_all | solution.py:160
  139.8 25.4 %collective-permute-start.27 = (bf16[8,32,512]{2,1,0:T(8,128)(2,1)S(1)}, bf16[8,32,512]{2,1,0:T(8,128)(2,1)}, u32[]{:S(2)}, u32[]{:S(2)}) collective-permute-start(bf16[8,32,512]{2,1,0:T(8,128)(2,1)S(1)} %collective-permute-done.22.a2b), channel_id=1, source_target_pairs={{0,1},{1,0},{2,3},{3,2},{4,5},{5,4},{6,7},{7,6},{8,9},{9,8},{10,11... | collective-permute-start | bytes 786440 | tf_op jit(solution)/shard_map/ppermute | solution.py:157
  140.2 0.8 copy-start.6
  140.2 25.0 %collective-permute-start.26 = (bf16[8,32,512]{2,1,0:T(8,128)(2,1)}, bf16[8,32,512]{2,1,0:T(8,128)(2,1)}, u32[]{:S(2)}, u32[]{:S(2)}) collective-permute-start(bf16[8,32,512]{2,1,0:T(8,128)(2,1)} %collective-permute-done.21.a2a), channel_id=1, source_target_pairs={{0,1},{1,0},{2,3},{3,2},{4,5},{5,4},{6,7},{7,6},{8,9},{9,8},{10,11... | collective-permute-start | bytes 786440 | tf_op jit(solution)/shard_map/ppermute | solution.py:157
  165.2 0.8 copy-start.5
Sparse Core Ops, SparseCore 0:
  10.1 79.5 all-gather.1

commit v2 on v1

v2 whole, which is shorter than its diff:
```python
import functools
import math

import jax
import jax.numpy as jnp
from jax import lax
from jax.experimental import pallas as pl
from jax.experimental.pallas import tpu as pltpu
from jax.sharding import PartitionSpec as P

F32 = jnp.float32
BF16 = jnp.bfloat16
VMEM_LIMIT = 60 * 1024 * 1024


def build_panel(panel, blk_ref, rows_ref, cols_ref, live_ref, owner, j):
    panel[...] = jnp.zeros_like(panel)
    count = live_ref[owner, j]
    for k in range(34):

        def place(k=k):
            r = pl.multiple_of((rows_ref[owner, j, k] - 8 * j) * 128, 128)
            c = pl.multiple_of((cols_ref[owner, j, k] - 8 * owner) * 128, 128)
            panel[pl.ds(r, 128), pl.ds(c, 128)] = blk_ref[0, 0, k]

        if k < 30:
            place()
        else:
            pl.when(k < count)(place)


def transpose_kernel(x_ref, o_ref):
    x = x_ref[...].reshape(512, 512).astype(F32)
    t = x.T.reshape(4, 16, 8, 512)
    for part in range(16):
        o_ref[part, pl.ds(0, 32)] = x_ref[part]
        o_ref[part, pl.ds(32, 32)] = t[:, part].reshape(32, 512).astype(BF16)


def partial_kernel(pos, rows, cols, live, cot_ref, blk_ref, keep, send0, send1, send2, send3, lhs, panel):
    j = pl.program_id(0)
    owner = pos[0]
    y = owner // 2
    core = owner % 2
    sends = (send0, send1, send2, send3)

    @pl.when(j == 0)
    def _():
        for d in range(4):
            group = (y + d) % 4
            lhs[pl.ds(d * 32, 32)] = cot_ref[group, core]
            lhs[pl.ds(128 + d * 32, 32)] = cot_ref[group, 1 - core]

    build_panel(panel, blk_ref, rows, cols, live, owner, j)
    res = lax.dot_general(lhs[...], panel[...], (((1,), (1,)), ((), ())), preferred_element_type=F32)
    for half in range(2):
        lanes = slice(half * 512, half * 512 + 512)
        for d in range(4):
            keep[d, half] = res[d * 32 : d * 32 + 32, lanes]
            sends[d][half] = res[128 + d * 32 : 128 + d * 32 + 32, lanes]


def place_chunks(lhs, group, core, x, halves):
    start = pl.multiple_of((group * 2 + core) * 32, 32)
    for h in range(halves):
        lhs[pl.ds(start, 32), pl.ds(h * 512, 512)] = x[h]


def out_kernel(pos, rows, cols, live, a0, am, ap, a2a, a2b, b0, bm, bp, b2a, b2b, blk_ref, out_ref, lhs, panel, acc):
    j = pl.program_id(0)
    owner = pos[0]
    y = owner // 2
    core = owner % 2
    for who, (x0, xm, xp, x2a, x2b) in ((core, (a0, am, ap, a2a, a2b)), (1 - core, (b0, bm, bp, b2a, b2b))):
        place_chunks(lhs, y, who, x0, 2)
        place_chunks(lhs, (y + 3) % 4, who, xm, 2)
        place_chunks(lhs, (y + 1) % 4, who, xp, 2)

        @pl.when(j < 4)
        def _():
            place_chunks(lhs, (y + 2) % 4, who, x2a, 2)

        @pl.when(j >= 4)
        def _():
            place_chunks(lhs, (y + 2) % 4, who, x2b, 2)

    @pl.when(j == 0)
    def _():
        acc[...] = jnp.zeros_like(acc)

    build_panel(panel, blk_ref, rows, cols, live, owner, j)
    acc[...] += jnp.dot(lhs[...], panel[...], preferred_element_type=F32)

    @pl.when(j == 7)
    def _():
        out_ref[...] = acc[...].astype(BF16)


def near_grad_kernel(pos, a0, am, ap, b0, bm, bp, g_ref, acc, lhs):
    i = pl.program_id(0)
    for at, piece in enumerate((a0, am, ap, b0, bm, bp)):

        @pl.when(i == at)
        def _(piece=piece):
            lhs[...] = piece[...].reshape(512, 512)

    @pl.when(i == 0)
    def _():
        acc[...] = jnp.zeros_like(acc)

    res = jnp.dot(lhs[...], g_ref[...].reshape(512, 1024), preferred_element_type=F32)
    acc[...] += res.reshape(64, 8, 1024)


def far_grad_kernel(scale, pos, rows, cols, live, a2a, a2b, b2a, b2b, g_ref, near_ref, out_ref, lhs, acc):
    i = pl.program_id(0)
    owner = pos[0]
    for at, (first, second) in enumerate(((a2a, a2b), (b2a, b2b))):

        @pl.when(i == at)
        def _(first=first, second=second):
            lhs[pl.ds(0, 256)] = first[...].reshape(256, 512)
            lhs[pl.ds(256, 256)] = second[...].reshape(256, 512)

    @pl.when(i == 0)
    def _():
        acc[...] = near_ref[...]

    res = jnp.dot(lhs[...], g_ref[...].reshape(512, 1024), preferred_element_type=F32)
    acc[...] += res.reshape(64, 8, 1024)

    @pl.when(i == 1)
    def _():
        def pick(j, carry):
            count = live[owner, j]
            for k in range(34):
                r = rows[owner, j, k]
                c = pl.multiple_of((cols[owner, j, k] - 8 * owner) * 128, 128)
                tile = acc[r, :, pl.ds(c, 128)] * scale
                if k >= 30:
                    tile = jnp.where(k < count, tile, 0.0)
                out_ref[0, j, k] = tile.astype(BF16)
            return carry

        lax.fori_loop(0, 8, pick, 0)


def on_device(context, blocks, row_blocks, col_blocks, live_counts, cotangent):
    owner = lax.axis_index("mp")
    pos = owner.astype(jnp.int32).reshape(1)
    tables = (pos, row_blocks, col_blocks, live_counts)
    params = pltpu.CompilerParams(vmem_limit_bytes=VMEM_LIMIT)
    barrier = lax.optimization_barrier

    def cost(flops, size):
        return pl.CostEstimate(flops=flops, bytes_accessed=size, transcendentals=0)

    def along_y(x, step):
        return lax.ppermute(x, "mp", [(i, (i + 2 * step) % 8) for i in range(8)])

    def other_core(x):
        return lax.ppermute(x, "mp", [(i, i ^ 1) for i in range(8)])

    def exchange(x):
        return lax.all_to_all(x, "seq", split_axis=0, concat_axis=0, tiled=True)

    cot_all = lax.all_gather(cotangent, "seq", axis=0, tiled=True)

    both = pl.pallas_call(
        transpose_kernel,
        out_shape=jax.ShapeDtypeStruct((16, 64, 512), BF16),
        compiler_params=params,
        name="feature_rows",
    )(context)
    both = exchange(both)
    tokens, class_rows = both[:, :32], both[:, 32:]

    blk_spec = pl.BlockSpec((1, 1, 34, 128, 128), lambda j, *_: (0, j, 0, 0, 0))
    part = jax.ShapeDtypeStruct((16, 32, 512), F32)
    part_spec = pl.BlockSpec((2, 32, 512), lambda j, *_: (j, 0, 0))
    keep, *sends = pl.pallas_call(
        partial_kernel,
        grid_spec=pltpu.PrefetchScalarGridSpec(
            num_scalar_prefetch=4,
            grid=(8,),
            in_specs=[pl.BlockSpec((4, 2, 32, 1024), lambda j, *_: (0, 0, 0, 0)), blk_spec],
            out_specs=[pl.BlockSpec((4, 2, 32, 512), lambda j, *_: (0, j, 0, 0))] + [part_spec] * 4,
            scratch_shapes=[pltpu.VMEM((256, 1024), BF16), pltpu.VMEM((1024, 1024), BF16)],
        ),
        out_shape=[jax.ShapeDtypeStruct((4, 16, 32, 512), F32)] + [part] * 4,
        compiler_params=params,
        cost_estimate=cost(4_300_000_000, 18_000_000),
        name="partial_context_grad",
    )(*tables, cotangent.reshape(4, 2, 32, 1024), blocks)
    r2, r1, r3, r0 = (other_core(sends[d]) for d in (2, 1, 3, 0))

    xm, xp = along_y(tokens, 1), along_y(tokens, -1)

    q2a, q2b = keep[2, :8] + r2[:8], keep[2, 8:] + r2[8:]
    q1b, q3a = keep[1, 8:] + r1[8:], keep[3, :8] + r3[:8]
    q2a, q2b, q1b, q3a, class_rows = barrier((q2a, q2b, q1b, q3a, class_rows))
    from_a, from_b = along_y(q2a, 1), along_y(q2b, -1)
    near_b, near_a = along_y(q1b, 1), along_y(q3a, -1)

    x2a, x2b = along_y(xm[:8], 1), along_y(xp[8:], -1)
    own = (tokens, xm, xp, x2a, x2b)
    x_pieces = own + tuple(other_core(piece) for piece in own)

    cm, cp = along_y(class_rows, 1), along_y(class_rows, -1)

    q1a, q3b = keep[1, :8] + r1[:8] + from_a, keep[3, 8:] + r3[8:] + from_b
    q1a, q3b, x_pieces = barrier((q1a, q3b, x_pieces))
    far_a, far_b = along_y(q1a, 1), along_y(q3b, -1)

    whole = pl.BlockSpec((2, 32, 512), lambda j, *_: (j, 0, 0))
    low = pl.BlockSpec((2, 32, 512), lambda j, *_: (jnp.minimum(j, 3), 0, 0))
    high = pl.BlockSpec((2, 32, 512), lambda j, *_: (jnp.maximum(j - 4, 0), 0, 0))
    outputs = pl.pallas_call(
        out_kernel,
        grid_spec=pltpu.PrefetchScalarGridSpec(
            num_scalar_prefetch=4,
            grid=(8,),
            in_specs=[whole, whole, whole, low, high] * 2 + [blk_spec],
            out_specs=pl.BlockSpec((256, 1024), lambda j, *_: (0, 0)),
            scratch_shapes=[
                pltpu.VMEM((256, 1024), BF16),
                pltpu.VMEM((1024, 1024), BF16),
                pltpu.VMEM((256, 1024), F32),
            ],
        ),
        out_shape=jax.ShapeDtypeStruct((256, 1024), BF16),
        compiler_params=params,
        cost_estimate=cost(4_300_000_000, 14_000_000),
        name="outputs",
    )(*tables, *x_pieces, blocks)

    outputs, cm, cp = barrier((outputs, cm, cp))
    c2a, c2b = along_y(cm[:8], 1), along_y(cp[8:], -1)

    near = (class_rows, cm, cp)
    near = near + tuple(other_core(piece) for piece in near)
    full = pl.BlockSpec((16, 32, 512), lambda i, *_: (0, 0, 0))
    part8 = pl.BlockSpec((8, 32, 512), lambda i, *_: (0, 0, 0))
    cot_groups = cot_all.reshape(16, 8, 32, 1024)

    def group(owner, chip_step, core_step):
        return lax.rem(lax.div(owner, 2) + chip_step, 4) * 2 + lax.rem(owner + core_step, 2)

    def near_group(i, pos):
        step = lax.rem(i, 3)
        chip_step = jnp.where(step == 1, 3, jnp.where(step == 2, 1, 0))
        return (0, group(pos[0], chip_step, lax.div(i, 3)), 0, 0)

    def far_group(i, pos, *_):
        return (0, group(pos[0], 2, i), 0, 0)

    total = jax.ShapeDtypeStruct((64, 8, 1024), F32)
    total_spec = pl.BlockSpec((64, 8, 1024), lambda i, *_: (0, 0, 0))
    near_grad = pl.pallas_call(
        near_grad_kernel,
        grid_spec=pltpu.PrefetchScalarGridSpec(
            num_scalar_prefetch=1,
            grid=(6,),
            in_specs=[full] * 6 + [pl.BlockSpec((16, 1, 32, 1024), near_group)],
            out_specs=total_spec,
            scratch_shapes=[pltpu.VMEM((512, 512), BF16)],
        ),
        out_shape=total,
        compiler_params=params,
        cost_estimate=cost(3_200_000_000, 11_000_000),
        name="near_weight_grad",
    )(pos, *near, cot_groups)

    sum_a = keep[0, :8] + r0[:8] + near_a + far_a
    sum_b = keep[0, 8:] + r0[8:] + near_b + far_b
    context_sum = jnp.concatenate([sum_a, sum_b], axis=0).astype(BF16)
    context_sum, near_grad = barrier((context_sum, near_grad))
    context_grad = exchange(context_sum)

    weight_grad = pl.pallas_call(
        functools.partial(far_grad_kernel, 1.0 / math.sqrt(4096)),
        grid_spec=pltpu.PrefetchScalarGridSpec(
            num_scalar_prefetch=4,
            grid=(2,),
            in_specs=[part8] * 4 + [pl.BlockSpec((16, 1, 32, 1024), far_group), total_spec],
            out_specs=pl.BlockSpec((1, 8, 34, 8, 128), lambda i, *_: (0, 0, 0, 0, 0)),
            scratch_shapes=[pltpu.VMEM((512, 512), BF16), pltpu.VMEM((64, 8, 1024), F32)],
        ),
        out_shape=jax.ShapeDtypeStruct((1, 8, 34, 8, 128), BF16),
        compiler_params=params,
        cost_estimate=cost(1_100_000_000, 6_000_000),
        name="far_weight_grad",
    )(*tables, c2a, c2b, other_core(c2a), other_core(c2b), cot_groups, near_grad)
    return (outputs, context_grad, weight_grad)


def solution(mesh):
    in_specs = (
        P(None, "mp", "seq"),
        P("mp", None, None, None, None),
        P(),
        P(),
        P(),
        P("seq", "mp"),
    )
    out_specs = (P("seq", "mp"), P(None, "mp", "seq"), P("mp", None, None, "seq", None))
    return jax.shard_map(
        on_device, mesh=mesh, in_specs=in_specs, out_specs=out_specs, check_vma=False
    )
```

time: 200 us -> 151 us (0.76)
  waiting for transfers between devices: 59.2 us -> 19.9 us
  Pallas kernels: 67.4 us -> 49.1 us
  other arithmetic: 3.44 us -> 8.42 us
  starting transfers between devices: 49.8 us -> 53.2 us
    ppermute x14, waiting for transfers between devices: 47.8 us -> 16.5 us  [along_y(): return lax.ppermute(x, 'mp', [(i, (i + 2 * step) % 8) for i in range(8)])]
    all_to_all x3 -> x2, waiting for transfers between devices: 10.6 us -> 0.01 us  [exchange(): return lax.all_to_all(x, 'seq', split_axis=0, concat_axis=0, tiled=True)]
    pallas_call x1, Pallas kernels: 24.1 us -> 14.8 us  [on_device(): pl.pallas_call(out_kernel, grid_spec=pltpu.PrefetchScalarGridSpec(num_sca...]
    pallas_call x2 -> x3, Pallas kernels: 26.7 us -> 19 us  [the longest x1 9.41 us: on_device(): pl.pallas_call(near_grad_kernel, grid_spec=pltpu.PrefetchScalarGridSpec(n...]
    all_to_all x3 -> x2, starting transfers between devices: 20.5 us -> 13.9 us  [exchange(): return lax.all_to_all(x, 'seq', split_axis=0, concat_axis=0, tiled=True)]
    ppermute x14, starting transfers between devices: 16.4 us -> 22.8 us  [other_core(): return lax.ppermute(x, 'mp', [(i, i ^ 1) for i in range(8)])]
    ppermute x14, starting transfers between devices: 12.9 us -> 16.5 us  [along_y(): return lax.ppermute(x, 'mp', [(i, (i + 2 * step) % 8) for i in range(8)])]
    add x2, other arithmetic: 2.07 us -> 5.35 us  [the longest x1 2.8 us: on_device(): q1a, q3b = (keep[1, :8] + r1[:8] + from_a, keep[3, 8:] + r3[8:] + from_b)]
  transfers between devices with their start and end apart: 32 -> 31, of which waited for: 7 -> 8; matrix products, arithmetic and copies ran while one was open for 3% -> 7% of each run, Pallas kernels for 22% -> 33%
where the time goes in v2:
time: 151 us; the launch traced here: 150 us
  starting transfers between devices  53.2 us (35%)
  Pallas kernels  49.1 us (33%)
  waiting for transfers between devices  19.9 us (13%)
  between operations  14.3 us (9%)
  other arithmetic  8.42 us (6%)
  local copies, waits for them, and re-layouts  4.8 us (3%)
    ppermute x14, starting transfers between devices, other_core(): return lax.ppermute(x, 'mp', [(i, i ^ 1) for i in range(8)])  22.8 us
    ppermute x14, starting transfers between devices, along_y(): return lax.ppermute(x, 'mp', [(i, (i + 2 * step) % 8) for i in range(8)])  16.5 us
    ppermute x14, waiting for transfers between devices, along_y(): return lax.ppermute(x, 'mp', [(i, (i + 2 * step) % 8) for i in range(8)])  16.5 us
    pallas_call x1, Pallas kernels, on_device(): pl.pallas_call(partial_kernel, grid_spec=pltpu.PrefetchScalarGridSpec(num...  15.3 us
    pallas_call x1, Pallas kernels, on_device(): pl.pallas_call(out_kernel, grid_spec=pltpu.PrefetchScalarGridSpec(num_sca...  14.8 us
    all_to_all x2, starting transfers between devices, exchange(): return lax.all_to_all(x, 'seq', split_axis=0, concat_axis=0, tiled=True)  13.9 us
    pallas_call x1, Pallas kernels, on_device(): pl.pallas_call(near_grad_kernel, grid_spec=pltpu.PrefetchScalarGridSpec(n...  9.41 us
    pallas_call x1, Pallas kernels, on_device(): pl.pallas_call(functools.partial(far_grad_kernel, 1.0 / math.sqrt(4096)),...  7.4 us
  transfers between devices with their start and end apart: 31, of which 8 were waited for; matrix products, arithmetic and copies ran while one was open for 7% of the time, Pallas kernels for 33%

profile of v2, /device:TPU:1, one launch (start us, length us, event | category | flops | bytes accessed | tf_op | source)
XLA Modules:
  0.0 149.7 jit_solution(9958992131115097183)
XLA Ops:
  7.2 0.7 all-gather.2.cloned.1.call-update
  7.9 2.2 %feature_rows.1 = bf16[16,64,512]{2,1,0:T(8,128)(2,1)} custom-call(bf16[16,32,512]{2,1,0:T(8,128)(2,1)} %x_ref.1), custom_call_target="tpu_custom_call" | custom-call | tf_op jit(solution)/shard_map/feature_rows/pallas_call | solution.py:169
  10.1 8.4 %all-to-all-start = ((bf16[16,64,512]{2,1,0:T(8,128)(2,1)}), bf16[16,64,512]{2,1,0:T(8,128)(2,1)S(1)}, u32[]{:S(2)}, u32[]{:S(2)}) async-start(bf16[16,64,512]{2,1,0:T(8,128)(2,1)} %feature_rows.1), calls=%async_computation | async-start | bytes 2097152 | tf_op jit(solution)/shard_map/all_to_all | solution.py:165
  18.6 15.3 %partial_context_grad.1 = (f32[4,16,32,512]{3,2,1,0:T(8,128)}, f32[16,32,512]{2,1,0:T(8,128)}, f32[16,32,512]{2,1,0:T(8,128)}, f32[16,32,512]{2,1,0:T(8,128)}, f32[16,32,512]{2,1,0:T(8,128)}) custom-call(s32[1]{0:T(128)} %bitcast.pos, s32[8,8,34]{2,1,0:T(8,128)} %rows.5, s32[8,8,34]{2,1,0:T(8,128)} %cols.5, s32[8,8]{1,0:T(8,128)} %live.5, ...), custom_call_target="tpu_custom_call" | custom-call | flops 4300000256 | bytes 18000000 | tf_op jit(solution)/shard_map/partial_context_grad/pallas_call | solution.py:181
  33.8 1.0 collective-permute-start.2
  34.9 0.4 collective-permute-start.1
  35.3 0.1 fusion.8
  35.4 1.3 collective-permute-start.5
  36.8 1.5 collective-permute-start.6
  38.3 6.1 %collective-permute-start.9 = (bf16[16,32,512]{2,1,0:T(8,128)(2,1)S(1)}, bf16[16,32,512]{2,1,0:T(8,128)(2,1)S(1)}, u32[]{:S(2)}, u32[]{:S(2)}) collective-permute-start(bf16[16,32,512]{2,1,0:T(8,128)(2,1)S(1)} %get-tuple-element.36.a0), channel_id=1, source_target_pairs={{0,1},{1,0},{2,3},{3,2},{4,5},{5,4},{6,7},{7,6},{8,9},{9,8},{10,11... | collective-permute-start | bytes 1572872 | tf_op jit(solution)/shard_map/ppermute | solution.py:162
  44.3 2.5 %slice_add_fusion.3 = (f32[8,32,512]{2,1,0:T(8,128)S(1)}, f32[8,32,512]{2,1,0:T(8,128)S(1)}, f32[8,32,512]{2,1,0:T(8,128)S(1)}, f32[8,32,512]{2,1,0:T(8,128)S(1)}) fusion(f32[16,32,512]{2,1,0:T(8,128)S(1)} %collective-permute-done.2, f32[4,16,32,512]{3,2,1,0:T(8,128)} %get-tuple-element.30, f32[16,32,512]{2,1,0:T(8,128)} %collective-permute-done, ...), kind=kLoop, calls=%fused_computation.10 | loop fusion | flops 524288 | bytes 6291456 | tf_op jit(solution)/shard_map/add | solution.py:200
  46.9 1.7 %collective-permute-start.4 = (f32[8,32,512]{2,1,0:T(8,128)S(1)}, f32[8,32,512]{2,1,0:T(8,128)S(1)}, u32[]{:S(2)}, u32[]{:S(2)}) collective-permute-start(f32[8,32,512]{2,1,0:T(8,128)S(1)} %get-tuple-element.35), channel_id=1, source_target_pairs={{0,6},{1,7},{2,0},{3,1},{4,2},{5,3},{6,4},{7,5},{8,14},{9,15},{10,... | collective-permute-start | bytes 1572872 | tf_op jit(solution)/shard_map/ppermute | solution.py:159
  48.8 2.7 %collective-permute-start.8 = (bf16[8,32,512]{2,1,0:T(8,128)(2,1)S(1)}, bf16[8,32,512]{2,1,0:T(8,128)(2,1)S(1)}, u32[]{:S(2)}, u32[]{:S(2)}) collective-permute-start(bf16[8,32,512]{2,1,0:T(8,128)(2,1)S(1)} %slice.97), channel_id=1, source_target_pairs={{0,6},{1,7},{2,0},{3,1},{4,2},{5,3},{6,4},{7,5},{8,14},{9,15},{10,... | collective-permute-start | bytes 786440 | tf_op jit(solution)/shard_map/ppermute | solution.py:159
  51.5 4.7 %collective-permute-start.10 = (bf16[16,32,512]{2,1,0:T(8,128)(2,1)S(1)}, bf16[16,32,512]{2,1,0:T(8,128)(2,1)S(1)}, u32[]{:S(2)}, u32[]{:S(2)}) collective-permute-start(bf16[16,32,512]{2,1,0:T(8,128)(2,1)S(1)} %collective-permute-done.5.am), channel_id=1, source_target_pairs={{0,1},{1,0},{2,3},{3,2},{4,5},{5,4},{6,7},{7,6},{8,9},{9,8},{10,11... | collective-permute-start | bytes 1572872 | tf_op jit(solution)/shard_map/ppermute | solution.py:162
  56.3 4.8 %collective-permute-done.4 = f32[8,32,512]{2,1,0:T(8,128)S(1)} collective-permute-done((f32[8,32,512]{2,1,0:T(8,128)S(1)}, f32[8,32,512]{2,1,0:T(8,128)S(1)}, u32[]{:S(2)}, u32[]{:S(2)}) %collective-permute-start.4) | collective-permute-done | bytes 524320 | tf_op jit(solution)/shard_map/ppermute | solution.py:159
  61.1 3.7 %collective-permute-start.11 = (bf16[16,32,512]{2,1,0:T(8,128)(2,1)S(1)}, bf16[16,32,512]{2,1,0:T(8,128)(2,1)S(1)}, u32[]{:S(2)}, u32[]{:S(2)}) collective-permute-start(bf16[16,32,512]{2,1,0:T(8,128)(2,1)S(1)} %collective-permute-done.6.ap), channel_id=1, source_target_pairs={{0,1},{1,0},{2,3},{3,2},{4,5},{5,4},{6,7},{7,6},{8,9},{9,8},{10,11... | collective-permute-start | bytes 1572872 | tf_op jit(solution)/shard_map/ppermute | solution.py:162
  64.7 4.1 %collective-permute-done.7.a2a = bf16[8,32,512]{2,1,0:T(8,128)(2,1)S(1)} collective-permute-done((bf16[8,32,512]{2,1,0:T(8,128)(2,1)S(1)}, bf16[8,32,512]{2,1,0:T(8,128)(2,1)S(1)}, u32[]{:S(2)}, u32[]{:S(2)}) %collective-permute-start.7) | collective-permute-done | bytes 262176 | tf_op jit(solution)/shard_map/ppermute | solution.py:159
  68.8 1.0 collective-permute-start.12
  69.9 0.4 collective-permute-start.16
  70.3 0.6 collective-permute-done.12.b2a
  71.0 0.4 collective-permute-done.13.b2b
  71.3 2.3 %collective-permute-start.15 = (bf16[16,32,512]{2,1,0:T(8,128)(2,1)S(1)}, bf16[16,32,512]{2,1,0:T(8,128)(2,1)S(1)}, u32[]{:S(2)}, u32[]{:S(2)}) collective-permute-start(bf16[16,32,512]{2,1,0:T(8,128)(2,1)S(1)} %get-tuple-element.46.a0), channel_id=1, source_target_pairs={{0,6},{1,7},{2,0},{3,1},{4,2},{5,3},{6,4},{7,5},{8,14},{9,15},{10,... | collective-permute-start | bytes 1572872 | tf_op jit(solution)/shard_map/ppermute | solution.py:159
  73.7 1.4 collective-permute-start.19
  75.1 2.8 %fusion.6 = (f32[8,32,512]{2,1,0:T(8,128)}, f32[8,32,512]{2,1,0:T(8,128)}) fusion(f32[8,32,512]{2,1,0:T(8,128)S(1)} %collective-permute-done.4, f32[16,32,512]{2,1,0:T(8,128)S(1)} %collective-permute-done.2, f32[4,16,32,512]{3,2,1,0:T(8,128)} %get-tuple-element.30, f32[8,32,512]{2,1,0:T(8,128)S(1)} %collective-permute-done.3, ...), kind=kLoop, calls=%fused_computation.9 | loop fusion | flops 524288 | bytes 4194304 | tf_op jit(solution)/shard_map/add | solution.py:211
  77.9 7.5 %collective-permute-done.14.am = bf16[16,32,512]{2,1,0:T(8,128)(2,1)S(1)} collective-permute-done((bf16[16,32,512]{2,1,0:T(8,128)(2,1)S(1)}, bf16[16,32,512]{2,1,0:T(8,128)(2,1)S(1)}, u32[]{:S(2)}, u32[]{:S(2)}) %collective-permute-start.14) | collective-permute-done | bytes 524320 | tf_op jit(solution)/shard_map/ppermute | solution.py:159
  85.5 2.7 %collective-permute-start.20 = (f32[8,32,512]{2,1,0:T(8,128)}, f32[8,32,512]{2,1,0:T(8,128)S(1)}, u32[]{:S(2)}, u32[]{:S(2)}) collective-permute-start(f32[8,32,512]{2,1,0:T(8,128)} %get-tuple-element.52), channel_id=1, source_target_pairs={{0,6},{1,7},{2,0},{3,1},{4,2},{5,3},{6,4},{7,5},{8,14},{9,15},{10,... | collective-permute-start | bytes 1572872 | tf_op jit(solution)/shard_map/ppermute | solution.py:159
  88.2 14.8 %outputs.1 = bf16[256,1024]{1,0:T(8,128)(2,1)} custom-call(s32[1]{0:T(128)} %bitcast.pos, s32[8,8,34]{2,1,0:T(8,128)} %rows.5, s32[8,8,34]{2,1,0:T(8,128)} %cols.5, s32[8,8]{1,0:T(8,128)} %live.5, bf16[16,32,512]{2,1,0:T(8,128)(2,1)} %copy-done.3, bf16[16,32,512]{2,1,0:T(8,128)(2,1)} %copy-done.9, bf16[16,32,512]{2,1,0:T(8,128)(2,1)} %copy-done.10, ...), custom_call_target="tpu_custom_call" | custom-call | flops 4300000256 | bytes 14000000 | tf_op jit(solution)/shard_map/outputs/pallas_call | solution.py:218
  103.1 2.6 %collective-permute-start.21 = (bf16[16,32,512]{2,1,0:T(8,128)(2,1)S(1)}, bf16[16,32,512]{2,1,0:T(8,128)(2,1)S(1)}, u32[]{:S(2)}, u32[]{:S(2)}) collective-permute-start(bf16[16,32,512]{2,1,0:T(8,128)(2,1)S(1)} %get-tuple-element.46.a0), channel_id=1, source_target_pairs={{0,1},{1,0},{2,3},{3,2},{4,5},{5,4},{6,7},{7,6},{8,9},{9,8},{10,11... | collective-permute-start | bytes 1572872 | tf_op jit(solution)/shard_map/ppermute | solution.py:162
  105.7 0.1 collective-permute-start.22
  105.8 0.4 collective-permute-start.23
  106.2 0.7 slice.86
  106.9 0.7 slice.87
  107.6 0.1 collective-permute-done.18
  107.8 2.7 %collective-permute-start.25 = (bf16[8,32,512]{2,1,0:T(8,128)(2,1)}, bf16[8,32,512]{2,1,0:T(8,128)(2,1)}, u32[]{:S(2)}, u32[]{:S(2)}) collective-permute-start(bf16[8,32,512]{2,1,0:T(8,128)(2,1)} %slice.87), channel_id=1, source_target_pairs={{0,6},{1,7},{2,0},{3,1},{4,2},{5,3},{6,4},{7,5},{8,14},{9,15},{10,... | collective-permute-start | bytes 786440 | tf_op jit(solution)/shard_map/ppermute | solution.py:159
  110.5 2.2 %fusion.5 = (bf16[8,32,512]{2,1,0:T(8,128)(2,1)S(1)}, bf16[8,32,512]{2,1,0:T(8,128)(2,1)S(1)}) fusion(f32[8,32,512]{2,1,0:T(8,128)S(1)} %collective-permute-done.18, f32[8,32,512]{2,1,0:T(8,128)} %collective-permute-done.17, f32[16,32,512]{2,1,0:T(8,128)} %collective-permute-done.16, f32[4,16,32,512]{3,2,1,0:T(8,128)} %get-tuple-element.30, ...), kind=kLoop, calls=%fused_computation.7 | loop fusion | flops 1048576 | bytes 4718592 | tf_op jit(solution)/shard_map/convert
  112.7 0.8 pad_maximum_fusion
  113.5 0.8 copy-done.4
  114.3 0.8 copy-done.5
  115.1 9.4 %near_weight_grad.1.near_ref = f32[64,8,1024]{2,1,0:T(8,128)} custom-call(s32[1]{0:T(128)} %bitcast.pos, bf16[16,32,512]{2,1,0:T(8,128)(2,1)} %copy-done, bf16[16,32,512]{2,1,0:T(8,128)(2,1)} %copy-done.1, bf16[16,32,512]{2,1,0:T(8,128)(2,1)} %copy-done.2, bf16[16,32,512]{2,1,0:T(8,128)(2,1)} %copy-done.4, bf16[16,32,512]{2,1,0:T(8,128)(2,1)} %copy-done.5, ...), custom_call_target="tpu_custom_call" | custom-call | flops 3200000000 | bytes 11000000 | tf_op jit(solution)/shard_map/near_weight_grad/pallas_call | solution.py:259
  124.5 5.4 %all-to-all-start.1 = ((bf16[16,32,512]{2,1,0:T(8,128)(2,1)}), bf16[16,32,512]{2,1,0:T(8,128)(2,1)S(1)}, u32[]{:S(2)}, u32[]{:S(2)}) async-start(bf16[16,32,512]{2,1,0:T(8,128)(2,1)} %pad_maximum_fusion), calls=%async_computation.1 | async-start | bytes 1048576 | tf_op jit(solution)/shard_map/all_to_all | solution.py:165
  130.0 2.1 %collective-permute-start.26 = (bf16[8,32,512]{2,1,0:T(8,128)(2,1)S(1)}, bf16[8,32,512]{2,1,0:T(8,128)(2,1)S(1)}, u32[]{:S(2)}, u32[]{:S(2)}) collective-permute-start(bf16[8,32,512]{2,1,0:T(8,128)(2,1)S(1)} %collective-permute-done.24.a2a), channel_id=1, source_target_pairs={{0,1},{1,0},{2,3},{3,2},{4,5},{5,4},{6,7},{7,6},{8,9},{9,8},{10,11... | collective-permute-start | bytes 786440 | tf_op jit(solution)/shard_map/ppermute | solution.py:162
  132.1 0.1 collective-permute-start.27
  132.2 1.1 collective-permute-done.26.b2a
  133.3 0.6 collective-permute-done.27.b2b
  133.9 0.1 copy-done.7
  134.0 0.7 copy-done.8
  134.7 7.4 %far_weight_grad.1 = bf16[1,8,34,8,128]{4,3,2,1,0:T(8,128)(2,1)} custom-call(s32[1]{0:T(128)} %bitcast.pos, s32[8,8,34]{2,1,0:T(8,128)} %rows.5, s32[8,8,34]{2,1,0:T(8,128)} %cols.5, s32[8,8]{1,0:T(8,128)} %live.5, bf16[8,32,512]{2,1,0:T(8,128)(2,1)} %copy-done.6, bf16[8,32,512]{2,1,0:T(8,128)(2,1)} %collective-permute-done.25.a2b, ...), custom_call_target="tpu_custom_call" | custom-call | flops 1100000000 | bytes 6000000 | tf_op jit(solution)/shard_map/far_weight_grad/pallas_call | solution.py:280
  142.1 0.8 copy.10
  (66 shorter events, 0.5 us)
Async XLA Ops:
  7.2 107.2 %all-gather.2.cloned.1.call-start = ((), (), s32[]{:S(2)}) async-start(), calls=%async_computation.2 | async-start | bytes 8912896 | tf_op jit(solution)/shard_map/all_gather | solution.py:167
  10.1 25.2 %all-to-all-start = ((bf16[16,64,512]{2,1,0:T(8,128)(2,1)}), bf16[16,64,512]{2,1,0:T(8,128)(2,1)S(1)}, u32[]{:S(2)}, u32[]{:S(2)}) async-start(bf16[16,64,512]{2,1,0:T(8,128)(2,1)} %feature_rows.1), calls=%async_computation | async-start | bytes 2097152 | tf_op jit(solution)/shard_map/all_to_all | solution.py:165
  33.8 4.4 %collective-permute-start.2 = (f32[16,32,512]{2,1,0:T(8,128)}, f32[16,32,512]{2,1,0:T(8,128)S(1)}, u32[]{:S(2)}, u32[]{:S(2)}) collective-permute-start(f32[16,32,512]{2,1,0:T(8,128)} %get-tuple-element.33), channel_id=1, source_target_pairs={{0,1},{1,0},{2,3},{3,2},{4,5},{5,4},{6,7},{7,6},{8,9},{9,8},{10,11... | collective-permute-start | bytes 3145736 | tf_op jit(solution)/shard_map/ppermute | solution.py:162
  34.8 9.5 %collective-permute-start = (f32[16,32,512]{2,1,0:T(8,128)}, f32[16,32,512]{2,1,0:T(8,128)}, u32[]{:S(2)}, u32[]{:S(2)}) collective-permute-start(f32[16,32,512]{2,1,0:T(8,128)} %get-tuple-element.31), channel_id=1, source_target_pairs={{0,1},{1,0},{2,3},{3,2},{4,5},{5,4},{6,7},{7,6},{8,9},{9,8},{10,11... | collective-permute-start | bytes 3145736 | tf_op jit(solution)/shard_map/ppermute | solution.py:162
  34.9 9.5 %collective-permute-start.1 = (f32[16,32,512]{2,1,0:T(8,128)}, f32[16,32,512]{2,1,0:T(8,128)}, u32[]{:S(2)}, u32[]{:S(2)}) collective-permute-start(f32[16,32,512]{2,1,0:T(8,128)} %get-tuple-element.32), channel_id=1, source_target_pairs={{0,1},{1,0},{2,3},{3,2},{4,5},{5,4},{6,7},{7,6},{8,9},{9,8},{10,11... | collective-permute-start | bytes 3145736 | tf_op jit(solution)/shard_map/ppermute | solution.py:162
  35.4 42.5 %copy-start.3 = (bf16[16,32,512]{2,1,0:T(8,128)(2,1)}, bf16[16,32,512]{2,1,0:T(8,128)(2,1)S(1)}, u32[]{:S(2)}) copy-start(bf16[16,32,512]{2,1,0:T(8,128)(2,1)S(1)} %get-tuple-element.36.a0) | copy-start | bytes 1572868
  35.4 67.6 %copy-start = (bf16[16,32,512]{2,1,0:T(8,128)(2,1)}, bf16[16,32,512]{2,1,0:T(8,128)(2,1)S(1)}, u32[]{:S(2)}) copy-start(bf16[16,32,512]{2,1,0:T(8,128)(2,1)S(1)} %get-tuple-element.46.a0) | copy-start | bytes 1572868
  35.4 13.2 %collective-permute-start.5 = (bf16[16,32,512]{2,1,0:T(8,128)(2,1)S(1)}, bf16[16,32,512]{2,1,0:T(8,128)(2,1)S(1)}, u32[]{:S(2)}, u32[]{:S(2)}) collective-permute-start(bf16[16,32,512]{2,1,0:T(8,128)(2,1)S(1)} %get-tuple-element.36.a0), channel_id=1, source_target_pairs={{0,2},{1,3},{2,4},{3,5},{4,6},{5,7},{6,0},{7,1},{8,10},{9,11},{10,... | collective-permute-start | bytes 1572872 | tf_op jit(solution)/shard_map/ppermute | solution.py:159
  36.8 12.0 %collective-permute-start.6 = (bf16[16,32,512]{2,1,0:T(8,128)(2,1)S(1)}, bf16[16,32,512]{2,1,0:T(8,128)(2,1)S(1)}, u32[]{:S(2)}, u32[]{:S(2)}) collective-permute-start(bf16[16,32,512]{2,1,0:T(8,128)(2,1)S(1)} %get-tuple-element.36.a0), channel_id=1, source_target_pairs={{0,6},{1,7},{2,0},{3,1},{4,2},{5,3},{6,4},{7,5},{8,14},{9,15},{10,... | collective-permute-start | bytes 1572872 | tf_op jit(solution)/shard_map/ppermute | solution.py:159
  38.3 13.3 %collective-permute-start.9 = (bf16[16,32,512]{2,1,0:T(8,128)(2,1)S(1)}, bf16[16,32,512]{2,1,0:T(8,128)(2,1)S(1)}, u32[]{:S(2)}, u32[]{:S(2)}) collective-permute-start(bf16[16,32,512]{2,1,0:T(8,128)(2,1)S(1)} %get-tuple-element.36.a0), channel_id=1, source_target_pairs={{0,1},{1,0},{2,3},{3,2},{4,5},{5,4},{6,7},{7,6},{8,9},{9,8},{10,11... | collective-permute-start | bytes 1572872 | tf_op jit(solution)/shard_map/ppermute | solution.py:162
  46.9 14.2 %collective-permute-start.4 = (f32[8,32,512]{2,1,0:T(8,128)S(1)}, f32[8,32,512]{2,1,0:T(8,128)S(1)}, u32[]{:S(2)}, u32[]{:S(2)}) collective-permute-start(f32[8,32,512]{2,1,0:T(8,128)S(1)} %get-tuple-element.35), channel_id=1, source_target_pairs={{0,6},{1,7},{2,0},{3,1},{4,2},{5,3},{6,4},{7,5},{8,14},{9,15},{10,... | collective-permute-start | bytes 1572872 | tf_op jit(solution)/shard_map/ppermute | solution.py:159
  48.6 21.3 %collective-permute-start.3 = (f32[8,32,512]{2,1,0:T(8,128)S(1)}, f32[8,32,512]{2,1,0:T(8,128)S(1)}, u32[]{:S(2)}, u32[]{:S(2)}) collective-permute-start(f32[8,32,512]{2,1,0:T(8,128)S(1)} %get-tuple-element.34), channel_id=1, source_target_pairs={{0,2},{1,3},{2,4},{3,5},{4,6},{5,7},{6,0},{7,1},{8,10},{9,11},{10,... | collective-permute-start | bytes 1572872 | tf_op jit(solution)/shard_map/ppermute | solution.py:159
  48.6 36.8 %copy-start.9 = (bf16[16,32,512]{2,1,0:T(8,128)(2,1)}, bf16[16,32,512]{2,1,0:T(8,128)(2,1)S(1)}, u32[]{:S(2)}) copy-start(bf16[16,32,512]{2,1,0:T(8,128)(2,1)S(1)} %collective-permute-done.5.am) | copy-start | bytes 1572868
  48.7 20.1 %collective-permute-start.7 = (bf16[8,32,512]{2,1,0:T(8,128)(2,1)S(1)}, bf16[8,32,512]{2,1,0:T(8,128)(2,1)S(1)}, u32[]{:S(2)}, u32[]{:S(2)}) collective-permute-start(bf16[8,32,512]{2,1,0:T(8,128)(2,1)S(1)} %slice.96), channel_id=1, source_target_pairs={{0,2},{1,3},{2,4},{3,5},{4,6},{5,7},{6,0},{7,1},{8,10},{9,11},{10,... | collective-permute-start | bytes 786440 | tf_op jit(solution)/shard_map/ppermute | solution.py:159
  48.8 36.7 %copy-start.10 = (bf16[16,32,512]{2,1,0:T(8,128)(2,1)}, bf16[16,32,512]{2,1,0:T(8,128)(2,1)S(1)}, u32[]{:S(2)}) copy-start(bf16[16,32,512]{2,1,0:T(8,128)(2,1)S(1)} %collective-permute-done.6.ap) | copy-start | bytes 1572868
  48.8 21.0 %collective-permute-start.8 = (bf16[8,32,512]{2,1,0:T(8,128)(2,1)S(1)}, bf16[8,32,512]{2,1,0:T(8,128)(2,1)S(1)}, u32[]{:S(2)}, u32[]{:S(2)}) collective-permute-start(bf16[8,32,512]{2,1,0:T(8,128)(2,1)S(1)} %slice.97), channel_id=1, source_target_pairs={{0,6},{1,7},{2,0},{3,1},{4,2},{5,3},{6,4},{7,5},{8,14},{9,15},{10,... | collective-permute-start | bytes 786440 | tf_op jit(solution)/shard_map/ppermute | solution.py:159
  51.5 33.9 %copy-start.11 = (bf16[16,32,512]{2,1,0:T(8,128)(2,1)}, bf16[16,32,512]{2,1,0:T(8,128)(2,1)S(1)}, u32[]{:S(2)}) copy-start(bf16[16,32,512]{2,1,0:T(8,128)(2,1)S(1)} %collective-permute-done.9.b0) | copy-start | bytes 1572868
  51.5 22.1 %collective-permute-start.10 = (bf16[16,32,512]{2,1,0:T(8,128)(2,1)S(1)}, bf16[16,32,512]{2,1,0:T(8,128)(2,1)S(1)}, u32[]{:S(2)}, u32[]{:S(2)}) collective-permute-start(bf16[16,32,512]{2,1,0:T(8,128)(2,1)S(1)} %collective-permute-done.5.am), channel_id=1, source_target_pairs={{0,1},{1,0},{2,3},{3,2},{4,5},{5,4},{6,7},{7,6},{8,9},{9,8},{10,11... | collective-permute-start | bytes 1572872 | tf_op jit(solution)/shard_map/ppermute | solution.py:162
  61.1 12.7 %collective-permute-start.11 = (bf16[16,32,512]{2,1,0:T(8,128)(2,1)S(1)}, bf16[16,32,512]{2,1,0:T(8,128)(2,1)S(1)}, u32[]{:S(2)}, u32[]{:S(2)}) collective-permute-start(bf16[16,32,512]{2,1,0:T(8,128)(2,1)S(1)} %collective-permute-done.6.ap), channel_id=1, source_target_pairs={{0,1},{1,0},{2,3},{3,2},{4,5},{5,4},{6,7},{7,6},{8,9},{9,8},{10,11... | collective-permute-start | bytes 1572872 | tf_op jit(solution)/shard_map/ppermute | solution.py:162
  68.8 19.5 %copy-start.14 = (bf16[8,32,512]{2,1,0:T(8,128)(2,1)}, bf16[8,32,512]{2,1,0:T(8,128)(2,1)S(1)}, u32[]{:S(2)}) copy-start(bf16[8,32,512]{2,1,0:T(8,128)(2,1)S(1)} %collective-permute-done.7.a2a) | copy-start | bytes 786436
  68.8 2.2 %collective-permute-start.12 = (bf16[8,32,512]{2,1,0:T(8,128)(2,1)S(1)}, bf16[8,32,512]{2,1,0:T(8,128)(2,1)S(1)}, u32[]{:S(2)}, u32[]{:S(2)}) collective-permute-start(bf16[8,32,512]{2,1,0:T(8,128)(2,1)S(1)} %collective-permute-done.7.a2a), channel_id=1, source_target_pairs={{0,1},{1,0},{2,3},{3,2},{4,5},{5,4},{6,7},{7,6},{8,9},{9,8},{10,11... | collective-permute-start | bytes 786440 | tf_op jit(solution)/shard_map/ppermute | solution.py:162
  69.8 15.7 %copy-start.15 = (bf16[8,32,512]{2,1,0:T(8,128)(2,1)}, bf16[8,32,512]{2,1,0:T(8,128)(2,1)S(1)}, u32[]{:S(2)}) copy-start(bf16[8,32,512]{2,1,0:T(8,128)(2,1)S(1)} %collective-permute-done.8.a2b) | copy-start | bytes 786436
  69.8 1.5 %collective-permute-start.13 = (bf16[8,32,512]{2,1,0:T(8,128)(2,1)S(1)}, bf16[8,32,512]{2,1,0:T(8,128)(2,1)S(1)}, u32[]{:S(2)}, u32[]{:S(2)}) collective-permute-start(bf16[8,32,512]{2,1,0:T(8,128)(2,1)S(1)} %collective-permute-done.8.a2b), channel_id=1, source_target_pairs={{0,1},{1,0},{2,3},{3,2},{4,5},{5,4},{6,7},{7,6},{8,9},{9,8},{10,11... | collective-permute-start | bytes 786440 | tf_op jit(solution)/shard_map/ppermute | solution.py:162
  69.9 33.2 %collective-permute-start.16 = (f32[16,32,512]{2,1,0:T(8,128)}, f32[16,32,512]{2,1,0:T(8,128)}, u32[]{:S(2)}, u32[]{:S(2)}) collective-permute-start(f32[16,32,512]{2,1,0:T(8,128)} %get-tuple-element.48), channel_id=1, source_target_pairs={{0,1},{1,0},{2,3},{3,2},{4,5},{5,4},{6,7},{7,6},{8,9},{9,8},{10,11... | collective-permute-start | bytes 3145736 | tf_op jit(solution)/shard_map/ppermute | solution.py:162
  71.0 14.5 %copy-start.16 = (bf16[8,32,512]{2,1,0:T(8,128)(2,1)}, bf16[8,32,512]{2,1,0:T(8,128)(2,1)S(1)}, u32[]{:S(2)}) copy-start(bf16[8,32,512]{2,1,0:T(8,128)(2,1)S(1)} %collective-permute-done.12.b2a) | copy-start | bytes 786436
  71.0 14.5 %collective-permute-start.14 = (bf16[16,32,512]{2,1,0:T(8,128)(2,1)S(1)}, bf16[16,32,512]{2,1,0:T(8,128)(2,1)S(1)}, u32[]{:S(2)}, u32[]{:S(2)}) collective-permute-start(bf16[16,32,512]{2,1,0:T(8,128)(2,1)S(1)} %get-tuple-element.46.a0), channel_id=1, source_target_pairs={{0,2},{1,3},{2,4},{3,5},{4,6},{5,7},{6,0},{7,1},{8,10},{9,11},{10,... | collective-permute-start | bytes 1572872 | tf_op jit(solution)/shard_map/ppermute | solution.py:159
  71.3 14.1 %copy-start.17 = (bf16[8,32,512]{2,1,0:T(8,128)(2,1)}, bf16[8,32,512]{2,1,0:T(8,128)(2,1)S(1)}, u32[]{:S(2)}) copy-start(bf16[8,32,512]{2,1,0:T(8,128)(2,1)S(1)} %collective-permute-done.13.b2b) | copy-start | bytes 786436
  71.3 14.1 %collective-permute-start.15 = (bf16[16,32,512]{2,1,0:T(8,128)(2,1)S(1)}, bf16[16,32,512]{2,1,0:T(8,128)(2,1)S(1)}, u32[]{:S(2)}, u32[]{:S(2)}) collective-permute-start(bf16[16,32,512]{2,1,0:T(8,128)(2,1)S(1)} %get-tuple-element.46.a0), channel_id=1, source_target_pairs={{0,6},{1,7},{2,0},{3,1},{4,2},{5,3},{6,4},{7,5},{8,14},{9,15},{10,... | collective-permute-start | bytes 1572872 | tf_op jit(solution)/shard_map/ppermute | solution.py:159
  73.6 11.8 %copy-start.12 = (bf16[16,32,512]{2,1,0:T(8,128)(2,1)}, bf16[16,32,512]{2,1,0:T(8,128)(2,1)S(1)}, u32[]{:S(2)}) copy-start(bf16[16,32,512]{2,1,0:T(8,128)(2,1)S(1)} %collective-permute-done.10.bm) | copy-start | bytes 1572868
  73.6 32.0 %collective-permute-start.17 = (f32[8,32,512]{2,1,0:T(8,128)S(1)}, f32[8,32,512]{2,1,0:T(8,128)}, u32[]{:S(2)}, u32[]{:S(2)}) collective-permute-start(f32[8,32,512]{2,1,0:T(8,128)S(1)} %get-tuple-element.49), channel_id=1, source_target_pairs={{0,6},{1,7},{2,0},{3,1},{4,2},{5,3},{6,4},{7,5},{8,14},{9,15},{10,... | collective-permute-start | bytes 1572872 | tf_op jit(solution)/shard_map/ppermute | solution.py:159
  73.7 11.8 %copy-start.13 = (bf16[16,32,512]{2,1,0:T(8,128)(2,1)}, bf16[16,32,512]{2,1,0:T(8,128)(2,1)S(1)}, u32[]{:S(2)}) copy-start(bf16[16,32,512]{2,1,0:T(8,128)(2,1)S(1)} %collective-permute-done.11.bp) | copy-start | bytes 1572868
  73.7 32.0 %collective-permute-start.19 = (f32[8,32,512]{2,1,0:T(8,128)S(1)}, f32[8,32,512]{2,1,0:T(8,128)}, u32[]{:S(2)}, u32[]{:S(2)}) collective-permute-start(f32[8,32,512]{2,1,0:T(8,128)S(1)} %get-tuple-element.51), channel_id=1, source_target_pairs={{0,2},{1,3},{2,4},{3,5},{4,6},{5,7},{6,0},{7,1},{8,10},{9,11},{10,... | collective-permute-start | bytes 1572872 | tf_op jit(solution)/shard_map/ppermute | solution.py:159
  85.4 20.8 %copy-start.1 = (bf16[16,32,512]{2,1,0:T(8,128)(2,1)}, bf16[16,32,512]{2,1,0:T(8,128)(2,1)S(1)}, u32[]{:S(2)}) copy-start(bf16[16,32,512]{2,1,0:T(8,128)(2,1)S(1)} %collective-permute-done.14.am) | copy-start | bytes 1572868
  85.4 22.4 %collective-permute-start.18 = (f32[8,32,512]{2,1,0:T(8,128)}, f32[8,32,512]{2,1,0:T(8,128)S(1)}, u32[]{:S(2)}, u32[]{:S(2)}) collective-permute-start(f32[8,32,512]{2,1,0:T(8,128)} %get-tuple-element.50), channel_id=1, source_target_pairs={{0,2},{1,3},{2,4},{3,5},{4,6},{5,7},{6,0},{7,1},{8,10},{9,11},{10,... | collective-permute-start | bytes 1572872 | tf_op jit(solution)/shard_map/ppermute | solution.py:159
  85.5 21.4 %copy-start.2 = (bf16[16,32,512]{2,1,0:T(8,128)(2,1)}, bf16[16,32,512]{2,1,0:T(8,128)(2,1)S(1)}, u32[]{:S(2)}) copy-start(bf16[16,32,512]{2,1,0:T(8,128)(2,1)S(1)} %collective-permute-done.15.ap) | copy-start | bytes 1572868
  85.5 22.3 %collective-permute-start.20 = (f32[8,32,512]{2,1,0:T(8,128)}, f32[8,32,512]{2,1,0:T(8,128)S(1)}, u32[]{:S(2)}, u32[]{:S(2)}) collective-permute-start(f32[8,32,512]{2,1,0:T(8,128)} %get-tuple-element.52), channel_id=1, source_target_pairs={{0,6},{1,7},{2,0},{3,1},{4,2},{5,3},{6,4},{7,5},{8,14},{9,15},{10,... | collective-permute-start | bytes 1572872 | tf_op jit(solution)/shard_map/ppermute | solution.py:159
  103.1 10.5 %collective-permute-start.21 = (bf16[16,32,512]{2,1,0:T(8,128)(2,1)S(1)}, bf16[16,32,512]{2,1,0:T(8,128)(2,1)S(1)}, u32[]{:S(2)}, u32[]{:S(2)}) collective-permute-start(bf16[16,32,512]{2,1,0:T(8,128)(2,1)S(1)} %get-tuple-element.46.a0), channel_id=1, source_target_pairs={{0,1},{1,0},{2,3},{3,2},{4,5},{5,4},{6,7},{7,6},{8,9},{9,8},{10,11... | collective-permute-start | bytes 1572872 | tf_op jit(solution)/shard_map/ppermute | solution.py:162
  105.7 7.9 %collective-permute-start.22 = (bf16[16,32,512]{2,1,0:T(8,128)(2,1)S(1)}, bf16[16,32,512]{2,1,0:T(8,128)(2,1)S(1)}, u32[]{:S(2)}, u32[]{:S(2)}) collective-permute-start(bf16[16,32,512]{2,1,0:T(8,128)(2,1)S(1)} %collective-permute-done.14.am), channel_id=1, source_target_pairs={{0,1},{1,0},{2,3},{3,2},{4,5},{5,4},{6,7},{7,6},{8,9},{9,8},{10,11... | collective-permute-start | bytes 1572872 | tf_op jit(solution)/shard_map/ppermute | solution.py:162
  105.8 8.5 %collective-permute-start.23 = (bf16[16,32,512]{2,1,0:T(8,128)(2,1)S(1)}, bf16[16,32,512]{2,1,0:T(8,128)(2,1)}, u32[]{:S(2)}, u32[]{:S(2)}) collective-permute-start(bf16[16,32,512]{2,1,0:T(8,128)(2,1)S(1)} %collective-permute-done.15.ap), channel_id=1, source_target_pairs={{0,1},{1,0},{2,3},{3,2},{4,5},{5,4},{6,7},{7,6},{8,9},{9,8},{10,11... | collective-permute-start | bytes 1572872 | tf_op jit(solution)/shard_map/ppermute | solution.py:162
  107.8 22.2 %collective-permute-start.24 = (bf16[8,32,512]{2,1,0:T(8,128)(2,1)}, bf16[8,32,512]{2,1,0:T(8,128)(2,1)S(1)}, u32[]{:S(2)}, u32[]{:S(2)}) collective-permute-start(bf16[8,32,512]{2,1,0:T(8,128)(2,1)} %slice.86), channel_id=1, source_target_pairs={{0,2},{1,3},{2,4},{3,5},{4,6},{5,7},{6,0},{7,1},{8,10},{9,11},{10,... | collective-permute-start | bytes 786440 | tf_op jit(solution)/shard_map/ppermute | solution.py:159
  107.8 24.4 %collective-permute-start.25 = (bf16[8,32,512]{2,1,0:T(8,128)(2,1)}, bf16[8,32,512]{2,1,0:T(8,128)(2,1)}, u32[]{:S(2)}, u32[]{:S(2)}) collective-permute-start(bf16[8,32,512]{2,1,0:T(8,128)(2,1)} %slice.87), channel_id=1, source_target_pairs={{0,6},{1,7},{2,0},{3,1},{4,2},{5,3},{6,4},{7,5},{8,14},{9,15},{10,... | collective-permute-start | bytes 786440 | tf_op jit(solution)/shard_map/ppermute | solution.py:159
  113.5 0.8 copy-start.4
  114.3 0.8 copy-start.5
  124.5 17.6 %all-to-all-start.1 = ((bf16[16,32,512]{2,1,0:T(8,128)(2,1)}), bf16[16,32,512]{2,1,0:T(8,128)(2,1)S(1)}, u32[]{:S(2)}, u32[]{:S(2)}) async-start(bf16[16,32,512]{2,1,0:T(8,128)(2,1)} %pad_maximum_fusion), calls=%async_computation.1 | async-start | bytes 1048576 | tf_op jit(solution)/shard_map/all_to_all | solution.py:165
  130.0 3.9 %copy-start.6 = (bf16[8,32,512]{2,1,0:T(8,128)(2,1)}, bf16[8,32,512]{2,1,0:T(8,128)(2,1)S(1)}, u32[]{:S(2)}) copy-start(bf16[8,32,512]{2,1,0:T(8,128)(2,1)S(1)} %collective-permute-done.24.a2a) | copy-start | bytes 786436
  130.0 3.3 %collective-permute-start.26 = (bf16[8,32,512]{2,1,0:T(8,128)(2,1)S(1)}, bf16[8,32,512]{2,1,0:T(8,128)(2,1)S(1)}, u32[]{:S(2)}, u32[]{:S(2)}) collective-permute-start(bf16[8,32,512]{2,1,0:T(8,128)(2,1)S(1)} %collective-permute-done.24.a2a), channel_id=1, source_target_pairs={{0,1},{1,0},{2,3},{3,2},{4,5},{5,4},{6,7},{7,6},{8,9},{9,8},{10,11... | collective-permute-start | bytes 786440 | tf_op jit(solution)/shard_map/ppermute | solution.py:162
  132.1 1.7 %collective-permute-start.27 = (bf16[8,32,512]{2,1,0:T(8,128)(2,1)}, bf16[8,32,512]{2,1,0:T(8,128)(2,1)S(1)}, u32[]{:S(2)}, u32[]{:S(2)}) collective-permute-start(bf16[8,32,512]{2,1,0:T(8,128)(2,1)} %collective-permute-done.25.a2b), channel_id=1, source_target_pairs={{0,1},{1,0},{2,3},{3,2},{4,5},{5,4},{6,7},{7,6},{8,9},{9,8},{10,11... | collective-permute-start | bytes 786440 | tf_op jit(solution)/shard_map/ppermute | solution.py:162
  134.0 0.7 copy-start.8
  (1 other events, 0.7 us)
Sparse Core Ops, SparseCore 0:
  10.1 78.8 all-gather.1

commit v3 on v2

--- a/solution.py
+++ b/solution.py
@@ -196,21 +196,16 @@
 
     xm, xp = along_y(tokens, 1), along_y(tokens, -1)
 
-    q2a, q2b = keep[2, :8] + r2[:8], keep[2, 8:] + r2[8:]
-    q1b, q3a = keep[1, 8:] + r1[8:], keep[3, :8] + r3[:8]
-    q2a, q2b, q1b, q3a, class_rows = barrier((q2a, q2b, q1b, q3a, class_rows))
+    q2a, q2b, xm, xp = barrier((keep[2, :8] + r2[:8], keep[2, 8:] + r2[8:], xm, xp))
+    x2a, x2b = along_y(xm[:8], 1), along_y(xp[8:], -1)
     from_a, from_b = along_y(q2a, 1), along_y(q2b, -1)
-    near_b, near_a = along_y(q1b, 1), along_y(q3a, -1)
-
-    x2a, x2b = along_y(xm[:8], 1), along_y(xp[8:], -1)
     own = (tokens, xm, xp, x2a, x2b)
     x_pieces = own + tuple(other_core(piece) for piece in own)
 
+    q1b, q3a = keep[1, 8:] + r1[8:], keep[3, :8] + r3[:8]
+    q1b, q3a, class_rows, x_pieces = barrier((q1b, q3a, class_rows, x_pieces))
     cm, cp = along_y(class_rows, 1), along_y(class_rows, -1)
-
-    q1a, q3b = keep[1, :8] + r1[:8] + from_a, keep[3, 8:] + r3[8:] + from_b
-    q1a, q3b, x_pieces = barrier((q1a, q3b, x_pieces))
-    far_a, far_b = along_y(q1a, 1), along_y(q3b, -1)
+    near_b, near_a = along_y(q1b, 1), along_y(q3a, -1)
 
     whole = pl.BlockSpec((2, 32, 512), lambda j, *_: (j, 0, 0))
     low = pl.BlockSpec((2, 32, 512), lambda j, *_: (jnp.minimum(j, 3), 0, 0))
@@ -234,7 +229,10 @@
         name="outputs",
     )(*tables, *x_pieces, blocks)
 
-    outputs, cm, cp = barrier((outputs, cm, cp))
+    outputs, cm, cp, from_a, from_b = barrier((outputs, cm, cp, from_a, from_b))
+    q1a, q3b = keep[1, :8] + r1[:8] + from_a, keep[3, 8:] + r3[8:] + from_b
+    far_a, far_b = along_y(q1a, 1), along_y(q3b, -1)
+
     c2a, c2b = along_y(cm[:8], 1), along_y(cp[8:], -1)
 
     near = (class_rows, cm, cp)

time: 151 us -> 153 us (1.013)
  starting transfers between devices: 53.2 us -> 57.1 us
  waiting for transfers between devices: 19.9 us -> 16.6 us
    ppermute x14, waiting for transfers between devices: 16.5 us -> 14.2 us  [along_y(): return lax.ppermute(x, 'mp', [(i, (i + 2 * step) % 8) for i in range(8)])]
  transfers between devices with their start and end apart: 31 -> 31, of which waited for: 8 -> 5; matrix products, arithmetic and copies ran while one was open for 7% -> 7% of each run, Pallas kernels for 33% -> 33%
where the time goes in v3:
time: 153 us; the launch traced here: 151 us
  starting transfers between devices  57.1 us (37%)
  Pallas kernels  49.4 us (32%)
  waiting for transfers between devices  16.6 us (11%)
  between operations  14.2 us (9%)
  other arithmetic  8.67 us (6%)
  local copies, waits for them, and re-layouts  5.41 us (4%)
    ppermute x14, starting transfers between devices, other_core(): return lax.ppermute(x, 'mp', [(i, i ^ 1) for i in range(8)])  24.1 us
    ppermute x14, starting transfers between devices, along_y(): return lax.ppermute(x, 'mp', [(i, (i + 2 * step) % 8) for i in range(8)])  18 us
    pallas_call x1, Pallas kernels, on_device(): pl.pallas_call(partial_kernel, grid_spec=pltpu.PrefetchScalarGridSpec(num...  15.3 us
    all_to_all x2, starting transfers between devices, exchange(): return lax.all_to_all(x, 'seq', split_axis=0, concat_axis=0, tiled=True)  15 us
    pallas_call x1, Pallas kernels, on_device(): pl.pallas_call(out_kernel, grid_spec=pltpu.PrefetchScalarGridSpec(num_sca...  15 us
    ppermute x14, waiting for transfers between devices, along_y(): return lax.ppermute(x, 'mp', [(i, (i + 2 * step) % 8) for i in range(8)])  14.2 us
    pallas_call x1, Pallas kernels, on_device(): pl.pallas_call(near_grad_kernel, grid_spec=pltpu.PrefetchScalarGridSpec(n...  9.41 us
    pallas_call x1, Pallas kernels, on_device(): pl.pallas_call(functools.partial(far_grad_kernel, 1.0 / math.sqrt(4096)),...  7.4 us
  transfers between devices with their start and end apart: 31, of which 5 were waited for; matrix products, arithmetic and copies ran while one was open for 7% of the time, Pallas kernels for 33%

profile of v3, /device:TPU:1, one launch (start us, length us, event | category | flops | bytes accessed | tf_op | source)
XLA Modules:
  0.0 151.3 jit_solution(12341179182021807797)
XLA Ops:
  7.2 0.7 all-gather.2.cloned.1.call-update
  7.9 2.3 %feature_rows.1 = bf16[16,64,512]{2,1,0:T(8,128)(2,1)} custom-call(bf16[16,32,512]{2,1,0:T(8,128)(2,1)} %x_ref.1), custom_call_target="tpu_custom_call" | custom-call | tf_op jit(solution)/shard_map/feature_rows/pallas_call | solution.py:169
  10.2 8.4 %all-to-all-start = ((bf16[16,64,512]{2,1,0:T(8,128)(2,1)}), bf16[16,64,512]{2,1,0:T(8,128)(2,1)S(1)}, u32[]{:S(2)}, u32[]{:S(2)}) async-start(bf16[16,64,512]{2,1,0:T(8,128)(2,1)} %feature_rows.1), calls=%async_computation | async-start | bytes 2097152 | tf_op jit(solution)/shard_map/all_to_all | solution.py:165
  18.6 15.3 %partial_context_grad.1 = (f32[4,16,32,512]{3,2,1,0:T(8,128)}, f32[16,32,512]{2,1,0:T(8,128)}, f32[16,32,512]{2,1,0:T(8,128)}, f32[16,32,512]{2,1,0:T(8,128)}, f32[16,32,512]{2,1,0:T(8,128)}) custom-call(s32[1]{0:T(128)} %bitcast.pos, s32[8,8,34]{2,1,0:T(8,128)} %rows.5, s32[8,8,34]{2,1,0:T(8,128)} %cols.5, s32[8,8]{1,0:T(8,128)} %live.5, ...), custom_call_target="tpu_custom_call" | custom-call | flops 4300000256 | bytes 18000000 | tf_op jit(solution)/shard_map/partial_context_grad/pallas_call | solution.py:181
  33.9 1.0 collective-permute-start.2
  34.9 0.4 collective-permute-start
  35.5 1.3 collective-permute-start.3
  36.8 1.5 collective-permute-start.4
  38.3 6.1 %collective-permute-start.7 = (bf16[16,32,512]{2,1,0:T(8,128)(2,1)S(1)}, bf16[16,32,512]{2,1,0:T(8,128)(2,1)S(1)}, u32[]{:S(2)}, u32[]{:S(2)}) collective-permute-start(bf16[16,32,512]{2,1,0:T(8,128)(2,1)S(1)} %get-tuple-element.38.a0), channel_id=1, source_target_pairs={{0,1},{1,0},{2,3},{3,2},{4,5},{5,4},{6,7},{7,6},{8,9},{9,8},{10,11... | collective-permute-start | bytes 1572872 | tf_op jit(solution)/shard_map/ppermute | solution.py:162
  44.4 3.5 %slice_add_fusion.4 = (f32[8,32,512]{2,1,0:T(8,128)}, f32[8,32,512]{2,1,0:T(8,128)}, f32[8,32,512]{2,1,0:T(8,128)S(1)}, f32[8,32,512]{2,1,0:T(8,128)S(1)}) fusion(f32[16,32,512]{2,1,0:T(8,128)} %collective-permute-done.2, f32[4,16,32,512]{3,2,1,0:T(8,128)} %get-tuple-element.32, f32[16,32,512]{2,1,0:T(8,128)S(1)} %collective-permute-done.1, ...), kind=kLoop, calls=%fused_computation.12 | loop fusion | flops 524288 | bytes 6291456 | tf_op jit(solution)/shard_map/add | solution.py:199
  47.9 0.1 collective-permute-start.5
  48.1 2.7 %collective-permute-start.6 = (bf16[8,32,512]{2,1,0:T(8,128)(2,1)S(1)}, bf16[8,32,512]{2,1,0:T(8,128)(2,1)S(1)}, u32[]{:S(2)}, u32[]{:S(2)}) collective-permute-start(bf16[8,32,512]{2,1,0:T(8,128)(2,1)S(1)} %slice.77), channel_id=1, source_target_pairs={{0,6},{1,7},{2,0},{3,1},{4,2},{5,3},{6,4},{7,5},{8,14},{9,15},{10,... | collective-permute-start | bytes 786440 | tf_op jit(solution)/shard_map/ppermute | solution.py:159
  50.8 5.0 %collective-permute-start.8 = (bf16[16,32,512]{2,1,0:T(8,128)(2,1)S(1)}, bf16[16,32,512]{2,1,0:T(8,128)(2,1)S(1)}, u32[]{:S(2)}, u32[]{:S(2)}) collective-permute-start(bf16[16,32,512]{2,1,0:T(8,128)(2,1)S(1)} %collective-permute-done.3.am), channel_id=1, source_target_pairs={{0,1},{1,0},{2,3},{3,2},{4,5},{5,4},{6,7},{7,6},{8,9},{9,8},{10,11... | collective-permute-start | bytes 1572872 | tf_op jit(solution)/shard_map/ppermute | solution.py:162
  55.8 4.2 %collective-permute-start.10 = (bf16[8,32,512]{2,1,0:T(8,128)(2,1)S(1)}, bf16[8,32,512]{2,1,0:T(8,128)(2,1)S(1)}, u32[]{:S(2)}, u32[]{:S(2)}) collective-permute-start(bf16[8,32,512]{2,1,0:T(8,128)(2,1)S(1)} %collective-permute-done.5.a2a), channel_id=1, source_target_pairs={{0,1},{1,0},{2,3},{3,2},{4,5},{5,4},{6,7},{7,6},{8,9},{9,8},{10,11... | collective-permute-start | bytes 786440 | tf_op jit(solution)/shard_map/ppermute | solution.py:162
  60.1 0.5 collective-permute-start.11
  60.6 1.1 collective-permute-start.14
  61.7 1.6 %collective-permute-start.15 = (f32[8,32,512]{2,1,0:T(8,128)}, f32[8,32,512]{2,1,0:T(8,128)}, u32[]{:S(2)}, u32[]{:S(2)}) collective-permute-start(f32[8,32,512]{2,1,0:T(8,128)} %get-tuple-element.50), channel_id=1, source_target_pairs={{0,6},{1,7},{2,0},{3,1},{4,2},{5,3},{6,4},{7,5},{8,14},{9,15},{10,... | collective-permute-start | bytes 1572872 | tf_op jit(solution)/shard_map/ppermute | solution.py:159
  63.4 0.6 copy-done.17
  64.1 2.7 %collective-permute-start.13 = (bf16[16,32,512]{2,1,0:T(8,128)(2,1)S(1)}, bf16[16,32,512]{2,1,0:T(8,128)(2,1)S(1)}, u32[]{:S(2)}, u32[]{:S(2)}) collective-permute-start(bf16[16,32,512]{2,1,0:T(8,128)(2,1)S(1)} %get-tuple-element.48.a0), channel_id=1, source_target_pairs={{0,6},{1,7},{2,0},{3,1},{4,2},{5,3},{6,4},{7,5},{8,14},{9,15},{10,... | collective-permute-start | bytes 1572872 | tf_op jit(solution)/shard_map/ppermute | solution.py:159
  66.7 1.3 collective-permute-start.16
  68.0 15.0 %outputs.1 = bf16[256,1024]{1,0:T(8,128)(2,1)} custom-call(s32[1]{0:T(128)} %bitcast.pos, s32[8,8,34]{2,1,0:T(8,128)} %rows.5, s32[8,8,34]{2,1,0:T(8,128)} %cols.5, s32[8,8]{1,0:T(8,128)} %live.5, bf16[16,32,512]{2,1,0:T(8,128)(2,1)} %copy-done.3, bf16[16,32,512]{2,1,0:T(8,128)(2,1)} %copy-done.9, bf16[16,32,512]{2,1,0:T(8,128)(2,1)} %copy-done.10, ...), custom_call_target="tpu_custom_call" | custom-call | flops 4300000256 | bytes 14000000 | tf_op jit(solution)/shard_map/outputs/pallas_call | solution.py:213
  83.0 0.3 collective-permute-start.17
  83.3 1.3 collective-permute-start.19
  84.6 2.3 %collective-permute-done.12.am = bf16[16,32,512]{2,1,0:T(8,128)(2,1)S(1)} collective-permute-done((bf16[16,32,512]{2,1,0:T(8,128)(2,1)S(1)}, bf16[16,32,512]{2,1,0:T(8,128)(2,1)S(1)}, u32[]{:S(2)}, u32[]{:S(2)}) %collective-permute-start.12) | collective-permute-done | bytes 524320 | tf_op jit(solution)/shard_map/ppermute | solution.py:159
  86.9 2.4 %fusion.4 = (f32[8,32,512]{2,1,0:T(8,128)S(1)}, f32[8,32,512]{2,1,0:T(8,128)S(1)}) fusion(f32[8,32,512]{2,1,0:T(8,128)} %collective-permute-done.14, f32[16,32,512]{2,1,0:T(8,128)} %collective-permute-done, f32[4,16,32,512]{3,2,1,0:T(8,128)} %get-tuple-element.32, f32[8,32,512]{2,1,0:T(8,128)} %collective-permute-done.15, ...), kind=kLoop, calls=%fused_computation.7 | loop fusion | flops 524288 | bytes 4194304 | tf_op jit(solution)/shard_map/add | solution.py:233
  89.3 0.6 collective-permute-start.18
  89.9 2.2 %collective-permute-start.20 = (f32[8,32,512]{2,1,0:T(8,128)S(1)}, f32[8,32,512]{2,1,0:T(8,128)S(1)}, u32[]{:S(2)}, u32[]{:S(2)}) collective-permute-start(f32[8,32,512]{2,1,0:T(8,128)S(1)} %get-tuple-element.66), channel_id=1, source_target_pairs={{0,6},{1,7},{2,0},{3,1},{4,2},{5,3},{6,4},{7,5},{8,14},{9,15},{10,... | collective-permute-start | bytes 1572872 | tf_op jit(solution)/shard_map/ppermute | solution.py:159
  92.0 1.8 %collective-permute-start.21 = (bf16[16,32,512]{2,1,0:T(8,128)(2,1)S(1)}, bf16[16,32,512]{2,1,0:T(8,128)(2,1)S(1)}, u32[]{:S(2)}, u32[]{:S(2)}) collective-permute-start(bf16[16,32,512]{2,1,0:T(8,128)(2,1)S(1)} %get-tuple-element.48.a0), channel_id=1, source_target_pairs={{0,1},{1,0},{2,3},{3,2},{4,5},{5,4},{6,7},{7,6},{8,9},{9,8},{10,11... | collective-permute-start | bytes 1572872 | tf_op jit(solution)/shard_map/ppermute | solution.py:162
  93.8 3.7 %collective-permute-done.17 = f32[8,32,512]{2,1,0:T(8,128)S(1)} collective-permute-done((f32[8,32,512]{2,1,0:T(8,128)S(1)}, f32[8,32,512]{2,1,0:T(8,128)S(1)}, u32[]{:S(2)}, u32[]{:S(2)}) %collective-permute-start.17) | collective-permute-done | bytes 524320 | tf_op jit(solution)/shard_map/ppermute | solution.py:159
  97.6 2.0 %collective-permute-start.22 = (bf16[16,32,512]{2,1,0:T(8,128)(2,1)S(1)}, bf16[16,32,512]{2,1,0:T(8,128)(2,1)S(1)}, u32[]{:S(2)}, u32[]{:S(2)}) collective-permute-start(bf16[16,32,512]{2,1,0:T(8,128)(2,1)S(1)} %collective-permute-done.12.am), channel_id=1, source_target_pairs={{0,1},{1,0},{2,3},{3,2},{4,5},{5,4},{6,7},{7,6},{8,9},{9,8},{10,11... | collective-permute-start | bytes 1572872 | tf_op jit(solution)/shard_map/ppermute | solution.py:162
  99.5 0.7 slice.86
  100.2 0.7 slice.87
  101.0 8.1 %collective-permute-done.18 = f32[8,32,512]{2,1,0:T(8,128)S(1)} collective-permute-done((f32[8,32,512]{2,1,0:T(8,128)S(1)}, f32[8,32,512]{2,1,0:T(8,128)S(1)}, u32[]{:S(2)}, u32[]{:S(2)}) %collective-permute-start.18) | collective-permute-done | bytes 524320 | tf_op jit(solution)/shard_map/ppermute | solution.py:159
  109.1 2.7 %collective-permute-start.25 = (bf16[8,32,512]{2,1,0:T(8,128)(2,1)}, bf16[8,32,512]{2,1,0:T(8,128)(2,1)}, u32[]{:S(2)}, u32[]{:S(2)}) collective-permute-start(bf16[8,32,512]{2,1,0:T(8,128)(2,1)} %slice.87), channel_id=1, source_target_pairs={{0,6},{1,7},{2,0},{3,1},{4,2},{5,3},{6,4},{7,5},{8,14},{9,15},{10,... | collective-permute-start | bytes 786440 | tf_op jit(solution)/shard_map/ppermute | solution.py:159
  111.7 1.9 %fusion.7 = (bf16[8,32,512]{2,1,0:T(8,128)(2,1)S(1)}, bf16[8,32,512]{2,1,0:T(8,128)(2,1)S(1)}) fusion(f32[8,32,512]{2,1,0:T(8,128)S(1)} %collective-permute-done.18, f32[8,32,512]{2,1,0:T(8,128)S(1)} %collective-permute-done.17, f32[16,32,512]{2,1,0:T(8,128)} %collective-permute-done.16, f32[4,16,32,512]{3,2,1,0:T(8,128)} %get-tuple-element.32, ...), kind=kLoop, calls=%fused_computation.11 | loop fusion | flops 1048576 | bytes 4718592 | tf_op jit(solution)/shard_map/convert
  113.7 0.8 pad_maximum_fusion
  114.5 0.8 copy-done.4
  115.3 0.8 copy-done.5
  116.1 9.4 %near_weight_grad.1.near_ref = f32[64,8,1024]{2,1,0:T(8,128)} custom-call(s32[1]{0:T(128)} %bitcast.pos, bf16[16,32,512]{2,1,0:T(8,128)(2,1)} %copy-done, bf16[16,32,512]{2,1,0:T(8,128)(2,1)} %copy-done.1, bf16[16,32,512]{2,1,0:T(8,128)(2,1)} %copy-done.2, bf16[16,32,512]{2,1,0:T(8,128)(2,1)} %copy-done.4, bf16[16,32,512]{2,1,0:T(8,128)(2,1)} %copy-done.5, ...), custom_call_target="tpu_custom_call" | custom-call | flops 3200000000 | bytes 11000000 | tf_op jit(solution)/shard_map/near_weight_grad/pallas_call | solution.py:257
  125.5 6.6 %all-to-all-start.1 = ((bf16[16,32,512]{2,1,0:T(8,128)(2,1)}), bf16[16,32,512]{2,1,0:T(8,128)(2,1)S(1)}, u32[]{:S(2)}, u32[]{:S(2)}) async-start(bf16[16,32,512]{2,1,0:T(8,128)(2,1)} %pad_maximum_fusion), calls=%async_computation.1 | async-start | bytes 1048576 | tf_op jit(solution)/shard_map/all_to_all | solution.py:165
  132.1 1.6 %collective-permute-start.26 = (bf16[8,32,512]{2,1,0:T(8,128)(2,1)S(1)}, bf16[8,32,512]{2,1,0:T(8,128)(2,1)S(1)}, u32[]{:S(2)}, u32[]{:S(2)}) collective-permute-start(bf16[8,32,512]{2,1,0:T(8,128)(2,1)S(1)} %collective-permute-done.24.a2a), channel_id=1, source_target_pairs={{0,1},{1,0},{2,3},{3,2},{4,5},{5,4},{6,7},{7,6},{8,9},{9,8},{10,11... | collective-permute-start | bytes 786440 | tf_op jit(solution)/shard_map/ppermute | solution.py:162
  133.8 0.1 collective-permute-start.27
  133.9 1.1 collective-permute-done.26.b2a
  134.9 0.6 collective-permute-done.27.b2b
  135.5 0.1 copy-done.7
  135.6 0.7 copy-done.8
  136.3 7.4 %far_weight_grad.1 = bf16[1,8,34,8,128]{4,3,2,1,0:T(8,128)(2,1)} custom-call(s32[1]{0:T(128)} %bitcast.pos, s32[8,8,34]{2,1,0:T(8,128)} %rows.5, s32[8,8,34]{2,1,0:T(8,128)} %cols.5, s32[8,8]{1,0:T(8,128)} %live.5, bf16[8,32,512]{2,1,0:T(8,128)(2,1)} %copy-done.6, bf16[8,32,512]{2,1,0:T(8,128)(2,1)} %collective-permute-done.25.a2b, ...), custom_call_target="tpu_custom_call" | custom-call | flops 1100000000 | bytes 6000000 | tf_op jit(solution)/shard_map/far_weight_grad/pallas_call | solution.py:278
  143.7 0.8 copy.10
  (66 shorter events, 0.4 us)
Async XLA Ops:
  7.2 108.2 %all-gather.2.cloned.1.call-start = ((), (), s32[]{:S(2)}) async-start(), calls=%async_computation.2 | async-start | bytes 8912896 | tf_op jit(solution)/shard_map/all_gather | solution.py:167
  10.2 25.2 %all-to-all-start = ((bf16[16,64,512]{2,1,0:T(8,128)(2,1)}), bf16[16,64,512]{2,1,0:T(8,128)(2,1)S(1)}, u32[]{:S(2)}, u32[]{:S(2)}) async-start(bf16[16,64,512]{2,1,0:T(8,128)(2,1)} %feature_rows.1), calls=%async_computation | async-start | bytes 2097152 | tf_op jit(solution)/shard_map/all_to_all | solution.py:165
  33.9 4.4 %collective-permute-start.2 = (f32[16,32,512]{2,1,0:T(8,128)}, f32[16,32,512]{2,1,0:T(8,128)}, u32[]{:S(2)}, u32[]{:S(2)}) collective-permute-start(f32[16,32,512]{2,1,0:T(8,128)} %get-tuple-element.35), channel_id=1, source_target_pairs={{0,1},{1,0},{2,3},{3,2},{4,5},{5,4},{6,7},{7,6},{8,9},{9,8},{10,11... | collective-permute-start | bytes 3145736 | tf_op jit(solution)/shard_map/ppermute | solution.py:162
  34.9 9.5 %collective-permute-start.1 = (f32[16,32,512]{2,1,0:T(8,128)}, f32[16,32,512]{2,1,0:T(8,128)S(1)}, u32[]{:S(2)}, u32[]{:S(2)}) collective-permute-start(f32[16,32,512]{2,1,0:T(8,128)} %get-tuple-element.34), channel_id=1, source_target_pairs={{0,1},{1,0},{2,3},{3,2},{4,5},{5,4},{6,7},{7,6},{8,9},{9,8},{10,11... | collective-permute-start | bytes 3145736 | tf_op jit(solution)/shard_map/ppermute | solution.py:162
  34.9 9.4 %collective-permute-start = (f32[16,32,512]{2,1,0:T(8,128)}, f32[16,32,512]{2,1,0:T(8,128)}, u32[]{:S(2)}, u32[]{:S(2)}) collective-permute-start(f32[16,32,512]{2,1,0:T(8,128)} %get-tuple-element.33), channel_id=1, source_target_pairs={{0,1},{1,0},{2,3},{3,2},{4,5},{5,4},{6,7},{7,6},{8,9},{9,8},{10,11... | collective-permute-start | bytes 3145736 | tf_op jit(solution)/shard_map/ppermute | solution.py:162
  35.5 27.9 %copy-start.3 = (bf16[16,32,512]{2,1,0:T(8,128)(2,1)}, bf16[16,32,512]{2,1,0:T(8,128)(2,1)S(1)}, u32[]{:S(2)}) copy-start(bf16[16,32,512]{2,1,0:T(8,128)(2,1)S(1)} %get-tuple-element.38.a0) | copy-start | bytes 1572868
  35.5 56.6 %copy-start = (bf16[16,32,512]{2,1,0:T(8,128)(2,1)}, bf16[16,32,512]{2,1,0:T(8,128)(2,1)S(1)}, u32[]{:S(2)}) copy-start(bf16[16,32,512]{2,1,0:T(8,128)(2,1)S(1)} %get-tuple-element.48.a0) | copy-start | bytes 1572868
  35.5 12.4 %collective-permute-start.3 = (bf16[16,32,512]{2,1,0:T(8,128)(2,1)S(1)}, bf16[16,32,512]{2,1,0:T(8,128)(2,1)S(1)}, u32[]{:S(2)}, u32[]{:S(2)}) collective-permute-start(bf16[16,32,512]{2,1,0:T(8,128)(2,1)S(1)} %get-tuple-element.38.a0), channel_id=1, source_target_pairs={{0,2},{1,3},{2,4},{3,5},{4,6},{5,7},{6,0},{7,1},{8,10},{9,11},{10,... | collective-permute-start | bytes 1572872 | tf_op jit(solution)/shard_map/ppermute | solution.py:159
  36.8 11.1 %collective-permute-start.4 = (bf16[16,32,512]{2,1,0:T(8,128)(2,1)S(1)}, bf16[16,32,512]{2,1,0:T(8,128)(2,1)S(1)}, u32[]{:S(2)}, u32[]{:S(2)}) collective-permute-start(bf16[16,32,512]{2,1,0:T(8,128)(2,1)S(1)} %get-tuple-element.38.a0), channel_id=1, source_target_pairs={{0,6},{1,7},{2,0},{3,1},{4,2},{5,3},{6,4},{7,5},{8,14},{9,15},{10,... | collective-permute-start | bytes 1572872 | tf_op jit(solution)/shard_map/ppermute | solution.py:159
  38.3 22.3 %collective-permute-start.7 = (bf16[16,32,512]{2,1,0:T(8,128)(2,1)S(1)}, bf16[16,32,512]{2,1,0:T(8,128)(2,1)S(1)}, u32[]{:S(2)}, u32[]{:S(2)}) collective-permute-start(bf16[16,32,512]{2,1,0:T(8,128)(2,1)S(1)} %get-tuple-element.38.a0), channel_id=1, source_target_pairs={{0,1},{1,0},{2,3},{3,2},{4,5},{5,4},{6,7},{7,6},{8,9},{9,8},{10,11... | collective-permute-start | bytes 1572872 | tf_op jit(solution)/shard_map/ppermute | solution.py:162
  47.9 15.5 %copy-start.9 = (bf16[16,32,512]{2,1,0:T(8,128)(2,1)}, bf16[16,32,512]{2,1,0:T(8,128)(2,1)S(1)}, u32[]{:S(2)}) copy-start(bf16[16,32,512]{2,1,0:T(8,128)(2,1)S(1)} %collective-permute-done.3.am) | copy-start | bytes 1572868
  47.9 16.1 %copy-start.10 = (bf16[16,32,512]{2,1,0:T(8,128)(2,1)}, bf16[16,32,512]{2,1,0:T(8,128)(2,1)S(1)}, u32[]{:S(2)}) copy-start(bf16[16,32,512]{2,1,0:T(8,128)(2,1)S(1)} %collective-permute-done.4.ap) | copy-start | bytes 1572868
  47.9 7.9 %collective-permute-start.5 = (bf16[8,32,512]{2,1,0:T(8,128)(2,1)S(1)}, bf16[8,32,512]{2,1,0:T(8,128)(2,1)S(1)}, u32[]{:S(2)}, u32[]{:S(2)}) collective-permute-start(bf16[8,32,512]{2,1,0:T(8,128)(2,1)S(1)} %slice.76), channel_id=1, source_target_pairs={{0,2},{1,3},{2,4},{3,5},{4,6},{5,7},{6,0},{7,1},{8,10},{9,11},{10,... | collective-permute-start | bytes 786440 | tf_op jit(solution)/shard_map/ppermute | solution.py:159
  48.1 12.0 %collective-permute-start.6 = (bf16[8,32,512]{2,1,0:T(8,128)(2,1)S(1)}, bf16[8,32,512]{2,1,0:T(8,128)(2,1)S(1)}, u32[]{:S(2)}, u32[]{:S(2)}) collective-permute-start(bf16[8,32,512]{2,1,0:T(8,128)(2,1)S(1)} %slice.77), channel_id=1, source_target_pairs={{0,6},{1,7},{2,0},{3,1},{4,2},{5,3},{6,4},{7,5},{8,14},{9,15},{10,... | collective-permute-start | bytes 786440 | tf_op jit(solution)/shard_map/ppermute | solution.py:159
  50.8 12.5 %collective-permute-start.8 = (bf16[16,32,512]{2,1,0:T(8,128)(2,1)S(1)}, bf16[16,32,512]{2,1,0:T(8,128)(2,1)S(1)}, u32[]{:S(2)}, u32[]{:S(2)}) collective-permute-start(bf16[16,32,512]{2,1,0:T(8,128)(2,1)S(1)} %collective-permute-done.3.am), channel_id=1, source_target_pairs={{0,1},{1,0},{2,3},{3,2},{4,5},{5,4},{6,7},{7,6},{8,9},{9,8},{10,11... | collective-permute-start | bytes 1572872 | tf_op jit(solution)/shard_map/ppermute | solution.py:162
  55.8 7.5 %collective-permute-start.9 = (bf16[16,32,512]{2,1,0:T(8,128)(2,1)S(1)}, bf16[16,32,512]{2,1,0:T(8,128)(2,1)S(1)}, u32[]{:S(2)}, u32[]{:S(2)}) collective-permute-start(bf16[16,32,512]{2,1,0:T(8,128)(2,1)S(1)} %collective-permute-done.4.ap), channel_id=1, source_target_pairs={{0,1},{1,0},{2,3},{3,2},{4,5},{5,4},{6,7},{7,6},{8,9},{9,8},{10,11... | collective-permute-start | bytes 1572872 | tf_op jit(solution)/shard_map/ppermute | solution.py:162
  55.8 12.2 %copy-start.14 = (bf16[8,32,512]{2,1,0:T(8,128)(2,1)}, bf16[8,32,512]{2,1,0:T(8,128)(2,1)S(1)}, u32[]{:S(2)}) copy-start(bf16[8,32,512]{2,1,0:T(8,128)(2,1)S(1)} %collective-permute-done.5.a2a) | copy-start | bytes 786436
  55.8 5.9 %collective-permute-start.10 = (bf16[8,32,512]{2,1,0:T(8,128)(2,1)S(1)}, bf16[8,32,512]{2,1,0:T(8,128)(2,1)S(1)}, u32[]{:S(2)}, u32[]{:S(2)}) collective-permute-start(bf16[8,32,512]{2,1,0:T(8,128)(2,1)S(1)} %collective-permute-done.5.a2a), channel_id=1, source_target_pairs={{0,1},{1,0},{2,3},{3,2},{4,5},{5,4},{6,7},{7,6},{8,9},{9,8},{10,11... | collective-permute-start | bytes 786440 | tf_op jit(solution)/shard_map/ppermute | solution.py:162
  60.1 3.3 %copy-start.15 = (bf16[8,32,512]{2,1,0:T(8,128)(2,1)}, bf16[8,32,512]{2,1,0:T(8,128)(2,1)S(1)}, u32[]{:S(2)}) copy-start(bf16[8,32,512]{2,1,0:T(8,128)(2,1)S(1)} %collective-permute-done.6.a2b) | copy-start | bytes 786436
  60.1 3.2 %collective-permute-start.11 = (bf16[8,32,512]{2,1,0:T(8,128)(2,1)S(1)}, bf16[8,32,512]{2,1,0:T(8,128)(2,1)S(1)}, u32[]{:S(2)}, u32[]{:S(2)}) collective-permute-start(bf16[8,32,512]{2,1,0:T(8,128)(2,1)S(1)} %collective-permute-done.6.a2b), channel_id=1, source_target_pairs={{0,1},{1,0},{2,3},{3,2},{4,5},{5,4},{6,7},{7,6},{8,9},{9,8},{10,11... | collective-permute-start | bytes 786440 | tf_op jit(solution)/shard_map/ppermute | solution.py:162
  60.6 6.1 %copy-start.11 = (bf16[16,32,512]{2,1,0:T(8,128)(2,1)}, bf16[16,32,512]{2,1,0:T(8,128)(2,1)S(1)}, u32[]{:S(2)}) copy-start(bf16[16,32,512]{2,1,0:T(8,128)(2,1)S(1)} %collective-permute-done.7.b0) | copy-start | bytes 1572868
  60.6 22.4 %collective-permute-start.14 = (f32[8,32,512]{2,1,0:T(8,128)}, f32[8,32,512]{2,1,0:T(8,128)}, u32[]{:S(2)}, u32[]{:S(2)}) collective-permute-start(f32[8,32,512]{2,1,0:T(8,128)} %get-tuple-element.49), channel_id=1, source_target_pairs={{0,2},{1,3},{2,4},{3,5},{4,6},{5,7},{6,0},{7,1},{8,10},{9,11},{10,... | collective-permute-start | bytes 1572872 | tf_op jit(solution)/shard_map/ppermute | solution.py:159
  61.7 1.7 %copy-start.16 = (bf16[8,32,512]{2,1,0:T(8,128)(2,1)}, bf16[8,32,512]{2,1,0:T(8,128)(2,1)S(1)}, u32[]{:S(2)}) copy-start(bf16[8,32,512]{2,1,0:T(8,128)(2,1)S(1)} %collective-permute-done.10.b2a) | copy-start | bytes 786436
  61.7 21.6 %collective-permute-start.15 = (f32[8,32,512]{2,1,0:T(8,128)}, f32[8,32,512]{2,1,0:T(8,128)}, u32[]{:S(2)}, u32[]{:S(2)}) collective-permute-start(f32[8,32,512]{2,1,0:T(8,128)} %get-tuple-element.50), channel_id=1, source_target_pairs={{0,6},{1,7},{2,0},{3,1},{4,2},{5,3},{6,4},{7,5},{8,14},{9,15},{10,... | collective-permute-start | bytes 1572872 | tf_op jit(solution)/shard_map/ppermute | solution.py:159
  63.3 0.7 copy-start.17
  63.3 3.4 %copy-start.12 = (bf16[16,32,512]{2,1,0:T(8,128)(2,1)}, bf16[16,32,512]{2,1,0:T(8,128)(2,1)S(1)}, u32[]{:S(2)}) copy-start(bf16[16,32,512]{2,1,0:T(8,128)(2,1)S(1)} %collective-permute-done.8.bm) | copy-start | bytes 1572868
  63.4 3.4 %copy-start.13 = (bf16[16,32,512]{2,1,0:T(8,128)(2,1)}, bf16[16,32,512]{2,1,0:T(8,128)(2,1)S(1)}, u32[]{:S(2)}) copy-start(bf16[16,32,512]{2,1,0:T(8,128)(2,1)S(1)} %collective-permute-done.9.bp) | copy-start | bytes 1572868
  64.0 22.8 %collective-permute-start.12 = (bf16[16,32,512]{2,1,0:T(8,128)(2,1)S(1)}, bf16[16,32,512]{2,1,0:T(8,128)(2,1)S(1)}, u32[]{:S(2)}, u32[]{:S(2)}) collective-permute-start(bf16[16,32,512]{2,1,0:T(8,128)(2,1)S(1)} %get-tuple-element.48.a0), channel_id=1, source_target_pairs={{0,2},{1,3},{2,4},{3,5},{4,6},{5,7},{6,0},{7,1},{8,10},{9,11},{10,... | collective-permute-start | bytes 1572872 | tf_op jit(solution)/shard_map/ppermute | solution.py:159
  64.1 22.8 %collective-permute-start.13 = (bf16[16,32,512]{2,1,0:T(8,128)(2,1)S(1)}, bf16[16,32,512]{2,1,0:T(8,128)(2,1)S(1)}, u32[]{:S(2)}, u32[]{:S(2)}) collective-permute-start(bf16[16,32,512]{2,1,0:T(8,128)(2,1)S(1)} %get-tuple-element.48.a0), channel_id=1, source_target_pairs={{0,6},{1,7},{2,0},{3,1},{4,2},{5,3},{6,4},{7,5},{8,14},{9,15},{10,... | collective-permute-start | bytes 1572872 | tf_op jit(solution)/shard_map/ppermute | solution.py:159
  66.7 25.3 %collective-permute-start.16 = (f32[16,32,512]{2,1,0:T(8,128)}, f32[16,32,512]{2,1,0:T(8,128)}, u32[]{:S(2)}, u32[]{:S(2)}) collective-permute-start(f32[16,32,512]{2,1,0:T(8,128)} %get-tuple-element.52), channel_id=1, source_target_pairs={{0,1},{1,0},{2,3},{3,2},{4,5},{5,4},{6,7},{7,6},{8,9},{9,8},{10,11... | collective-permute-start | bytes 3145736 | tf_op jit(solution)/shard_map/ppermute | solution.py:162
  83.0 14.5 %collective-permute-start.17 = (f32[8,32,512]{2,1,0:T(8,128)S(1)}, f32[8,32,512]{2,1,0:T(8,128)S(1)}, u32[]{:S(2)}, u32[]{:S(2)}) collective-permute-start(f32[8,32,512]{2,1,0:T(8,128)S(1)} %get-tuple-element.53), channel_id=1, source_target_pairs={{0,6},{1,7},{2,0},{3,1},{4,2},{5,3},{6,4},{7,5},{8,14},{9,15},{10,... | collective-permute-start | bytes 1572872 | tf_op jit(solution)/shard_map/ppermute | solution.py:159
  83.3 16.2 %collective-permute-start.19 = (f32[8,32,512]{2,1,0:T(8,128)S(1)}, f32[8,32,512]{2,1,0:T(8,128)S(1)}, u32[]{:S(2)}, u32[]{:S(2)}) collective-permute-start(f32[8,32,512]{2,1,0:T(8,128)S(1)} %get-tuple-element.55), channel_id=1, source_target_pairs={{0,2},{1,3},{2,4},{3,5},{4,6},{5,7},{6,0},{7,1},{8,10},{9,11},{10,... | collective-permute-start | bytes 1572872 | tf_op jit(solution)/shard_map/ppermute | solution.py:159
  86.9 26.8 %copy-start.1 = (bf16[16,32,512]{2,1,0:T(8,128)(2,1)}, bf16[16,32,512]{2,1,0:T(8,128)(2,1)S(1)}, u32[]{:S(2)}) copy-start(bf16[16,32,512]{2,1,0:T(8,128)(2,1)S(1)} %collective-permute-done.12.am) | copy-start | bytes 1572868
  86.9 26.8 %copy-start.2 = (bf16[16,32,512]{2,1,0:T(8,128)(2,1)}, bf16[16,32,512]{2,1,0:T(8,128)(2,1)S(1)}, u32[]{:S(2)}) copy-start(bf16[16,32,512]{2,1,0:T(8,128)(2,1)S(1)} %collective-permute-done.13.ap) | copy-start | bytes 1572868
  89.3 19.8 %collective-permute-start.18 = (f32[8,32,512]{2,1,0:T(8,128)S(1)}, f32[8,32,512]{2,1,0:T(8,128)S(1)}, u32[]{:S(2)}, u32[]{:S(2)}) collective-permute-start(f32[8,32,512]{2,1,0:T(8,128)S(1)} %get-tuple-element.65), channel_id=1, source_target_pairs={{0,2},{1,3},{2,4},{3,5},{4,6},{5,7},{6,0},{7,1},{8,10},{9,11},{10,... | collective-permute-start | bytes 1572872 | tf_op jit(solution)/shard_map/ppermute | solution.py:159
  89.9 19.2 %collective-permute-start.20 = (f32[8,32,512]{2,1,0:T(8,128)S(1)}, f32[8,32,512]{2,1,0:T(8,128)S(1)}, u32[]{:S(2)}, u32[]{:S(2)}) collective-permute-start(f32[8,32,512]{2,1,0:T(8,128)S(1)} %get-tuple-element.66), channel_id=1, source_target_pairs={{0,6},{1,7},{2,0},{3,1},{4,2},{5,3},{6,4},{7,5},{8,14},{9,15},{10,... | collective-permute-start | bytes 1572872 | tf_op jit(solution)/shard_map/ppermute | solution.py:159
  92.0 22.5 %collective-permute-start.21 = (bf16[16,32,512]{2,1,0:T(8,128)(2,1)S(1)}, bf16[16,32,512]{2,1,0:T(8,128)(2,1)S(1)}, u32[]{:S(2)}, u32[]{:S(2)}) collective-permute-start(bf16[16,32,512]{2,1,0:T(8,128)(2,1)S(1)} %get-tuple-element.48.a0), channel_id=1, source_target_pairs={{0,1},{1,0},{2,3},{3,2},{4,5},{5,4},{6,7},{7,6},{8,9},{9,8},{10,11... | collective-permute-start | bytes 1572872 | tf_op jit(solution)/shard_map/ppermute | solution.py:162
  97.6 17.0 %collective-permute-start.22 = (bf16[16,32,512]{2,1,0:T(8,128)(2,1)S(1)}, bf16[16,32,512]{2,1,0:T(8,128)(2,1)S(1)}, u32[]{:S(2)}, u32[]{:S(2)}) collective-permute-start(bf16[16,32,512]{2,1,0:T(8,128)(2,1)S(1)} %collective-permute-done.12.am), channel_id=1, source_target_pairs={{0,1},{1,0},{2,3},{3,2},{4,5},{5,4},{6,7},{7,6},{8,9},{9,8},{10,11... | collective-permute-start | bytes 1572872 | tf_op jit(solution)/shard_map/ppermute | solution.py:162
  99.5 15.8 %collective-permute-start.23 = (bf16[16,32,512]{2,1,0:T(8,128)(2,1)S(1)}, bf16[16,32,512]{2,1,0:T(8,128)(2,1)}, u32[]{:S(2)}, u32[]{:S(2)}) collective-permute-start(bf16[16,32,512]{2,1,0:T(8,128)(2,1)S(1)} %collective-permute-done.13.ap), channel_id=1, source_target_pairs={{0,1},{1,0},{2,3},{3,2},{4,5},{5,4},{6,7},{7,6},{8,9},{9,8},{10,11... | collective-permute-start | bytes 1572872 | tf_op jit(solution)/shard_map/ppermute | solution.py:162
  109.1 23.1 %collective-permute-start.24 = (bf16[8,32,512]{2,1,0:T(8,128)(2,1)}, bf16[8,32,512]{2,1,0:T(8,128)(2,1)S(1)}, u32[]{:S(2)}, u32[]{:S(2)}) collective-permute-start(bf16[8,32,512]{2,1,0:T(8,128)(2,1)} %slice.86), channel_id=1, source_target_pairs={{0,2},{1,3},{2,4},{3,5},{4,6},{5,7},{6,0},{7,1},{8,10},{9,11},{10,... | collective-permute-start | bytes 786440 | tf_op jit(solution)/shard_map/ppermute | solution.py:159
  109.1 24.7 %collective-permute-start.25 = (bf16[8,32,512]{2,1,0:T(8,128)(2,1)}, bf16[8,32,512]{2,1,0:T(8,128)(2,1)}, u32[]{:S(2)}, u32[]{:S(2)}) collective-permute-start(bf16[8,32,512]{2,1,0:T(8,128)(2,1)} %slice.87), channel_id=1, source_target_pairs={{0,6},{1,7},{2,0},{3,1},{4,2},{5,3},{6,4},{7,5},{8,14},{9,15},{10,... | collective-permute-start | bytes 786440 | tf_op jit(solution)/shard_map/ppermute | solution.py:159
  114.5 0.8 copy-start.4
  115.3 0.8 copy-start.5
  125.5 18.2 %all-to-all-start.1 = ((bf16[16,32,512]{2,1,0:T(8,128)(2,1)}), bf16[16,32,512]{2,1,0:T(8,128)(2,1)S(1)}, u32[]{:S(2)}, u32[]{:S(2)}) async-start(bf16[16,32,512]{2,1,0:T(8,128)(2,1)} %pad_maximum_fusion), calls=%async_computation.1 | async-start | bytes 1048576 | tf_op jit(solution)/shard_map/all_to_all | solution.py:165
  132.1 3.4 %copy-start.6 = (bf16[8,32,512]{2,1,0:T(8,128)(2,1)}, bf16[8,32,512]{2,1,0:T(8,128)(2,1)S(1)}, u32[]{:S(2)}) copy-start(bf16[8,32,512]{2,1,0:T(8,128)(2,1)S(1)} %collective-permute-done.24.a2a) | copy-start | bytes 786436
  132.1 2.8 %collective-permute-start.26 = (bf16[8,32,512]{2,1,0:T(8,128)(2,1)S(1)}, bf16[8,32,512]{2,1,0:T(8,128)(2,1)S(1)}, u32[]{:S(2)}, u32[]{:S(2)}) collective-permute-start(bf16[8,32,512]{2,1,0:T(8,128)(2,1)S(1)} %collective-permute-done.24.a2a), channel_id=1, source_target_pairs={{0,1},{1,0},{2,3},{3,2},{4,5},{5,4},{6,7},{7,6},{8,9},{9,8},{10,11... | collective-permute-start | bytes 786440 | tf_op jit(solution)/shard_map/ppermute | solution.py:162
  133.8 1.7 %collective-permute-start.27 = (bf16[8,32,512]{2,1,0:T(8,128)(2,1)}, bf16[8,32,512]{2,1,0:T(8,128)(2,1)S(1)}, u32[]{:S(2)}, u32[]{:S(2)}) collective-permute-start(bf16[8,32,512]{2,1,0:T(8,128)(2,1)} %collective-permute-done.25.a2b), channel_id=1, source_target_pairs={{0,1},{1,0},{2,3},{3,2},{4,5},{5,4},{6,7},{7,6},{8,9},{9,8},{10,11... | collective-permute-start | bytes 786440 | tf_op jit(solution)/shard_map/ppermute | solution.py:162
  134.9 0.7 copy-start.7
  (1 other events, 0.7 us)
Sparse Core Ops, SparseCore 0:
  10.1 78.8 all-gather.1

commit v4 on v2

--- a/solution.py
+++ b/solution.py
@@ -37,12 +37,12 @@
         o_ref[part, pl.ds(32, 32)] = t[:, part].reshape(32, 512).astype(BF16)
 
 
-def partial_kernel(pos, rows, cols, live, cot_ref, blk_ref, keep, send0, send1, send2, send3, lhs, panel):
+def partial_kernel(pos, rows, cols, live, cot_ref, blk_ref, keep, across, rest, lhs, panel):
     j = pl.program_id(0)
     owner = pos[0]
     y = owner // 2
     core = owner % 2
-    sends = (send0, send1, send2, send3)
+    sends = (rest.at[0], rest.at[1], across, rest.at[2])
 
     @pl.when(j == 0)
     def _():
@@ -172,45 +172,53 @@
         compiler_params=params,
         name="feature_rows",
     )(context)
+    both, cot_own = barrier((both, cotangent))
     both = exchange(both)
     tokens, class_rows = both[:, :32], both[:, 32:]
 
     blk_spec = pl.BlockSpec((1, 1, 34, 128, 128), lambda j, *_: (0, j, 0, 0, 0))
-    part = jax.ShapeDtypeStruct((16, 32, 512), F32)
-    part_spec = pl.BlockSpec((2, 32, 512), lambda j, *_: (j, 0, 0))
-    keep, *sends = pl.pallas_call(
+    keep, across, rest = pl.pallas_call(
         partial_kernel,
         grid_spec=pltpu.PrefetchScalarGridSpec(
             num_scalar_prefetch=4,
             grid=(8,),
             in_specs=[pl.BlockSpec((4, 2, 32, 1024), lambda j, *_: (0, 0, 0, 0)), blk_spec],
-            out_specs=[pl.BlockSpec((4, 2, 32, 512), lambda j, *_: (0, j, 0, 0))] + [part_spec] * 4,
+            out_specs=[
+                pl.BlockSpec((4, 2, 32, 512), lambda j, *_: (0, j, 0, 0)),
+                pl.BlockSpec((2, 32, 512), lambda j, *_: (j, 0, 0)),
+                pl.BlockSpec((3, 2, 32, 512), lambda j, *_: (0, j, 0, 0)),
+            ],
             scratch_shapes=[pltpu.VMEM((256, 1024), BF16), pltpu.VMEM((1024, 1024), BF16)],
         ),
-        out_shape=[jax.ShapeDtypeStruct((4, 16, 32, 512), F32)] + [part] * 4,
-        compiler_params=params,
-        cost_estimate=cost(4_300_000_000, 18_000_000),
+        out_shape=[
+            jax.ShapeDtypeStruct((4, 16, 32, 512), F32),
+            jax.ShapeDtypeStruct((16, 32, 512), F32),
+            jax.ShapeDtypeStruct((3, 16, 32, 512), F32),
+        ],
+        compiler_params=params,
+        cost_estimate=cost(4_300_000_000, 52_000_000),
         name="partial_context_grad",
-    )(*tables, cotangent.reshape(4, 2, 32, 1024), blocks)
-    r2, r1, r3, r0 = (other_core(sends[d]) for d in (2, 1, 3, 0))
+    )(*tables, cot_own.reshape(4, 2, 32, 1024), blocks)
+    across = other_core(across)
 
     xm, xp = along_y(tokens, 1), along_y(tokens, -1)
-
-    q2a, q2b = keep[2, :8] + r2[:8], keep[2, 8:] + r2[8:]
-    q1b, q3a = keep[1, 8:] + r1[8:], keep[3, :8] + r3[:8]
-    q2a, q2b, q1b, q3a, class_rows = barrier((q2a, q2b, q1b, q3a, class_rows))
+    rest, _ = barrier((rest, tokens))
+    rest = other_core(rest)
+
+    q2a, q2b, xm, xp = barrier((keep[2, :8] + across[:8], keep[2, 8:] + across[8:], xm, xp))
+    xma, xpb, q2a, q2b = barrier((xm[:8], xp[8:], q2a, q2b))
+    x2a, x2b = along_y(xma, 1), along_y(xpb, -1)
     from_a, from_b = along_y(q2a, 1), along_y(q2b, -1)
-    near_b, near_a = along_y(q1b, 1), along_y(q3a, -1)
-
-    x2a, x2b = along_y(xm[:8], 1), along_y(xp[8:], -1)
     own = (tokens, xm, xp, x2a, x2b)
     x_pieces = own + tuple(other_core(piece) for piece in own)
 
+    class_rows, x2a, x2b = barrier((class_rows, x2a, x2b))
     cm, cp = along_y(class_rows, 1), along_y(class_rows, -1)
 
-    q1a, q3b = keep[1, :8] + r1[:8] + from_a, keep[3, 8:] + r3[8:] + from_b
-    q1a, q3b, x_pieces = barrier((q1a, q3b, x_pieces))
-    far_a, far_b = along_y(q1a, 1), along_y(q3b, -1)
+    q1 = jnp.concatenate([keep[1, :8] + rest[1, :8] + from_a, keep[1, 8:] + rest[1, 8:]], axis=0)
+    q3 = jnp.concatenate([keep[3, :8] + rest[2, :8], keep[3, 8:] + rest[2, 8:] + from_b], axis=0)
+    q1, q3, x_pieces = barrier((q1, q3, x_pieces))
+    sum_m, sum_p = along_y(q1, 1), along_y(q3, -1)
 
     whole = pl.BlockSpec((2, 32, 512), lambda j, *_: (j, 0, 0))
     low = pl.BlockSpec((2, 32, 512), lambda j, *_: (jnp.minimum(j, 3), 0, 0))
@@ -230,7 +238,7 @@
         ),
         out_shape=jax.ShapeDtypeStruct((256, 1024), BF16),
         compiler_params=params,
-        cost_estimate=cost(4_300_000_000, 14_000_000),
+        cost_estimate=cost(4_300_000_000, 52_000_000),
         name="outputs",
     )(*tables, *x_pieces, blocks)
 
@@ -267,14 +275,12 @@
         ),
         out_shape=total,
         compiler_params=params,
-        cost_estimate=cost(3_200_000_000, 11_000_000),
+        cost_estimate=cost(3_200_000_000, 32_000_000),
         name="near_weight_grad",
     )(pos, *near, cot_groups)
 
-    sum_a = keep[0, :8] + r0[:8] + near_a + far_a
-    sum_b = keep[0, 8:] + r0[8:] + near_b + far_b
-    context_sum = jnp.concatenate([sum_a, sum_b], axis=0).astype(BF16)
-    context_sum, near_grad = barrier((context_sum, near_grad))
+    sum_m, sum_p, near_grad = barrier((sum_m, sum_p, near_grad))
+    context_sum = (keep[0] + rest[0] + sum_m + sum_p).astype(BF16)
     context_grad = exchange(context_sum)
 
     weight_grad = pl.pallas_call(
@@ -288,7 +294,7 @@
         ),
         out_shape=jax.ShapeDtypeStruct((1, 8, 34, 8, 128), BF16),
         compiler_params=params,
-        cost_estimate=cost(1_100_000_000, 6_000_000),
+        cost_estimate=cost(1_100_000_000, 25_000_000),
         name="far_weight_grad",
     )(*tables, c2a, c2b, other_core(c2a), other_core(c2b), cot_groups, near_grad)
     return (outputs, context_grad, weight_grad)

time: 151 us -> 150 us (level)
  starting transfers between devices: 53.2 us -> 40.4 us
  waiting for transfers between devices: 19.9 us -> 32 us
  other arithmetic: 8.42 us -> 6.53 us
    ppermute x14 -> x12, starting transfers between devices: 22.8 us -> 12.2 us  [other_core(): return lax.ppermute(x, 'mp', [(i, i ^ 1) for i in range(8)])]
    ppermute x14 -> x12, waiting for transfers between devices: 16.5 us -> 23 us  [along_y(): return lax.ppermute(x, 'mp', [(i, (i + 2 * step) % 8) for i in range(8)])]
    ppermute x14 -> x12, waiting for transfers between devices: 2.69 us -> 7.22 us  [other_core(): return lax.ppermute(x, 'mp', [(i, i ^ 1) for i in range(8)])]
    add x2 -> x3, other arithmetic: 5.35 us -> 1.99 us  [the longest x1 1.41 us: on_device(): keep[2, 8:] + across[8:]]
    convert_element_type x0 -> x1, other arithmetic: none -> 3.05 us  [on_device(): context_sum = (keep[0] + rest[0] + sum_m + sum_p).astype(BF16)]
    another operation x1 -> x0, other arithmetic: 2.23 us -> none
    ppermute x14 -> x12, starting transfers between devices: 16.5 us -> 14.6 us  [along_y(): return lax.ppermute(x, 'mp', [(i, (i + 2 * step) % 8) for i in range(8)])]
    slice x2, local copies, waits for them, and re-layouts: 1.44 us -> 3.34 us  [on_device(): c2a, c2b = (along_y(cm[:8], 1), along_y(cp[8:], -1))]
  transfers between devices with their start and end apart: 31 -> 27, of which waited for: 8 -> 7; matrix products, arithmetic and copies ran while one was open for 7% -> 7% of each run, Pallas kernels for 33% -> 33%
where the time goes in v4:
time: 150 us; the launch traced here: 148 us
  Pallas kernels  49.2 us (33%)
  starting transfers between devices  40.4 us (27%)
  waiting for transfers between devices  32 us (21%)
  between operations  14.3 us (10%)
  other arithmetic  6.53 us (4%)
  local copies, waits for them, and re-layouts  6.02 us (4%)
    ppermute x12, waiting for transfers between devices, along_y(): return lax.ppermute(x, 'mp', [(i, (i + 2 * step) % 8) for i in range(8)])  23 us
    pallas_call x1, Pallas kernels, on_device(): pl.pallas_call(partial_kernel, grid_spec=pltpu.PrefetchScalarGridSpec(num...  15.3 us
    pallas_call x1, Pallas kernels, on_device(): pl.pallas_call(out_kernel, grid_spec=pltpu.PrefetchScalarGridSpec(num_sca...  14.9 us
    ppermute x12, starting transfers between devices, along_y(): return lax.ppermute(x, 'mp', [(i, (i + 2 * step) % 8) for i in range(8)])  14.6 us
    all_to_all x2, starting transfers between devices, exchange(): return lax.all_to_all(x, 'seq', split_axis=0, concat_axis=0, tiled=True)  13.6 us
    ppermute x12, starting transfers between devices, other_core(): return lax.ppermute(x, 'mp', [(i, i ^ 1) for i in range(8)])  12.2 us
    pallas_call x1, Pallas kernels, on_device(): pl.pallas_call(near_grad_kernel, grid_spec=pltpu.PrefetchScalarGridSpec(n...  9.44 us
    pallas_call x1, Pallas kernels, on_device(): pl.pallas_call(functools.partial(far_grad_kernel, 1.0 / math.sqrt(4096)),...  7.4 us
  transfers between devices with their start and end apart: 27, of which 7 were waited for; matrix products, arithmetic and copies ran while one was open for 7% of the time, Pallas kernels for 33%

profile of v4, /device:TPU:1, one launch (start us, length us, event | category | flops | bytes accessed | tf_op | source)
XLA Modules:
  0.0 148.4 jit_solution(2410803640699380301)
XLA Ops:
  7.2 0.7 all-gather.2.cloned.1.call-update
  7.9 2.2 %feature_rows.1 = bf16[16,64,512]{2,1,0:T(8,128)(2,1)} custom-call(bf16[16,32,512]{2,1,0:T(8,128)(2,1)} %x_ref.1), custom_call_target="tpu_custom_call" | custom-call | tf_op jit(solution)/shard_map/feature_rows/pallas_call | solution.py:169
  10.1 8.4 %all-to-all-start = ((bf16[16,64,512]{2,1,0:T(8,128)(2,1)}), bf16[16,64,512]{2,1,0:T(8,128)(2,1)S(1)}, u32[]{:S(2)}, u32[]{:S(2)}) async-start(bf16[16,64,512]{2,1,0:T(8,128)(2,1)} %feature_rows.1), calls=%async_computation | async-start | bytes 2097152 | tf_op jit(solution)/shard_map/all_to_all | solution.py:165
  18.6 15.3 %partial_context_grad.1 = (f32[4,16,32,512]{3,2,1,0:T(8,128)}, f32[16,32,512]{2,1,0:T(8,128)}, f32[3,16,32,512]{3,2,1,0:T(8,128)}) custom-call(s32[1]{0:T(128)} %bitcast.pos, s32[8,8,34]{2,1,0:T(8,128)} %rows.5, s32[8,8,34]{2,1,0:T(8,128)} %cols.5, s32[8,8]{1,0:T(8,128)} %live.5, bf16[4,2,32,1024]{3,2,1,0:T(8,128)(2,1)} %bitcast.29, ...), custom_call_target="tpu_custom_call" | custom-call | flops 4300000256 | bytes 52000000 | tf_op jit(solution)/shard_map/partial_context_grad/pallas_call | solution.py:180
  33.9 1.1 all-to-all-done
  35.0 0.1 fusion.10
  35.1 5.9 %collective-permute-start = (f32[3,16,32,512]{3,2,1,0:T(8,128)}, f32[3,16,32,512]{3,2,1,0:T(8,128)S(1)}, u32[]{:S(2)}, u32[]{:S(2)}) collective-permute-start(f32[3,16,32,512]{3,2,1,0:T(8,128)} %get-tuple-element.40), channel_id=1, source_target_pairs={{0,1},{1,0},{2,3},{3,2},{4,5},{5,4},{6,7},{7,6},{8,9},{9,8},{10,11... | collective-permute-start | bytes 9437192 | tf_op jit(solution)/shard_map/ppermute | solution.py:162
  41.0 0.1 collective-permute-start.1
  41.1 1.4 collective-permute-start.2
  42.5 1.6 %collective-permute-start.3 = (bf16[16,32,512]{2,1,0:T(8,128)(2,1)S(1)}, bf16[16,32,512]{2,1,0:T(8,128)(2,1)S(1)}, u32[]{:S(2)}, u32[]{:S(2)}) collective-permute-start(bf16[16,32,512]{2,1,0:T(8,128)(2,1)S(1)} %get-tuple-element.50.a0), channel_id=1, source_target_pairs={{0,6},{1,7},{2,0},{3,1},{4,2},{5,3},{6,4},{7,5},{8,14},{9,15},{10,... | collective-permute-start | bytes 1572872 | tf_op jit(solution)/shard_map/ppermute | solution.py:159
  44.1 3.9 %collective-permute-done.1 = f32[16,32,512]{2,1,0:T(8,128)S(1)} collective-permute-done((f32[16,32,512]{2,1,0:T(8,128)}, f32[16,32,512]{2,1,0:T(8,128)S(1)}, u32[]{:S(2)}, u32[]{:S(2)}) %collective-permute-start.1) | collective-permute-done | bytes 1048608 | tf_op jit(solution)/shard_map/ppermute | solution.py:162
  48.0 1.4 slice_add_fusion.4
  49.4 6.7 %collective-permute-done.2.am = bf16[16,32,512]{2,1,0:T(8,128)(2,1)S(1)} collective-permute-done((bf16[16,32,512]{2,1,0:T(8,128)(2,1)S(1)}, bf16[16,32,512]{2,1,0:T(8,128)(2,1)S(1)}, u32[]{:S(2)}, u32[]{:S(2)}) %collective-permute-start.2) | collective-permute-done | bytes 524320 | tf_op jit(solution)/shard_map/ppermute | solution.py:159
  56.2 2.4 %collective-permute-start.5 = (f32[8,32,512]{2,1,0:T(8,128)S(1)}, f32[8,32,512]{2,1,0:T(8,128)S(1)}, u32[]{:S(2)}, u32[]{:S(2)}) collective-permute-start(f32[8,32,512]{2,1,0:T(8,128)S(1)} %get-tuple-element.47), channel_id=1, source_target_pairs={{0,6},{1,7},{2,0},{3,1},{4,2},{5,3},{6,4},{7,5},{8,14},{9,15},{10,... | collective-permute-start | bytes 1572872 | tf_op jit(solution)/shard_map/ppermute | solution.py:159
  58.6 2.7 %collective-permute-start.7 = (bf16[8,32,512]{2,1,0:T(8,128)(2,1)S(1)}, bf16[8,32,512]{2,1,0:T(8,128)(2,1)S(1)}, u32[]{:S(2)}, u32[]{:S(2)}) collective-permute-start(bf16[8,32,512]{2,1,0:T(8,128)(2,1)S(1)} %slice.68), channel_id=1, source_target_pairs={{0,6},{1,7},{2,0},{3,1},{4,2},{5,3},{6,4},{7,5},{8,14},{9,15},{10,... | collective-permute-start | bytes 786440 | tf_op jit(solution)/shard_map/ppermute | solution.py:159
  61.3 16.2 %collective-permute-done.6.a2a = bf16[8,32,512]{2,1,0:T(8,128)(2,1)S(1)} collective-permute-done((bf16[8,32,512]{2,1,0:T(8,128)(2,1)S(1)}, bf16[8,32,512]{2,1,0:T(8,128)(2,1)S(1)}, u32[]{:S(2)}, u32[]{:S(2)}) %collective-permute-start.6) | collective-permute-done | bytes 262176 | tf_op jit(solution)/shard_map/ppermute | solution.py:159
  77.5 2.2 %collective-permute-start.8 = (bf16[16,32,512]{2,1,0:T(8,128)(2,1)S(1)}, bf16[16,32,512]{2,1,0:T(8,128)(2,1)S(1)}, u32[]{:S(2)}, u32[]{:S(2)}) collective-permute-start(bf16[16,32,512]{2,1,0:T(8,128)(2,1)S(1)} %get-tuple-element.50.a0), channel_id=1, source_target_pairs={{0,1},{1,0},{2,3},{3,2},{4,5},{5,4},{6,7},{7,6},{8,9},{9,8},{10,11... | collective-permute-start | bytes 1572872 | tf_op jit(solution)/shard_map/ppermute | solution.py:162
  79.8 0.1 collective-permute-start.9
  79.8 0.4 collective-permute-start.10
  80.3 0.1 collective-permute-start.11
  80.4 0.4 collective-permute-start.12
  80.8 0.4 fusion.5
  81.2 0.2 fusion.6
  81.5 1.6 %collective-permute-done.11.b2a = bf16[8,32,512]{2,1,0:T(8,128)(2,1)S(1)} collective-permute-done((bf16[8,32,512]{2,1,0:T(8,128)(2,1)S(1)}, bf16[8,32,512]{2,1,0:T(8,128)(2,1)S(1)}, u32[]{:S(2)}, u32[]{:S(2)}) %collective-permute-start.11) | collective-permute-done | bytes 262176 | tf_op jit(solution)/shard_map/ppermute | solution.py:162
  83.2 1.0 collective-permute-start.14
  84.2 1.5 %pad_maximum_fusion = (f32[16,32,512]{2,1,0:T(8,128)}, f32[16,32,512]{2,1,0:T(8,128)}) fusion(f32[8,32,512]{2,1,0:T(8,128)S(1)} %get-tuple-element.70, f32[8,32,512]{2,1,0:T(8,128)S(1)} %get-tuple-element.72, f32[8,32,512]{2,1,0:T(8,128)S(1)} %get-tuple-element.71, f32[8,32,512]{2,1,0:T(8,128)S(1)} %get-tuple-element.69), kind=kLoop, calls=%fused_computation.5 | loop fusion | flops 524288 | bytes 4194304 | tf_op jit(solution)/shard_map/concatenate | solution.py:218
  85.7 0.8 collective-permute-start.17
  86.5 0.8 copy-done.9
  87.3 0.1 copy-done.10
  87.5 0.4 collective-permute-start.15
  87.9 2.3 %collective-permute-start.16 = (f32[16,32,512]{2,1,0:T(8,128)}, f32[16,32,512]{2,1,0:T(8,128)}, u32[]{:S(2)}, u32[]{:S(2)}) collective-permute-start(f32[16,32,512]{2,1,0:T(8,128)} %get-tuple-element.63), channel_id=1, source_target_pairs={{0,6},{1,7},{2,0},{3,1},{4,2},{5,3},{6,4},{7,5},{8,14},{9,15},{10,... | collective-permute-start | bytes 3145736 | tf_op jit(solution)/shard_map/ppermute | solution.py:159
  90.2 14.9 %outputs.1 = bf16[256,1024]{1,0:T(8,128)(2,1)} custom-call(s32[1]{0:T(128)} %bitcast.pos, s32[8,8,34]{2,1,0:T(8,128)} %rows.5, s32[8,8,34]{2,1,0:T(8,128)} %cols.5, s32[8,8]{1,0:T(8,128)} %live.5, bf16[16,32,512]{2,1,0:T(8,128)(2,1)} %copy-done.2, bf16[16,32,512]{2,1,0:T(8,128)(2,1)} %copy-done.6, bf16[16,32,512]{2,1,0:T(8,128)(2,1)} %copy-done.7, ...), custom_call_target="tpu_custom_call" | custom-call | flops 4300000256 | bytes 52000000 | tf_op jit(solution)/shard_map/outputs/pallas_call | solution.py:226
  105.0 0.6 collective-permute-start.18
  105.6 0.1 collective-permute-start.19
  105.7 1.7 %slice.78 = bf16[8,32,512]{2,1,0:T(8,128)(2,1)} slice(bf16[16,32,512]{2,1,0:T(8,128)(2,1)} %collective-permute-done.13.am), slice={[0:8], [0:32], [0:512]} | slice | bytes 524288 | tf_op jit(solution)/shard_map/slice | solution.py:246
  107.4 1.7 %slice.79 = bf16[8,32,512]{2,1,0:T(8,128)(2,1)} slice(bf16[16,32,512]{2,1,0:T(8,128)(2,1)} %collective-permute-done.14.ap), slice={[8:16], [0:32], [0:512]} | slice | bytes 524288 | tf_op jit(solution)/shard_map/slice | solution.py:246
  109.1 2.7 %collective-permute-start.21 = (bf16[8,32,512]{2,1,0:T(8,128)(2,1)}, bf16[8,32,512]{2,1,0:T(8,128)(2,1)}, u32[]{:S(2)}, u32[]{:S(2)}) collective-permute-start(bf16[8,32,512]{2,1,0:T(8,128)(2,1)} %slice.79), channel_id=1, source_target_pairs={{0,6},{1,7},{2,0},{3,1},{4,2},{5,3},{6,4},{7,5},{8,14},{9,15},{10,... | collective-permute-start | bytes 786440 | tf_op jit(solution)/shard_map/ppermute | solution.py:159
  111.8 9.4 %near_weight_grad.1.near_ref = f32[64,8,1024]{2,1,0:T(8,128)} custom-call(s32[1]{0:T(128)} %bitcast.pos, bf16[16,32,512]{2,1,0:T(8,128)(2,1)} %copy-done.1, bf16[16,32,512]{2,1,0:T(8,128)(2,1)} %collective-permute-done.13.am, bf16[16,32,512]{2,1,0:T(8,128)(2,1)} %collective-permute-done.14.ap, bf16[16,32,512]{2,1,0:T(8,128)(2,1)} %collective-permute-done.17.b0, ...), custom_call_target="tpu_custom_call" | custom-call | flops 3200000000 | bytes 32000000 | tf_op jit(solution)/shard_map/near_weight_grad/pallas_call | solution.py:267
  121.2 3.1 %fusion.3 = bf16[16,32,512]{2,1,0:T(8,128)(2,1)} fusion(f32[16,32,512]{2,1,0:T(8,128)} %collective-permute-done.16, f32[16,32,512]{2,1,0:T(8,128)} %collective-permute-done.15, f32[3,16,32,512]{3,2,1,0:T(8,128)S(1)} %collective-permute-done, f32[4,16,32,512]{3,2,1,0:T(8,128)} %get-tuple-element.37), kind=kLoop, calls=%fused_computation.4 | loop fusion | flops 1048576 | bytes 4718592 | tf_op jit(solution)/shard_map/convert_element_type | solution.py:283
  124.3 5.2 %all-to-all-start.1 = ((bf16[16,32,512]{2,1,0:T(8,128)(2,1)}), bf16[16,32,512]{2,1,0:T(8,128)(2,1)S(1)}, u32[]{:S(2)}, u32[]{:S(2)}) async-start(bf16[16,32,512]{2,1,0:T(8,128)(2,1)} %fusion.3), calls=%async_computation.1 | async-start | bytes 1048576 | tf_op jit(solution)/shard_map/all_to_all | solution.py:165
  129.5 1.3 collective-permute-start.22
  130.8 0.1 collective-permute-start.23
  130.9 1.1 collective-permute-done.22.b2a
  132.0 0.6 collective-permute-done.23.b2b
  132.6 0.1 copy-done.4
  132.7 0.7 copy-done.5
  133.4 7.4 %far_weight_grad.1 = bf16[1,8,34,8,128]{4,3,2,1,0:T(8,128)(2,1)} custom-call(s32[1]{0:T(128)} %bitcast.pos, s32[8,8,34]{2,1,0:T(8,128)} %rows.5, s32[8,8,34]{2,1,0:T(8,128)} %cols.5, s32[8,8]{1,0:T(8,128)} %live.5, bf16[8,32,512]{2,1,0:T(8,128)(2,1)} %copy-done.3, bf16[8,32,512]{2,1,0:T(8,128)(2,1)} %collective-permute-done.21.a2b, ...), custom_call_target="tpu_custom_call" | custom-call | flops 1100000000 | bytes 25000000 | tf_op jit(solution)/shard_map/far_weight_grad/pallas_call | solution.py:286
  140.8 0.8 copy.10
  (53 shorter events, 0.3 us)
Async XLA Ops:
  7.2 104.6 %all-gather.2.cloned.1.call-start = ((), (), s32[]{:S(2)}) async-start(), calls=%async_computation.2 | async-start | bytes 8912896 | tf_op jit(solution)/shard_map/all_gather | solution.py:167
  10.1 24.9 %all-to-all-start = ((bf16[16,64,512]{2,1,0:T(8,128)(2,1)}), bf16[16,64,512]{2,1,0:T(8,128)(2,1)S(1)}, u32[]{:S(2)}, u32[]{:S(2)}) async-start(bf16[16,64,512]{2,1,0:T(8,128)(2,1)} %feature_rows.1), calls=%async_computation | async-start | bytes 2097152 | tf_op jit(solution)/shard_map/all_to_all | solution.py:165
  35.0 45.8 %copy-start = (f32[4,16,32,512]{3,2,1,0:T(8,128)S(1)}, f32[4,16,32,512]{3,2,1,0:T(8,128)}, u32[]{:S(2)}) copy-start(f32[4,16,32,512]{3,2,1,0:T(8,128)} %get-tuple-element.37) | copy-start | bytes 12582916
  35.1 46.1 %copy-start.2 = (bf16[16,32,512]{2,1,0:T(8,128)(2,1)}, bf16[16,32,512]{2,1,0:T(8,128)(2,1)S(1)}, u32[]{:S(2)}) copy-start(bf16[16,32,512]{2,1,0:T(8,128)(2,1)S(1)} %get-tuple-element.50.a0) | copy-start | bytes 1572868
  35.1 50.6 %copy-start.1 = (bf16[16,32,512]{2,1,0:T(8,128)(2,1)}, bf16[16,32,512]{2,1,0:T(8,128)(2,1)S(1)}, u32[]{:S(2)}) copy-start(bf16[16,32,512]{2,1,0:T(8,128)(2,1)S(1)} %get-tuple-element.60.a0) | copy-start | bytes 1572868
  35.1 45.3 %collective-permute-start = (f32[3,16,32,512]{3,2,1,0:T(8,128)}, f32[3,16,32,512]{3,2,1,0:T(8,128)S(1)}, u32[]{:S(2)}, u32[]{:S(2)}) collective-permute-start(f32[3,16,32,512]{3,2,1,0:T(8,128)} %get-tuple-element.40), channel_id=1, source_target_pairs={{0,1},{1,0},{2,3},{3,2},{4,5},{5,4},{6,7},{7,6},{8,9},{9,8},{10,11... | collective-permute-start | bytes 9437192 | tf_op jit(solution)/shard_map/ppermute | solution.py:162
  41.0 7.0 %collective-permute-start.1 = (f32[16,32,512]{2,1,0:T(8,128)}, f32[16,32,512]{2,1,0:T(8,128)S(1)}, u32[]{:S(2)}, u32[]{:S(2)}) collective-permute-start(f32[16,32,512]{2,1,0:T(8,128)} %get-tuple-element.41), channel_id=1, source_target_pairs={{0,1},{1,0},{2,3},{3,2},{4,5},{5,4},{6,7},{7,6},{8,9},{9,8},{10,11... | collective-permute-start | bytes 3145736 | tf_op jit(solution)/shard_map/ppermute | solution.py:162
  41.1 15.0 %collective-permute-start.2 = (bf16[16,32,512]{2,1,0:T(8,128)(2,1)S(1)}, bf16[16,32,512]{2,1,0:T(8,128)(2,1)S(1)}, u32[]{:S(2)}, u32[]{:S(2)}) collective-permute-start(bf16[16,32,512]{2,1,0:T(8,128)(2,1)S(1)} %get-tuple-element.50.a0), channel_id=1, source_target_pairs={{0,2},{1,3},{2,4},{3,5},{4,6},{5,7},{6,0},{7,1},{8,10},{9,11},{10,... | collective-permute-start | bytes 1572872 | tf_op jit(solution)/shard_map/ppermute | solution.py:159
  42.5 13.7 %collective-permute-start.3 = (bf16[16,32,512]{2,1,0:T(8,128)(2,1)S(1)}, bf16[16,32,512]{2,1,0:T(8,128)(2,1)S(1)}, u32[]{:S(2)}, u32[]{:S(2)}) collective-permute-start(bf16[16,32,512]{2,1,0:T(8,128)(2,1)S(1)} %get-tuple-element.50.a0), channel_id=1, source_target_pairs={{0,6},{1,7},{2,0},{3,1},{4,2},{5,3},{6,4},{7,5},{8,14},{9,15},{10,... | collective-permute-start | bytes 1572872 | tf_op jit(solution)/shard_map/ppermute | solution.py:159
  56.1 25.3 %copy-start.6 = (bf16[16,32,512]{2,1,0:T(8,128)(2,1)}, bf16[16,32,512]{2,1,0:T(8,128)(2,1)S(1)}, u32[]{:S(2)}) copy-start(bf16[16,32,512]{2,1,0:T(8,128)(2,1)S(1)} %collective-permute-done.2.am) | copy-start | bytes 1572868
  56.1 25.3 %copy-start.7 = (bf16[16,32,512]{2,1,0:T(8,128)(2,1)}, bf16[16,32,512]{2,1,0:T(8,128)(2,1)S(1)}, u32[]{:S(2)}) copy-start(bf16[16,32,512]{2,1,0:T(8,128)(2,1)S(1)} %collective-permute-done.3.ap) | copy-start | bytes 1572868
  56.2 23.7 %collective-permute-start.5 = (f32[8,32,512]{2,1,0:T(8,128)S(1)}, f32[8,32,512]{2,1,0:T(8,128)S(1)}, u32[]{:S(2)}, u32[]{:S(2)}) collective-permute-start(f32[8,32,512]{2,1,0:T(8,128)S(1)} %get-tuple-element.47), channel_id=1, source_target_pairs={{0,6},{1,7},{2,0},{3,1},{4,2},{5,3},{6,4},{7,5},{8,14},{9,15},{10,... | collective-permute-start | bytes 1572872 | tf_op jit(solution)/shard_map/ppermute | solution.py:159
  58.6 21.7 %collective-permute-start.4 = (f32[8,32,512]{2,1,0:T(8,128)S(1)}, f32[8,32,512]{2,1,0:T(8,128)S(1)}, u32[]{:S(2)}, u32[]{:S(2)}) collective-permute-start(f32[8,32,512]{2,1,0:T(8,128)S(1)} %get-tuple-element.46), channel_id=1, source_target_pairs={{0,2},{1,3},{2,4},{3,5},{4,6},{5,7},{6,0},{7,1},{8,10},{9,11},{10,... | collective-permute-start | bytes 1572872 | tf_op jit(solution)/shard_map/ppermute | solution.py:159
  58.6 18.9 %collective-permute-start.6 = (bf16[8,32,512]{2,1,0:T(8,128)(2,1)S(1)}, bf16[8,32,512]{2,1,0:T(8,128)(2,1)S(1)}, u32[]{:S(2)}, u32[]{:S(2)}) collective-permute-start(bf16[8,32,512]{2,1,0:T(8,128)(2,1)S(1)} %slice.67), channel_id=1, source_target_pairs={{0,2},{1,3},{2,4},{3,5},{4,6},{5,7},{6,0},{7,1},{8,10},{9,11},{10,... | collective-permute-start | bytes 786440 | tf_op jit(solution)/shard_map/ppermute | solution.py:159
  58.6 21.2 %collective-permute-start.7 = (bf16[8,32,512]{2,1,0:T(8,128)(2,1)S(1)}, bf16[8,32,512]{2,1,0:T(8,128)(2,1)S(1)}, u32[]{:S(2)}, u32[]{:S(2)}) collective-permute-start(bf16[8,32,512]{2,1,0:T(8,128)(2,1)S(1)} %slice.68), channel_id=1, source_target_pairs={{0,6},{1,7},{2,0},{3,1},{4,2},{5,3},{6,4},{7,5},{8,14},{9,15},{10,... | collective-permute-start | bytes 786440 | tf_op jit(solution)/shard_map/ppermute | solution.py:159
  77.5 8.2 %copy-start.11 = (bf16[8,32,512]{2,1,0:T(8,128)(2,1)}, bf16[8,32,512]{2,1,0:T(8,128)(2,1)S(1)}, u32[]{:S(2)}) copy-start(bf16[8,32,512]{2,1,0:T(8,128)(2,1)S(1)} %collective-permute-done.6.a2a) | copy-start | bytes 786436
  77.5 3.9 %collective-permute-start.8 = (bf16[16,32,512]{2,1,0:T(8,128)(2,1)S(1)}, bf16[16,32,512]{2,1,0:T(8,128)(2,1)S(1)}, u32[]{:S(2)}, u32[]{:S(2)}) collective-permute-start(bf16[16,32,512]{2,1,0:T(8,128)(2,1)S(1)} %get-tuple-element.50.a0), channel_id=1, source_target_pairs={{0,1},{1,0},{2,3},{3,2},{4,5},{5,4},{6,7},{7,6},{8,9},{9,8},{10,11... | collective-permute-start | bytes 1572872 | tf_op jit(solution)/shard_map/ppermute | solution.py:162
  79.8 5.9 %copy-start.12 = (bf16[8,32,512]{2,1,0:T(8,128)(2,1)}, bf16[8,32,512]{2,1,0:T(8,128)(2,1)S(1)}, u32[]{:S(2)}) copy-start(bf16[8,32,512]{2,1,0:T(8,128)(2,1)S(1)} %collective-permute-done.7.a2b) | copy-start | bytes 786436
  79.8 6.8 %collective-permute-start.9 = (bf16[16,32,512]{2,1,0:T(8,128)(2,1)S(1)}, bf16[16,32,512]{2,1,0:T(8,128)(2,1)S(1)}, u32[]{:S(2)}, u32[]{:S(2)}) collective-permute-start(bf16[16,32,512]{2,1,0:T(8,128)(2,1)S(1)} %collective-permute-done.2.am), channel_id=1, source_target_pairs={{0,1},{1,0},{2,3},{3,2},{4,5},{5,4},{6,7},{7,6},{8,9},{9,8},{10,11... | collective-permute-start | bytes 1572872 | tf_op jit(solution)/shard_map/ppermute | solution.py:162
  79.8 6.7 %collective-permute-start.10 = (bf16[16,32,512]{2,1,0:T(8,128)(2,1)S(1)}, bf16[16,32,512]{2,1,0:T(8,128)(2,1)S(1)}, u32[]{:S(2)}, u32[]{:S(2)}) collective-permute-start(bf16[16,32,512]{2,1,0:T(8,128)(2,1)S(1)} %collective-permute-done.3.ap), channel_id=1, source_target_pairs={{0,1},{1,0},{2,3},{3,2},{4,5},{5,4},{6,7},{7,6},{8,9},{9,8},{10,11... | collective-permute-start | bytes 1572872 | tf_op jit(solution)/shard_map/ppermute | solution.py:162
  80.3 2.9 %collective-permute-start.11 = (bf16[8,32,512]{2,1,0:T(8,128)(2,1)S(1)}, bf16[8,32,512]{2,1,0:T(8,128)(2,1)S(1)}, u32[]{:S(2)}, u32[]{:S(2)}) collective-permute-start(bf16[8,32,512]{2,1,0:T(8,128)(2,1)S(1)} %collective-permute-done.6.a2a), channel_id=1, source_target_pairs={{0,1},{1,0},{2,3},{3,2},{4,5},{5,4},{6,7},{7,6},{8,9},{9,8},{10,11... | collective-permute-start | bytes 786440 | tf_op jit(solution)/shard_map/ppermute | solution.py:162
  80.4 5.3 %collective-permute-start.12 = (bf16[8,32,512]{2,1,0:T(8,128)(2,1)S(1)}, bf16[8,32,512]{2,1,0:T(8,128)(2,1)S(1)}, u32[]{:S(2)}, u32[]{:S(2)}) collective-permute-start(bf16[8,32,512]{2,1,0:T(8,128)(2,1)S(1)} %collective-permute-done.7.a2b), channel_id=1, source_target_pairs={{0,1},{1,0},{2,3},{3,2},{4,5},{5,4},{6,7},{7,6},{8,9},{9,8},{10,11... | collective-permute-start | bytes 786440 | tf_op jit(solution)/shard_map/ppermute | solution.py:162
  81.4 5.1 %copy-start.8 = (bf16[16,32,512]{2,1,0:T(8,128)(2,1)}, bf16[16,32,512]{2,1,0:T(8,128)(2,1)S(1)}, u32[]{:S(2)}) copy-start(bf16[16,32,512]{2,1,0:T(8,128)(2,1)S(1)} %collective-permute-done.8.b0) | copy-start | bytes 1572868
  81.4 23.6 %collective-permute-start.13 = (bf16[16,32,512]{2,1,0:T(8,128)(2,1)S(1)}, bf16[16,32,512]{2,1,0:T(8,128)(2,1)}, u32[]{:S(2)}, u32[]{:S(2)}) collective-permute-start(bf16[16,32,512]{2,1,0:T(8,128)(2,1)S(1)} %get-tuple-element.60.a0), channel_id=1, source_target_pairs={{0,2},{1,3},{2,4},{3,5},{4,6},{5,7},{6,0},{7,1},{8,10},{9,11},{10,... | collective-permute-start | bytes 1572872 | tf_op jit(solution)/shard_map/ppermute | solution.py:159
  83.2 4.7 %copy-start.13 = (bf16[8,32,512]{2,1,0:T(8,128)(2,1)}, bf16[8,32,512]{2,1,0:T(8,128)(2,1)S(1)}, u32[]{:S(2)}) copy-start(bf16[8,32,512]{2,1,0:T(8,128)(2,1)S(1)} %collective-permute-done.11.b2a) | copy-start | bytes 786436
  83.2 21.9 %collective-permute-start.14 = (bf16[16,32,512]{2,1,0:T(8,128)(2,1)S(1)}, bf16[16,32,512]{2,1,0:T(8,128)(2,1)}, u32[]{:S(2)}, u32[]{:S(2)}) collective-permute-start(bf16[16,32,512]{2,1,0:T(8,128)(2,1)S(1)} %get-tuple-element.60.a0), channel_id=1, source_target_pairs={{0,6},{1,7},{2,0},{3,1},{4,2},{5,3},{6,4},{7,5},{8,14},{9,15},{10,... | collective-permute-start | bytes 1572872 | tf_op jit(solution)/shard_map/ppermute | solution.py:159
  85.7 2.2 %copy-start.14 = (bf16[8,32,512]{2,1,0:T(8,128)(2,1)}, bf16[8,32,512]{2,1,0:T(8,128)(2,1)S(1)}, u32[]{:S(2)}) copy-start(bf16[8,32,512]{2,1,0:T(8,128)(2,1)S(1)} %collective-permute-done.12.b2b) | copy-start | bytes 786436
  85.7 23.4 %collective-permute-start.17 = (bf16[16,32,512]{2,1,0:T(8,128)(2,1)S(1)}, bf16[16,32,512]{2,1,0:T(8,128)(2,1)}, u32[]{:S(2)}, u32[]{:S(2)}) collective-permute-start(bf16[16,32,512]{2,1,0:T(8,128)(2,1)S(1)} %get-tuple-element.60.a0), channel_id=1, source_target_pairs={{0,1},{1,0},{2,3},{3,2},{4,5},{5,4},{6,7},{7,6},{8,9},{9,8},{10,11... | collective-permute-start | bytes 1572872 | tf_op jit(solution)/shard_map/ppermute | solution.py:162
  86.5 0.8 copy-start.9
  86.5 0.9 copy-start.10
  87.5 33.7 %collective-permute-start.15 = (f32[16,32,512]{2,1,0:T(8,128)}, f32[16,32,512]{2,1,0:T(8,128)}, u32[]{:S(2)}, u32[]{:S(2)}) collective-permute-start(f32[16,32,512]{2,1,0:T(8,128)} %get-tuple-element.62), channel_id=1, source_target_pairs={{0,2},{1,3},{2,4},{3,5},{4,6},{5,7},{6,0},{7,1},{8,10},{9,11},{10,... | collective-permute-start | bytes 3145736 | tf_op jit(solution)/shard_map/ppermute | solution.py:159
  87.9 33.3 %collective-permute-start.16 = (f32[16,32,512]{2,1,0:T(8,128)}, f32[16,32,512]{2,1,0:T(8,128)}, u32[]{:S(2)}, u32[]{:S(2)}) collective-permute-start(f32[16,32,512]{2,1,0:T(8,128)} %get-tuple-element.63), channel_id=1, source_target_pairs={{0,6},{1,7},{2,0},{3,1},{4,2},{5,3},{6,4},{7,5},{8,14},{9,15},{10,... | collective-permute-start | bytes 3145736 | tf_op jit(solution)/shard_map/ppermute | solution.py:159
  105.0 4.0 %collective-permute-start.18 = (bf16[16,32,512]{2,1,0:T(8,128)(2,1)}, bf16[16,32,512]{2,1,0:T(8,128)(2,1)}, u32[]{:S(2)}, u32[]{:S(2)}) collective-permute-start(bf16[16,32,512]{2,1,0:T(8,128)(2,1)} %collective-permute-done.13.am), channel_id=1, source_target_pairs={{0,1},{1,0},{2,3},{3,2},{4,5},{5,4},{6,7},{7,6},{8,9},{9,8},{10,11... | collective-permute-start | bytes 1572872 | tf_op jit(solution)/shard_map/ppermute | solution.py:162
  105.6 6.1 %collective-permute-start.19 = (bf16[16,32,512]{2,1,0:T(8,128)(2,1)}, bf16[16,32,512]{2,1,0:T(8,128)(2,1)}, u32[]{:S(2)}, u32[]{:S(2)}) collective-permute-start(bf16[16,32,512]{2,1,0:T(8,128)(2,1)} %collective-permute-done.14.ap), channel_id=1, source_target_pairs={{0,1},{1,0},{2,3},{3,2},{4,5},{5,4},{6,7},{7,6},{8,9},{9,8},{10,11... | collective-permute-start | bytes 1572872 | tf_op jit(solution)/shard_map/ppermute | solution.py:162
  109.1 20.4 %collective-permute-start.20 = (bf16[8,32,512]{2,1,0:T(8,128)(2,1)}, bf16[8,32,512]{2,1,0:T(8,128)(2,1)S(1)}, u32[]{:S(2)}, u32[]{:S(2)}) collective-permute-start(bf16[8,32,512]{2,1,0:T(8,128)(2,1)} %slice.78), channel_id=1, source_target_pairs={{0,2},{1,3},{2,4},{3,5},{4,6},{5,7},{6,0},{7,1},{8,10},{9,11},{10,... | collective-permute-start | bytes 786440 | tf_op jit(solution)/shard_map/ppermute | solution.py:159
  109.1 21.8 %collective-permute-start.21 = (bf16[8,32,512]{2,1,0:T(8,128)(2,1)}, bf16[8,32,512]{2,1,0:T(8,128)(2,1)}, u32[]{:S(2)}, u32[]{:S(2)}) collective-permute-start(bf16[8,32,512]{2,1,0:T(8,128)(2,1)} %slice.79), channel_id=1, source_target_pairs={{0,6},{1,7},{2,0},{3,1},{4,2},{5,3},{6,4},{7,5},{8,14},{9,15},{10,... | collective-permute-start | bytes 786440 | tf_op jit(solution)/shard_map/ppermute | solution.py:159
  124.3 16.5 %all-to-all-start.1 = ((bf16[16,32,512]{2,1,0:T(8,128)(2,1)}), bf16[16,32,512]{2,1,0:T(8,128)(2,1)S(1)}, u32[]{:S(2)}, u32[]{:S(2)}) async-start(bf16[16,32,512]{2,1,0:T(8,128)(2,1)} %fusion.3), calls=%async_computation.1 | async-start | bytes 1048576 | tf_op jit(solution)/shard_map/all_to_all | solution.py:165
  129.5 3.1 %copy-start.3 = (bf16[8,32,512]{2,1,0:T(8,128)(2,1)}, bf16[8,32,512]{2,1,0:T(8,128)(2,1)S(1)}, u32[]{:S(2)}) copy-start(bf16[8,32,512]{2,1,0:T(8,128)(2,1)S(1)} %collective-permute-done.20.a2a) | copy-start | bytes 786436
  129.5 2.5 %collective-permute-start.22 = (bf16[8,32,512]{2,1,0:T(8,128)(2,1)S(1)}, bf16[8,32,512]{2,1,0:T(8,128)(2,1)S(1)}, u32[]{:S(2)}, u32[]{:S(2)}) collective-permute-start(bf16[8,32,512]{2,1,0:T(8,128)(2,1)S(1)} %collective-permute-done.20.a2a), channel_id=1, source_target_pairs={{0,1},{1,0},{2,3},{3,2},{4,5},{5,4},{6,7},{7,6},{8,9},{9,8},{10,11... | collective-permute-start | bytes 786440 | tf_op jit(solution)/shard_map/ppermute | solution.py:162
  130.8 1.7 %collective-permute-start.23 = (bf16[8,32,512]{2,1,0:T(8,128)(2,1)}, bf16[8,32,512]{2,1,0:T(8,128)(2,1)S(1)}, u32[]{:S(2)}, u32[]{:S(2)}) collective-permute-start(bf16[8,32,512]{2,1,0:T(8,128)(2,1)} %collective-permute-done.21.a2b), channel_id=1, source_target_pairs={{0,1},{1,0},{2,3},{3,2},{4,5},{5,4},{6,7},{7,6},{8,9},{9,8},{10,11... | collective-permute-start | bytes 786440 | tf_op jit(solution)/shard_map/ppermute | solution.py:162
  132.0 0.7 copy-start.4
  132.7 0.7 copy-start.5
Sparse Core Ops, SparseCore 0:
  10.1 78.8 all-gather.1

commit v5 on v4

v5 whole, which is shorter than its diff:
```python
import functools
import math

import jax
import jax.numpy as jnp
from jax import lax
from jax.experimental import pallas as pl
from jax.experimental.pallas import tpu as pltpu
from jax.sharding import PartitionSpec as P

F32 = jnp.float32
BF16 = jnp.bfloat16
VMEM_LIMIT = 60 * 1024 * 1024


def build_panel(panel, blk_ref, rows_ref, cols_ref, live_ref, owner, j):
    panel[...] = jnp.zeros_like(panel)
    count = live_ref[owner, j]
    for k in range(34):

        def place(k=k):
            r = pl.multiple_of((rows_ref[owner, j, k] - 8 * j) * 128, 128)
            c = pl.multiple_of((cols_ref[owner, j, k] - 8 * owner) * 128, 128)
            panel[pl.ds(r, 128), pl.ds(c, 128)] = blk_ref[j, k]

        if k < 30:
            place()
        else:
            pl.when(k < count)(place)


def start_all(copies):
    for copy in copies:
        copy.start()


def wait_all(copies):
    for copy in copies:
        copy.wait()


def transpose_kernel(x_ref, o_ref):
    x = x_ref[...].reshape(512, 512).astype(F32)
    t = x.T.reshape(4, 16, 8, 512)
    for part in range(16):
        o_ref[part, pl.ds(0, 32)] = x_ref[part]
        o_ref[part, pl.ds(32, 32)] = t[:, part].reshape(32, 512).astype(BF16)


def partial_kernel(
    pos, rows, cols, live, cot, blk, keep, across, rest,
    lhs, blk_v, panel, keep_v, across_v, rest_v, cot_sem, blk_sem, out_sem,
):
    owner = pos[0]
    y = owner // 2
    core = owner % 2
    cot_copies = []
    for d in range(4):
        for side in range(2):
            who = core if side == 0 else 1 - core
            cot_copies.append(
                pltpu.make_async_copy(
                    cot.at[(y + d) % 4, who], lhs.at[pl.ds(side * 128 + d * 32, 32)], cot_sem.at[side * 4 + d]
                )
            )
    start_all(cot_copies)
    start_all([pltpu.make_async_copy(blk.at[0, j], blk_v.at[j], blk_sem.at[j]) for j in range(8)])
    wait_all(cot_copies)

    def out_copies(j):
        part = pl.ds(j * 2, 2)
        return (
            pltpu.make_async_copy(keep_v.at[:, part], keep.at[:, part], out_sem.at[j, 0]),
            pltpu.make_async_copy(across_v.at[part], across.at[part], out_sem.at[j, 1]),
            pltpu.make_async_copy(rest_v.at[:, part], rest.at[:, part], out_sem.at[j, 2]),
        )

    def step(j, carry):
        pltpu.make_async_copy(blk.at[0, j], blk_v.at[j], blk_sem.at[j]).wait()
        build_panel(panel, blk_v, rows, cols, live, owner, j)
        res = lax.dot_general(lhs[...], panel[...], (((1,), (1,)), ((), ())), preferred_element_type=F32)
        for half in range(2):
            lanes = slice(half * 512, half * 512 + 512)
            at = j * 2 + half
            for d in range(4):
                keep_v[d, at] = res[d * 32 : d * 32 + 32, lanes]
            rest_v[0, at] = res[128:160, lanes]
            rest_v[1, at] = res[160:192, lanes]
            across_v[at] = res[192:224, lanes]
            rest_v[2, at] = res[224:256, lanes]
        start_all(out_copies(j))
        return carry

    lax.fori_loop(0, 8, step, 0)
    for j in range(8):
        wait_all(out_copies(j))


def out_kernel(
    pos, rows, cols, live, a0, am, ap, a2a, a2b, b0, bm, bp, b2a, b2b, blk, out_ref,
    lhs, blk_v, panel, acc, x_sem, blk_sem,
):
    owner = pos[0]
    y = owner // 2
    core = owner % 2
    start_all([pltpu.make_async_copy(blk.at[0, j], blk_v.at[j], blk_sem.at[j]) for j in range(8)])
    x_copies = []
    for who, pieces in ((core, (a0, am, ap, a2a, a2b)), (1 - core, (b0, bm, bp, b2a, b2b))):
        places = (
            lhs.at[:, y, who],
            lhs.at[:, (y + 3) % 4, who],
            lhs.at[:, (y + 1) % 4, who],
            lhs.at[pl.ds(0, 8), (y + 2) % 4, who],
            lhs.at[pl.ds(8, 8), (y + 2) % 4, who],
        )
        for piece, place in zip(pieces, places):
            x_copies.append(pltpu.make_async_copy(piece, place, x_sem.at[len(x_copies)]))
    start_all(x_copies)
    acc[...] = jnp.zeros_like(acc)
    wait_all(x_copies)

    def step(j, carry):
        pltpu.make_async_copy(blk.at[0, j], blk_v.at[j], blk_sem.at[j]).wait()
        build_panel(panel, blk_v, rows, cols, live, owner, j)
        for half in range(2):
            acc[...] += jnp.dot(
                lhs[j * 2 + half].reshape(256, 512), panel[pl.ds(half * 512, 512)], preferred_element_type=F32
            )
        return carry

    lax.fori_loop(0, 8, step, 0)
    out_ref[...] = acc[...].astype(BF16)


def token_group(owner, chip_step, core_step):
    return ((owner // 2 + chip_step) % 4) * 2 + (owner + core_step) % 2


def near_grad_kernel(pos, a0, am, ap, b0, bm, bp, g, total, x_v, g_v, acc, x_sem, g_sem, out_sem):
    owner = pos[0]
    copies = []
    for at, piece in enumerate((a0, am, ap, b0, bm, bp)):
        group = token_group(owner, (0, 3, 1)[at % 3], at // 3)
        copies.append(
            (
                pltpu.make_async_copy(piece, x_v.at[at], x_sem.at[at]),
                pltpu.make_async_copy(g.at[:, group], g_v.at[at], g_sem.at[at]),
            )
        )
        start_all(copies[-1])
    for at in range(6):
        wait_all(copies[at])
        x, cot = x_v[at].reshape(512, 512), g_v[at].reshape(512, 1024)
        res = jnp.dot(x, cot, preferred_element_type=F32).reshape(64, 8, 1024)
        if at == 0:
            acc[...] = res
        else:
            acc[...] += res
    out = pltpu.make_async_copy(acc, total, out_sem.at[0])
    out.start()
    out.wait()


def far_grad_kernel(scale, pos, rows, cols, live, a2a, a2b, b2a, b2b, g, near, out_ref, x_v, g_v, acc, x_sem, g_sem, near_sem):
    owner = pos[0]
    near_copy = pltpu.make_async_copy(near, acc, near_sem.at[0])
    near_copy.start()
    copies = []
    for at, (first, second) in enumerate(((a2a, a2b), (b2a, b2b))):
        group = token_group(owner, 2, at)
        copies.append(
            (
                pltpu.make_async_copy(first, x_v.at[at, pl.ds(0, 8)], x_sem.at[at, 0]),
                pltpu.make_async_copy(second, x_v.at[at, pl.ds(8, 8)], x_sem.at[at, 1]),
                pltpu.make_async_copy(g.at[:, group], g_v.at[at], g_sem.at[at]),
            )
        )
        start_all(copies[-1])
    near_copy.wait()
    for at in range(2):
        wait_all(copies[at])
        x, cot = x_v[at].reshape(512, 512), g_v[at].reshape(512, 1024)
        acc[...] += jnp.dot(x, cot, preferred_element_type=F32).reshape(64, 8, 1024)

    def pick(j, carry):
        count = live[owner, j]
        for k in range(34):
            r = rows[owner, j, k]
            c = pl.multiple_of((cols[owner, j, k] - 8 * owner) * 128, 128)
            tile = acc[r, :, pl.ds(c, 128)] * scale
            if k >= 30:
                tile = jnp.where(k < count, tile, 0.0)
            out_ref[0, j, k] = tile.astype(BF16)
        return carry

    lax.fori_loop(0, 8, pick, 0)


def on_device(context, blocks, row_blocks, col_blocks, live_counts, cotangent):
    owner = lax.axis_index("mp")
    pos = owner.astype(jnp.int32).reshape(1)
    tables = (pos, row_blocks, col_blocks, live_counts)
    params = pltpu.CompilerParams(vmem_limit_bytes=VMEM_LIMIT)
    barrier = lax.optimization_barrier

    def cost(flops, size):
        return pl.CostEstimate(flops=flops, bytes_accessed=size, transcendentals=0)

    def along_y(x, step):
        return lax.ppermute(x, "mp", [(i, (i + 2 * step) % 8) for i in range(8)])

    def other_core(x):
        return lax.ppermute(x, "mp", [(i, i ^ 1) for i in range(8)])

    def exchange(x):
        return lax.all_to_all(x, "seq", split_axis=0, concat_axis=0, tiled=True)

    cot_all = lax.all_gather(cotangent, "seq", axis=0, tiled=True)

    both = pl.pallas_call(
        transpose_kernel,
        out_shape=jax.ShapeDtypeStruct((16, 64, 512), BF16),
        compiler_params=params,
        name="feature_rows",
    )(context)
    both, cot_own = barrier((both, cotangent))
    both = exchange(both)
    tokens, class_rows = both[:, :32], both[:, 32:]

    scalars = [pl.BlockSpec(memory_space=pltpu.SMEM)] * 4
    anywhere = pl.BlockSpec(memory_space=pl.ANY)
    keep, across, rest = pl.pallas_call(
        partial_kernel,
        in_specs=scalars + [anywhere] * 2,
        out_specs=[anywhere] * 3,
        out_shape=[
            jax.ShapeDtypeStruct((4, 16, 32, 512), F32),
            jax.ShapeDtypeStruct((16, 32, 512), F32),
            jax.ShapeDtypeStruct((3, 16, 32, 512), F32),
        ],
        scratch_shapes=[
            pltpu.VMEM((256, 1024), BF16),
            pltpu.VMEM((8, 34, 128, 128), BF16),
            pltpu.VMEM((1024, 1024), BF16),
            pltpu.VMEM((4, 16, 32, 512), F32),
            pltpu.VMEM((16, 32, 512), F32),
            pltpu.VMEM((3, 16, 32, 512), F32),
            pltpu.SemaphoreType.DMA((8,)),
            pltpu.SemaphoreType.DMA((8,)),
            pltpu.SemaphoreType.DMA((8, 3)),
        ],
        compiler_params=params,
        cost_estimate=cost(4_300_000_000, 40_000_000),
        name="partial_context_grad",
    )(*tables, cot_own.reshape(4, 2, 32, 1024), blocks)
    across = other_core(across)

    xm, xp = along_y(tokens, 1), along_y(tokens, -1)
    rest, _ = barrier((rest, tokens))
    rest = other_core(rest)

    q2a, q2b, xm, xp = barrier((keep[2, :8] + across[:8], keep[2, 8:] + across[8:], xm, xp))
    x2a, x2b = along_y(xm[:8], 1), along_y(xp[8:], -1)
    x2a, x2b, q2a, q2b, class_rows = barrier((x2a, x2b, q2a, q2b, class_rows))
    from_a, from_b = along_y(q2a, 1), along_y(q2b, -1)
    own = (tokens, xm, xp, x2a, x2b)
    x_pieces = own + tuple(other_core(piece) for piece in own)

    cm, cp = along_y(class_rows, 1), along_y(class_rows, -1)

    outputs = pl.pallas_call(
        out_kernel,
        in_specs=scalars + [anywhere] * 11,
        out_shape=jax.ShapeDtypeStruct((256, 1024), BF16),
        scratch_shapes=[
            pltpu.VMEM((16, 4, 2, 32, 512), BF16),
            pltpu.VMEM((8, 34, 128, 128), BF16),
            pltpu.VMEM((1024, 1024), BF16),
            pltpu.VMEM((256, 1024), F32),
            pltpu.SemaphoreType.DMA((10,)),
            pltpu.SemaphoreType.DMA((8,)),
        ],
        compiler_params=params,
        cost_estimate=cost(4_300_000_000, 40_000_000),
        name="outputs",
    )(*tables, *x_pieces, blocks)

    outputs, cm, cp, from_a, from_b = barrier((outputs, cm, cp, from_a, from_b))
    q1 = jnp.concatenate([keep[1, :8] + rest[1, :8] + from_a, keep[1, 8:] + rest[1, 8:]], axis=0)
    q3 = jnp.concatenate([keep[3, :8] + rest[2, :8], keep[3, 8:] + rest[2, 8:] + from_b], axis=0)
    sum_m, sum_p = along_y(q1, 1), along_y(q3, -1)
    c2a, c2b = along_y(cm[:8], 1), along_y(cp[8:], -1)

    near = (class_rows, cm, cp)
    near = near + tuple(other_core(piece) for piece in near)
    cot_groups = cot_all.reshape(16, 8, 32, 1024)
    near_grad = pl.pallas_call(
        near_grad_kernel,
        in_specs=scalars[:1] + [anywhere] * 7,
        out_specs=anywhere,
        out_shape=jax.ShapeDtypeStruct((64, 8, 1024), F32),
        scratch_shapes=[
            pltpu.VMEM((6, 16, 32, 512), BF16),
            pltpu.VMEM((6, 16, 32, 1024), BF16),
            pltpu.VMEM((64, 8, 1024), F32),
            pltpu.SemaphoreType.DMA((6,)),
            pltpu.SemaphoreType.DMA((6,)),
            pltpu.SemaphoreType.DMA((1,)),
        ],
        compiler_params=params,
        cost_estimate=cost(3_200_000_000, 25_000_000),
        name="near_weight_grad",
    )(pos, *near, cot_groups)

    sum_m, sum_p, near_grad = barrier((sum_m, sum_p, near_grad))
    context_sum = (keep[0] + rest[0] + sum_m + sum_p).astype(BF16)
    context_grad = exchange(context_sum)

    weight_grad = pl.pallas_call(
        functools.partial(far_grad_kernel, 1.0 / math.sqrt(4096)),
        in_specs=scalars + [anywhere] * 6,
        out_shape=jax.ShapeDtypeStruct((1, 8, 34, 8, 128), BF16),
        scratch_shapes=[
            pltpu.VMEM((2, 16, 32, 512), BF16),
            pltpu.VMEM((2, 16, 32, 1024), BF16),
            pltpu.VMEM((64, 8, 1024), F32),
            pltpu.SemaphoreType.DMA((2, 2)),
            pltpu.SemaphoreType.DMA((2,)),
            pltpu.SemaphoreType.DMA((1,)),
        ],
        compiler_params=params,
        cost_estimate=cost(1_100_000_000, 18_000_000),
        name="far_weight_grad",
    )(*tables, c2a, c2b, other_core(c2a), other_core(c2b), cot_groups, near_grad)
    return (outputs, context_grad, weight_grad)


def solution(mesh):
    in_specs = (
        P(None, "mp", "seq"),
        P("mp", None, None, None, None),
        P(),
        P(),
        P(),
        P("seq", "mp"),
    )
    out_specs = (P("seq", "mp"), P(None, "mp", "seq"), P("mp", None, None, "seq", None))
    return jax.shard_map(
        on_device, mesh=mesh, in_specs=in_specs, out_specs=out_specs, check_vma=False
    )
```

time: 150 us -> 155 us (1.033)
  starting transfers between devices: 40.4 us -> 46.6 us
  waiting for transfers between devices: 32 us -> 26 us
  other arithmetic: 6.53 us -> 10.9 us
    ppermute x12, waiting for transfers between devices: 23 us -> 17.4 us  [along_y(): return lax.ppermute(x, 'mp', [(i, (i + 2 * step) % 8) for i in range(8)])]
    ppermute x12, starting transfers between devices: 12.2 us -> 17.3 us  [other_core(): return lax.ppermute(x, 'mp', [(i, i ^ 1) for i in range(8)])]
  transfers between devices with their start and end apart: 27 -> 27, of which waited for: 7 -> 11; matrix products, arithmetic and copies ran while one was open for 7% -> 9% of each run, Pallas kernels for 33% -> 32%
where the time goes in v5:
time: 155 us; the launch traced here: 153 us
  Pallas kernels  48.3 us (31%)
  starting transfers between devices  46.6 us (30%)
  waiting for transfers between devices  26 us (17%)
  between operations  14.2 us (9%)
  other arithmetic  10.9 us (7%)
  local copies, waits for them, and re-layouts  7.39 us (5%)
    ppermute x12, waiting for transfers between devices, along_y(): return lax.ppermute(x, 'mp', [(i, (i + 2 * step) % 8) for i in range(8)])  17.4 us
    ppermute x12, starting transfers between devices, other_core(): return lax.ppermute(x, 'mp', [(i, i ^ 1) for i in range(8)])  17.3 us
    pallas_call x1, Pallas kernels, on_device(): pl.pallas_call(out_kernel, in_specs=scalars + [anywhere] * 11, out_shape=...  16.7 us
    pallas_call x1, Pallas kernels, on_device(): pl.pallas_call(partial_kernel, in_specs=scalars + [anywhere] * 2, out_spe...  15.9 us
    ppermute x12, starting transfers between devices, along_y(): return lax.ppermute(x, 'mp', [(i, (i + 2 * step) % 8) for i in range(8)])  15.6 us
    all_to_all x2, starting transfers between devices, exchange(): return lax.all_to_all(x, 'seq', split_axis=0, concat_axis=0, tiled=True)  13.6 us
    ppermute x12, waiting for transfers between devices, other_core(): return lax.ppermute(x, 'mp', [(i, i ^ 1) for i in range(8)])  7.38 us
    pallas_call x1, Pallas kernels, on_device(): pl.pallas_call(functools.partial(far_grad_kernel, 1.0 / math.sqrt(4096)),...  6.96 us
  transfers between devices with their start and end apart: 27, of which 11 were waited for; matrix products, arithmetic and copies ran while one was open for 9% of the time, Pallas kernels for 32%

profile of v5, /device:TPU:1, one launch (start us, length us, event | category | flops | bytes accessed | tf_op | source)
XLA Modules:
  0.0 153.4 jit_solution(16229435922388321052)
XLA Ops:
  7.2 0.7 all-gather.2.cloned.1.call-update
  7.9 2.2 %feature_rows.1 = bf16[16,64,512]{2,1,0:T(8,128)(2,1)} custom-call(bf16[16,32,512]{2,1,0:T(8,128)(2,1)} %x_ref.1), custom_call_target="tpu_custom_call" | custom-call | tf_op jit(solution)/shard_map/feature_rows/pallas_call | solution.py:220
  10.1 8.4 %all-to-all-start = ((bf16[16,64,512]{2,1,0:T(8,128)(2,1)}), bf16[16,64,512]{2,1,0:T(8,128)(2,1)S(1)}, u32[]{:S(2)}, u32[]{:S(2)}) async-start(bf16[16,64,512]{2,1,0:T(8,128)(2,1)} %feature_rows.1), calls=%async_computation | async-start | bytes 2097152 | tf_op jit(solution)/shard_map/all_to_all | solution.py:216
  18.6 15.9 %partial_context_grad.1 = (f32[4,16,32,512]{3,2,1,0:T(8,128)}, f32[16,32,512]{2,1,0:T(8,128)}, f32[3,16,32,512]{3,2,1,0:T(8,128)}) custom-call(s32[1]{0:T(128)} %bitcast.pos, s32[8,8,34]{2,1,0:T(8,128)} %rows.5, s32[8,8,34]{2,1,0:T(8,128)} %cols.5, s32[8,8]{1,0:T(8,128)} %live.5, bf16[4,2,32,1024]{3,2,1,0:T(8,128)(2,1)} %bitcast.29, ...), custom_call_target="tpu_custom_call" | custom-call | flops 4300000256 | bytes 40000000 | tf_op jit(solution)/shard_map/partial_context_grad/pallas_call | solution.py:232
  34.5 0.5 all-to-all-done
  35.1 5.9 %collective-permute-start.14 = (f32[3,16,32,512]{3,2,1,0:T(8,128)}, f32[3,16,32,512]{3,2,1,0:T(8,128)S(1)}, u32[]{:S(2)}, u32[]{:S(2)}) collective-permute-start(f32[3,16,32,512]{3,2,1,0:T(8,128)} %get-tuple-element.41), channel_id=1, source_target_pairs={{0,1},{1,0},{2,3},{3,2},{4,5},{5,4},{6,7},{7,6},{8,9},{9,8},{10,11... | collective-permute-start | bytes 9437192 | tf_op jit(solution)/shard_map/ppermute | solution.py:213
  41.1 1.4 collective-permute-start.1
  42.5 1.6 %collective-permute-start.2 = (bf16[16,32,512]{2,1,0:T(8,128)(2,1)S(1)}, bf16[16,32,512]{2,1,0:T(8,128)(2,1)S(1)}, u32[]{:S(2)}, u32[]{:S(2)}) collective-permute-start(bf16[16,32,512]{2,1,0:T(8,128)(2,1)S(1)} %get-tuple-element.56.a0), channel_id=1, source_target_pairs={{0,6},{1,7},{2,0},{3,1},{4,2},{5,3},{6,4},{7,5},{8,14},{9,15},{10,... | collective-permute-start | bytes 1572872 | tf_op jit(solution)/shard_map/ppermute | solution.py:210
  44.1 0.7 collective-permute-start.5
  44.8 4.0 %collective-permute-done = f32[16,32,512]{2,1,0:T(8,128)S(1)} collective-permute-done((f32[16,32,512]{2,1,0:T(8,128)}, f32[16,32,512]{2,1,0:T(8,128)S(1)}, u32[]{:S(2)}, u32[]{:S(2)}) %collective-permute-start) | collective-permute-done | bytes 1048608 | tf_op jit(solution)/shard_map/ppermute | solution.py:213
  48.7 2.4 %slice_add_fusion.5 = (f32[8,32,512]{2,1,0:T(8,128)}, f32[8,32,512]{2,1,0:T(8,128)}) fusion(f32[16,32,512]{2,1,0:T(8,128)S(1)} %collective-permute-done, f32[4,16,32,512]{3,2,1,0:T(8,128)} %get-tuple-element.28), kind=kLoop, calls=%fused_computation.17 | loop fusion | flops 262144 | bytes 3145728 | tf_op jit(solution)/shard_map/add | solution.py:262
  51.1 5.0 %collective-permute-done.1.am = bf16[16,32,512]{2,1,0:T(8,128)(2,1)S(1)} collective-permute-done((bf16[16,32,512]{2,1,0:T(8,128)(2,1)S(1)}, bf16[16,32,512]{2,1,0:T(8,128)(2,1)S(1)}, u32[]{:S(2)}, u32[]{:S(2)}) %collective-permute-start.1) | collective-permute-done | bytes 524320 | tf_op jit(solution)/shard_map/ppermute | solution.py:210
  56.2 0.7 collective-permute-start.3
  56.8 2.2 %collective-permute-start.4 = (bf16[8,32,512]{2,1,0:T(8,128)(2,1)S(1)}, bf16[8,32,512]{2,1,0:T(8,128)(2,1)S(1)}, u32[]{:S(2)}, u32[]{:S(2)}) collective-permute-start(bf16[8,32,512]{2,1,0:T(8,128)(2,1)S(1)} %slice.66), channel_id=1, source_target_pairs={{0,6},{1,7},{2,0},{3,1},{4,2},{5,3},{6,4},{7,5},{8,14},{9,15},{10,... | collective-permute-start | bytes 786440 | tf_op jit(solution)/shard_map/ppermute | solution.py:210
  59.0 1.4 collective-permute-start.6
  60.4 4.2 %collective-permute-done.3.a2a = bf16[8,32,512]{2,1,0:T(8,128)(2,1)S(1)} collective-permute-done((bf16[8,32,512]{2,1,0:T(8,128)(2,1)S(1)}, bf16[8,32,512]{2,1,0:T(8,128)(2,1)S(1)}, u32[]{:S(2)}, u32[]{:S(2)}) %collective-permute-start.3) | collective-permute-done | bytes 262176 | tf_op jit(solution)/shard_map/ppermute | solution.py:210
  64.5 1.6 %collective-permute-start.7 = (bf16[16,32,512]{2,1,0:T(8,128)(2,1)S(1)}, bf16[16,32,512]{2,1,0:T(8,128)(2,1)S(1)}, u32[]{:S(2)}, u32[]{:S(2)}) collective-permute-start(bf16[16,32,512]{2,1,0:T(8,128)(2,1)S(1)} %collective-permute-done.2.ap), channel_id=1, source_target_pairs={{0,1},{1,0},{2,3},{3,2},{4,5},{5,4},{6,7},{7,6},{8,9},{9,8},{10,11... | collective-permute-start | bytes 1572872 | tf_op jit(solution)/shard_map/ppermute | solution.py:213
  66.3 0.4 collective-permute-start.9
  66.7 1.4 collective-permute-done.8.b2a
  68.1 0.4 collective-permute-done.9.b2b
  68.4 2.4 %collective-permute-start.11 = (bf16[16,32,512]{2,1,0:T(8,128)(2,1)S(1)}, bf16[16,32,512]{2,1,0:T(8,128)(2,1)}, u32[]{:S(2)}, u32[]{:S(2)}) collective-permute-start(bf16[16,32,512]{2,1,0:T(8,128)(2,1)S(1)} %get-tuple-element.36.a0), channel_id=1, source_target_pairs={{0,6},{1,7},{2,0},{3,1},{4,2},{5,3},{6,4},{7,5},{8,14},{9,15},{10,... | collective-permute-start | bytes 1572872 | tf_op jit(solution)/shard_map/ppermute | solution.py:210
  71.0 0.7 copy-done.9
  71.6 0.8 copy-done.10
  72.4 2.0 %collective-permute-start.13 = (f32[8,32,512]{2,1,0:T(8,128)}, f32[8,32,512]{2,1,0:T(8,128)}, u32[]{:S(2)}, u32[]{:S(2)}) collective-permute-start(f32[8,32,512]{2,1,0:T(8,128)} %get-tuple-element.38), channel_id=1, source_target_pairs={{0,6},{1,7},{2,0},{3,1},{4,2},{5,3},{6,4},{7,5},{8,14},{9,15},{10,... | collective-permute-start | bytes 1572872 | tf_op jit(solution)/shard_map/ppermute | solution.py:210
  74.4 16.7 %outputs.1 = bf16[256,1024]{1,0:T(8,128)(2,1)} custom-call(s32[1]{0:T(128)} %bitcast.pos, s32[8,8,34]{2,1,0:T(8,128)} %rows.5, s32[8,8,34]{2,1,0:T(8,128)} %cols.5, s32[8,8]{1,0:T(8,128)} %live.5, bf16[16,32,512]{2,1,0:T(8,128)(2,1)} %copy-done.1, bf16[16,32,512]{2,1,0:T(8,128)(2,1)} %copy-done.6, bf16[16,32,512]{2,1,0:T(8,128)(2,1)} %copy-done.7, ...), custom_call_target="tpu_custom_call" | custom-call | flops 4300000256 | bytes 40000000 | tf_op jit(solution)/shard_map/outputs/pallas_call | solution.py:271
  91.2 2.6 %collective-permute-done.12 = f32[8,32,512]{2,1,0:T(8,128)} collective-permute-done((f32[8,32,512]{2,1,0:T(8,128)}, f32[8,32,512]{2,1,0:T(8,128)}, u32[]{:S(2)}, u32[]{:S(2)}) %collective-permute-start.12) | collective-permute-done | bytes 524320 | tf_op jit(solution)/shard_map/ppermute | solution.py:210
  93.8 1.4 fusion.6
  95.2 1.9 %fusion.5 = (f32[8,32,512]{2,1,0:T(8,128)S(1)}, f32[8,32,512]{2,1,0:T(8,128)S(1)}) fusion(f32[8,32,512]{2,1,0:T(8,128)} %collective-permute-done.13, f32[3,16,32,512]{3,2,1,0:T(8,128)S(1)} %collective-permute-done.14, f32[4,16,32,512]{3,2,1,0:T(8,128)} %get-tuple-element.28, f32[8,32,512]{2,1,0:T(8,128)} %collective-permute-done.12), kind=kLoop, calls=%fused_computation.9 | loop fusion | flops 524288 | bytes 4194304 | tf_op jit(solution)/shard_map/add | solution.py:290
  97.1 1.1 pad_maximum_fusion
  98.2 1.1 pad_maximum_fusion.1
  99.3 2.6 %collective-permute-start.16 = (f32[16,32,512]{2,1,0:T(8,128)}, f32[16,32,512]{2,1,0:T(8,128)}, u32[]{:S(2)}, u32[]{:S(2)}) collective-permute-start(f32[16,32,512]{2,1,0:T(8,128)} %pad_maximum_fusion.1), channel_id=1, source_target_pairs={{0,6},{1,7},{2,0},{3,1},{4,2},{5,3},{6,4},{7,5},{8,14},{9,15},{10,... | collective-permute-start | bytes 3145736 | tf_op jit(solution)/shard_map/ppermute | solution.py:210
  101.9 1.8 %collective-permute-start.17 = (bf16[16,32,512]{2,1,0:T(8,128)(2,1)S(1)}, bf16[16,32,512]{2,1,0:T(8,128)(2,1)S(1)}, u32[]{:S(2)}, u32[]{:S(2)}) collective-permute-start(bf16[16,32,512]{2,1,0:T(8,128)(2,1)S(1)} %get-tuple-element.36.a0), channel_id=1, source_target_pairs={{0,1},{1,0},{2,3},{3,2},{4,5},{5,4},{6,7},{7,6},{8,9},{9,8},{10,11... | collective-permute-start | bytes 1572872 | tf_op jit(solution)/shard_map/ppermute | solution.py:213
  103.7 0.5 collective-permute-start.19
  104.2 1.7 %slice.78 = bf16[8,32,512]{2,1,0:T(8,128)(2,1)} slice(bf16[16,32,512]{2,1,0:T(8,128)(2,1)} %collective-permute-done.10.am), slice={[0:8], [0:32], [0:512]} | slice | bytes 524288 | tf_op jit(solution)/shard_map/slice | solution.py:292
  105.9 1.7 %slice.79 = bf16[8,32,512]{2,1,0:T(8,128)(2,1)} slice(bf16[16,32,512]{2,1,0:T(8,128)(2,1)} %collective-permute-done.11.ap), slice={[8:16], [0:32], [0:512]} | slice | bytes 524288 | tf_op jit(solution)/shard_map/slice | solution.py:292
  107.6 0.8 copy-done.2
  108.4 2.7 %collective-permute-start.21 = (bf16[8,32,512]{2,1,0:T(8,128)(2,1)}, bf16[8,32,512]{2,1,0:T(8,128)(2,1)}, u32[]{:S(2)}, u32[]{:S(2)}) collective-permute-start(bf16[8,32,512]{2,1,0:T(8,128)(2,1)} %slice.79), channel_id=1, source_target_pairs={{0,6},{1,7},{2,0},{3,1},{4,2},{5,3},{6,4},{7,5},{8,14},{9,15},{10,... | collective-permute-start | bytes 786440 | tf_op jit(solution)/shard_map/ppermute | solution.py:210
  111.0 6.5 %near_weight_grad.1.near = f32[64,8,1024]{2,1,0:T(8,128)} custom-call(s32[1]{0:T(128)} %bitcast.pos, bf16[16,32,512]{2,1,0:T(8,128)(2,1)} %copy-done, bf16[16,32,512]{2,1,0:T(8,128)(2,1)} %collective-permute-done.10.am, bf16[16,32,512]{2,1,0:T(8,128)(2,1)} %collective-permute-done.11.ap, bf16[16,32,512]{2,1,0:T(8,128)(2,1)} %copy-done.2, ...), custom_call_target="tpu_custom_call" | custom-call | flops 3200000000 | bytes 25000000 | tf_op jit(solution)/shard_map/near_weight_grad/pallas_call | solution.py:297
  117.6 5.6 %collective-permute-done.15 = f32[16,32,512]{2,1,0:T(8,128)} collective-permute-done((f32[16,32,512]{2,1,0:T(8,128)}, f32[16,32,512]{2,1,0:T(8,128)}, u32[]{:S(2)}, u32[]{:S(2)}) %collective-permute-start.15) | collective-permute-done | bytes 1048608 | tf_op jit(solution)/shard_map/ppermute | solution.py:210
  123.2 3.0 %fusion.3 = bf16[16,32,512]{2,1,0:T(8,128)(2,1)} fusion(f32[16,32,512]{2,1,0:T(8,128)} %collective-permute-done.16, f32[16,32,512]{2,1,0:T(8,128)} %collective-permute-done.15, f32[3,16,32,512]{3,2,1,0:T(8,128)S(1)} %collective-permute-done.14, f32[4,16,32,512]{3,2,1,0:T(8,128)} %get-tuple-element.28), kind=kLoop, calls=%fused_computation.4 | loop fusion | flops 1048576 | bytes 4718592 | tf_op jit(solution)/shard_map/convert_element_type | solution.py:316
  126.3 5.2 %all-to-all-start.1 = ((bf16[16,32,512]{2,1,0:T(8,128)(2,1)}), bf16[16,32,512]{2,1,0:T(8,128)(2,1)S(1)}, u32[]{:S(2)}, u32[]{:S(2)}) async-start(bf16[16,32,512]{2,1,0:T(8,128)(2,1)} %fusion.3), calls=%async_computation.1 | async-start | bytes 1048576 | tf_op jit(solution)/shard_map/all_to_all | solution.py:216
  131.5 4.8 %collective-permute-start.22 = (bf16[8,32,512]{2,1,0:T(8,128)(2,1)S(1)}, bf16[8,32,512]{2,1,0:T(8,128)(2,1)S(1)}, u32[]{:S(2)}, u32[]{:S(2)}) collective-permute-start(bf16[8,32,512]{2,1,0:T(8,128)(2,1)S(1)} %collective-permute-done.20.a2a), channel_id=1, source_target_pairs={{0,1},{1,0},{2,3},{3,2},{4,5},{5,4},{6,7},{7,6},{8,9},{9,8},{10,11... | collective-permute-start | bytes 786440 | tf_op jit(solution)/shard_map/ppermute | solution.py:213
  136.4 1.1 collective-permute-done.22.b2a
  137.4 0.6 collective-permute-done.23.b2b
  138.0 0.1 copy-done.4
  138.1 0.7 copy-done.5
  138.8 7.0 %far_weight_grad.1 = bf16[1,8,34,8,128]{4,3,2,1,0:T(8,128)(2,1)} custom-call(s32[1]{0:T(128)} %bitcast.pos, s32[8,8,34]{2,1,0:T(8,128)} %rows.5, s32[8,8,34]{2,1,0:T(8,128)} %cols.5, s32[8,8]{1,0:T(8,128)} %live.5, bf16[8,32,512]{2,1,0:T(8,128)(2,1)} %copy-done.3, bf16[8,32,512]{2,1,0:T(8,128)(2,1)} %collective-permute-done.21.a2b, ...), custom_call_target="tpu_custom_call" | custom-call | flops 1100000000 | bytes 18000000 | tf_op jit(solution)/shard_map/far_weight_grad/pallas_call | solution.py:319
  145.8 0.8 copy.10
  (54 shorter events, 0.8 us)
Async XLA Ops:
  7.2 103.9 %all-gather.2.cloned.1.call-start = ((), (), s32[]{:S(2)}) async-start(), calls=%async_computation.2 | async-start | bytes 8912896 | tf_op jit(solution)/shard_map/all_gather | solution.py:218
  10.1 24.9 %all-to-all-start = ((bf16[16,64,512]{2,1,0:T(8,128)(2,1)}), bf16[16,64,512]{2,1,0:T(8,128)(2,1)S(1)}, u32[]{:S(2)}, u32[]{:S(2)}) async-start(bf16[16,64,512]{2,1,0:T(8,128)(2,1)} %feature_rows.1), calls=%async_computation | async-start | bytes 2097152 | tf_op jit(solution)/shard_map/all_to_all | solution.py:216
  35.1 33.0 %copy-start.1 = (bf16[16,32,512]{2,1,0:T(8,128)(2,1)}, bf16[16,32,512]{2,1,0:T(8,128)(2,1)S(1)}, u32[]{:S(2)}) copy-start(bf16[16,32,512]{2,1,0:T(8,128)(2,1)S(1)} %get-tuple-element.56.a0) | copy-start | bytes 1572868
  35.1 66.8 %copy-start = (bf16[16,32,512]{2,1,0:T(8,128)(2,1)}, bf16[16,32,512]{2,1,0:T(8,128)(2,1)S(1)}, u32[]{:S(2)}) copy-start(bf16[16,32,512]{2,1,0:T(8,128)(2,1)S(1)} %get-tuple-element.36.a0) | copy-start | bytes 1572868
  35.1 58.7 %collective-permute-start.14 = (f32[3,16,32,512]{3,2,1,0:T(8,128)}, f32[3,16,32,512]{3,2,1,0:T(8,128)S(1)}, u32[]{:S(2)}, u32[]{:S(2)}) collective-permute-start(f32[3,16,32,512]{3,2,1,0:T(8,128)} %get-tuple-element.41), channel_id=1, source_target_pairs={{0,1},{1,0},{2,3},{3,2},{4,5},{5,4},{6,7},{7,6},{8,9},{9,8},{10,11... | collective-permute-start | bytes 9437192 | tf_op jit(solution)/shard_map/ppermute | solution.py:213
  41.0 7.7 %collective-permute-start = (f32[16,32,512]{2,1,0:T(8,128)}, f32[16,32,512]{2,1,0:T(8,128)S(1)}, u32[]{:S(2)}, u32[]{:S(2)}) collective-permute-start(f32[16,32,512]{2,1,0:T(8,128)} %get-tuple-element.29), channel_id=1, source_target_pairs={{0,1},{1,0},{2,3},{3,2},{4,5},{5,4},{6,7},{7,6},{8,9},{9,8},{10,11... | collective-permute-start | bytes 3145736 | tf_op jit(solution)/shard_map/ppermute | solution.py:213
  41.1 15.0 %collective-permute-start.1 = (bf16[16,32,512]{2,1,0:T(8,128)(2,1)S(1)}, bf16[16,32,512]{2,1,0:T(8,128)(2,1)S(1)}, u32[]{:S(2)}, u32[]{:S(2)}) collective-permute-start(bf16[16,32,512]{2,1,0:T(8,128)(2,1)S(1)} %get-tuple-element.56.a0), channel_id=1, source_target_pairs={{0,2},{1,3},{2,4},{3,5},{4,6},{5,7},{6,0},{7,1},{8,10},{9,11},{10,... | collective-permute-start | bytes 1572872 | tf_op jit(solution)/shard_map/ppermute | solution.py:210
  42.5 13.7 %collective-permute-start.2 = (bf16[16,32,512]{2,1,0:T(8,128)(2,1)S(1)}, bf16[16,32,512]{2,1,0:T(8,128)(2,1)S(1)}, u32[]{:S(2)}, u32[]{:S(2)}) collective-permute-start(bf16[16,32,512]{2,1,0:T(8,128)(2,1)S(1)} %get-tuple-element.56.a0), channel_id=1, source_target_pairs={{0,6},{1,7},{2,0},{3,1},{4,2},{5,3},{6,4},{7,5},{8,14},{9,15},{10,... | collective-permute-start | bytes 1572872 | tf_op jit(solution)/shard_map/ppermute | solution.py:210
  44.1 22.2 %collective-permute-start.5 = (bf16[16,32,512]{2,1,0:T(8,128)(2,1)S(1)}, bf16[16,32,512]{2,1,0:T(8,128)(2,1)S(1)}, u32[]{:S(2)}, u32[]{:S(2)}) collective-permute-start(bf16[16,32,512]{2,1,0:T(8,128)(2,1)S(1)} %get-tuple-element.56.a0), channel_id=1, source_target_pairs={{0,1},{1,0},{2,3},{3,2},{4,5},{5,4},{6,7},{7,6},{8,9},{9,8},{10,11... | collective-permute-start | bytes 1572872 | tf_op jit(solution)/shard_map/ppermute | solution.py:213
  56.1 12.3 %copy-start.6 = (bf16[16,32,512]{2,1,0:T(8,128)(2,1)}, bf16[16,32,512]{2,1,0:T(8,128)(2,1)S(1)}, u32[]{:S(2)}) copy-start(bf16[16,32,512]{2,1,0:T(8,128)(2,1)S(1)} %collective-permute-done.1.am) | copy-start | bytes 1572868
  56.1 14.7 %copy-start.7 = (bf16[16,32,512]{2,1,0:T(8,128)(2,1)}, bf16[16,32,512]{2,1,0:T(8,128)(2,1)S(1)}, u32[]{:S(2)}) copy-start(bf16[16,32,512]{2,1,0:T(8,128)(2,1)S(1)} %collective-permute-done.2.ap) | copy-start | bytes 1572868
  56.2 8.4 %collective-permute-start.3 = (bf16[8,32,512]{2,1,0:T(8,128)(2,1)S(1)}, bf16[8,32,512]{2,1,0:T(8,128)(2,1)S(1)}, u32[]{:S(2)}, u32[]{:S(2)}) collective-permute-start(bf16[8,32,512]{2,1,0:T(8,128)(2,1)S(1)} %slice.65), channel_id=1, source_target_pairs={{0,2},{1,3},{2,4},{3,5},{4,6},{5,7},{6,0},{7,1},{8,10},{9,11},{10,... | collective-permute-start | bytes 786440 | tf_op jit(solution)/shard_map/ppermute | solution.py:210
  56.8 9.3 %collective-permute-start.4 = (bf16[8,32,512]{2,1,0:T(8,128)(2,1)S(1)}, bf16[8,32,512]{2,1,0:T(8,128)(2,1)S(1)}, u32[]{:S(2)}, u32[]{:S(2)}) collective-permute-start(bf16[8,32,512]{2,1,0:T(8,128)(2,1)S(1)} %slice.66), channel_id=1, source_target_pairs={{0,6},{1,7},{2,0},{3,1},{4,2},{5,3},{6,4},{7,5},{8,14},{9,15},{10,... | collective-permute-start | bytes 786440 | tf_op jit(solution)/shard_map/ppermute | solution.py:210
  59.0 11.9 %collective-permute-start.6 = (bf16[16,32,512]{2,1,0:T(8,128)(2,1)S(1)}, bf16[16,32,512]{2,1,0:T(8,128)(2,1)S(1)}, u32[]{:S(2)}, u32[]{:S(2)}) collective-permute-start(bf16[16,32,512]{2,1,0:T(8,128)(2,1)S(1)} %collective-permute-done.1.am), channel_id=1, source_target_pairs={{0,1},{1,0},{2,3},{3,2},{4,5},{5,4},{6,7},{7,6},{8,9},{9,8},{10,11... | collective-permute-start | bytes 1572872 | tf_op jit(solution)/shard_map/ppermute | solution.py:213
  64.5 9.9 %copy-start.11 = (bf16[8,32,512]{2,1,0:T(8,128)(2,1)}, bf16[8,32,512]{2,1,0:T(8,128)(2,1)S(1)}, u32[]{:S(2)}) copy-start(bf16[8,32,512]{2,1,0:T(8,128)(2,1)S(1)} %collective-permute-done.3.a2a) | copy-start | bytes 786436
  64.5 6.4 %collective-permute-start.7 = (bf16[16,32,512]{2,1,0:T(8,128)(2,1)S(1)}, bf16[16,32,512]{2,1,0:T(8,128)(2,1)S(1)}, u32[]{:S(2)}, u32[]{:S(2)}) collective-permute-start(bf16[16,32,512]{2,1,0:T(8,128)(2,1)S(1)} %collective-permute-done.2.ap), channel_id=1, source_target_pairs={{0,1},{1,0},{2,3},{3,2},{4,5},{5,4},{6,7},{7,6},{8,9},{9,8},{10,11... | collective-permute-start | bytes 1572872 | tf_op jit(solution)/shard_map/ppermute | solution.py:213
  66.2 4.8 %copy-start.12 = (bf16[8,32,512]{2,1,0:T(8,128)(2,1)}, bf16[8,32,512]{2,1,0:T(8,128)(2,1)S(1)}, u32[]{:S(2)}) copy-start(bf16[8,32,512]{2,1,0:T(8,128)(2,1)S(1)} %collective-permute-done.4.a2b) | copy-start | bytes 786436
  66.2 1.9 %collective-permute-start.8 = (bf16[8,32,512]{2,1,0:T(8,128)(2,1)S(1)}, bf16[8,32,512]{2,1,0:T(8,128)(2,1)S(1)}, u32[]{:S(2)}, u32[]{:S(2)}) collective-permute-start(bf16[8,32,512]{2,1,0:T(8,128)(2,1)S(1)} %collective-permute-done.3.a2a), channel_id=1, source_target_pairs={{0,1},{1,0},{2,3},{3,2},{4,5},{5,4},{6,7},{7,6},{8,9},{9,8},{10,11... | collective-permute-start | bytes 786440 | tf_op jit(solution)/shard_map/ppermute | solution.py:213
  66.3 4.7 %copy-start.8 = (bf16[16,32,512]{2,1,0:T(8,128)(2,1)}, bf16[16,32,512]{2,1,0:T(8,128)(2,1)S(1)}, u32[]{:S(2)}) copy-start(bf16[16,32,512]{2,1,0:T(8,128)(2,1)S(1)} %collective-permute-done.5.b0) | copy-start | bytes 1572868
  66.3 2.2 %collective-permute-start.9 = (bf16[8,32,512]{2,1,0:T(8,128)(2,1)S(1)}, bf16[8,32,512]{2,1,0:T(8,128)(2,1)S(1)}, u32[]{:S(2)}, u32[]{:S(2)}) collective-permute-start(bf16[8,32,512]{2,1,0:T(8,128)(2,1)S(1)} %collective-permute-done.4.a2b), channel_id=1, source_target_pairs={{0,1},{1,0},{2,3},{3,2},{4,5},{5,4},{6,7},{7,6},{8,9},{9,8},{10,11... | collective-permute-start | bytes 786440 | tf_op jit(solution)/shard_map/ppermute | solution.py:213
  68.1 2.9 %copy-start.13 = (bf16[8,32,512]{2,1,0:T(8,128)(2,1)}, bf16[8,32,512]{2,1,0:T(8,128)(2,1)S(1)}, u32[]{:S(2)}) copy-start(bf16[8,32,512]{2,1,0:T(8,128)(2,1)S(1)} %collective-permute-done.8.b2a) | copy-start | bytes 786436
  68.1 23.1 %collective-permute-start.10 = (bf16[16,32,512]{2,1,0:T(8,128)(2,1)S(1)}, bf16[16,32,512]{2,1,0:T(8,128)(2,1)}, u32[]{:S(2)}, u32[]{:S(2)}) collective-permute-start(bf16[16,32,512]{2,1,0:T(8,128)(2,1)S(1)} %get-tuple-element.36.a0), channel_id=1, source_target_pairs={{0,2},{1,3},{2,4},{3,5},{4,6},{5,7},{6,0},{7,1},{8,10},{9,11},{10,... | collective-permute-start | bytes 1572872 | tf_op jit(solution)/shard_map/ppermute | solution.py:210
  68.4 2.5 %copy-start.14 = (bf16[8,32,512]{2,1,0:T(8,128)(2,1)}, bf16[8,32,512]{2,1,0:T(8,128)(2,1)S(1)}, u32[]{:S(2)}) copy-start(bf16[8,32,512]{2,1,0:T(8,128)(2,1)S(1)} %collective-permute-done.9.b2b) | copy-start | bytes 786436
  68.4 22.7 %collective-permute-start.11 = (bf16[16,32,512]{2,1,0:T(8,128)(2,1)S(1)}, bf16[16,32,512]{2,1,0:T(8,128)(2,1)}, u32[]{:S(2)}, u32[]{:S(2)}) collective-permute-start(bf16[16,32,512]{2,1,0:T(8,128)(2,1)S(1)} %get-tuple-element.36.a0), channel_id=1, source_target_pairs={{0,6},{1,7},{2,0},{3,1},{4,2},{5,3},{6,4},{7,5},{8,14},{9,15},{10,... | collective-permute-start | bytes 1572872 | tf_op jit(solution)/shard_map/ppermute | solution.py:210
  70.8 0.8 copy-start.9
  70.8 22.9 %collective-permute-start.12 = (f32[8,32,512]{2,1,0:T(8,128)}, f32[8,32,512]{2,1,0:T(8,128)}, u32[]{:S(2)}, u32[]{:S(2)}) collective-permute-start(f32[8,32,512]{2,1,0:T(8,128)} %get-tuple-element.37), channel_id=1, source_target_pairs={{0,2},{1,3},{2,4},{3,5},{4,6},{5,7},{6,0},{7,1},{8,10},{9,11},{10,... | collective-permute-start | bytes 1572872 | tf_op jit(solution)/shard_map/ppermute | solution.py:210
  71.6 0.8 copy-start.10
  72.4 21.3 %collective-permute-start.13 = (f32[8,32,512]{2,1,0:T(8,128)}, f32[8,32,512]{2,1,0:T(8,128)}, u32[]{:S(2)}, u32[]{:S(2)}) collective-permute-start(f32[8,32,512]{2,1,0:T(8,128)} %get-tuple-element.38), channel_id=1, source_target_pairs={{0,6},{1,7},{2,0},{3,1},{4,2},{5,3},{6,4},{7,5},{8,14},{9,15},{10,... | collective-permute-start | bytes 1572872 | tf_op jit(solution)/shard_map/ppermute | solution.py:210
  98.2 25.0 %collective-permute-start.15 = (f32[16,32,512]{2,1,0:T(8,128)}, f32[16,32,512]{2,1,0:T(8,128)}, u32[]{:S(2)}, u32[]{:S(2)}) collective-permute-start(f32[16,32,512]{2,1,0:T(8,128)} %pad_maximum_fusion), channel_id=1, source_target_pairs={{0,2},{1,3},{2,4},{3,5},{4,6},{5,7},{6,0},{7,1},{8,10},{9,11},{10,... | collective-permute-start | bytes 3145736 | tf_op jit(solution)/shard_map/ppermute | solution.py:210
  99.3 23.9 %collective-permute-start.16 = (f32[16,32,512]{2,1,0:T(8,128)}, f32[16,32,512]{2,1,0:T(8,128)}, u32[]{:S(2)}, u32[]{:S(2)}) collective-permute-start(f32[16,32,512]{2,1,0:T(8,128)} %pad_maximum_fusion.1), channel_id=1, source_target_pairs={{0,6},{1,7},{2,0},{3,1},{4,2},{5,3},{6,4},{7,5},{8,14},{9,15},{10,... | collective-permute-start | bytes 3145736 | tf_op jit(solution)/shard_map/ppermute | solution.py:210
  101.9 5.6 %collective-permute-start.17 = (bf16[16,32,512]{2,1,0:T(8,128)(2,1)S(1)}, bf16[16,32,512]{2,1,0:T(8,128)(2,1)S(1)}, u32[]{:S(2)}, u32[]{:S(2)}) collective-permute-start(bf16[16,32,512]{2,1,0:T(8,128)(2,1)S(1)} %get-tuple-element.36.a0), channel_id=1, source_target_pairs={{0,1},{1,0},{2,3},{3,2},{4,5},{5,4},{6,7},{7,6},{8,9},{9,8},{10,11... | collective-permute-start | bytes 1572872 | tf_op jit(solution)/shard_map/ppermute | solution.py:213
  103.7 4.7 %collective-permute-start.18 = (bf16[16,32,512]{2,1,0:T(8,128)(2,1)}, bf16[16,32,512]{2,1,0:T(8,128)(2,1)}, u32[]{:S(2)}, u32[]{:S(2)}) collective-permute-start(bf16[16,32,512]{2,1,0:T(8,128)(2,1)} %collective-permute-done.10.am), channel_id=1, source_target_pairs={{0,1},{1,0},{2,3},{3,2},{4,5},{5,4},{6,7},{7,6},{8,9},{9,8},{10,11... | collective-permute-start | bytes 1572872 | tf_op jit(solution)/shard_map/ppermute | solution.py:213
  103.7 7.3 %collective-permute-start.19 = (bf16[16,32,512]{2,1,0:T(8,128)(2,1)}, bf16[16,32,512]{2,1,0:T(8,128)(2,1)}, u32[]{:S(2)}, u32[]{:S(2)}) collective-permute-start(bf16[16,32,512]{2,1,0:T(8,128)(2,1)} %collective-permute-done.11.ap), channel_id=1, source_target_pairs={{0,1},{1,0},{2,3},{3,2},{4,5},{5,4},{6,7},{7,6},{8,9},{9,8},{10,11... | collective-permute-start | bytes 1572872 | tf_op jit(solution)/shard_map/ppermute | solution.py:213
  107.6 0.8 copy-start.2
  108.3 23.1 %collective-permute-start.20 = (bf16[8,32,512]{2,1,0:T(8,128)(2,1)}, bf16[8,32,512]{2,1,0:T(8,128)(2,1)S(1)}, u32[]{:S(2)}, u32[]{:S(2)}) collective-permute-start(bf16[8,32,512]{2,1,0:T(8,128)(2,1)} %slice.78), channel_id=1, source_target_pairs={{0,2},{1,3},{2,4},{3,5},{4,6},{5,7},{6,0},{7,1},{8,10},{9,11},{10,... | collective-permute-start | bytes 786440 | tf_op jit(solution)/shard_map/ppermute | solution.py:210
  108.4 27.9 %collective-permute-start.21 = (bf16[8,32,512]{2,1,0:T(8,128)(2,1)}, bf16[8,32,512]{2,1,0:T(8,128)(2,1)}, u32[]{:S(2)}, u32[]{:S(2)}) collective-permute-start(bf16[8,32,512]{2,1,0:T(8,128)(2,1)} %slice.79), channel_id=1, source_target_pairs={{0,6},{1,7},{2,0},{3,1},{4,2},{5,3},{6,4},{7,5},{8,14},{9,15},{10,... | collective-permute-start | bytes 786440 | tf_op jit(solution)/shard_map/ppermute | solution.py:210
  126.3 19.5 %all-to-all-start.1 = ((bf16[16,32,512]{2,1,0:T(8,128)(2,1)}), bf16[16,32,512]{2,1,0:T(8,128)(2,1)S(1)}, u32[]{:S(2)}, u32[]{:S(2)}) async-start(bf16[16,32,512]{2,1,0:T(8,128)(2,1)} %fusion.3), calls=%async_computation.1 | async-start | bytes 1048576 | tf_op jit(solution)/shard_map/all_to_all | solution.py:216
  131.5 6.5 %copy-start.3 = (bf16[8,32,512]{2,1,0:T(8,128)(2,1)}, bf16[8,32,512]{2,1,0:T(8,128)(2,1)S(1)}, u32[]{:S(2)}) copy-start(bf16[8,32,512]{2,1,0:T(8,128)(2,1)S(1)} %collective-permute-done.20.a2a) | copy-start | bytes 786436
  131.5 5.9 %collective-permute-start.22 = (bf16[8,32,512]{2,1,0:T(8,128)(2,1)S(1)}, bf16[8,32,512]{2,1,0:T(8,128)(2,1)S(1)}, u32[]{:S(2)}, u32[]{:S(2)}) collective-permute-start(bf16[8,32,512]{2,1,0:T(8,128)(2,1)S(1)} %collective-permute-done.20.a2a), channel_id=1, source_target_pairs={{0,1},{1,0},{2,3},{3,2},{4,5},{5,4},{6,7},{7,6},{8,9},{9,8},{10,11... | collective-permute-start | bytes 786440 | tf_op jit(solution)/shard_map/ppermute | solution.py:213
  136.2 1.7 %collective-permute-start.23 = (bf16[8,32,512]{2,1,0:T(8,128)(2,1)}, bf16[8,32,512]{2,1,0:T(8,128)(2,1)S(1)}, u32[]{:S(2)}, u32[]{:S(2)}) collective-permute-start(bf16[8,32,512]{2,1,0:T(8,128)(2,1)} %collective-permute-done.21.a2b), channel_id=1, source_target_pairs={{0,1},{1,0},{2,3},{3,2},{4,5},{5,4},{6,7},{7,6},{8,9},{9,8},{10,11... | collective-permute-start | bytes 786440 | tf_op jit(solution)/shard_map/ppermute | solution.py:213
  137.4 0.7 copy-start.4
  138.1 0.7 copy-start.5
Sparse Core Ops, SparseCore 0:
  10.1 78.8 all-gather.1

commit v6 on v5

--- a/solution.py
+++ b/solution.py
@@ -17,16 +17,12 @@
     panel[...] = jnp.zeros_like(panel)
     count = live_ref[owner, j]
     for k in range(34):
-
-        def place(k=k):
-            r = pl.multiple_of((rows_ref[owner, j, k] - 8 * j) * 128, 128)
-            c = pl.multiple_of((cols_ref[owner, j, k] - 8 * owner) * 128, 128)
-            panel[pl.ds(r, 128), pl.ds(c, 128)] = blk_ref[j, k]
-
-        if k < 30:
-            place()
-        else:
-            pl.when(k < count)(place)
+        r = pl.multiple_of((rows_ref[owner, j, k] - 8 * j) * 128, 128)
+        c = pl.multiple_of((cols_ref[owner, j, k] - 8 * owner) * 128, 128)
+        block = blk_ref[k]
+        if k >= 30:
+            block = jnp.where(k < count, block, jnp.zeros_like(block))
+        panel[pl.ds(r, 128), pl.ds(c, 128)] = block
 
 
 def start_all(copies):
@@ -47,10 +43,9 @@
         o_ref[part, pl.ds(32, 32)] = t[:, part].reshape(32, 512).astype(BF16)
 
 
-def partial_kernel(
-    pos, rows, cols, live, cot, blk, keep, across, rest,
-    lhs, blk_v, panel, keep_v, across_v, rest_v, cot_sem, blk_sem, out_sem,
-):
+def partial_kernel(pos, rows, cols, live, cot, blk, keep, across, rest, dense, *scratch):
+    lhs, keep_v, across_v, rest_v, cot_sem, blk_sem, out_sem = scratch[:7]
+    blk_v, panels = scratch[7:15], scratch[15:23]
     owner = pos[0]
     y = owner // 2
     core = owner % 2
@@ -63,22 +58,20 @@
                     cot.at[(y + d) % 4, who], lhs.at[pl.ds(side * 128 + d * 32, 32)], cot_sem.at[side * 4 + d]
                 )
             )
+    blk_copies = [pltpu.make_async_copy(blk.at[0, j], blk_v[j], blk_sem.at[j]) for j in range(8)]
     start_all(cot_copies)
-    start_all([pltpu.make_async_copy(blk.at[0, j], blk_v.at[j], blk_sem.at[j]) for j in range(8)])
+    start_all(blk_copies)
+
+    out_copies = []
+    blk_copies[0].wait()
+    build_panel(panels[0], blk_v[0], rows, cols, live, owner, 0)
     wait_all(cot_copies)
-
-    def out_copies(j):
-        part = pl.ds(j * 2, 2)
-        return (
-            pltpu.make_async_copy(keep_v.at[:, part], keep.at[:, part], out_sem.at[j, 0]),
-            pltpu.make_async_copy(across_v.at[part], across.at[part], out_sem.at[j, 1]),
-            pltpu.make_async_copy(rest_v.at[:, part], rest.at[:, part], out_sem.at[j, 2]),
-        )
-
-    def step(j, carry):
-        pltpu.make_async_copy(blk.at[0, j], blk_v.at[j], blk_sem.at[j]).wait()
-        build_panel(panel, blk_v, rows, cols, live, owner, j)
-        res = lax.dot_general(lhs[...], panel[...], (((1,), (1,)), ((), ())), preferred_element_type=F32)
+    for j in range(8):
+        if j < 7:
+            blk_copies[j + 1].wait()
+        res = lax.dot_general(lhs[...], panels[j][...], (((1,), (1,)), ((), ())), preferred_element_type=F32)
+        if j < 7:
+            build_panel(panels[j + 1], blk_v[j + 1], rows, cols, live, owner, j + 1)
         for half in range(2):
             lanes = slice(half * 512, half * 512 + 512)
             at = j * 2 + half
@@ -88,22 +81,22 @@
             rest_v[1, at] = res[160:192, lanes]
             across_v[at] = res[192:224, lanes]
             rest_v[2, at] = res[224:256, lanes]
-        start_all(out_copies(j))
-        return carry
-
-    lax.fori_loop(0, 8, step, 0)
-    for j in range(8):
-        wait_all(out_copies(j))
-
-
-def out_kernel(
-    pos, rows, cols, live, a0, am, ap, a2a, a2b, b0, bm, bp, b2a, b2b, blk, out_ref,
-    lhs, blk_v, panel, acc, x_sem, blk_sem,
-):
+        part = pl.ds(j * 2, 2)
+        step_copies = [
+            pltpu.make_async_copy(panels[j], dense.at[j], out_sem.at[j, 0]),
+            pltpu.make_async_copy(keep_v.at[:, part], keep.at[:, part], out_sem.at[j, 1]),
+            pltpu.make_async_copy(across_v.at[part], across.at[part], out_sem.at[j, 2]),
+            pltpu.make_async_copy(rest_v.at[:, part], rest.at[:, part], out_sem.at[j, 3]),
+        ]
+        start_all(step_copies)
+        out_copies += step_copies
+    wait_all(out_copies)
+
+
+def out_kernel(pos, a0, am, ap, a2a, a2b, b0, bm, bp, b2a, b2b, dense, out_ref, lhs, panels, acc, x_sem, dense_sem):
     owner = pos[0]
     y = owner // 2
     core = owner % 2
-    start_all([pltpu.make_async_copy(blk.at[0, j], blk_v.at[j], blk_sem.at[j]) for j in range(8)])
     x_copies = []
     for who, pieces in ((core, (a0, am, ap, a2a, a2b)), (1 - core, (b0, bm, bp, b2a, b2b))):
         places = (
@@ -115,21 +108,20 @@
         )
         for piece, place in zip(pieces, places):
             x_copies.append(pltpu.make_async_copy(piece, place, x_sem.at[len(x_copies)]))
+    dense_copies = [pltpu.make_async_copy(dense.at[j], panels.at[j], dense_sem.at[j]) for j in range(8)]
     start_all(x_copies)
-    acc[...] = jnp.zeros_like(acc)
+    start_all(dense_copies)
     wait_all(x_copies)
-
-    def step(j, carry):
-        pltpu.make_async_copy(blk.at[0, j], blk_v.at[j], blk_sem.at[j]).wait()
-        build_panel(panel, blk_v, rows, cols, live, owner, j)
-        for half in range(2):
-            acc[...] += jnp.dot(
-                lhs[j * 2 + half].reshape(256, 512), panel[pl.ds(half * 512, 512)], preferred_element_type=F32
-            )
-        return carry
-
-    lax.fori_loop(0, 8, step, 0)
-    out_ref[...] = acc[...].astype(BF16)
+    for j in range(8):
+        dense_copies[j].wait()
+        first = jnp.dot(lhs[j * 2].reshape(256, 512), panels[j, :512], preferred_element_type=F32)
+        second = jnp.dot(lhs[j * 2 + 1].reshape(256, 512), panels[j, 512:], preferred_element_type=F32)
+        if j == 0:
+            acc[...] = first + second
+        elif j < 7:
+            acc[...] += first + second
+        else:
+            out_ref[...] = (acc[...] + first + second).astype(BF16)
 
 
 def token_group(owner, chip_step, core_step):
@@ -229,66 +221,67 @@
 
     scalars = [pl.BlockSpec(memory_space=pltpu.SMEM)] * 4
     anywhere = pl.BlockSpec(memory_space=pl.ANY)
-    keep, across, rest = pl.pallas_call(
+    keep, across, rest, dense = pl.pallas_call(
         partial_kernel,
         in_specs=scalars + [anywhere] * 2,
-        out_specs=[anywhere] * 3,
+        out_specs=[anywhere] * 4,
         out_shape=[
             jax.ShapeDtypeStruct((4, 16, 32, 512), F32),
             jax.ShapeDtypeStruct((16, 32, 512), F32),
             jax.ShapeDtypeStruct((3, 16, 32, 512), F32),
+            jax.ShapeDtypeStruct((8, 1024, 1024), BF16),
         ],
         scratch_shapes=[
             pltpu.VMEM((256, 1024), BF16),
-            pltpu.VMEM((8, 34, 128, 128), BF16),
-            pltpu.VMEM((1024, 1024), BF16),
             pltpu.VMEM((4, 16, 32, 512), F32),
             pltpu.VMEM((16, 32, 512), F32),
             pltpu.VMEM((3, 16, 32, 512), F32),
             pltpu.SemaphoreType.DMA((8,)),
             pltpu.SemaphoreType.DMA((8,)),
-            pltpu.SemaphoreType.DMA((8, 3)),
-        ],
-        compiler_params=params,
-        cost_estimate=cost(4_300_000_000, 40_000_000),
+            pltpu.SemaphoreType.DMA((8, 4)),
+        ]
+        + [pltpu.VMEM((34, 128, 128), BF16)] * 8
+        + [pltpu.VMEM((1024, 1024), BF16)] * 8,
+        compiler_params=params,
+        cost_estimate=cost(4_300_000_000, 45_000_000),
         name="partial_context_grad",
     )(*tables, cot_own.reshape(4, 2, 32, 1024), blocks)
     across = other_core(across)
 
+    q2a, q2b = keep[2, :8] + across[:8], keep[2, 8:] + across[8:]
+    q2a, q2b, tokens, rest = barrier((q2a, q2b, tokens, rest))
+    from_a, from_b = along_y(q2a, 1), along_y(q2b, -1)
     xm, xp = along_y(tokens, 1), along_y(tokens, -1)
-    rest, _ = barrier((rest, tokens))
     rest = other_core(rest)
-
-    q2a, q2b, xm, xp = barrier((keep[2, :8] + across[:8], keep[2, 8:] + across[8:], xm, xp))
     x2a, x2b = along_y(xm[:8], 1), along_y(xp[8:], -1)
-    x2a, x2b, q2a, q2b, class_rows = barrier((x2a, x2b, q2a, q2b, class_rows))
-    from_a, from_b = along_y(q2a, 1), along_y(q2b, -1)
+    x2a, x2b, class_rows = barrier((x2a, x2b, class_rows))
     own = (tokens, xm, xp, x2a, x2b)
     x_pieces = own + tuple(other_core(piece) for piece in own)
 
     cm, cp = along_y(class_rows, 1), along_y(class_rows, -1)
 
+    q1 = jnp.concatenate([keep[1, :8] + rest[1, :8] + from_a, keep[1, 8:] + rest[1, 8:]], axis=0)
+    q3 = jnp.concatenate([keep[3, :8] + rest[2, :8], keep[3, 8:] + rest[2, 8:] + from_b], axis=0)
+    q1, q3, x_pieces = barrier((q1, q3, x_pieces))
+    sum_m, sum_p = along_y(q1, 1), along_y(q3, -1)
+
     outputs = pl.pallas_call(
         out_kernel,
-        in_specs=scalars + [anywhere] * 11,
+        in_specs=scalars[:1] + [anywhere] * 11,
         out_shape=jax.ShapeDtypeStruct((256, 1024), BF16),
         scratch_shapes=[
             pltpu.VMEM((16, 4, 2, 32, 512), BF16),
-            pltpu.VMEM((8, 34, 128, 128), BF16),
-            pltpu.VMEM((1024, 1024), BF16),
+            pltpu.VMEM((8, 1024, 1024), BF16),
             pltpu.VMEM((256, 1024), F32),
             pltpu.SemaphoreType.DMA((10,)),
             pltpu.SemaphoreType.DMA((8,)),
         ],
         compiler_params=params,
-        cost_estimate=cost(4_300_000_000, 40_000_000),
+        cost_estimate=cost(4_300_000_000, 30_000_000),
         name="outputs",
-    )(*tables, *x_pieces, blocks)
-
-    outputs, cm, cp, from_a, from_b = barrier((outputs, cm, cp, from_a, from_b))
-    q1 = jnp.concatenate([keep[1, :8] + rest[1, :8] + from_a, keep[1, 8:] + rest[1, 8:]], axis=0)
-    q3 = jnp.concatenate([keep[3, :8] + rest[2, :8], keep[3, 8:] + rest[2, 8:] + from_b], axis=0)
-    sum_m, sum_p = along_y(q1, 1), along_y(q3, -1)
+    )(pos, *x_pieces, dense)
+
+    outputs, cm, cp = barrier((outputs, cm, cp))
     c2a, c2b = along_y(cm[:8], 1), along_y(cp[8:], -1)
 
     near = (class_rows, cm, cp)

time: 155 us -> 145 us (0.935)
  starting transfers between devices: 46.6 us -> 41.5 us
  other arithmetic: 10.9 us -> 6.57 us
  waiting for transfers between devices: 26 us -> 30.2 us
  Pallas kernels: 48.3 us -> 44.5 us
    ppermute x12, waiting for transfers between devices: 17.4 us -> 25.6 us  [along_y(): return lax.ppermute(x, 'mp', [(i, (i + 2 * step) % 8) for i in range(8)])]
    ppermute x12, starting transfers between devices: 17.3 us -> 11 us  [other_core(): return lax.ppermute(x, 'mp', [(i, i ^ 1) for i in range(8)])]
    pallas_call x1, Pallas kernels: 16.7 us -> 12.7 us  [on_device(): pl.pallas_call(out_kernel, in_specs=scalars[:1] + [anywhere] * 11, out_sh...]
    ppermute x12, waiting for transfers between devices: 7.38 us -> 3.9 us  [other_core(): return lax.ppermute(x, 'mp', [(i, i ^ 1) for i in range(8)])]
    unnamed x31 -> x33, local copies, waits for them, and re-layouts: 3.91 us -> 3.45 us
  transfers between devices with their start and end apart: 27 -> 27, of which waited for: 11 -> 8; matrix products, arithmetic and copies ran while one was open for 9% -> 7% of each run, Pallas kernels for 32% -> 31%
where the time goes in v6:
time: 145 us; the launch traced here: 144 us
  Pallas kernels  44.5 us (31%)
  starting transfers between devices  41.5 us (29%)
  waiting for transfers between devices  30.2 us (21%)
  between operations  14.3 us (10%)
  local copies, waits for them, and re-layouts  6.8 us (5%)
  other arithmetic  6.57 us (5%)
    ppermute x12, waiting for transfers between devices, along_y(): return lax.ppermute(x, 'mp', [(i, (i + 2 * step) % 8) for i in range(8)])  25.6 us
    ppermute x12, starting transfers between devices, along_y(): return lax.ppermute(x, 'mp', [(i, (i + 2 * step) % 8) for i in range(8)])  16.8 us
    pallas_call x1, Pallas kernels, on_device(): pl.pallas_call(partial_kernel, in_specs=scalars + [anywhere] * 2, out_spe...  16 us
    all_to_all x2, starting transfers between devices, exchange(): return lax.all_to_all(x, 'seq', split_axis=0, concat_axis=0, tiled=True)  13.6 us
    pallas_call x1, Pallas kernels, on_device(): pl.pallas_call(out_kernel, in_specs=scalars[:1] + [anywhere] * 11, out_sh...  12.7 us
    ppermute x12, starting transfers between devices, other_core(): return lax.ppermute(x, 'mp', [(i, i ^ 1) for i in range(8)])  11 us
    pallas_call x1, Pallas kernels, on_device(): pl.pallas_call(functools.partial(far_grad_kernel, 1.0 / math.sqrt(4096)),...  6.96 us
    pallas_call x1, Pallas kernels, on_device(): pl.pallas_call(near_grad_kernel, in_specs=scalars[:1] + [anywhere] * 7, o...  6.57 us
  transfers between devices with their start and end apart: 27, of which 8 were waited for; matrix products, arithmetic and copies ran while one was open for 7% of the time, Pallas kernels for 31%

profile of v6, /device:TPU:1, one launch (start us, length us, event | category | flops | bytes accessed | tf_op | source)
XLA Modules:
  0.0 143.9 jit_solution(5797332263151208240)
XLA Ops:
  7.2 0.7 all-gather.2.cloned.1.call-update
  7.9 2.2 %feature_rows.1 = bf16[16,64,512]{2,1,0:T(8,128)(2,1)} custom-call(bf16[16,32,512]{2,1,0:T(8,128)(2,1)} %x_ref.1), custom_call_target="tpu_custom_call" | custom-call | tf_op jit(solution)/shard_map/feature_rows/pallas_call | solution.py:212
  10.1 8.4 %all-to-all-start = ((bf16[16,64,512]{2,1,0:T(8,128)(2,1)}), bf16[16,64,512]{2,1,0:T(8,128)(2,1)S(1)}, u32[]{:S(2)}, u32[]{:S(2)}) async-start(bf16[16,64,512]{2,1,0:T(8,128)(2,1)} %feature_rows.1), calls=%async_computation | async-start | bytes 2097152 | tf_op jit(solution)/shard_map/all_to_all | solution.py:208
  18.6 16.0 %partial_context_grad.1 = (f32[4,16,32,512]{3,2,1,0:T(8,128)}, f32[16,32,512]{2,1,0:T(8,128)}, f32[3,16,32,512]{3,2,1,0:T(8,128)}, bf16[8,1024,1024]{2,1,0:T(8,128)(2,1)}) custom-call(s32[1]{0:T(128)} %bitcast.pos, s32[8,8,34]{2,1,0:T(8,128)} %rows.3, s32[8,8,34]{2,1,0:T(8,128)} %cols.3, s32[8,8]{1,0:T(8,128)} %live.3, bf16[4,2,32,1024]{3,2,1,0:T(8,128)(2,1)} %bitcast.29, ...), custom_call_target="tpu_custom_call" | custom-call | flops 4300000256 | bytes 45000000 | tf_op jit(solution)/shard_map/partial_context_grad/pallas_call | solution.py:224
  34.6 1.2 collective-permute-start
  35.7 0.9 fusion.10
  36.6 1.6 %collective-permute-done = f32[16,32,512]{2,1,0:T(8,128)S(1)} collective-permute-done((f32[16,32,512]{2,1,0:T(8,128)}, f32[16,32,512]{2,1,0:T(8,128)S(1)}, u32[]{:S(2)}, u32[]{:S(2)}) %collective-permute-start) | collective-permute-done | bytes 1048608 | tf_op jit(solution)/shard_map/ppermute | solution.py:205
  38.2 1.4 slice_add_fusion.5
  39.7 4.3 %collective-permute-start.1 = (f32[3,16,32,512]{3,2,1,0:T(8,128)}, f32[3,16,32,512]{3,2,1,0:T(8,128)S(1)}, u32[]{:S(2)}, u32[]{:S(2)}) collective-permute-start(f32[3,16,32,512]{3,2,1,0:T(8,128)} %get-tuple-element.39), channel_id=1, source_target_pairs={{0,1},{1,0},{2,3},{3,2},{4,5},{5,4},{6,7},{7,6},{8,9},{9,8},{10,11... | collective-permute-start | bytes 9437192 | tf_op jit(solution)/shard_map/ppermute | solution.py:205
  44.0 1.4 collective-permute-start.4
  45.4 1.6 %collective-permute-start.5 = (bf16[16,32,512]{2,1,0:T(8,128)(2,1)S(1)}, bf16[16,32,512]{2,1,0:T(8,128)(2,1)S(1)}, u32[]{:S(2)}, u32[]{:S(2)}) collective-permute-start(bf16[16,32,512]{2,1,0:T(8,128)(2,1)S(1)} %get-tuple-element.45.a0), channel_id=1, source_target_pairs={{0,6},{1,7},{2,0},{3,1},{4,2},{5,3},{6,4},{7,5},{8,14},{9,15},{10,... | collective-permute-start | bytes 1572872 | tf_op jit(solution)/shard_map/ppermute | solution.py:202
  47.0 2.7 %collective-permute-start.3 = (f32[8,32,512]{2,1,0:T(8,128)S(1)}, f32[8,32,512]{2,1,0:T(8,128)S(1)}, u32[]{:S(2)}, u32[]{:S(2)}) collective-permute-start(f32[8,32,512]{2,1,0:T(8,128)S(1)} %get-tuple-element.41), channel_id=1, source_target_pairs={{0,6},{1,7},{2,0},{3,1},{4,2},{5,3},{6,4},{7,5},{8,14},{9,15},{10,... | collective-permute-start | bytes 1572872 | tf_op jit(solution)/shard_map/ppermute | solution.py:202
  49.6 9.6 %collective-permute-done.4.am = bf16[16,32,512]{2,1,0:T(8,128)(2,1)S(1)} collective-permute-done((bf16[16,32,512]{2,1,0:T(8,128)(2,1)S(1)}, bf16[16,32,512]{2,1,0:T(8,128)(2,1)S(1)}, u32[]{:S(2)}, u32[]{:S(2)}) %collective-permute-start.4) | collective-permute-done | bytes 524320 | tf_op jit(solution)/shard_map/ppermute | solution.py:202
  59.4 2.7 %collective-permute-start.7 = (bf16[8,32,512]{2,1,0:T(8,128)(2,1)S(1)}, bf16[8,32,512]{2,1,0:T(8,128)(2,1)S(1)}, u32[]{:S(2)}, u32[]{:S(2)}) collective-permute-start(bf16[8,32,512]{2,1,0:T(8,128)(2,1)S(1)} %slice.88), channel_id=1, source_target_pairs={{0,6},{1,7},{2,0},{3,1},{4,2},{5,3},{6,4},{7,5},{8,14},{9,15},{10,... | collective-permute-start | bytes 786440 | tf_op jit(solution)/shard_map/ppermute | solution.py:202
  62.1 14.0 %collective-permute-done.6.a2a = bf16[8,32,512]{2,1,0:T(8,128)(2,1)S(1)} collective-permute-done((bf16[8,32,512]{2,1,0:T(8,128)(2,1)S(1)}, bf16[8,32,512]{2,1,0:T(8,128)(2,1)S(1)}, u32[]{:S(2)}, u32[]{:S(2)}) %collective-permute-start.6) | collective-permute-done | bytes 262176 | tf_op jit(solution)/shard_map/ppermute | solution.py:202
  76.1 0.6 collective-permute-start.8
  76.8 0.4 collective-permute-start.9
  77.2 0.1 collective-permute-start.11
  77.3 0.4 collective-permute-start.12
  77.7 0.4 fusion.5
  78.1 0.2 fusion.6
  78.4 1.1 collective-permute-start.13
  79.5 0.6 collective-permute-done.11.b2a
  80.1 1.9 %collective-permute-start.14 = (bf16[16,32,512]{2,1,0:T(8,128)(2,1)}, bf16[16,32,512]{2,1,0:T(8,128)(2,1)}, u32[]{:S(2)}, u32[]{:S(2)}) collective-permute-start(bf16[16,32,512]{2,1,0:T(8,128)(2,1)} %get-tuple-element.56.a0), channel_id=1, source_target_pairs={{0,6},{1,7},{2,0},{3,1},{4,2},{5,3},{6,4},{7,5},{8,14},{9,15},{10,... | collective-permute-start | bytes 1572872 | tf_op jit(solution)/shard_map/ppermute | solution.py:202
  82.0 1.5 %pad_maximum_fusion = (f32[16,32,512]{2,1,0:T(8,128)}, f32[16,32,512]{2,1,0:T(8,128)}) fusion(f32[8,32,512]{2,1,0:T(8,128)S(1)} %get-tuple-element.66, f32[8,32,512]{2,1,0:T(8,128)S(1)} %get-tuple-element.68, f32[8,32,512]{2,1,0:T(8,128)S(1)} %get-tuple-element.67, f32[8,32,512]{2,1,0:T(8,128)S(1)} %get-tuple-element.65), kind=kLoop, calls=%fused_computation.5 | loop fusion | flops 524288 | bytes 4194304 | tf_op jit(solution)/shard_map/concatenate | solution.py:263
  83.6 0.7 collective-permute-start.17
  84.3 0.8 copy-done.6
  85.1 0.2 copy-done.7
  85.3 2.7 %collective-permute-start.16 = (f32[16,32,512]{2,1,0:T(8,128)}, f32[16,32,512]{2,1,0:T(8,128)}, u32[]{:S(2)}, u32[]{:S(2)}) collective-permute-start(f32[16,32,512]{2,1,0:T(8,128)} %get-tuple-element.59), channel_id=1, source_target_pairs={{0,6},{1,7},{2,0},{3,1},{4,2},{5,3},{6,4},{7,5},{8,14},{9,15},{10,... | collective-permute-start | bytes 3145736 | tf_op jit(solution)/shard_map/ppermute | solution.py:202
  88.0 12.7 %outputs.1 = bf16[256,1024]{1,0:T(8,128)(2,1)} custom-call(s32[1]{0:T(128)} %bitcast.pos, bf16[16,32,512]{2,1,0:T(8,128)(2,1)} %copy-done.1, bf16[16,32,512]{2,1,0:T(8,128)(2,1)} %copy-done.2, bf16[16,32,512]{2,1,0:T(8,128)(2,1)} %copy-done.3, bf16[8,32,512]{2,1,0:T(8,128)(2,1)} %copy-done.9, bf16[8,32,512]{2,1,0:T(8,128)(2,1)} %copy-done.10, ...), custom_call_target="tpu_custom_call" | custom-call | flops 4300000256 | bytes 30000000 | tf_op jit(solution)/shard_map/outputs/pallas_call | solution.py:268
  100.8 0.7 collective-permute-start.18
  101.6 0.7 slice.78
  102.3 1.7 %slice.79 = bf16[8,32,512]{2,1,0:T(8,128)(2,1)} slice(bf16[16,32,512]{2,1,0:T(8,128)(2,1)} %collective-permute-done.14.ap), slice={[8:16], [0:32], [0:512]} | slice | bytes 524288 | tf_op jit(solution)/shard_map/slice | solution.py:285
  104.0 0.8 copy-done.8
  104.8 2.7 %collective-permute-start.21 = (bf16[8,32,512]{2,1,0:T(8,128)(2,1)}, bf16[8,32,512]{2,1,0:T(8,128)(2,1)}, u32[]{:S(2)}, u32[]{:S(2)}) collective-permute-start(bf16[8,32,512]{2,1,0:T(8,128)(2,1)} %slice.79), channel_id=1, source_target_pairs={{0,6},{1,7},{2,0},{3,1},{4,2},{5,3},{6,4},{7,5},{8,14},{9,15},{10,... | collective-permute-start | bytes 786440 | tf_op jit(solution)/shard_map/ppermute | solution.py:202
  107.5 6.6 %near_weight_grad.1.near = f32[64,8,1024]{2,1,0:T(8,128)} custom-call(s32[1]{0:T(128)} %bitcast.pos, bf16[16,32,512]{2,1,0:T(8,128)(2,1)} %get-tuple-element.56.a0, bf16[16,32,512]{2,1,0:T(8,128)(2,1)} %copy-done.4, bf16[16,32,512]{2,1,0:T(8,128)(2,1)} %collective-permute-done.14.ap, bf16[16,32,512]{2,1,0:T(8,128)(2,1)} %collective-permute-done.17.b0, ...), custom_call_target="tpu_custom_call" | custom-call | flops 3200000000 | bytes 25000000 | tf_op jit(solution)/shard_map/near_weight_grad/pallas_call | solution.py:290
  114.0 1.6 %collective-permute-done.15 = f32[16,32,512]{2,1,0:T(8,128)} collective-permute-done((f32[16,32,512]{2,1,0:T(8,128)}, f32[16,32,512]{2,1,0:T(8,128)}, u32[]{:S(2)}, u32[]{:S(2)}) %collective-permute-start.15) | collective-permute-done | bytes 1048608 | tf_op jit(solution)/shard_map/ppermute | solution.py:202
  115.7 0.3 collective-permute-done.16
  116.0 3.0 %fusion.3 = bf16[16,32,512]{2,1,0:T(8,128)(2,1)} fusion(f32[16,32,512]{2,1,0:T(8,128)} %collective-permute-done.16, f32[16,32,512]{2,1,0:T(8,128)} %collective-permute-done.15, f32[3,16,32,512]{3,2,1,0:T(8,128)S(1)} %collective-permute-done.1, f32[4,16,32,512]{3,2,1,0:T(8,128)} %get-tuple-element.35), kind=kLoop, calls=%fused_computation.4 | loop fusion | flops 1048576 | bytes 4718592 | tf_op jit(solution)/shard_map/convert_element_type | solution.py:309
  119.1 5.2 %all-to-all-start.1 = ((bf16[16,32,512]{2,1,0:T(8,128)(2,1)}), bf16[16,32,512]{2,1,0:T(8,128)(2,1)S(1)}, u32[]{:S(2)}, u32[]{:S(2)}) async-start(bf16[16,32,512]{2,1,0:T(8,128)(2,1)} %fusion.3), calls=%async_computation.1 | async-start | bytes 1048576 | tf_op jit(solution)/shard_map/all_to_all | solution.py:208
  124.3 2.4 %collective-permute-start.22 = (bf16[8,32,512]{2,1,0:T(8,128)(2,1)S(1)}, bf16[8,32,512]{2,1,0:T(8,128)(2,1)S(1)}, u32[]{:S(2)}, u32[]{:S(2)}) collective-permute-start(bf16[8,32,512]{2,1,0:T(8,128)(2,1)S(1)} %collective-permute-done.20.a2a), channel_id=1, source_target_pairs={{0,1},{1,0},{2,3},{3,2},{4,5},{5,4},{6,7},{7,6},{8,9},{9,8},{10,11... | collective-permute-start | bytes 786440 | tf_op jit(solution)/shard_map/ppermute | solution.py:205
  126.7 0.1 collective-permute-start.23
  126.8 1.1 collective-permute-done.22.b2a
  127.8 0.6 collective-permute-done.23.b2b
  128.4 0.1 copy-done.14
  128.5 0.7 copy-done.15
  129.2 7.0 %far_weight_grad.1 = bf16[1,8,34,8,128]{4,3,2,1,0:T(8,128)(2,1)} custom-call(s32[1]{0:T(128)} %bitcast.pos, s32[8,8,34]{2,1,0:T(8,128)} %rows.3, s32[8,8,34]{2,1,0:T(8,128)} %cols.3, s32[8,8]{1,0:T(8,128)} %live.3, bf16[8,32,512]{2,1,0:T(8,128)(2,1)} %copy-done.13, bf16[8,32,512]{2,1,0:T(8,128)(2,1)} %collective-permute-done.21.a2b, ...), custom_call_target="tpu_custom_call" | custom-call | flops 1100000000 | bytes 18000000 | tf_op jit(solution)/shard_map/far_weight_grad/pallas_call | solution.py:312
  136.2 0.8 copy.10
  (55 shorter events, 0.5 us)
Async XLA Ops:
  7.2 100.3 %all-gather.2.cloned.1.call-start = ((), (), s32[]{:S(2)}) async-start(), calls=%async_computation.2 | async-start | bytes 8912896 | tf_op jit(solution)/shard_map/all_gather | solution.py:210
  10.1 25.6 %all-to-all-start = ((bf16[16,64,512]{2,1,0:T(8,128)(2,1)}), bf16[16,64,512]{2,1,0:T(8,128)(2,1)S(1)}, u32[]{:S(2)}, u32[]{:S(2)}) async-start(bf16[16,64,512]{2,1,0:T(8,128)(2,1)} %feature_rows.1), calls=%async_computation | async-start | bytes 2097152 | tf_op jit(solution)/shard_map/all_to_all | solution.py:208
  34.6 3.7 %collective-permute-start = (f32[16,32,512]{2,1,0:T(8,128)}, f32[16,32,512]{2,1,0:T(8,128)S(1)}, u32[]{:S(2)}, u32[]{:S(2)}) collective-permute-start(f32[16,32,512]{2,1,0:T(8,128)} %get-tuple-element.36), channel_id=1, source_target_pairs={{0,1},{1,0},{2,3},{3,2},{4,5},{5,4},{6,7},{7,6},{8,9},{9,8},{10,11... | collective-permute-start | bytes 3145736 | tf_op jit(solution)/shard_map/ppermute | solution.py:205
  35.7 42.0 %copy-start = (f32[4,16,32,512]{3,2,1,0:T(8,128)S(1)}, f32[4,16,32,512]{3,2,1,0:T(8,128)}, u32[]{:S(2)}) copy-start(f32[4,16,32,512]{3,2,1,0:T(8,128)} %get-tuple-element.35) | copy-start | bytes 12582916
  36.6 41.5 %copy-start.1 = (bf16[16,32,512]{2,1,0:T(8,128)(2,1)}, bf16[16,32,512]{2,1,0:T(8,128)(2,1)S(1)}, u32[]{:S(2)}) copy-start(bf16[16,32,512]{2,1,0:T(8,128)(2,1)S(1)} %get-tuple-element.45.a0) | copy-start | bytes 1572868
  39.7 37.6 %collective-permute-start.1 = (f32[3,16,32,512]{3,2,1,0:T(8,128)}, f32[3,16,32,512]{3,2,1,0:T(8,128)S(1)}, u32[]{:S(2)}, u32[]{:S(2)}) collective-permute-start(f32[3,16,32,512]{3,2,1,0:T(8,128)} %get-tuple-element.39), channel_id=1, source_target_pairs={{0,1},{1,0},{2,3},{3,2},{4,5},{5,4},{6,7},{7,6},{8,9},{9,8},{10,11... | collective-permute-start | bytes 9437192 | tf_op jit(solution)/shard_map/ppermute | solution.py:205
  44.0 15.3 %collective-permute-start.4 = (bf16[16,32,512]{2,1,0:T(8,128)(2,1)S(1)}, bf16[16,32,512]{2,1,0:T(8,128)(2,1)S(1)}, u32[]{:S(2)}, u32[]{:S(2)}) collective-permute-start(bf16[16,32,512]{2,1,0:T(8,128)(2,1)S(1)} %get-tuple-element.45.a0), channel_id=1, source_target_pairs={{0,2},{1,3},{2,4},{3,5},{4,6},{5,7},{6,0},{7,1},{8,10},{9,11},{10,... | collective-permute-start | bytes 1572872 | tf_op jit(solution)/shard_map/ppermute | solution.py:202
  45.4 14.0 %collective-permute-start.5 = (bf16[16,32,512]{2,1,0:T(8,128)(2,1)S(1)}, bf16[16,32,512]{2,1,0:T(8,128)(2,1)S(1)}, u32[]{:S(2)}, u32[]{:S(2)}) collective-permute-start(bf16[16,32,512]{2,1,0:T(8,128)(2,1)S(1)} %get-tuple-element.45.a0), channel_id=1, source_target_pairs={{0,6},{1,7},{2,0},{3,1},{4,2},{5,3},{6,4},{7,5},{8,14},{9,15},{10,... | collective-permute-start | bytes 1572872 | tf_op jit(solution)/shard_map/ppermute | solution.py:202
  47.0 29.8 %collective-permute-start.2 = (f32[8,32,512]{2,1,0:T(8,128)S(1)}, f32[8,32,512]{2,1,0:T(8,128)S(1)}, u32[]{:S(2)}, u32[]{:S(2)}) collective-permute-start(f32[8,32,512]{2,1,0:T(8,128)S(1)} %get-tuple-element.40), channel_id=1, source_target_pairs={{0,2},{1,3},{2,4},{3,5},{4,6},{5,7},{6,0},{7,1},{8,10},{9,11},{10,... | collective-permute-start | bytes 1572872 | tf_op jit(solution)/shard_map/ppermute | solution.py:202
  47.0 30.2 %collective-permute-start.3 = (f32[8,32,512]{2,1,0:T(8,128)S(1)}, f32[8,32,512]{2,1,0:T(8,128)S(1)}, u32[]{:S(2)}, u32[]{:S(2)}) collective-permute-start(f32[8,32,512]{2,1,0:T(8,128)S(1)} %get-tuple-element.41), channel_id=1, source_target_pairs={{0,6},{1,7},{2,0},{3,1},{4,2},{5,3},{6,4},{7,5},{8,14},{9,15},{10,... | collective-permute-start | bytes 1572872 | tf_op jit(solution)/shard_map/ppermute | solution.py:202
  59.3 19.1 %copy-start.2 = (bf16[16,32,512]{2,1,0:T(8,128)(2,1)}, bf16[16,32,512]{2,1,0:T(8,128)(2,1)S(1)}, u32[]{:S(2)}) copy-start(bf16[16,32,512]{2,1,0:T(8,128)(2,1)S(1)} %collective-permute-done.4.am) | copy-start | bytes 1572868
  59.3 16.8 %collective-permute-start.6 = (bf16[8,32,512]{2,1,0:T(8,128)(2,1)S(1)}, bf16[8,32,512]{2,1,0:T(8,128)(2,1)S(1)}, u32[]{:S(2)}, u32[]{:S(2)}) collective-permute-start(bf16[8,32,512]{2,1,0:T(8,128)(2,1)S(1)} %slice.87), channel_id=1, source_target_pairs={{0,2},{1,3},{2,4},{3,5},{4,6},{5,7},{6,0},{7,1},{8,10},{9,11},{10,... | collective-permute-start | bytes 786440 | tf_op jit(solution)/shard_map/ppermute | solution.py:202
  59.4 24.1 %copy-start.3 = (bf16[16,32,512]{2,1,0:T(8,128)(2,1)}, bf16[16,32,512]{2,1,0:T(8,128)(2,1)S(1)}, u32[]{:S(2)}) copy-start(bf16[16,32,512]{2,1,0:T(8,128)(2,1)S(1)} %collective-permute-done.5.ap) | copy-start | bytes 1572868
  59.4 17.3 %collective-permute-start.7 = (bf16[8,32,512]{2,1,0:T(8,128)(2,1)S(1)}, bf16[8,32,512]{2,1,0:T(8,128)(2,1)S(1)}, u32[]{:S(2)}, u32[]{:S(2)}) collective-permute-start(bf16[8,32,512]{2,1,0:T(8,128)(2,1)S(1)} %slice.88), channel_id=1, source_target_pairs={{0,6},{1,7},{2,0},{3,1},{4,2},{5,3},{6,4},{7,5},{8,14},{9,15},{10,... | collective-permute-start | bytes 786440 | tf_op jit(solution)/shard_map/ppermute | solution.py:202
  76.1 7.4 %copy-start.9 = (bf16[8,32,512]{2,1,0:T(8,128)(2,1)}, bf16[8,32,512]{2,1,0:T(8,128)(2,1)S(1)}, u32[]{:S(2)}) copy-start(bf16[8,32,512]{2,1,0:T(8,128)(2,1)S(1)} %collective-permute-done.6.a2a) | copy-start | bytes 786436
  76.1 2.2 %collective-permute-start.8 = (bf16[16,32,512]{2,1,0:T(8,128)(2,1)S(1)}, bf16[16,32,512]{2,1,0:T(8,128)(2,1)S(1)}, u32[]{:S(2)}, u32[]{:S(2)}) collective-permute-start(bf16[16,32,512]{2,1,0:T(8,128)(2,1)S(1)} %get-tuple-element.45.a0), channel_id=1, source_target_pairs={{0,1},{1,0},{2,3},{3,2},{4,5},{5,4},{6,7},{7,6},{8,9},{9,8},{10,11... | collective-permute-start | bytes 1572872 | tf_op jit(solution)/shard_map/ppermute | solution.py:205
  76.7 6.9 %copy-start.10 = (bf16[8,32,512]{2,1,0:T(8,128)(2,1)}, bf16[8,32,512]{2,1,0:T(8,128)(2,1)S(1)}, u32[]{:S(2)}) copy-start(bf16[8,32,512]{2,1,0:T(8,128)(2,1)S(1)} %collective-permute-done.7.a2b) | copy-start | bytes 786436
  76.7 7.6 %collective-permute-start.10 = (bf16[16,32,512]{2,1,0:T(8,128)(2,1)S(1)}, bf16[16,32,512]{2,1,0:T(8,128)(2,1)S(1)}, u32[]{:S(2)}, u32[]{:S(2)}) collective-permute-start(bf16[16,32,512]{2,1,0:T(8,128)(2,1)S(1)} %collective-permute-done.5.ap), channel_id=1, source_target_pairs={{0,1},{1,0},{2,3},{3,2},{4,5},{5,4},{6,7},{7,6},{8,9},{9,8},{10,11... | collective-permute-start | bytes 1572872 | tf_op jit(solution)/shard_map/ppermute | solution.py:205
  76.8 7.5 %collective-permute-start.9 = (bf16[16,32,512]{2,1,0:T(8,128)(2,1)S(1)}, bf16[16,32,512]{2,1,0:T(8,128)(2,1)S(1)}, u32[]{:S(2)}, u32[]{:S(2)}) collective-permute-start(bf16[16,32,512]{2,1,0:T(8,128)(2,1)S(1)} %collective-permute-done.4.am), channel_id=1, source_target_pairs={{0,1},{1,0},{2,3},{3,2},{4,5},{5,4},{6,7},{7,6},{8,9},{9,8},{10,11... | collective-permute-start | bytes 1572872 | tf_op jit(solution)/shard_map/ppermute | solution.py:205
  77.2 2.9 %collective-permute-start.11 = (bf16[8,32,512]{2,1,0:T(8,128)(2,1)S(1)}, bf16[8,32,512]{2,1,0:T(8,128)(2,1)S(1)}, u32[]{:S(2)}, u32[]{:S(2)}) collective-permute-start(bf16[8,32,512]{2,1,0:T(8,128)(2,1)S(1)} %collective-permute-done.6.a2a), channel_id=1, source_target_pairs={{0,1},{1,0},{2,3},{3,2},{4,5},{5,4},{6,7},{7,6},{8,9},{9,8},{10,11... | collective-permute-start | bytes 786440 | tf_op jit(solution)/shard_map/ppermute | solution.py:205
  77.3 6.2 %collective-permute-start.12 = (bf16[8,32,512]{2,1,0:T(8,128)(2,1)S(1)}, bf16[8,32,512]{2,1,0:T(8,128)(2,1)S(1)}, u32[]{:S(2)}, u32[]{:S(2)}) collective-permute-start(bf16[8,32,512]{2,1,0:T(8,128)(2,1)S(1)} %collective-permute-done.7.a2b), channel_id=1, source_target_pairs={{0,1},{1,0},{2,3},{3,2},{4,5},{5,4},{6,7},{7,6},{8,9},{9,8},{10,11... | collective-permute-start | bytes 786440 | tf_op jit(solution)/shard_map/ppermute | solution.py:205
  78.4 6.0 %copy-start.5 = (bf16[16,32,512]{2,1,0:T(8,128)(2,1)}, bf16[16,32,512]{2,1,0:T(8,128)(2,1)S(1)}, u32[]{:S(2)}) copy-start(bf16[16,32,512]{2,1,0:T(8,128)(2,1)S(1)} %collective-permute-done.8.b0) | copy-start | bytes 1572868
  78.4 22.4 %collective-permute-start.13 = (bf16[16,32,512]{2,1,0:T(8,128)(2,1)}, bf16[16,32,512]{2,1,0:T(8,128)(2,1)S(1)}, u32[]{:S(2)}, u32[]{:S(2)}) collective-permute-start(bf16[16,32,512]{2,1,0:T(8,128)(2,1)} %get-tuple-element.56.a0), channel_id=1, source_target_pairs={{0,2},{1,3},{2,4},{3,5},{4,6},{5,7},{6,0},{7,1},{8,10},{9,11},{10,... | collective-permute-start | bytes 1572872 | tf_op jit(solution)/shard_map/ppermute | solution.py:202
  80.1 5.2 %copy-start.11 = (bf16[8,32,512]{2,1,0:T(8,128)(2,1)}, bf16[8,32,512]{2,1,0:T(8,128)(2,1)S(1)}, u32[]{:S(2)}) copy-start(bf16[8,32,512]{2,1,0:T(8,128)(2,1)S(1)} %collective-permute-done.11.b2a) | copy-start | bytes 786436
  80.1 20.7 %collective-permute-start.14 = (bf16[16,32,512]{2,1,0:T(8,128)(2,1)}, bf16[16,32,512]{2,1,0:T(8,128)(2,1)}, u32[]{:S(2)}, u32[]{:S(2)}) collective-permute-start(bf16[16,32,512]{2,1,0:T(8,128)(2,1)} %get-tuple-element.56.a0), channel_id=1, source_target_pairs={{0,6},{1,7},{2,0},{3,1},{4,2},{5,3},{6,4},{7,5},{8,14},{9,15},{10,... | collective-permute-start | bytes 1572872 | tf_op jit(solution)/shard_map/ppermute | solution.py:202
  83.6 4.4 %copy-start.12 = (bf16[8,32,512]{2,1,0:T(8,128)(2,1)}, bf16[8,32,512]{2,1,0:T(8,128)(2,1)S(1)}, u32[]{:S(2)}) copy-start(bf16[8,32,512]{2,1,0:T(8,128)(2,1)S(1)} %collective-permute-done.12.b2b) | copy-start | bytes 786436
  83.6 20.4 %collective-permute-start.17 = (bf16[16,32,512]{2,1,0:T(8,128)(2,1)}, bf16[16,32,512]{2,1,0:T(8,128)(2,1)}, u32[]{:S(2)}, u32[]{:S(2)}) collective-permute-start(bf16[16,32,512]{2,1,0:T(8,128)(2,1)} %get-tuple-element.56.a0), channel_id=1, source_target_pairs={{0,1},{1,0},{2,3},{3,2},{4,5},{5,4},{6,7},{7,6},{8,9},{9,8},{10,11... | collective-permute-start | bytes 1572872 | tf_op jit(solution)/shard_map/ppermute | solution.py:205
  84.3 0.8 copy-start.6
  84.3 1.0 copy-start.7
  85.3 30.4 %collective-permute-start.15 = (f32[16,32,512]{2,1,0:T(8,128)}, f32[16,32,512]{2,1,0:T(8,128)}, u32[]{:S(2)}, u32[]{:S(2)}) collective-permute-start(f32[16,32,512]{2,1,0:T(8,128)} %get-tuple-element.58), channel_id=1, source_target_pairs={{0,2},{1,3},{2,4},{3,5},{4,6},{5,7},{6,0},{7,1},{8,10},{9,11},{10,... | collective-permute-start | bytes 3145736 | tf_op jit(solution)/shard_map/ppermute | solution.py:202
  85.3 30.7 %collective-permute-start.16 = (f32[16,32,512]{2,1,0:T(8,128)}, f32[16,32,512]{2,1,0:T(8,128)}, u32[]{:S(2)}, u32[]{:S(2)}) collective-permute-start(f32[16,32,512]{2,1,0:T(8,128)} %get-tuple-element.59), channel_id=1, source_target_pairs={{0,6},{1,7},{2,0},{3,1},{4,2},{5,3},{6,4},{7,5},{8,14},{9,15},{10,... | collective-permute-start | bytes 3145736 | tf_op jit(solution)/shard_map/ppermute | solution.py:202
  100.8 0.8 copy-start.4
  100.8 3.2 %collective-permute-start.18 = (bf16[16,32,512]{2,1,0:T(8,128)(2,1)S(1)}, bf16[16,32,512]{2,1,0:T(8,128)(2,1)S(1)}, u32[]{:S(2)}, u32[]{:S(2)}) collective-permute-start(bf16[16,32,512]{2,1,0:T(8,128)(2,1)S(1)} %collective-permute-done.13.am), channel_id=1, source_target_pairs={{0,1},{1,0},{2,3},{3,2},{4,5},{5,4},{6,7},{7,6},{8,9},{9,8},{10,11... | collective-permute-start | bytes 1572872 | tf_op jit(solution)/shard_map/ppermute | solution.py:205
  101.4 6.0 %collective-permute-start.19 = (bf16[16,32,512]{2,1,0:T(8,128)(2,1)}, bf16[16,32,512]{2,1,0:T(8,128)(2,1)}, u32[]{:S(2)}, u32[]{:S(2)}) collective-permute-start(bf16[16,32,512]{2,1,0:T(8,128)(2,1)} %collective-permute-done.14.ap), channel_id=1, source_target_pairs={{0,1},{1,0},{2,3},{3,2},{4,5},{5,4},{6,7},{7,6},{8,9},{9,8},{10,11... | collective-permute-start | bytes 1572872 | tf_op jit(solution)/shard_map/ppermute | solution.py:205
  104.0 20.3 %collective-permute-start.20 = (bf16[8,32,512]{2,1,0:T(8,128)(2,1)}, bf16[8,32,512]{2,1,0:T(8,128)(2,1)S(1)}, u32[]{:S(2)}, u32[]{:S(2)}) collective-permute-start(bf16[8,32,512]{2,1,0:T(8,128)(2,1)} %slice.78), channel_id=1, source_target_pairs={{0,2},{1,3},{2,4},{3,5},{4,6},{5,7},{6,0},{7,1},{8,10},{9,11},{10,... | collective-permute-start | bytes 786440 | tf_op jit(solution)/shard_map/ppermute | solution.py:202
  104.0 0.8 copy-start.8
  104.8 21.9 %collective-permute-start.21 = (bf16[8,32,512]{2,1,0:T(8,128)(2,1)}, bf16[8,32,512]{2,1,0:T(8,128)(2,1)}, u32[]{:S(2)}, u32[]{:S(2)}) collective-permute-start(bf16[8,32,512]{2,1,0:T(8,128)(2,1)} %slice.79), channel_id=1, source_target_pairs={{0,6},{1,7},{2,0},{3,1},{4,2},{5,3},{6,4},{7,5},{8,14},{9,15},{10,... | collective-permute-start | bytes 786440 | tf_op jit(solution)/shard_map/ppermute | solution.py:202
  119.1 17.1 %all-to-all-start.1 = ((bf16[16,32,512]{2,1,0:T(8,128)(2,1)}), bf16[16,32,512]{2,1,0:T(8,128)(2,1)S(1)}, u32[]{:S(2)}, u32[]{:S(2)}) async-start(bf16[16,32,512]{2,1,0:T(8,128)(2,1)} %fusion.3), calls=%async_computation.1 | async-start | bytes 1048576 | tf_op jit(solution)/shard_map/all_to_all | solution.py:208
  124.3 4.1 %copy-start.13 = (bf16[8,32,512]{2,1,0:T(8,128)(2,1)}, bf16[8,32,512]{2,1,0:T(8,128)(2,1)S(1)}, u32[]{:S(2)}) copy-start(bf16[8,32,512]{2,1,0:T(8,128)(2,1)S(1)} %collective-permute-done.20.a2a) | copy-start | bytes 786436
  124.3 3.5 %collective-permute-start.22 = (bf16[8,32,512]{2,1,0:T(8,128)(2,1)S(1)}, bf16[8,32,512]{2,1,0:T(8,128)(2,1)S(1)}, u32[]{:S(2)}, u32[]{:S(2)}) collective-permute-start(bf16[8,32,512]{2,1,0:T(8,128)(2,1)S(1)} %collective-permute-done.20.a2a), channel_id=1, source_target_pairs={{0,1},{1,0},{2,3},{3,2},{4,5},{5,4},{6,7},{7,6},{8,9},{9,8},{10,11... | collective-permute-start | bytes 786440 | tf_op jit(solution)/shard_map/ppermute | solution.py:205
  126.7 1.7 %collective-permute-start.23 = (bf16[8,32,512]{2,1,0:T(8,128)(2,1)}, bf16[8,32,512]{2,1,0:T(8,128)(2,1)S(1)}, u32[]{:S(2)}, u32[]{:S(2)}) collective-permute-start(bf16[8,32,512]{2,1,0:T(8,128)(2,1)} %collective-permute-done.21.a2b), channel_id=1, source_target_pairs={{0,1},{1,0},{2,3},{3,2},{4,5},{5,4},{6,7},{7,6},{8,9},{9,8},{10,11... | collective-permute-start | bytes 786440 | tf_op jit(solution)/shard_map/ppermute | solution.py:205
  127.8 0.7 copy-start.14
  128.5 0.7 copy-start.15
Sparse Core Ops, SparseCore 0:
  10.1 78.8 all-gather.1

commit v7 on v6

--- a/solution.py
+++ b/solution.py
@@ -43,7 +43,7 @@
         o_ref[part, pl.ds(32, 32)] = t[:, part].reshape(32, 512).astype(BF16)
 
 
-def partial_kernel(pos, rows, cols, live, cot, blk, keep, across, rest, dense, *scratch):
+def partial_kernel(pos, rows, cols, live, cot, blk, keep, across, rest, *scratch):
     lhs, keep_v, across_v, rest_v, cot_sem, blk_sem, out_sem = scratch[:7]
     blk_v, panels = scratch[7:15], scratch[15:23]
     owner = pos[0]
@@ -83,13 +83,23 @@
             rest_v[2, at] = res[224:256, lanes]
         part = pl.ds(j * 2, 2)
         step_copies = [
-            pltpu.make_async_copy(panels[j], dense.at[j], out_sem.at[j, 0]),
-            pltpu.make_async_copy(keep_v.at[:, part], keep.at[:, part], out_sem.at[j, 1]),
-            pltpu.make_async_copy(across_v.at[part], across.at[part], out_sem.at[j, 2]),
-            pltpu.make_async_copy(rest_v.at[:, part], rest.at[:, part], out_sem.at[j, 3]),
+            pltpu.make_async_copy(keep_v.at[:, part], keep.at[:, part], out_sem.at[j, 0]),
+            pltpu.make_async_copy(across_v.at[part], across.at[part], out_sem.at[j, 1]),
+            pltpu.make_async_copy(rest_v.at[:, part], rest.at[:, part], out_sem.at[j, 2]),
         ]
         start_all(step_copies)
         out_copies += step_copies
+    wait_all(out_copies)
+
+
+def dense_kernel(pos, rows, cols, live, blk, dense, blk_v, panels, blk_sem, out_sem):
+    blk_copies = [pltpu.make_async_copy(blk.at[0, j], blk_v.at[j], blk_sem.at[j]) for j in range(8)]
+    out_copies = [pltpu.make_async_copy(panels.at[j], dense.at[j], out_sem.at[j]) for j in range(8)]
+    start_all(blk_copies)
+    for j in range(8):
+        blk_copies[j].wait()
+        build_panel(panels.at[j], blk_v.at[j], rows, cols, live, pos[0], j)
+        out_copies[j].start()
     wait_all(out_copies)
 
 
@@ -221,15 +231,14 @@
 
     scalars = [pl.BlockSpec(memory_space=pltpu.SMEM)] * 4
     anywhere = pl.BlockSpec(memory_space=pl.ANY)
-    keep, across, rest, dense = pl.pallas_call(
+    keep, across, rest = pl.pallas_call(
         partial_kernel,
         in_specs=scalars + [anywhere] * 2,
-        out_specs=[anywhere] * 4,
+        out_specs=[anywhere] * 3,
         out_shape=[
             jax.ShapeDtypeStruct((4, 16, 32, 512), F32),
             jax.ShapeDtypeStruct((16, 32, 512), F32),
             jax.ShapeDtypeStruct((3, 16, 32, 512), F32),
-            jax.ShapeDtypeStruct((8, 1024, 1024), BF16),
         ],
         scratch_shapes=[
             pltpu.VMEM((256, 1024), BF16),
@@ -238,7 +247,7 @@
             pltpu.VMEM((3, 16, 32, 512), F32),
             pltpu.SemaphoreType.DMA((8,)),
             pltpu.SemaphoreType.DMA((8,)),
-            pltpu.SemaphoreType.DMA((8, 4)),
+            pltpu.SemaphoreType.DMA((8, 3)),
         ]
         + [pltpu.VMEM((34, 128, 128), BF16)] * 8
         + [pltpu.VMEM((1024, 1024), BF16)] * 8,
@@ -253,7 +262,23 @@
     from_a, from_b = along_y(q2a, 1), along_y(q2b, -1)
     xm, xp = along_y(tokens, 1), along_y(tokens, -1)
     rest = other_core(rest)
-    x2a, x2b = along_y(xm[:8], 1), along_y(xp[8:], -1)
+    xma, xpb, blk_later = barrier((xm[:8], xp[8:], blocks))
+    x2a, x2b = along_y(xma, 1), along_y(xpb, -1)
+    dense = pl.pallas_call(
+        dense_kernel,
+        in_specs=scalars + [anywhere],
+        out_specs=anywhere,
+        out_shape=jax.ShapeDtypeStruct((8, 1024, 1024), BF16),
+        scratch_shapes=[
+            pltpu.VMEM((8, 34, 128, 128), BF16),
+            pltpu.VMEM((8, 1024, 1024), BF16),
+            pltpu.SemaphoreType.DMA((8,)),
+            pltpu.SemaphoreType.DMA((8,)),
+        ],
+        compiler_params=params,
+        cost_estimate=cost(0, 30_000_000),
+        name="dense_panels",
+    )(*tables, blk_later)
     x2a, x2b, class_rows = barrier((x2a, x2b, class_rows))
     own = (tokens, xm, xp, x2a, x2b)
     x_pieces = own + tuple(other_core(piece) for piece in own)

time: 145 us -> 149 us (1.028)
  waiting for transfers between devices: 30.2 us -> 18.4 us
  Pallas kernels: 44.5 us -> 53.8 us
  other arithmetic: 6.57 us -> 10.3 us
  local copies, waits for them, and re-layouts: 6.8 us -> 9.77 us
    ppermute x12, waiting for transfers between devices: 25.6 us -> 14.4 us  [along_y(): return lax.ppermute(x, 'mp', [(i, (i + 2 * step) % 8) for i in range(8)])]
    pallas_call x0 -> x1, Pallas kernels: none -> 10.3 us  [on_device(): pl.pallas_call(dense_kernel, in_specs=scalars + [anywhere], out_specs=any...]
    add x1, other arithmetic: 0.37 us -> 1.95 us  [on_device(): keep[3, 8:] + rest[2, 8:] + from_b]
    unnamed x33 -> x25, local copies, waits for them, and re-layouts: 3.45 us -> 4.92 us
  transfers between devices with their start and end apart: 27 -> 27, of which waited for: 8 -> 7; matrix products, arithmetic and copies ran while one was open for 7% -> 10% of each run, Pallas kernels for 31% -> 36%
where the time goes in v7:
time: 149 us; the launch traced here: 148 us
  Pallas kernels  53.8 us (36%)
  starting transfers between devices  41.7 us (28%)
  waiting for transfers between devices  18.4 us (12%)
  between operations  14.2 us (10%)
  other arithmetic  10.3 us (7%)
  local copies, waits for them, and re-layouts  9.77 us (7%)
    ppermute x12, starting transfers between devices, along_y(): return lax.ppermute(x, 'mp', [(i, (i + 2 * step) % 8) for i in range(8)])  16.4 us
    pallas_call x1, Pallas kernels, on_device(): pl.pallas_call(partial_kernel, in_specs=scalars + [anywhere] * 2, out_spe...  15 us
    ppermute x12, waiting for transfers between devices, along_y(): return lax.ppermute(x, 'mp', [(i, (i + 2 * step) % 8) for i in range(8)])  14.4 us
    all_to_all x2, starting transfers between devices, exchange(): return lax.all_to_all(x, 'seq', split_axis=0, concat_axis=0, tiled=True)  13.5 us
    pallas_call x1, Pallas kernels, on_device(): pl.pallas_call(out_kernel, in_specs=scalars[:1] + [anywhere] * 11, out_sh...  12.7 us
    ppermute x12, starting transfers between devices, other_core(): return lax.ppermute(x, 'mp', [(i, i ^ 1) for i in range(8)])  11.8 us
    pallas_call x1, Pallas kernels, on_device(): pl.pallas_call(dense_kernel, in_specs=scalars + [anywhere], out_specs=any...  10.3 us
    pallas_call x1, Pallas kernels, on_device(): pl.pallas_call(functools.partial(far_grad_kernel, 1.0 / math.sqrt(4096)),...  6.96 us
  transfers between devices with their start and end apart: 27, of which 7 were waited for; matrix products, arithmetic and copies ran while one was open for 10% of the time, Pallas kernels for 36%

profile of v7, /device:TPU:1, one launch (start us, length us, event | category | flops | bytes accessed | tf_op | source)
XLA Modules:
  0.0 148.2 jit_solution(3243993299611957505)
XLA Ops:
  7.2 0.7 all-gather.2.cloned.1.call-update
  7.9 2.3 %feature_rows.1 = bf16[16,64,512]{2,1,0:T(8,128)(2,1)} custom-call(bf16[16,32,512]{2,1,0:T(8,128)(2,1)} %x_ref.1), custom_call_target="tpu_custom_call" | custom-call | tf_op jit(solution)/shard_map/feature_rows/pallas_call | solution.py:222
  10.1 8.4 %all-to-all-start = ((bf16[16,64,512]{2,1,0:T(8,128)(2,1)}), bf16[16,64,512]{2,1,0:T(8,128)(2,1)S(1)}, u32[]{:S(2)}, u32[]{:S(2)}) async-start(bf16[16,64,512]{2,1,0:T(8,128)(2,1)} %feature_rows.1), calls=%async_computation | async-start | bytes 2097152 | tf_op jit(solution)/shard_map/all_to_all | solution.py:218
  18.6 15.0 %partial_context_grad.1 = (f32[4,16,32,512]{3,2,1,0:T(8,128)}, f32[16,32,512]{2,1,0:T(8,128)}, f32[3,16,32,512]{3,2,1,0:T(8,128)}) custom-call(s32[1]{0:T(128)} %bitcast.pos, s32[8,8,34]{2,1,0:T(8,128)} %rows.5, s32[8,8,34]{2,1,0:T(8,128)} %cols.5, s32[8,8]{1,0:T(8,128)} %live.5, bf16[4,2,32,1024]{3,2,1,0:T(8,128)(2,1)} %bitcast.29, ...), custom_call_target="tpu_custom_call" | custom-call | flops 4300000256 | bytes 45000000 | tf_op jit(solution)/shard_map/partial_context_grad/pallas_call | solution.py:234
  33.6 1.2 collective-permute-start
  34.8 0.3 all-to-all-done
  35.0 0.9 fusion.10
  35.9 1.3 collective-permute-done
  37.3 2.4 %slice_add_fusion.5 = (f32[8,32,512]{2,1,0:T(8,128)}, f32[8,32,512]{2,1,0:T(8,128)}) fusion(f32[16,32,512]{2,1,0:T(8,128)S(1)} %collective-permute-done, f32[4,16,32,512]{3,2,1,0:T(8,128)} %get-tuple-element.37), kind=kLoop, calls=%fused_computation.17 | loop fusion | flops 262144 | bytes 3145728 | tf_op jit(solution)/shard_map/add | solution.py:260
  39.7 4.7 %collective-permute-start.1 = (f32[3,16,32,512]{3,2,1,0:T(8,128)}, f32[3,16,32,512]{3,2,1,0:T(8,128)S(1)}, u32[]{:S(2)}, u32[]{:S(2)}) collective-permute-start(f32[3,16,32,512]{3,2,1,0:T(8,128)} %get-tuple-element.41), channel_id=1, source_target_pairs={{0,1},{1,0},{2,3},{3,2},{4,5},{5,4},{6,7},{7,6},{8,9},{9,8},{10,11... | collective-permute-start | bytes 9437192 | tf_op jit(solution)/shard_map/ppermute | solution.py:215
  44.4 1.4 collective-permute-start.4
  45.7 1.6 %collective-permute-start.5 = (bf16[16,32,512]{2,1,0:T(8,128)(2,1)S(1)}, bf16[16,32,512]{2,1,0:T(8,128)(2,1)S(1)}, u32[]{:S(2)}, u32[]{:S(2)}) collective-permute-start(bf16[16,32,512]{2,1,0:T(8,128)(2,1)S(1)} %get-tuple-element.49.a0), channel_id=1, source_target_pairs={{0,6},{1,7},{2,0},{3,1},{4,2},{5,3},{6,4},{7,5},{8,14},{9,15},{10,... | collective-permute-start | bytes 1572872 | tf_op jit(solution)/shard_map/ppermute | solution.py:212
  47.3 2.7 %collective-permute-start.3 = (f32[8,32,512]{2,1,0:T(8,128)}, f32[8,32,512]{2,1,0:T(8,128)}, u32[]{:S(2)}, u32[]{:S(2)}) collective-permute-start(f32[8,32,512]{2,1,0:T(8,128)} %get-tuple-element.43), channel_id=1, source_target_pairs={{0,6},{1,7},{2,0},{3,1},{4,2},{5,3},{6,4},{7,5},{8,14},{9,15},{10,... | collective-permute-start | bytes 1572872 | tf_op jit(solution)/shard_map/ppermute | solution.py:212
  50.0 9.7 %collective-permute-done.4.am = bf16[16,32,512]{2,1,0:T(8,128)(2,1)S(1)} collective-permute-done((bf16[16,32,512]{2,1,0:T(8,128)(2,1)S(1)}, bf16[16,32,512]{2,1,0:T(8,128)(2,1)S(1)}, u32[]{:S(2)}, u32[]{:S(2)}) %collective-permute-start.4) | collective-permute-done | bytes 524320 | tf_op jit(solution)/shard_map/ppermute | solution.py:212
  59.7 0.8 slice.87
  60.6 0.8 slice.88
  61.5 2.7 %collective-permute-start.7 = (bf16[8,32,512]{2,1,0:T(8,128)(2,1)}, bf16[8,32,512]{2,1,0:T(8,128)(2,1)}, u32[]{:S(2)}, u32[]{:S(2)}) collective-permute-start(bf16[8,32,512]{2,1,0:T(8,128)(2,1)} %slice.88), channel_id=1, source_target_pairs={{0,6},{1,7},{2,0},{3,1},{4,2},{5,3},{6,4},{7,5},{8,14},{9,15},{10,... | collective-permute-start | bytes 786440 | tf_op jit(solution)/shard_map/ppermute | solution.py:212
  64.2 10.3 %dense_panels.1.dense = bf16[8,1024,1024]{2,1,0:T(8,128)(2,1)} custom-call(s32[1]{0:T(128)} %bitcast.pos, s32[8,8,34]{2,1,0:T(8,128)} %rows.5, s32[8,8,34]{2,1,0:T(8,128)} %cols.5, s32[8,8]{1,0:T(8,128)} %live.5, bf16[1,8,34,128,128]{4,3,2,1,0:T(8,128)(2,1)} %blk.2), custom_call_target="tpu_custom_call" | custom-call | bytes 30000000 | tf_op jit(solution)/shard_map/dense_panels/pallas_call | solution.py:267
  74.5 2.1 %collective-permute-done.6.a2a = bf16[8,32,512]{2,1,0:T(8,128)(2,1)S(1)} collective-permute-done((bf16[8,32,512]{2,1,0:T(8,128)(2,1)}, bf16[8,32,512]{2,1,0:T(8,128)(2,1)S(1)}, u32[]{:S(2)}, u32[]{:S(2)}) %collective-permute-start.6) | collective-permute-done | bytes 262176 | tf_op jit(solution)/shard_map/ppermute | solution.py:212
  76.6 0.5 collective-permute-start.8
  77.2 0.4 collective-permute-start.9
  77.7 0.4 collective-permute-start.12
  78.1 2.0 %fusion.5 = (f32[8,32,512]{2,1,0:T(8,128)S(1)}, f32[8,32,512]{2,1,0:T(8,128)S(1)}) fusion(f32[8,32,512]{2,1,0:T(8,128)} %collective-permute-done.3, f32[3,16,32,512]{3,2,1,0:T(8,128)S(1)} %collective-permute-done.1, f32[4,16,32,512]{3,2,1,0:T(8,128)} %get-tuple-element.37, f32[8,32,512]{2,1,0:T(8,128)} %collective-permute-done.2), kind=kLoop, calls=%fused_computation.9 | loop fusion | flops 524288 | bytes 4194304 | tf_op jit(solution)/shard_map/add | solution.py:289
  80.1 1.4 fusion.6
  81.5 0.8 copy-done.4
  82.3 0.9 collective-permute-start.13
  83.2 0.7 copy-done.7
  84.0 1.7 %collective-permute-start.14 = (bf16[16,32,512]{2,1,0:T(8,128)(2,1)}, bf16[16,32,512]{2,1,0:T(8,128)(2,1)}, u32[]{:S(2)}, u32[]{:S(2)}) collective-permute-start(bf16[16,32,512]{2,1,0:T(8,128)(2,1)} %get-tuple-element.60.a0), channel_id=1, source_target_pairs={{0,6},{1,7},{2,0},{3,1},{4,2},{5,3},{6,4},{7,5},{8,14},{9,15},{10,... | collective-permute-start | bytes 1572872 | tf_op jit(solution)/shard_map/ppermute | solution.py:212
  85.7 1.5 pad_maximum_fusion
  87.2 0.7 copy-done.8
  87.9 0.6 collective-permute-start.17
  88.5 2.6 %collective-permute-start.16 = (f32[16,32,512]{2,1,0:T(8,128)}, f32[16,32,512]{2,1,0:T(8,128)}, u32[]{:S(2)}, u32[]{:S(2)}) collective-permute-start(f32[16,32,512]{2,1,0:T(8,128)} %get-tuple-element.63), channel_id=1, source_target_pairs={{0,6},{1,7},{2,0},{3,1},{4,2},{5,3},{6,4},{7,5},{8,14},{9,15},{10,... | collective-permute-start | bytes 3145736 | tf_op jit(solution)/shard_map/ppermute | solution.py:212
  91.2 12.7 %outputs.1 = bf16[256,1024]{1,0:T(8,128)(2,1)} custom-call(s32[1]{0:T(128)} %bitcast.pos, bf16[16,32,512]{2,1,0:T(8,128)(2,1)} %copy-done, bf16[16,32,512]{2,1,0:T(8,128)(2,1)} %copy-done.1, bf16[16,32,512]{2,1,0:T(8,128)(2,1)} %copy-done.2, bf16[8,32,512]{2,1,0:T(8,128)(2,1)} %copy-done.6, bf16[8,32,512]{2,1,0:T(8,128)(2,1)} %collective-permute-done.7.a2b, ...), custom_call_target="tpu_custom_call" | custom-call | flops 4300000256 | bytes 30000000 | tf_op jit(solution)/shard_map/outputs/pallas_call | solution.py:293
  103.9 0.7 collective-permute-start.18
  104.7 0.7 slice.78
  105.5 1.7 %slice.79 = bf16[8,32,512]{2,1,0:T(8,128)(2,1)} slice(bf16[16,32,512]{2,1,0:T(8,128)(2,1)} %collective-permute-done.14.ap), slice={[8:16], [0:32], [0:512]} | slice | bytes 524288 | tf_op jit(solution)/shard_map/slice | solution.py:310
  107.2 0.8 copy-done.5
  108.0 2.7 %collective-permute-start.21 = (bf16[8,32,512]{2,1,0:T(8,128)(2,1)}, bf16[8,32,512]{2,1,0:T(8,128)(2,1)}, u32[]{:S(2)}, u32[]{:S(2)}) collective-permute-start(bf16[8,32,512]{2,1,0:T(8,128)(2,1)} %slice.79), channel_id=1, source_target_pairs={{0,6},{1,7},{2,0},{3,1},{4,2},{5,3},{6,4},{7,5},{8,14},{9,15},{10,... | collective-permute-start | bytes 786440 | tf_op jit(solution)/shard_map/ppermute | solution.py:212
  110.7 6.6 %near_weight_grad.1.near = f32[64,8,1024]{2,1,0:T(8,128)} custom-call(s32[1]{0:T(128)} %bitcast.pos, bf16[16,32,512]{2,1,0:T(8,128)(2,1)} %get-tuple-element.60.a0, bf16[16,32,512]{2,1,0:T(8,128)(2,1)} %copy-done.3, bf16[16,32,512]{2,1,0:T(8,128)(2,1)} %collective-permute-done.14.ap, bf16[16,32,512]{2,1,0:T(8,128)(2,1)} %collective-permute-done.17.b0, ...), custom_call_target="tpu_custom_call" | custom-call | flops 3200000000 | bytes 25000000 | tf_op jit(solution)/shard_map/near_weight_grad/pallas_call | solution.py:315
  117.2 2.6 %collective-permute-done.15 = f32[16,32,512]{2,1,0:T(8,128)} collective-permute-done((f32[16,32,512]{2,1,0:T(8,128)}, f32[16,32,512]{2,1,0:T(8,128)}, u32[]{:S(2)}, u32[]{:S(2)}) %collective-permute-start.15) | collective-permute-done | bytes 1048608 | tf_op jit(solution)/shard_map/ppermute | solution.py:212
  119.8 3.0 %fusion.3 = bf16[16,32,512]{2,1,0:T(8,128)(2,1)} fusion(f32[16,32,512]{2,1,0:T(8,128)} %collective-permute-done.16, f32[16,32,512]{2,1,0:T(8,128)} %collective-permute-done.15, f32[3,16,32,512]{3,2,1,0:T(8,128)S(1)} %collective-permute-done.1, f32[4,16,32,512]{3,2,1,0:T(8,128)} %get-tuple-element.37), kind=kLoop, calls=%fused_computation.4 | loop fusion | flops 1048576 | bytes 4718592 | tf_op jit(solution)/shard_map/convert_element_type | solution.py:334
  122.9 5.0 %all-to-all-start.1 = ((bf16[16,32,512]{2,1,0:T(8,128)(2,1)}), bf16[16,32,512]{2,1,0:T(8,128)(2,1)S(1)}, u32[]{:S(2)}, u32[]{:S(2)}) async-start(bf16[16,32,512]{2,1,0:T(8,128)(2,1)} %fusion.3), calls=%async_computation.1 | async-start | bytes 1048576 | tf_op jit(solution)/shard_map/all_to_all | solution.py:218
  128.0 3.0 %collective-permute-start.22 = (bf16[8,32,512]{2,1,0:T(8,128)(2,1)S(1)}, bf16[8,32,512]{2,1,0:T(8,128)(2,1)S(1)}, u32[]{:S(2)}, u32[]{:S(2)}) collective-permute-start(bf16[8,32,512]{2,1,0:T(8,128)(2,1)S(1)} %collective-permute-done.20.a2a), channel_id=1, source_target_pairs={{0,1},{1,0},{2,3},{3,2},{4,5},{5,4},{6,7},{7,6},{8,9},{9,8},{10,11... | collective-permute-start | bytes 786440 | tf_op jit(solution)/shard_map/ppermute | solution.py:215
  131.1 1.1 collective-permute-done.22.b2a
  132.1 0.6 collective-permute-done.23.b2b
  132.8 0.7 copy-done.11
  133.6 7.0 %far_weight_grad.1 = bf16[1,8,34,8,128]{4,3,2,1,0:T(8,128)(2,1)} custom-call(s32[1]{0:T(128)} %bitcast.pos, s32[8,8,34]{2,1,0:T(8,128)} %rows.5, s32[8,8,34]{2,1,0:T(8,128)} %cols.5, s32[8,8]{1,0:T(8,128)} %live.5, bf16[8,32,512]{2,1,0:T(8,128)(2,1)} %copy-done.9, bf16[8,32,512]{2,1,0:T(8,128)(2,1)} %collective-permute-done.21.a2b, ...), custom_call_target="tpu_custom_call" | custom-call | flops 1100000000 | bytes 18000000 | tf_op jit(solution)/shard_map/far_weight_grad/pallas_call | solution.py:337
  140.5 0.8 copy.10
  (48 shorter events, 0.9 us)
Async XLA Ops:
  7.2 103.5 %all-gather.2.cloned.1.call-start = ((), (), s32[]{:S(2)}) async-start(), calls=%async_computation.2 | async-start | bytes 8912896 | tf_op jit(solution)/shard_map/all_gather | solution.py:220
  10.1 24.9 %all-to-all-start = ((bf16[16,64,512]{2,1,0:T(8,128)(2,1)}), bf16[16,64,512]{2,1,0:T(8,128)(2,1)S(1)}, u32[]{:S(2)}, u32[]{:S(2)}) async-start(bf16[16,64,512]{2,1,0:T(8,128)(2,1)} %feature_rows.1), calls=%async_computation | async-start | bytes 2097152 | tf_op jit(solution)/shard_map/all_to_all | solution.py:218
  33.6 3.7 %collective-permute-start = (f32[16,32,512]{2,1,0:T(8,128)}, f32[16,32,512]{2,1,0:T(8,128)S(1)}, u32[]{:S(2)}, u32[]{:S(2)}) collective-permute-start(f32[16,32,512]{2,1,0:T(8,128)} %get-tuple-element.38), channel_id=1, source_target_pairs={{0,1},{1,0},{2,3},{3,2},{4,5},{5,4},{6,7},{7,6},{8,9},{9,8},{10,11... | collective-permute-start | bytes 3145736 | tf_op jit(solution)/shard_map/ppermute | solution.py:215
  35.9 40.6 %copy-start = (bf16[16,32,512]{2,1,0:T(8,128)(2,1)}, bf16[16,32,512]{2,1,0:T(8,128)(2,1)S(1)}, u32[]{:S(2)}) copy-start(bf16[16,32,512]{2,1,0:T(8,128)(2,1)S(1)} %get-tuple-element.49.a0) | copy-start | bytes 1572868
  39.7 38.0 %collective-permute-start.1 = (f32[3,16,32,512]{3,2,1,0:T(8,128)}, f32[3,16,32,512]{3,2,1,0:T(8,128)S(1)}, u32[]{:S(2)}, u32[]{:S(2)}) collective-permute-start(f32[3,16,32,512]{3,2,1,0:T(8,128)} %get-tuple-element.41), channel_id=1, source_target_pairs={{0,1},{1,0},{2,3},{3,2},{4,5},{5,4},{6,7},{7,6},{8,9},{9,8},{10,11... | collective-permute-start | bytes 9437192 | tf_op jit(solution)/shard_map/ppermute | solution.py:215
  44.4 15.4 %collective-permute-start.4 = (bf16[16,32,512]{2,1,0:T(8,128)(2,1)S(1)}, bf16[16,32,512]{2,1,0:T(8,128)(2,1)S(1)}, u32[]{:S(2)}, u32[]{:S(2)}) collective-permute-start(bf16[16,32,512]{2,1,0:T(8,128)(2,1)S(1)} %get-tuple-element.49.a0), channel_id=1, source_target_pairs={{0,2},{1,3},{2,4},{3,5},{4,6},{5,7},{6,0},{7,1},{8,10},{9,11},{10,... | collective-permute-start | bytes 1572872 | tf_op jit(solution)/shard_map/ppermute | solution.py:212
  45.7 14.8 %collective-permute-start.5 = (bf16[16,32,512]{2,1,0:T(8,128)(2,1)S(1)}, bf16[16,32,512]{2,1,0:T(8,128)(2,1)S(1)}, u32[]{:S(2)}, u32[]{:S(2)}) collective-permute-start(bf16[16,32,512]{2,1,0:T(8,128)(2,1)S(1)} %get-tuple-element.49.a0), channel_id=1, source_target_pairs={{0,6},{1,7},{2,0},{3,1},{4,2},{5,3},{6,4},{7,5},{8,14},{9,15},{10,... | collective-permute-start | bytes 1572872 | tf_op jit(solution)/shard_map/ppermute | solution.py:212
  47.3 29.8 %collective-permute-start.2 = (f32[8,32,512]{2,1,0:T(8,128)}, f32[8,32,512]{2,1,0:T(8,128)}, u32[]{:S(2)}, u32[]{:S(2)}) collective-permute-start(f32[8,32,512]{2,1,0:T(8,128)} %get-tuple-element.42), channel_id=1, source_target_pairs={{0,2},{1,3},{2,4},{3,5},{4,6},{5,7},{6,0},{7,1},{8,10},{9,11},{10,... | collective-permute-start | bytes 1572872 | tf_op jit(solution)/shard_map/ppermute | solution.py:212
  47.3 30.2 %collective-permute-start.3 = (f32[8,32,512]{2,1,0:T(8,128)}, f32[8,32,512]{2,1,0:T(8,128)}, u32[]{:S(2)}, u32[]{:S(2)}) collective-permute-start(f32[8,32,512]{2,1,0:T(8,128)} %get-tuple-element.43), channel_id=1, source_target_pairs={{0,6},{1,7},{2,0},{3,1},{4,2},{5,3},{6,4},{7,5},{8,14},{9,15},{10,... | collective-permute-start | bytes 1572872 | tf_op jit(solution)/shard_map/ppermute | solution.py:212
  59.7 0.9 copy-start.1
  60.6 0.9 copy-start.2
  61.5 15.1 %collective-permute-start.6 = (bf16[8,32,512]{2,1,0:T(8,128)(2,1)}, bf16[8,32,512]{2,1,0:T(8,128)(2,1)S(1)}, u32[]{:S(2)}, u32[]{:S(2)}) collective-permute-start(bf16[8,32,512]{2,1,0:T(8,128)(2,1)} %slice.87), channel_id=1, source_target_pairs={{0,2},{1,3},{2,4},{3,5},{4,6},{5,7},{6,0},{7,1},{8,10},{9,11},{10,... | collective-permute-start | bytes 786440 | tf_op jit(solution)/shard_map/ppermute | solution.py:212
  61.5 15.6 %collective-permute-start.7 = (bf16[8,32,512]{2,1,0:T(8,128)(2,1)}, bf16[8,32,512]{2,1,0:T(8,128)(2,1)}, u32[]{:S(2)}, u32[]{:S(2)}) collective-permute-start(bf16[8,32,512]{2,1,0:T(8,128)(2,1)} %slice.88), channel_id=1, source_target_pairs={{0,6},{1,7},{2,0},{3,1},{4,2},{5,3},{6,4},{7,5},{8,14},{9,15},{10,... | collective-permute-start | bytes 786440 | tf_op jit(solution)/shard_map/ppermute | solution.py:212
  76.6 10.6 %copy-start.6 = (bf16[8,32,512]{2,1,0:T(8,128)(2,1)}, bf16[8,32,512]{2,1,0:T(8,128)(2,1)S(1)}, u32[]{:S(2)}) copy-start(bf16[8,32,512]{2,1,0:T(8,128)(2,1)S(1)} %collective-permute-done.6.a2a) | copy-start | bytes 786436
  76.6 4.9 %collective-permute-start.8 = (bf16[16,32,512]{2,1,0:T(8,128)(2,1)S(1)}, bf16[16,32,512]{2,1,0:T(8,128)(2,1)S(1)}, u32[]{:S(2)}, u32[]{:S(2)}) collective-permute-start(bf16[16,32,512]{2,1,0:T(8,128)(2,1)S(1)} %get-tuple-element.49.a0), channel_id=1, source_target_pairs={{0,1},{1,0},{2,3},{3,2},{4,5},{5,4},{6,7},{7,6},{8,9},{9,8},{10,11... | collective-permute-start | bytes 1572872 | tf_op jit(solution)/shard_map/ppermute | solution.py:215
  77.1 11.4 %collective-permute-start.10 = (bf16[16,32,512]{2,1,0:T(8,128)(2,1)}, bf16[16,32,512]{2,1,0:T(8,128)(2,1)}, u32[]{:S(2)}, u32[]{:S(2)}) collective-permute-start(bf16[16,32,512]{2,1,0:T(8,128)(2,1)} %copy-done.2), channel_id=1, source_target_pairs={{0,1},{1,0},{2,3},{3,2},{4,5},{5,4},{6,7},{7,6},{8,9},{9,8},{10,11... | collective-permute-start | bytes 1572872 | tf_op jit(solution)/shard_map/ppermute | solution.py:215
  77.2 11.3 %collective-permute-start.9 = (bf16[16,32,512]{2,1,0:T(8,128)(2,1)}, bf16[16,32,512]{2,1,0:T(8,128)(2,1)}, u32[]{:S(2)}, u32[]{:S(2)}) collective-permute-start(bf16[16,32,512]{2,1,0:T(8,128)(2,1)} %copy-done.1), channel_id=1, source_target_pairs={{0,1},{1,0},{2,3},{3,2},{4,5},{5,4},{6,7},{7,6},{8,9},{9,8},{10,11... | collective-permute-start | bytes 1572872 | tf_op jit(solution)/shard_map/ppermute | solution.py:215
  77.6 5.6 %collective-permute-start.11 = (bf16[8,32,512]{2,1,0:T(8,128)(2,1)S(1)}, bf16[8,32,512]{2,1,0:T(8,128)(2,1)S(1)}, u32[]{:S(2)}, u32[]{:S(2)}) collective-permute-start(bf16[8,32,512]{2,1,0:T(8,128)(2,1)S(1)} %collective-permute-done.6.a2a), channel_id=1, source_target_pairs={{0,1},{1,0},{2,3},{3,2},{4,5},{5,4},{6,7},{7,6},{8,9},{9,8},{10,11... | collective-permute-start | bytes 786440 | tf_op jit(solution)/shard_map/ppermute | solution.py:215
  77.7 9.5 %collective-permute-start.12 = (bf16[8,32,512]{2,1,0:T(8,128)(2,1)}, bf16[8,32,512]{2,1,0:T(8,128)(2,1)S(1)}, u32[]{:S(2)}, u32[]{:S(2)}) collective-permute-start(bf16[8,32,512]{2,1,0:T(8,128)(2,1)} %collective-permute-done.7.a2b), channel_id=1, source_target_pairs={{0,1},{1,0},{2,3},{3,2},{4,5},{5,4},{6,7},{7,6},{8,9},{9,8},{10,11... | collective-permute-start | bytes 786440 | tf_op jit(solution)/shard_map/ppermute | solution.py:215
  81.5 0.8 copy-start.4
  82.3 21.6 %collective-permute-start.13 = (bf16[16,32,512]{2,1,0:T(8,128)(2,1)}, bf16[16,32,512]{2,1,0:T(8,128)(2,1)S(1)}, u32[]{:S(2)}, u32[]{:S(2)}) collective-permute-start(bf16[16,32,512]{2,1,0:T(8,128)(2,1)} %get-tuple-element.60.a0), channel_id=1, source_target_pairs={{0,2},{1,3},{2,4},{3,5},{4,6},{5,7},{6,0},{7,1},{8,10},{9,11},{10,... | collective-permute-start | bytes 1572872 | tf_op jit(solution)/shard_map/ppermute | solution.py:212
  83.2 0.7 copy-start.7
  84.0 20.0 %collective-permute-start.14 = (bf16[16,32,512]{2,1,0:T(8,128)(2,1)}, bf16[16,32,512]{2,1,0:T(8,128)(2,1)}, u32[]{:S(2)}, u32[]{:S(2)}) collective-permute-start(bf16[16,32,512]{2,1,0:T(8,128)(2,1)} %get-tuple-element.60.a0), channel_id=1, source_target_pairs={{0,6},{1,7},{2,0},{3,1},{4,2},{5,3},{6,4},{7,5},{8,14},{9,15},{10,... | collective-permute-start | bytes 1572872 | tf_op jit(solution)/shard_map/ppermute | solution.py:212
  87.2 0.7 copy-start.8
  87.9 19.3 %collective-permute-start.17 = (bf16[16,32,512]{2,1,0:T(8,128)(2,1)}, bf16[16,32,512]{2,1,0:T(8,128)(2,1)}, u32[]{:S(2)}, u32[]{:S(2)}) collective-permute-start(bf16[16,32,512]{2,1,0:T(8,128)(2,1)} %get-tuple-element.60.a0), channel_id=1, source_target_pairs={{0,1},{1,0},{2,3},{3,2},{4,5},{5,4},{6,7},{7,6},{8,9},{9,8},{10,11... | collective-permute-start | bytes 1572872 | tf_op jit(solution)/shard_map/ppermute | solution.py:215
  88.5 31.3 %collective-permute-start.15 = (f32[16,32,512]{2,1,0:T(8,128)}, f32[16,32,512]{2,1,0:T(8,128)}, u32[]{:S(2)}, u32[]{:S(2)}) collective-permute-start(f32[16,32,512]{2,1,0:T(8,128)} %get-tuple-element.62), channel_id=1, source_target_pairs={{0,2},{1,3},{2,4},{3,5},{4,6},{5,7},{6,0},{7,1},{8,10},{9,11},{10,... | collective-permute-start | bytes 3145736 | tf_op jit(solution)/shard_map/ppermute | solution.py:212
  88.5 31.3 %collective-permute-start.16 = (f32[16,32,512]{2,1,0:T(8,128)}, f32[16,32,512]{2,1,0:T(8,128)}, u32[]{:S(2)}, u32[]{:S(2)}) collective-permute-start(f32[16,32,512]{2,1,0:T(8,128)} %get-tuple-element.63), channel_id=1, source_target_pairs={{0,6},{1,7},{2,0},{3,1},{4,2},{5,3},{6,4},{7,5},{8,14},{9,15},{10,... | collective-permute-start | bytes 3145736 | tf_op jit(solution)/shard_map/ppermute | solution.py:212
  103.9 0.8 copy-start.3
  103.9 3.2 %collective-permute-start.18 = (bf16[16,32,512]{2,1,0:T(8,128)(2,1)S(1)}, bf16[16,32,512]{2,1,0:T(8,128)(2,1)S(1)}, u32[]{:S(2)}, u32[]{:S(2)}) collective-permute-start(bf16[16,32,512]{2,1,0:T(8,128)(2,1)S(1)} %collective-permute-done.13.am), channel_id=1, source_target_pairs={{0,1},{1,0},{2,3},{3,2},{4,5},{5,4},{6,7},{7,6},{8,9},{9,8},{10,11... | collective-permute-start | bytes 1572872 | tf_op jit(solution)/shard_map/ppermute | solution.py:215
  104.6 6.0 %collective-permute-start.19 = (bf16[16,32,512]{2,1,0:T(8,128)(2,1)}, bf16[16,32,512]{2,1,0:T(8,128)(2,1)}, u32[]{:S(2)}, u32[]{:S(2)}) collective-permute-start(bf16[16,32,512]{2,1,0:T(8,128)(2,1)} %collective-permute-done.14.ap), channel_id=1, source_target_pairs={{0,1},{1,0},{2,3},{3,2},{4,5},{5,4},{6,7},{7,6},{8,9},{9,8},{10,11... | collective-permute-start | bytes 1572872 | tf_op jit(solution)/shard_map/ppermute | solution.py:215
  107.2 20.8 %collective-permute-start.20 = (bf16[8,32,512]{2,1,0:T(8,128)(2,1)}, bf16[8,32,512]{2,1,0:T(8,128)(2,1)S(1)}, u32[]{:S(2)}, u32[]{:S(2)}) collective-permute-start(bf16[8,32,512]{2,1,0:T(8,128)(2,1)} %slice.78), channel_id=1, source_target_pairs={{0,2},{1,3},{2,4},{3,5},{4,6},{5,7},{6,0},{7,1},{8,10},{9,11},{10,... | collective-permute-start | bytes 786440 | tf_op jit(solution)/shard_map/ppermute | solution.py:212
  107.2 0.8 copy-start.5
  108.0 23.0 %collective-permute-start.21 = (bf16[8,32,512]{2,1,0:T(8,128)(2,1)}, bf16[8,32,512]{2,1,0:T(8,128)(2,1)}, u32[]{:S(2)}, u32[]{:S(2)}) collective-permute-start(bf16[8,32,512]{2,1,0:T(8,128)(2,1)} %slice.79), channel_id=1, source_target_pairs={{0,6},{1,7},{2,0},{3,1},{4,2},{5,3},{6,4},{7,5},{8,14},{9,15},{10,... | collective-permute-start | bytes 786440 | tf_op jit(solution)/shard_map/ppermute | solution.py:212
  122.9 17.7 %all-to-all-start.1 = ((bf16[16,32,512]{2,1,0:T(8,128)(2,1)}), bf16[16,32,512]{2,1,0:T(8,128)(2,1)S(1)}, u32[]{:S(2)}, u32[]{:S(2)}) async-start(bf16[16,32,512]{2,1,0:T(8,128)(2,1)} %fusion.3), calls=%async_computation.1 | async-start | bytes 1048576 | tf_op jit(solution)/shard_map/all_to_all | solution.py:218
  127.9 4.8 %copy-start.9 = (bf16[8,32,512]{2,1,0:T(8,128)(2,1)}, bf16[8,32,512]{2,1,0:T(8,128)(2,1)S(1)}, u32[]{:S(2)}) copy-start(bf16[8,32,512]{2,1,0:T(8,128)(2,1)S(1)} %collective-permute-done.20.a2a) | copy-start | bytes 786436
  128.0 4.2 %collective-permute-start.22 = (bf16[8,32,512]{2,1,0:T(8,128)(2,1)S(1)}, bf16[8,32,512]{2,1,0:T(8,128)(2,1)S(1)}, u32[]{:S(2)}, u32[]{:S(2)}) collective-permute-start(bf16[8,32,512]{2,1,0:T(8,128)(2,1)S(1)} %collective-permute-done.20.a2a), channel_id=1, source_target_pairs={{0,1},{1,0},{2,3},{3,2},{4,5},{5,4},{6,7},{7,6},{8,9},{9,8},{10,11... | collective-permute-start | bytes 786440 | tf_op jit(solution)/shard_map/ppermute | solution.py:215
  131.0 1.7 %collective-permute-start.23 = (bf16[8,32,512]{2,1,0:T(8,128)(2,1)}, bf16[8,32,512]{2,1,0:T(8,128)(2,1)S(1)}, u32[]{:S(2)}, u32[]{:S(2)}) collective-permute-start(bf16[8,32,512]{2,1,0:T(8,128)(2,1)} %collective-permute-done.21.a2b), channel_id=1, source_target_pairs={{0,1},{1,0},{2,3},{3,2},{4,5},{5,4},{6,7},{7,6},{8,9},{9,8},{10,11... | collective-permute-start | bytes 786440 | tf_op jit(solution)/shard_map/ppermute | solution.py:215
  132.1 0.7 copy-start.10
  132.8 0.7 copy-start.11
Sparse Core Ops, SparseCore 0:
  10.1 78.8 all-gather.1

commit v8 on v6

--- a/solution.py
+++ b/solution.py
@@ -39,8 +39,7 @@
     x = x_ref[...].reshape(512, 512).astype(F32)
     t = x.T.reshape(4, 16, 8, 512)
     for part in range(16):
-        o_ref[part, pl.ds(0, 32)] = x_ref[part]
-        o_ref[part, pl.ds(32, 32)] = t[:, part].reshape(32, 512).astype(BF16)
+        o_ref[part] = t[:, part].reshape(32, 512).astype(BF16)
 
 
 def partial_kernel(pos, rows, cols, live, cot, blk, keep, across, rest, dense, *scratch):
@@ -209,15 +208,7 @@
 
     cot_all = lax.all_gather(cotangent, "seq", axis=0, tiled=True)
 
-    both = pl.pallas_call(
-        transpose_kernel,
-        out_shape=jax.ShapeDtypeStruct((16, 64, 512), BF16),
-        compiler_params=params,
-        name="feature_rows",
-    )(context)
-    both, cot_own = barrier((both, cotangent))
-    both = exchange(both)
-    tokens, class_rows = both[:, :32], both[:, 32:]
+    tokens = exchange(context)
 
     scalars = [pl.BlockSpec(memory_space=pltpu.SMEM)] * 4
     anywhere = pl.BlockSpec(memory_space=pl.ANY)
@@ -245,14 +236,24 @@
         compiler_params=params,
         cost_estimate=cost(4_300_000_000, 45_000_000),
         name="partial_context_grad",
-    )(*tables, cot_own.reshape(4, 2, 32, 1024), blocks)
+    )(*tables, cotangent.reshape(4, 2, 32, 1024), blocks)
+    across, tokens = barrier((across, tokens))
     across = other_core(across)
 
     q2a, q2b = keep[2, :8] + across[:8], keep[2, 8:] + across[8:]
-    q2a, q2b, tokens, rest = barrier((q2a, q2b, tokens, rest))
+    q2a, q2b, tokens, rest, context = barrier((q2a, q2b, tokens, rest, context))
     from_a, from_b = along_y(q2a, 1), along_y(q2b, -1)
     xm, xp = along_y(tokens, 1), along_y(tokens, -1)
     rest = other_core(rest)
+
+    by_class = pl.pallas_call(
+        transpose_kernel,
+        out_shape=jax.ShapeDtypeStruct((16, 32, 512), BF16),
+        compiler_params=params,
+        name="feature_rows",
+    )(context)
+    class_rows = exchange(by_class)
+
     x2a, x2b = along_y(xm[:8], 1), along_y(xp[8:], -1)
     x2a, x2b, class_rows = barrier((x2a, x2b, class_rows))
     own = (tokens, xm, xp, x2a, x2b)

time: 145 us -> 144 us (level)
  waiting for transfers between devices: 30.2 us -> 21.3 us
  other arithmetic: 6.57 us -> 10.2 us
  starting transfers between devices: 41.5 us -> 45.1 us
    ppermute x12, waiting for transfers between devices: 25.6 us -> 16.5 us  [along_y(): return lax.ppermute(x, 'mp', [(i, (i + 2 * step) % 8) for i in range(8)])]
    all_to_all x2 -> x3, starting transfers between devices: 13.6 us -> 22.4 us  [exchange(): return lax.all_to_all(x, 'seq', split_axis=0, concat_axis=0, tiled=True)]
    ppermute x12, starting transfers between devices: 11 us -> 7.6 us  [other_core(): return lax.ppermute(x, 'mp', [(i, i ^ 1) for i in range(8)])]
    slice x2, local copies, waits for them, and re-layouts: 0.04 us -> 1.96 us  [on_device(): x2a, x2b = (along_y(xm[:8], 1), along_y(xp[8:], -1))]
    ppermute x12, starting transfers between devices: 16.8 us -> 15.1 us  [along_y(): return lax.ppermute(x, 'mp', [(i, (i + 2 * step) % 8) for i in range(8)])]
    add x1, other arithmetic: 0.37 us -> 1.86 us  [on_device(): keep[3, 8:] + rest[2, 8:] + from_b]
    unnamed x33 -> x19, local copies, waits for them, and re-layouts: 3.45 us -> 3.83 us
  transfers between devices with their start and end apart: 27 -> 28, of which waited for: 8 -> 7; matrix products, arithmetic and copies ran while one was open for 7% -> 10% of each run, Pallas kernels for 31% -> 31%
where the time goes in v8:
time: 144 us; the launch traced here: 143 us
  starting transfers between devices  45.1 us (31%)
  Pallas kernels  44.1 us (31%)
  waiting for transfers between devices  21.3 us (15%)
  between operations  14.2 us (10%)
  other arithmetic  10.2 us (7%)
  local copies, waits for them, and re-layouts  8.16 us (6%)
    all_to_all x3, starting transfers between devices, exchange(): return lax.all_to_all(x, 'seq', split_axis=0, concat_axis=0, tiled=True)  22.4 us
    ppermute x12, waiting for transfers between devices, along_y(): return lax.ppermute(x, 'mp', [(i, (i + 2 * step) % 8) for i in range(8)])  16.5 us
    pallas_call x1, Pallas kernels, on_device(): pl.pallas_call(partial_kernel, in_specs=scalars + [anywhere] * 2, out_spe...  15.7 us
    ppermute x12, starting transfers between devices, along_y(): return lax.ppermute(x, 'mp', [(i, (i + 2 * step) % 8) for i in range(8)])  15.1 us
    pallas_call x1, Pallas kernels, on_device(): pl.pallas_call(out_kernel, in_specs=scalars[:1] + [anywhere] * 11, out_sh...  12.7 us
    ppermute x12, starting transfers between devices, other_core(): return lax.ppermute(x, 'mp', [(i, i ^ 1) for i in range(8)])  7.6 us
    pallas_call x1, Pallas kernels, on_device(): pl.pallas_call(functools.partial(far_grad_kernel, 1.0 / math.sqrt(4096)),...  6.96 us
    pallas_call x1, Pallas kernels, on_device(): pl.pallas_call(near_grad_kernel, in_specs=scalars[:1] + [anywhere] * 7, o...  6.58 us
  transfers between devices with their start and end apart: 28, of which 7 were waited for; matrix products, arithmetic and copies ran while one was open for 10% of the time, Pallas kernels for 31%

profile of v8, /device:TPU:1, one launch (start us, length us, event | category | flops | bytes accessed | tf_op | source)
XLA Modules:
  0.0 143.1 jit_solution(17215174019726542979)
XLA Ops:
  7.2 0.7 all-gather.2.cloned.1.call-update
  7.9 8.4 %all-to-all-start = ((bf16[16,32,512]{2,1,0:T(8,128)(2,1)}), bf16[16,32,512]{2,1,0:T(8,128)(2,1)S(1)}, u32[]{:S(2)}, u32[]{:S(2)}) async-start(bf16[16,32,512]{2,1,0:T(8,128)(2,1)} %x_ref), calls=%async_computation | async-start | bytes 1048576 | tf_op jit(solution)/shard_map/all_to_all | solution.py:207
  16.3 15.7 %partial_context_grad.1 = (f32[4,16,32,512]{3,2,1,0:T(8,128)}, f32[16,32,512]{2,1,0:T(8,128)}, f32[3,16,32,512]{3,2,1,0:T(8,128)}, bf16[8,1024,1024]{2,1,0:T(8,128)(2,1)}) custom-call(s32[1]{0:T(128)} %bitcast.pos, s32[8,8,34]{2,1,0:T(8,128)} %rows.3, s32[8,8,34]{2,1,0:T(8,128)} %cols.3, s32[8,8]{1,0:T(8,128)} %live.3, bf16[4,2,32,1024]{3,2,1,0:T(8,128)(2,1)} %bitcast.29, ...), custom_call_target="tpu_custom_call" | custom-call | flops 4300000256 | bytes 45000000 | tf_op jit(solution)/shard_map/partial_context_grad/pallas_call | solution.py:215
  32.1 1.0 collective-permute-start
  33.1 2.5 %collective-permute-done = f32[16,32,512]{2,1,0:T(8,128)S(1)} collective-permute-done((f32[16,32,512]{2,1,0:T(8,128)}, f32[16,32,512]{2,1,0:T(8,128)S(1)}, u32[]{:S(2)}, u32[]{:S(2)}) %collective-permute-start) | collective-permute-done | bytes 1048608 | tf_op jit(solution)/shard_map/ppermute | solution.py:204
  35.6 2.4 %slice_add_fusion.5 = (f32[8,32,512]{2,1,0:T(8,128)}, f32[8,32,512]{2,1,0:T(8,128)}) fusion(f32[16,32,512]{2,1,0:T(8,128)S(1)} %collective-permute-done, f32[4,16,32,512]{3,2,1,0:T(8,128)} %get-tuple-element.35), kind=kLoop, calls=%fused_computation.17 | loop fusion | flops 262144 | bytes 3145728 | tf_op jit(solution)/shard_map/add | solution.py:243
  38.0 0.4 collective-permute-start.1
  38.4 1.3 collective-permute-start.4
  39.7 1.5 %collective-permute-start.5 = (bf16[16,32,512]{2,1,0:T(8,128)(2,1)}, bf16[16,32,512]{2,1,0:T(8,128)(2,1)}, u32[]{:S(2)}, u32[]{:S(2)}) collective-permute-start(bf16[16,32,512]{2,1,0:T(8,128)(2,1)} %copy-done), channel_id=1, source_target_pairs={{0,6},{1,7},{2,0},{3,1},{4,2},{5,3},{6,4},{7,5},{8,14},{9,15},{10,... | collective-permute-start | bytes 1572872 | tf_op jit(solution)/shard_map/ppermute | solution.py:201
  41.2 1.5 %collective-permute-start.3 = (f32[8,32,512]{2,1,0:T(8,128)}, f32[8,32,512]{2,1,0:T(8,128)}, u32[]{:S(2)}, u32[]{:S(2)}) collective-permute-start(f32[8,32,512]{2,1,0:T(8,128)} %get-tuple-element.42), channel_id=1, source_target_pairs={{0,6},{1,7},{2,0},{3,1},{4,2},{5,3},{6,4},{7,5},{8,14},{9,15},{10,... | collective-permute-start | bytes 1572872 | tf_op jit(solution)/shard_map/ppermute | solution.py:201
  42.7 2.1 %feature_rows.1 = bf16[16,32,512]{2,1,0:T(8,128)(2,1)} custom-call(bf16[16,32,512]{2,1,0:T(8,128)(2,1)} %x_ref), custom_call_target="tpu_custom_call" | custom-call | tf_op jit(solution)/shard_map/feature_rows/pallas_call | solution.py:249
  44.7 7.0 %all-to-all-start.1 = ((bf16[16,32,512]{2,1,0:T(8,128)(2,1)}), bf16[16,32,512]{2,1,0:T(8,128)(2,1)}, u32[]{:S(2)}, u32[]{:S(2)}) async-start(bf16[16,32,512]{2,1,0:T(8,128)(2,1)} %feature_rows.1), calls=%async_computation.1 | async-start | bytes 1048576 | tf_op jit(solution)/shard_map/all_to_all | solution.py:207
  51.7 1.8 %collective-permute-done.4.am = bf16[16,32,512]{2,1,0:T(8,128)(2,1)} collective-permute-done((bf16[16,32,512]{2,1,0:T(8,128)(2,1)}, bf16[16,32,512]{2,1,0:T(8,128)(2,1)}, u32[]{:S(2)}, u32[]{:S(2)}) %collective-permute-start.4) | collective-permute-done | bytes 524320 | tf_op jit(solution)/shard_map/ppermute | solution.py:201
  53.5 1.0 slice.78
  54.6 1.0 slice.79
  55.6 2.7 %collective-permute-start.7 = (bf16[8,32,512]{2,1,0:T(8,128)(2,1)S(1)}, bf16[8,32,512]{2,1,0:T(8,128)(2,1)}, u32[]{:S(2)}, u32[]{:S(2)}) collective-permute-start(bf16[8,32,512]{2,1,0:T(8,128)(2,1)S(1)} %slice.79), channel_id=1, source_target_pairs={{0,6},{1,7},{2,0},{3,1},{4,2},{5,3},{6,4},{7,5},{8,14},{9,15},{10,... | collective-permute-start | bytes 786440 | tf_op jit(solution)/shard_map/ppermute | solution.py:201
  58.3 12.1 %collective-permute-done.6.a2a = bf16[8,32,512]{2,1,0:T(8,128)(2,1)S(1)} collective-permute-done((bf16[8,32,512]{2,1,0:T(8,128)(2,1)S(1)}, bf16[8,32,512]{2,1,0:T(8,128)(2,1)S(1)}, u32[]{:S(2)}, u32[]{:S(2)}) %collective-permute-start.6) | collective-permute-done | bytes 262176 | tf_op jit(solution)/shard_map/ppermute | solution.py:201
  70.4 0.7 collective-permute-start.8
  71.3 0.4 collective-permute-start.10
  71.7 0.3 collective-permute-start.11
  71.9 0.2 collective-permute-start.12
  72.2 1.9 %fusion.5 = (f32[8,32,512]{2,1,0:T(8,128)S(1)}, f32[8,32,512]{2,1,0:T(8,128)S(1)}) fusion(f32[8,32,512]{2,1,0:T(8,128)} %collective-permute-done.3, f32[3,16,32,512]{3,2,1,0:T(8,128)S(1)} %collective-permute-done.1, f32[4,16,32,512]{3,2,1,0:T(8,128)} %get-tuple-element.35, f32[8,32,512]{2,1,0:T(8,128)} %collective-permute-done.2), kind=kLoop, calls=%fused_computation.9 | loop fusion | flops 524288 | bytes 4194304 | tf_op jit(solution)/shard_map/add | solution.py:265
  74.0 1.4 %fusion.6 = (f32[8,32,512]{2,1,0:T(8,128)S(1)}, f32[8,32,512]{2,1,0:T(8,128)S(1)}) fusion(f32[3,16,32,512]{3,2,1,0:T(8,128)S(1)} %collective-permute-done.1, f32[4,16,32,512]{3,2,1,0:T(8,128)} %get-tuple-element.35), kind=kLoop, calls=%fused_computation.11 | loop fusion | flops 262144 | bytes 3145728 | tf_op jit(solution)/shard_map/add | solution.py:265
  75.5 1.2 collective-permute-start.13
  76.7 0.7 copy-done.4
  77.4 1.5 %collective-permute-start.14 = (bf16[16,32,512]{2,1,0:T(8,128)(2,1)}, bf16[16,32,512]{2,1,0:T(8,128)(2,1)}, u32[]{:S(2)}, u32[]{:S(2)}) collective-permute-start(bf16[16,32,512]{2,1,0:T(8,128)(2,1)} %all-to-all-done.1.a0), channel_id=1, source_target_pairs={{0,6},{1,7},{2,0},{3,1},{4,2},{5,3},{6,4},{7,5},{8,14},{9,15},{10,... | collective-permute-start | bytes 1572872 | tf_op jit(solution)/shard_map/ppermute | solution.py:201
  79.0 1.5 %pad_maximum_fusion = (f32[16,32,512]{2,1,0:T(8,128)}, f32[16,32,512]{2,1,0:T(8,128)}) fusion(f32[8,32,512]{2,1,0:T(8,128)S(1)} %get-tuple-element.68, f32[8,32,512]{2,1,0:T(8,128)S(1)} %get-tuple-element.70, f32[8,32,512]{2,1,0:T(8,128)S(1)} %get-tuple-element.69, f32[8,32,512]{2,1,0:T(8,128)S(1)} %get-tuple-element.67), kind=kLoop, calls=%fused_computation.5 | loop fusion | flops 524288 | bytes 4194304 | tf_op jit(solution)/shard_map/concatenate | solution.py:264
  80.4 0.7 copy-done.5
  81.1 0.8 collective-permute-start.17
  82.0 2.7 %collective-permute-start.16 = (f32[16,32,512]{2,1,0:T(8,128)}, f32[16,32,512]{2,1,0:T(8,128)}, u32[]{:S(2)}, u32[]{:S(2)}) collective-permute-start(f32[16,32,512]{2,1,0:T(8,128)} %get-tuple-element.61), channel_id=1, source_target_pairs={{0,6},{1,7},{2,0},{3,1},{4,2},{5,3},{6,4},{7,5},{8,14},{9,15},{10,... | collective-permute-start | bytes 3145736 | tf_op jit(solution)/shard_map/ppermute | solution.py:201
  84.7 12.7 %outputs.1 = bf16[256,1024]{1,0:T(8,128)(2,1)} custom-call(s32[1]{0:T(128)} %bitcast.pos, bf16[16,32,512]{2,1,0:T(8,128)(2,1)} %copy-done, bf16[16,32,512]{2,1,0:T(8,128)(2,1)} %collective-permute-done.4.am, bf16[16,32,512]{2,1,0:T(8,128)(2,1)} %collective-permute-done.5.ap, bf16[8,32,512]{2,1,0:T(8,128)(2,1)} %copy-done.3, ...), custom_call_target="tpu_custom_call" | custom-call | flops 4300000256 | bytes 30000000 | tf_op jit(solution)/shard_map/outputs/pallas_call | solution.py:269
  97.4 0.7 collective-permute-start.18
  98.2 0.7 slice.70
  99.0 1.7 %slice.71 = bf16[8,32,512]{2,1,0:T(8,128)(2,1)} slice(bf16[16,32,512]{2,1,0:T(8,128)(2,1)} %collective-permute-done.14.ap), slice={[8:16], [0:32], [0:512]} | slice | bytes 524288 | tf_op jit(solution)/shard_map/slice | solution.py:286
  100.6 0.8 copy-done.2
  101.4 2.7 %collective-permute-start.21 = (bf16[8,32,512]{2,1,0:T(8,128)(2,1)}, bf16[8,32,512]{2,1,0:T(8,128)(2,1)}, u32[]{:S(2)}, u32[]{:S(2)}) collective-permute-start(bf16[8,32,512]{2,1,0:T(8,128)(2,1)} %slice.71), channel_id=1, source_target_pairs={{0,6},{1,7},{2,0},{3,1},{4,2},{5,3},{6,4},{7,5},{8,14},{9,15},{10,... | collective-permute-start | bytes 786440 | tf_op jit(solution)/shard_map/ppermute | solution.py:201
  104.1 6.6 %near_weight_grad.1.near = f32[64,8,1024]{2,1,0:T(8,128)} custom-call(s32[1]{0:T(128)} %bitcast.pos, bf16[16,32,512]{2,1,0:T(8,128)(2,1)} %all-to-all-done.1.a0, bf16[16,32,512]{2,1,0:T(8,128)(2,1)} %copy-done.1, bf16[16,32,512]{2,1,0:T(8,128)(2,1)} %collective-permute-done.14.ap, bf16[16,32,512]{2,1,0:T(8,128)(2,1)} %collective-permute-done.17.b0, ...), custom_call_target="tpu_custom_call" | custom-call | flops 3200000000 | bytes 25000000 | tf_op jit(solution)/shard_map/near_weight_grad/pallas_call | solution.py:291
  110.7 2.1 %collective-permute-done.15 = f32[16,32,512]{2,1,0:T(8,128)} collective-permute-done((f32[16,32,512]{2,1,0:T(8,128)}, f32[16,32,512]{2,1,0:T(8,128)}, u32[]{:S(2)}, u32[]{:S(2)}) %collective-permute-start.15) | collective-permute-done | bytes 1048608 | tf_op jit(solution)/shard_map/ppermute | solution.py:201
  112.8 0.4 collective-permute-done.16
  113.2 3.0 %fusion.3 = bf16[16,32,512]{2,1,0:T(8,128)(2,1)} fusion(f32[16,32,512]{2,1,0:T(8,128)} %collective-permute-done.16, f32[16,32,512]{2,1,0:T(8,128)} %collective-permute-done.15, f32[3,16,32,512]{3,2,1,0:T(8,128)S(1)} %collective-permute-done.1, f32[4,16,32,512]{3,2,1,0:T(8,128)} %get-tuple-element.35), kind=kLoop, calls=%fused_computation.4 | loop fusion | flops 1048576 | bytes 4718592 | tf_op jit(solution)/shard_map/convert_element_type | solution.py:310
  116.2 6.9 %all-to-all-start.2 = ((bf16[16,32,512]{2,1,0:T(8,128)(2,1)}), bf16[16,32,512]{2,1,0:T(8,128)(2,1)S(1)}, u32[]{:S(2)}, u32[]{:S(2)}) async-start(bf16[16,32,512]{2,1,0:T(8,128)(2,1)} %fusion.3), calls=%async_computation.2 | async-start | bytes 1048576 | tf_op jit(solution)/shard_map/all_to_all | solution.py:207
  123.2 2.7 %collective-permute-start.22 = (bf16[8,32,512]{2,1,0:T(8,128)(2,1)S(1)}, bf16[8,32,512]{2,1,0:T(8,128)(2,1)S(1)}, u32[]{:S(2)}, u32[]{:S(2)}) collective-permute-start(bf16[8,32,512]{2,1,0:T(8,128)(2,1)S(1)} %collective-permute-done.20.a2a), channel_id=1, source_target_pairs={{0,1},{1,0},{2,3},{3,2},{4,5},{5,4},{6,7},{7,6},{8,9},{9,8},{10,11... | collective-permute-start | bytes 786440 | tf_op jit(solution)/shard_map/ppermute | solution.py:204
  126.0 1.1 collective-permute-done.22.b2a
  127.1 0.6 collective-permute-done.23.b2b
  127.7 0.1 copy-done.7
  127.8 0.7 copy-done.8
  128.5 7.0 %far_weight_grad.1 = bf16[1,8,34,8,128]{4,3,2,1,0:T(8,128)(2,1)} custom-call(s32[1]{0:T(128)} %bitcast.pos, s32[8,8,34]{2,1,0:T(8,128)} %rows.3, s32[8,8,34]{2,1,0:T(8,128)} %cols.3, s32[8,8]{1,0:T(8,128)} %live.3, bf16[8,32,512]{2,1,0:T(8,128)(2,1)} %copy-done.6, bf16[8,32,512]{2,1,0:T(8,128)(2,1)} %collective-permute-done.21.a2b, ...), custom_call_target="tpu_custom_call" | custom-call | flops 1100000000 | bytes 18000000 | tf_op jit(solution)/shard_map/far_weight_grad/pallas_call | solution.py:313
  135.5 0.8 copy.10
  (42 shorter events, 0.5 us)
Async XLA Ops:
  7.2 96.9 %all-gather.2.cloned.1.call-start = ((), (), s32[]{:S(2)}) async-start(), calls=%async_computation.3 | async-start | bytes 8912896 | tf_op jit(solution)/shard_map/all_gather | solution.py:209
  7.9 24.2 %all-to-all-start = ((bf16[16,32,512]{2,1,0:T(8,128)(2,1)}), bf16[16,32,512]{2,1,0:T(8,128)(2,1)S(1)}, u32[]{:S(2)}, u32[]{:S(2)}) async-start(bf16[16,32,512]{2,1,0:T(8,128)(2,1)} %x_ref), calls=%async_computation | async-start | bytes 1048576 | tf_op jit(solution)/shard_map/all_to_all | solution.py:207
  32.1 5.9 %copy-start = (bf16[16,32,512]{2,1,0:T(8,128)(2,1)}, bf16[16,32,512]{2,1,0:T(8,128)(2,1)S(1)}, u32[]{:S(2)}) copy-start(bf16[16,32,512]{2,1,0:T(8,128)(2,1)S(1)} %all-to-all-done.a0) | copy-start | bytes 1572868
  32.1 3.5 %collective-permute-start = (f32[16,32,512]{2,1,0:T(8,128)}, f32[16,32,512]{2,1,0:T(8,128)S(1)}, u32[]{:S(2)}, u32[]{:S(2)}) collective-permute-start(f32[16,32,512]{2,1,0:T(8,128)} %get-tuple-element.37), channel_id=1, source_target_pairs={{0,1},{1,0},{2,3},{3,2},{4,5},{5,4},{6,7},{7,6},{8,9},{9,8},{10,11... | collective-permute-start | bytes 3145736 | tf_op jit(solution)/shard_map/ppermute | solution.py:204
  38.0 33.9 %collective-permute-start.1 = (f32[3,16,32,512]{3,2,1,0:T(8,128)}, f32[3,16,32,512]{3,2,1,0:T(8,128)S(1)}, u32[]{:S(2)}, u32[]{:S(2)}) collective-permute-start(f32[3,16,32,512]{3,2,1,0:T(8,128)} %get-tuple-element.40), channel_id=1, source_target_pairs={{0,1},{1,0},{2,3},{3,2},{4,5},{5,4},{6,7},{7,6},{8,9},{9,8},{10,11... | collective-permute-start | bytes 9437192 | tf_op jit(solution)/shard_map/ppermute | solution.py:204
  38.4 15.1 %collective-permute-start.4 = (bf16[16,32,512]{2,1,0:T(8,128)(2,1)}, bf16[16,32,512]{2,1,0:T(8,128)(2,1)}, u32[]{:S(2)}, u32[]{:S(2)}) collective-permute-start(bf16[16,32,512]{2,1,0:T(8,128)(2,1)} %copy-done), channel_id=1, source_target_pairs={{0,2},{1,3},{2,4},{3,5},{4,6},{5,7},{6,0},{7,1},{8,10},{9,11},{10,... | collective-permute-start | bytes 1572872 | tf_op jit(solution)/shard_map/ppermute | solution.py:201
  39.7 14.9 %collective-permute-start.5 = (bf16[16,32,512]{2,1,0:T(8,128)(2,1)}, bf16[16,32,512]{2,1,0:T(8,128)(2,1)}, u32[]{:S(2)}, u32[]{:S(2)}) collective-permute-start(bf16[16,32,512]{2,1,0:T(8,128)(2,1)} %copy-done), channel_id=1, source_target_pairs={{0,6},{1,7},{2,0},{3,1},{4,2},{5,3},{6,4},{7,5},{8,14},{9,15},{10,... | collective-permute-start | bytes 1572872 | tf_op jit(solution)/shard_map/ppermute | solution.py:201
  41.2 30.1 %collective-permute-start.3 = (f32[8,32,512]{2,1,0:T(8,128)}, f32[8,32,512]{2,1,0:T(8,128)}, u32[]{:S(2)}, u32[]{:S(2)}) collective-permute-start(f32[8,32,512]{2,1,0:T(8,128)} %get-tuple-element.42), channel_id=1, source_target_pairs={{0,6},{1,7},{2,0},{3,1},{4,2},{5,3},{6,4},{7,5},{8,14},{9,15},{10,... | collective-permute-start | bytes 1572872 | tf_op jit(solution)/shard_map/ppermute | solution.py:201
  42.7 29.0 %collective-permute-start.2 = (f32[8,32,512]{2,1,0:T(8,128)}, f32[8,32,512]{2,1,0:T(8,128)}, u32[]{:S(2)}, u32[]{:S(2)}) collective-permute-start(f32[8,32,512]{2,1,0:T(8,128)} %get-tuple-element.41), channel_id=1, source_target_pairs={{0,2},{1,3},{2,4},{3,5},{4,6},{5,7},{6,0},{7,1},{8,10},{9,11},{10,... | collective-permute-start | bytes 1572872 | tf_op jit(solution)/shard_map/ppermute | solution.py:201
  44.7 26.5 %all-to-all-start.1 = ((bf16[16,32,512]{2,1,0:T(8,128)(2,1)}), bf16[16,32,512]{2,1,0:T(8,128)(2,1)}, u32[]{:S(2)}, u32[]{:S(2)}) async-start(bf16[16,32,512]{2,1,0:T(8,128)(2,1)} %feature_rows.1), calls=%async_computation.1 | async-start | bytes 1048576 | tf_op jit(solution)/shard_map/all_to_all | solution.py:207
  54.5 15.9 %collective-permute-start.6 = (bf16[8,32,512]{2,1,0:T(8,128)(2,1)S(1)}, bf16[8,32,512]{2,1,0:T(8,128)(2,1)S(1)}, u32[]{:S(2)}, u32[]{:S(2)}) collective-permute-start(bf16[8,32,512]{2,1,0:T(8,128)(2,1)S(1)} %slice.78), channel_id=1, source_target_pairs={{0,2},{1,3},{2,4},{3,5},{4,6},{5,7},{6,0},{7,1},{8,10},{9,11},{10,... | collective-permute-start | bytes 786440 | tf_op jit(solution)/shard_map/ppermute | solution.py:201
  55.6 15.5 %collective-permute-start.7 = (bf16[8,32,512]{2,1,0:T(8,128)(2,1)S(1)}, bf16[8,32,512]{2,1,0:T(8,128)(2,1)}, u32[]{:S(2)}, u32[]{:S(2)}) collective-permute-start(bf16[8,32,512]{2,1,0:T(8,128)(2,1)S(1)} %slice.79), channel_id=1, source_target_pairs={{0,6},{1,7},{2,0},{3,1},{4,2},{5,3},{6,4},{7,5},{8,14},{9,15},{10,... | collective-permute-start | bytes 786440 | tf_op jit(solution)/shard_map/ppermute | solution.py:201
  70.4 10.0 %copy-start.3 = (bf16[8,32,512]{2,1,0:T(8,128)(2,1)}, bf16[8,32,512]{2,1,0:T(8,128)(2,1)S(1)}, u32[]{:S(2)}) copy-start(bf16[8,32,512]{2,1,0:T(8,128)(2,1)S(1)} %collective-permute-done.6.a2a) | copy-start | bytes 786436
  70.4 5.1 %collective-permute-start.8 = (bf16[16,32,512]{2,1,0:T(8,128)(2,1)}, bf16[16,32,512]{2,1,0:T(8,128)(2,1)}, u32[]{:S(2)}, u32[]{:S(2)}) collective-permute-start(bf16[16,32,512]{2,1,0:T(8,128)(2,1)} %copy-done), channel_id=1, source_target_pairs={{0,1},{1,0},{2,3},{3,2},{4,5},{5,4},{6,7},{7,6},{8,9},{9,8},{10,11... | collective-permute-start | bytes 1572872 | tf_op jit(solution)/shard_map/ppermute | solution.py:204
  71.1 10.8 %collective-permute-start.9 = (bf16[16,32,512]{2,1,0:T(8,128)(2,1)}, bf16[16,32,512]{2,1,0:T(8,128)(2,1)}, u32[]{:S(2)}, u32[]{:S(2)}) collective-permute-start(bf16[16,32,512]{2,1,0:T(8,128)(2,1)} %collective-permute-done.4.am), channel_id=1, source_target_pairs={{0,1},{1,0},{2,3},{3,2},{4,5},{5,4},{6,7},{7,6},{8,9},{9,8},{10,11... | collective-permute-start | bytes 1572872 | tf_op jit(solution)/shard_map/ppermute | solution.py:204
  71.3 10.7 %collective-permute-start.10 = (bf16[16,32,512]{2,1,0:T(8,128)(2,1)}, bf16[16,32,512]{2,1,0:T(8,128)(2,1)}, u32[]{:S(2)}, u32[]{:S(2)}) collective-permute-start(bf16[16,32,512]{2,1,0:T(8,128)(2,1)} %collective-permute-done.5.ap), channel_id=1, source_target_pairs={{0,1},{1,0},{2,3},{3,2},{4,5},{5,4},{6,7},{7,6},{8,9},{9,8},{10,11... | collective-permute-start | bytes 1572872 | tf_op jit(solution)/shard_map/ppermute | solution.py:204
  71.7 5.1 %collective-permute-start.11 = (bf16[8,32,512]{2,1,0:T(8,128)(2,1)S(1)}, bf16[8,32,512]{2,1,0:T(8,128)(2,1)S(1)}, u32[]{:S(2)}, u32[]{:S(2)}) collective-permute-start(bf16[8,32,512]{2,1,0:T(8,128)(2,1)S(1)} %collective-permute-done.6.a2a), channel_id=1, source_target_pairs={{0,1},{1,0},{2,3},{3,2},{4,5},{5,4},{6,7},{7,6},{8,9},{9,8},{10,11... | collective-permute-start | bytes 786440 | tf_op jit(solution)/shard_map/ppermute | solution.py:204
  71.9 8.5 %collective-permute-start.12 = (bf16[8,32,512]{2,1,0:T(8,128)(2,1)}, bf16[8,32,512]{2,1,0:T(8,128)(2,1)S(1)}, u32[]{:S(2)}, u32[]{:S(2)}) collective-permute-start(bf16[8,32,512]{2,1,0:T(8,128)(2,1)} %collective-permute-done.7.a2b), channel_id=1, source_target_pairs={{0,1},{1,0},{2,3},{3,2},{4,5},{5,4},{6,7},{7,6},{8,9},{9,8},{10,11... | collective-permute-start | bytes 786440 | tf_op jit(solution)/shard_map/ppermute | solution.py:204
  75.5 21.9 %collective-permute-start.13 = (bf16[16,32,512]{2,1,0:T(8,128)(2,1)}, bf16[16,32,512]{2,1,0:T(8,128)(2,1)S(1)}, u32[]{:S(2)}, u32[]{:S(2)}) collective-permute-start(bf16[16,32,512]{2,1,0:T(8,128)(2,1)} %all-to-all-done.1.a0), channel_id=1, source_target_pairs={{0,2},{1,3},{2,4},{3,5},{4,6},{5,7},{6,0},{7,1},{8,10},{9,11},{10,... | collective-permute-start | bytes 1572872 | tf_op jit(solution)/shard_map/ppermute | solution.py:201
  76.7 0.7 copy-start.4
  77.4 20.0 %collective-permute-start.14 = (bf16[16,32,512]{2,1,0:T(8,128)(2,1)}, bf16[16,32,512]{2,1,0:T(8,128)(2,1)}, u32[]{:S(2)}, u32[]{:S(2)}) collective-permute-start(bf16[16,32,512]{2,1,0:T(8,128)(2,1)} %all-to-all-done.1.a0), channel_id=1, source_target_pairs={{0,6},{1,7},{2,0},{3,1},{4,2},{5,3},{6,4},{7,5},{8,14},{9,15},{10,... | collective-permute-start | bytes 1572872 | tf_op jit(solution)/shard_map/ppermute | solution.py:201
  80.4 0.7 copy-start.5
  81.1 19.5 %collective-permute-start.17 = (bf16[16,32,512]{2,1,0:T(8,128)(2,1)}, bf16[16,32,512]{2,1,0:T(8,128)(2,1)}, u32[]{:S(2)}, u32[]{:S(2)}) collective-permute-start(bf16[16,32,512]{2,1,0:T(8,128)(2,1)} %all-to-all-done.1.a0), channel_id=1, source_target_pairs={{0,1},{1,0},{2,3},{3,2},{4,5},{5,4},{6,7},{7,6},{8,9},{9,8},{10,11... | collective-permute-start | bytes 1572872 | tf_op jit(solution)/shard_map/ppermute | solution.py:204
  82.0 30.8 %collective-permute-start.15 = (f32[16,32,512]{2,1,0:T(8,128)}, f32[16,32,512]{2,1,0:T(8,128)}, u32[]{:S(2)}, u32[]{:S(2)}) collective-permute-start(f32[16,32,512]{2,1,0:T(8,128)} %get-tuple-element.60), channel_id=1, source_target_pairs={{0,2},{1,3},{2,4},{3,5},{4,6},{5,7},{6,0},{7,1},{8,10},{9,11},{10,... | collective-permute-start | bytes 3145736 | tf_op jit(solution)/shard_map/ppermute | solution.py:201
  82.0 31.2 %collective-permute-start.16 = (f32[16,32,512]{2,1,0:T(8,128)}, f32[16,32,512]{2,1,0:T(8,128)}, u32[]{:S(2)}, u32[]{:S(2)}) collective-permute-start(f32[16,32,512]{2,1,0:T(8,128)} %get-tuple-element.61), channel_id=1, source_target_pairs={{0,6},{1,7},{2,0},{3,1},{4,2},{5,3},{6,4},{7,5},{8,14},{9,15},{10,... | collective-permute-start | bytes 3145736 | tf_op jit(solution)/shard_map/ppermute | solution.py:201
  97.4 0.8 copy-start.1
  97.4 3.2 %collective-permute-start.18 = (bf16[16,32,512]{2,1,0:T(8,128)(2,1)S(1)}, bf16[16,32,512]{2,1,0:T(8,128)(2,1)S(1)}, u32[]{:S(2)}, u32[]{:S(2)}) collective-permute-start(bf16[16,32,512]{2,1,0:T(8,128)(2,1)S(1)} %collective-permute-done.13.am), channel_id=1, source_target_pairs={{0,1},{1,0},{2,3},{3,2},{4,5},{5,4},{6,7},{7,6},{8,9},{9,8},{10,11... | collective-permute-start | bytes 1572872 | tf_op jit(solution)/shard_map/ppermute | solution.py:204
  98.1 6.0 %collective-permute-start.19 = (bf16[16,32,512]{2,1,0:T(8,128)(2,1)}, bf16[16,32,512]{2,1,0:T(8,128)(2,1)}, u32[]{:S(2)}, u32[]{:S(2)}) collective-permute-start(bf16[16,32,512]{2,1,0:T(8,128)(2,1)} %collective-permute-done.14.ap), channel_id=1, source_target_pairs={{0,1},{1,0},{2,3},{3,2},{4,5},{5,4},{6,7},{7,6},{8,9},{9,8},{10,11... | collective-permute-start | bytes 1572872 | tf_op jit(solution)/shard_map/ppermute | solution.py:204
  100.6 22.6 %collective-permute-start.20 = (bf16[8,32,512]{2,1,0:T(8,128)(2,1)}, bf16[8,32,512]{2,1,0:T(8,128)(2,1)S(1)}, u32[]{:S(2)}, u32[]{:S(2)}) collective-permute-start(bf16[8,32,512]{2,1,0:T(8,128)(2,1)} %slice.70), channel_id=1, source_target_pairs={{0,2},{1,3},{2,4},{3,5},{4,6},{5,7},{6,0},{7,1},{8,10},{9,11},{10,... | collective-permute-start | bytes 786440 | tf_op jit(solution)/shard_map/ppermute | solution.py:201
  100.6 0.8 copy-start.2
  101.4 24.5 %collective-permute-start.21 = (bf16[8,32,512]{2,1,0:T(8,128)(2,1)}, bf16[8,32,512]{2,1,0:T(8,128)(2,1)}, u32[]{:S(2)}, u32[]{:S(2)}) collective-permute-start(bf16[8,32,512]{2,1,0:T(8,128)(2,1)} %slice.71), channel_id=1, source_target_pairs={{0,6},{1,7},{2,0},{3,1},{4,2},{5,3},{6,4},{7,5},{8,14},{9,15},{10,... | collective-permute-start | bytes 786440 | tf_op jit(solution)/shard_map/ppermute | solution.py:201
  116.2 19.2 %all-to-all-start.2 = ((bf16[16,32,512]{2,1,0:T(8,128)(2,1)}), bf16[16,32,512]{2,1,0:T(8,128)(2,1)S(1)}, u32[]{:S(2)}, u32[]{:S(2)}) async-start(bf16[16,32,512]{2,1,0:T(8,128)(2,1)} %fusion.3), calls=%async_computation.2 | async-start | bytes 1048576 | tf_op jit(solution)/shard_map/all_to_all | solution.py:207
  123.2 4.5 %copy-start.6 = (bf16[8,32,512]{2,1,0:T(8,128)(2,1)}, bf16[8,32,512]{2,1,0:T(8,128)(2,1)S(1)}, u32[]{:S(2)}) copy-start(bf16[8,32,512]{2,1,0:T(8,128)(2,1)S(1)} %collective-permute-done.20.a2a) | copy-start | bytes 786436
  123.2 3.9 %collective-permute-start.22 = (bf16[8,32,512]{2,1,0:T(8,128)(2,1)S(1)}, bf16[8,32,512]{2,1,0:T(8,128)(2,1)S(1)}, u32[]{:S(2)}, u32[]{:S(2)}) collective-permute-start(bf16[8,32,512]{2,1,0:T(8,128)(2,1)S(1)} %collective-permute-done.20.a2a), channel_id=1, source_target_pairs={{0,1},{1,0},{2,3},{3,2},{4,5},{5,4},{6,7},{7,6},{8,9},{9,8},{10,11... | collective-permute-start | bytes 786440 | tf_op jit(solution)/shard_map/ppermute | solution.py:204
  125.9 1.7 %collective-permute-start.23 = (bf16[8,32,512]{2,1,0:T(8,128)(2,1)}, bf16[8,32,512]{2,1,0:T(8,128)(2,1)S(1)}, u32[]{:S(2)}, u32[]{:S(2)}) collective-permute-start(bf16[8,32,512]{2,1,0:T(8,128)(2,1)} %collective-permute-done.21.a2b), channel_id=1, source_target_pairs={{0,1},{1,0},{2,3},{3,2},{4,5},{5,4},{6,7},{7,6},{8,9},{9,8},{10,11... | collective-permute-start | bytes 786440 | tf_op jit(solution)/shard_map/ppermute | solution.py:204
  127.1 0.7 copy-start.7
  127.8 0.7 copy-start.8
Sparse Core Ops, SparseCore 0:
  10.1 79.6 all-gather.1

commit v9 on v8

--- a/solution.py
+++ b/solution.py
@@ -261,8 +261,9 @@
 
     cm, cp = along_y(class_rows, 1), along_y(class_rows, -1)
 
-    q1 = jnp.concatenate([keep[1, :8] + rest[1, :8] + from_a, keep[1, 8:] + rest[1, 8:]], axis=0)
-    q3 = jnp.concatenate([keep[3, :8] + rest[2, :8], keep[3, 8:] + rest[2, 8:] + from_b], axis=0)
+    p0, p1, p3 = barrier((keep[0] + rest[0], keep[1] + rest[1], keep[3] + rest[2]))
+    q1 = jnp.concatenate([p1[:8] + from_a, p1[8:]], axis=0)
+    q3 = jnp.concatenate([p3[:8], p3[8:] + from_b], axis=0)
     q1, q3, x_pieces = barrier((q1, q3, x_pieces))
     sum_m, sum_p = along_y(q1, 1), along_y(q3, -1)
 
@@ -307,7 +308,7 @@
     )(pos, *near, cot_groups)
 
     sum_m, sum_p, near_grad = barrier((sum_m, sum_p, near_grad))
-    context_sum = (keep[0] + rest[0] + sum_m + sum_p).astype(BF16)
+    context_sum = (p0 + sum_m + sum_p).astype(BF16)
     context_grad = exchange(context_sum)
 
     weight_grad = pl.pallas_call(

time: 144 us -> 146 us (1.014)
  waiting for transfers between devices: 21.3 us -> 16.6 us
  starting transfers between devices: 45.1 us -> 49.6 us
  other arithmetic: 10.2 us -> 12.1 us
    ppermute x12, waiting for transfers between devices: 16.5 us -> 11.8 us  [along_y(): return lax.ppermute(x, 'mp', [(i, (i + 2 * step) % 8) for i in range(8)])]
    ppermute x12, starting transfers between devices: 7.6 us -> 10.2 us  [other_core(): return lax.ppermute(x, 'mp', [(i, i ^ 1) for i in range(8)])]
    add x2, other arithmetic: 3.31 us -> 5.41 us  [the longest x1 3.83 us: on_device(): keep[3] + rest[2]]
    ppermute x12, starting transfers between devices: 15.1 us -> 17 us  [along_y(): return lax.ppermute(x, 'mp', [(i, (i + 2 * step) % 8) for i in range(8)])]
    unnamed x19 -> x23, local copies, waits for them, and re-layouts: 3.83 us -> 4.47 us
  transfers between devices with their start and end apart: 28 -> 28, of which waited for: 7 -> 7; matrix products, arithmetic and copies ran while one was open for 10% -> 11% of each run, Pallas kernels for 31% -> 30%
where the time goes in v9:
time: 146 us; the launch traced here: 145 us
  starting transfers between devices  49.6 us (34%)
  Pallas kernels  44.1 us (30%)
  waiting for transfers between devices  16.6 us (11%)
  between operations  14.2 us (10%)
  other arithmetic  12.1 us (8%)
  local copies, waits for them, and re-layouts  7.88 us (5%)
    all_to_all x3, starting transfers between devices, exchange(): return lax.all_to_all(x, 'seq', split_axis=0, concat_axis=0, tiled=True)  22.4 us
    ppermute x12, starting transfers between devices, along_y(): return lax.ppermute(x, 'mp', [(i, (i + 2 * step) % 8) for i in range(8)])  17 us
    pallas_call x1, Pallas kernels, on_device(): pl.pallas_call(partial_kernel, in_specs=scalars + [anywhere] * 2, out_spe...  15.7 us
    pallas_call x1, Pallas kernels, on_device(): pl.pallas_call(out_kernel, in_specs=scalars[:1] + [anywhere] * 11, out_sh...  12.7 us
    ppermute x12, waiting for transfers between devices, along_y(): return lax.ppermute(x, 'mp', [(i, (i + 2 * step) % 8) for i in range(8)])  11.8 us
    ppermute x12, starting transfers between devices, other_core(): return lax.ppermute(x, 'mp', [(i, i ^ 1) for i in range(8)])  10.2 us
    pallas_call x1, Pallas kernels, on_device(): pl.pallas_call(functools.partial(far_grad_kernel, 1.0 / math.sqrt(4096)),...  6.96 us
    pallas_call x1, Pallas kernels, on_device(): pl.pallas_call(near_grad_kernel, in_specs=scalars[:1] + [anywhere] * 7, o...  6.58 us
  transfers between devices with their start and end apart: 28, of which 7 were waited for; matrix products, arithmetic and copies ran while one was open for 11% of the time, Pallas kernels for 30%

profile of v9, /device:TPU:1, one launch (start us, length us, event | category | flops | bytes accessed | tf_op | source)
XLA Modules:
  0.0 144.6 jit_solution(10938674983670990443)
XLA Ops:
  7.2 0.7 all-gather.2.cloned.1.call-update
  7.9 8.4 %all-to-all-start = ((bf16[16,32,512]{2,1,0:T(8,128)(2,1)}), bf16[16,32,512]{2,1,0:T(8,128)(2,1)S(1)}, u32[]{:S(2)}, u32[]{:S(2)}) async-start(bf16[16,32,512]{2,1,0:T(8,128)(2,1)} %x_ref), calls=%async_computation | async-start | bytes 1048576 | tf_op jit(solution)/shard_map/all_to_all | solution.py:207
  16.3 15.7 %partial_context_grad.1 = (f32[4,16,32,512]{3,2,1,0:T(8,128)}, f32[16,32,512]{2,1,0:T(8,128)}, f32[3,16,32,512]{3,2,1,0:T(8,128)}, bf16[8,1024,1024]{2,1,0:T(8,128)(2,1)}) custom-call(s32[1]{0:T(128)} %bitcast.pos, s32[8,8,34]{2,1,0:T(8,128)} %rows.3, s32[8,8,34]{2,1,0:T(8,128)} %cols.3, s32[8,8]{1,0:T(8,128)} %live.3, bf16[4,2,32,1024]{3,2,1,0:T(8,128)(2,1)} %bitcast.15, ...), custom_call_target="tpu_custom_call" | custom-call | flops 4300000256 | bytes 45000000 | tf_op jit(solution)/shard_map/partial_context_grad/pallas_call | solution.py:215
  32.1 1.0 collective-permute-start
  33.1 2.5 %collective-permute-done = f32[16,32,512]{2,1,0:T(8,128)S(1)} collective-permute-done((f32[16,32,512]{2,1,0:T(8,128)}, f32[16,32,512]{2,1,0:T(8,128)S(1)}, u32[]{:S(2)}, u32[]{:S(2)}) %collective-permute-start) | collective-permute-done | bytes 1048608 | tf_op jit(solution)/shard_map/ppermute | solution.py:204
  35.6 2.4 %slice_add_fusion.3 = (f32[8,32,512]{2,1,0:T(8,128)}, f32[8,32,512]{2,1,0:T(8,128)}) fusion(f32[16,32,512]{2,1,0:T(8,128)S(1)} %collective-permute-done, f32[4,16,32,512]{3,2,1,0:T(8,128)} %get-tuple-element.38), kind=kLoop, calls=%fused_computation.9 | loop fusion | flops 262144 | bytes 3145728 | tf_op jit(solution)/shard_map/add | solution.py:243
  38.0 0.4 collective-permute-start.1
  38.4 1.3 collective-permute-start.4
  39.7 1.4 %collective-permute-start.5 = (bf16[16,32,512]{2,1,0:T(8,128)(2,1)}, bf16[16,32,512]{2,1,0:T(8,128)(2,1)}, u32[]{:S(2)}, u32[]{:S(2)}) collective-permute-start(bf16[16,32,512]{2,1,0:T(8,128)(2,1)} %copy-done.1), channel_id=1, source_target_pairs={{0,6},{1,7},{2,0},{3,1},{4,2},{5,3},{6,4},{7,5},{8,14},{9,15},{10,... | collective-permute-start | bytes 1572872 | tf_op jit(solution)/shard_map/ppermute | solution.py:201
  41.1 2.1 %feature_rows.1 = bf16[16,32,512]{2,1,0:T(8,128)(2,1)} custom-call(bf16[16,32,512]{2,1,0:T(8,128)(2,1)} %x_ref), custom_call_target="tpu_custom_call" | custom-call | tf_op jit(solution)/shard_map/feature_rows/pallas_call | solution.py:249
  43.2 7.0 %all-to-all-start.1 = ((bf16[16,32,512]{2,1,0:T(8,128)(2,1)}), bf16[16,32,512]{2,1,0:T(8,128)(2,1)}, u32[]{:S(2)}, u32[]{:S(2)}) async-start(bf16[16,32,512]{2,1,0:T(8,128)(2,1)} %feature_rows.1), calls=%async_computation.1 | async-start | bytes 1048576 | tf_op jit(solution)/shard_map/all_to_all | solution.py:207
  50.2 3.3 %collective-permute-done.4.am = bf16[16,32,512]{2,1,0:T(8,128)(2,1)} collective-permute-done((bf16[16,32,512]{2,1,0:T(8,128)(2,1)}, bf16[16,32,512]{2,1,0:T(8,128)(2,1)}, u32[]{:S(2)}, u32[]{:S(2)}) %collective-permute-start.4) | collective-permute-done | bytes 524320 | tf_op jit(solution)/shard_map/ppermute | solution.py:201
  53.4 1.0 slice.77
  54.5 1.0 slice.78
  55.5 2.7 %collective-permute-start.7 = (bf16[8,32,512]{2,1,0:T(8,128)(2,1)S(1)}, bf16[8,32,512]{2,1,0:T(8,128)(2,1)}, u32[]{:S(2)}, u32[]{:S(2)}) collective-permute-start(bf16[8,32,512]{2,1,0:T(8,128)(2,1)S(1)} %slice.78), channel_id=1, source_target_pairs={{0,6},{1,7},{2,0},{3,1},{4,2},{5,3},{6,4},{7,5},{8,14},{9,15},{10,... | collective-permute-start | bytes 786440 | tf_op jit(solution)/shard_map/ppermute | solution.py:201
  58.2 2.7 %collective-permute-start.3 = (f32[8,32,512]{2,1,0:T(8,128)}, f32[8,32,512]{2,1,0:T(8,128)}, u32[]{:S(2)}, u32[]{:S(2)}) collective-permute-start(f32[8,32,512]{2,1,0:T(8,128)} %get-tuple-element.47), channel_id=1, source_target_pairs={{0,6},{1,7},{2,0},{3,1},{4,2},{5,3},{6,4},{7,5},{8,14},{9,15},{10,... | collective-permute-start | bytes 1572872 | tf_op jit(solution)/shard_map/ppermute | solution.py:201
  60.9 1.9 %collective-permute-done.6.a2a = bf16[8,32,512]{2,1,0:T(8,128)(2,1)S(1)} collective-permute-done((bf16[8,32,512]{2,1,0:T(8,128)(2,1)S(1)}, bf16[8,32,512]{2,1,0:T(8,128)(2,1)S(1)}, u32[]{:S(2)}, u32[]{:S(2)}) %collective-permute-start.6) | collective-permute-done | bytes 262176 | tf_op jit(solution)/shard_map/ppermute | solution.py:201
  62.7 3.1 %collective-permute-start.8 = (bf16[16,32,512]{2,1,0:T(8,128)(2,1)}, bf16[16,32,512]{2,1,0:T(8,128)(2,1)}, u32[]{:S(2)}, u32[]{:S(2)}) collective-permute-start(bf16[16,32,512]{2,1,0:T(8,128)(2,1)} %copy-done.1), channel_id=1, source_target_pairs={{0,1},{1,0},{2,3},{3,2},{4,5},{5,4},{6,7},{7,6},{8,9},{9,8},{10,11... | collective-permute-start | bytes 1572872 | tf_op jit(solution)/shard_map/ppermute | solution.py:204
  65.8 0.6 collective-permute-start.9
  66.4 1.6 %copy-done = f32[3,16,32,512]{3,2,1,0:T(8,128)} copy-done((f32[3,16,32,512]{3,2,1,0:T(8,128)}, f32[3,16,32,512]{3,2,1,0:T(8,128)S(1)}, u32[]{:S(2)}) %copy-start) | copy-done | bytes 3145752
  68.0 0.5 collective-permute-start.10
  68.5 3.8 %fusion = (f32[16,32,512]{2,1,0:T(8,128)S(1)}, f32[16,32,512]{2,1,0:T(8,128)S(1)}, f32[16,32,512]{2,1,0:T(8,128)S(1)}) fusion(f32[3,16,32,512]{3,2,1,0:T(8,128)} %copy-done, f32[4,16,32,512]{3,2,1,0:T(8,128)} %get-tuple-element.38), kind=kLoop, calls=%fused_computation.1 | loop fusion | flops 786432 | bytes 9437184 | tf_op jit(solution)/shard_map/add | solution.py:264
  72.4 1.6 %collective-permute-done.2 = f32[8,32,512]{2,1,0:T(8,128)} collective-permute-done((f32[8,32,512]{2,1,0:T(8,128)}, f32[8,32,512]{2,1,0:T(8,128)}, u32[]{:S(2)}, u32[]{:S(2)}) %collective-permute-start.2) | collective-permute-done | bytes 524320 | tf_op jit(solution)/shard_map/ppermute | solution.py:201
  74.0 1.8 %collective-permute-start.11 = (bf16[8,32,512]{2,1,0:T(8,128)(2,1)S(1)}, bf16[8,32,512]{2,1,0:T(8,128)(2,1)}, u32[]{:S(2)}, u32[]{:S(2)}) collective-permute-start(bf16[8,32,512]{2,1,0:T(8,128)(2,1)S(1)} %collective-permute-done.6.a2a), channel_id=1, source_target_pairs={{0,1},{1,0},{2,3},{3,2},{4,5},{5,4},{6,7},{7,6},{8,9},{9,8},{10,11... | collective-permute-start | bytes 786440 | tf_op jit(solution)/shard_map/ppermute | solution.py:204
  76.1 1.6 %slice_add_fusion.6 = (f32[8,32,512]{2,1,0:T(8,128)S(1)}, f32[8,32,512]{2,1,0:T(8,128)S(1)}, f32[8,32,512]{2,1,0:T(8,128)S(1)}, f32[8,32,512]{2,1,0:T(8,128)S(1)}) fusion(f32[8,32,512]{2,1,0:T(8,128)} %collective-permute-done.2, f32[16,32,512]{2,1,0:T(8,128)S(1)} %get-tuple-element.44, f32[8,32,512]{2,1,0:T(8,128)} %collective-permute-done.3, ...), kind=kLoop, calls=%fused_computation.12 | loop fusion | flops 262144 | bytes 5242880 | tf_op jit(solution)/shard_map/add | solution.py:265
  77.6 1.0 pad_maximum_fusion
  78.7 0.8 collective-permute-start.13
  79.5 2.7 %collective-permute-start.14 = (bf16[16,32,512]{2,1,0:T(8,128)(2,1)}, bf16[16,32,512]{2,1,0:T(8,128)(2,1)S(1)}, u32[]{:S(2)}, u32[]{:S(2)}) collective-permute-start(bf16[16,32,512]{2,1,0:T(8,128)(2,1)} %all-to-all-done.1.a0), channel_id=1, source_target_pairs={{0,6},{1,7},{2,0},{3,1},{4,2},{5,3},{6,4},{7,5},{8,14},{9,15},{10,... | collective-permute-start | bytes 1572872 | tf_op jit(solution)/shard_map/ppermute | solution.py:201
  82.1 1.0 pad_maximum_fusion.1
  83.2 0.3 collective-permute-start.17
  83.5 0.4 copy-done.7
  83.9 2.7 %collective-permute-start.16 = (f32[16,32,512]{2,1,0:T(8,128)}, f32[16,32,512]{2,1,0:T(8,128)}, u32[]{:S(2)}, u32[]{:S(2)}) collective-permute-start(f32[16,32,512]{2,1,0:T(8,128)} %pad_maximum_fusion.1), channel_id=1, source_target_pairs={{0,6},{1,7},{2,0},{3,1},{4,2},{5,3},{6,4},{7,5},{8,14},{9,15},{10,... | collective-permute-start | bytes 3145736 | tf_op jit(solution)/shard_map/ppermute | solution.py:201
  86.6 12.7 %outputs.1 = bf16[256,1024]{1,0:T(8,128)(2,1)} custom-call(s32[1]{0:T(128)} %bitcast.pos, bf16[16,32,512]{2,1,0:T(8,128)(2,1)} %copy-done.1, bf16[16,32,512]{2,1,0:T(8,128)(2,1)} %collective-permute-done.4.am, bf16[16,32,512]{2,1,0:T(8,128)(2,1)} %collective-permute-done.5.ap, bf16[8,32,512]{2,1,0:T(8,128)(2,1)} %copy-done.6, ...), custom_call_target="tpu_custom_call" | custom-call | flops 4300000256 | bytes 30000000 | tf_op jit(solution)/shard_map/outputs/pallas_call | solution.py:270
  99.4 0.9 collective-permute-start.18
  100.4 0.7 slice.70
  101.1 0.7 slice.71
  101.9 0.8 copy-done.5
  102.7 2.7 %collective-permute-start.21 = (bf16[8,32,512]{2,1,0:T(8,128)(2,1)}, bf16[8,32,512]{2,1,0:T(8,128)(2,1)}, u32[]{:S(2)}, u32[]{:S(2)}) collective-permute-start(bf16[8,32,512]{2,1,0:T(8,128)(2,1)} %slice.71), channel_id=1, source_target_pairs={{0,6},{1,7},{2,0},{3,1},{4,2},{5,3},{6,4},{7,5},{8,14},{9,15},{10,... | collective-permute-start | bytes 786440 | tf_op jit(solution)/shard_map/ppermute | solution.py:201
  105.4 6.6 %near_weight_grad.1.near = f32[64,8,1024]{2,1,0:T(8,128)} custom-call(s32[1]{0:T(128)} %bitcast.pos, bf16[16,32,512]{2,1,0:T(8,128)(2,1)} %all-to-all-done.1.a0, bf16[16,32,512]{2,1,0:T(8,128)(2,1)} %copy-done.2, bf16[16,32,512]{2,1,0:T(8,128)(2,1)} %copy-done.3, bf16[16,32,512]{2,1,0:T(8,128)(2,1)} %collective-permute-done.17.b0, ...), custom_call_target="tpu_custom_call" | custom-call | flops 3200000000 | bytes 25000000 | tf_op jit(solution)/shard_map/near_weight_grad/pallas_call | solution.py:292
  112.0 5.1 %collective-permute-done.15 = f32[16,32,512]{2,1,0:T(8,128)S(1)} collective-permute-done((f32[16,32,512]{2,1,0:T(8,128)}, f32[16,32,512]{2,1,0:T(8,128)S(1)}, u32[]{:S(2)}, u32[]{:S(2)}) %collective-permute-start.15) | collective-permute-done | bytes 1048608 | tf_op jit(solution)/shard_map/ppermute | solution.py:201
  117.0 2.3 %add_convert_fusion = bf16[16,32,512]{2,1,0:T(8,128)(2,1)} fusion(f32[16,32,512]{2,1,0:T(8,128)} %collective-permute-done.16, f32[16,32,512]{2,1,0:T(8,128)S(1)} %get-tuple-element.65, f32[16,32,512]{2,1,0:T(8,128)S(1)} %collective-permute-done.15), kind=kLoop, calls=%fused_computation.8 | loop fusion | flops 786432 | bytes 3670016 | tf_op jit(solution)/shard_map/convert_element_type | solution.py:311
  119.3 7.0 %all-to-all-start.2 = ((bf16[16,32,512]{2,1,0:T(8,128)(2,1)}), bf16[16,32,512]{2,1,0:T(8,128)(2,1)S(1)}, u32[]{:S(2)}, u32[]{:S(2)}) async-start(bf16[16,32,512]{2,1,0:T(8,128)(2,1)} %add_convert_fusion), calls=%async_computation.2 | async-start | bytes 1048576 | tf_op jit(solution)/shard_map/all_to_all | solution.py:207
  126.3 1.1 collective-permute-start.22
  127.5 1.1 collective-permute-done.22.b2a
  128.5 0.6 collective-permute-done.23.b2b
  129.3 0.7 copy-done.10
  130.0 7.0 %far_weight_grad.1 = bf16[1,8,34,8,128]{4,3,2,1,0:T(8,128)(2,1)} custom-call(s32[1]{0:T(128)} %bitcast.pos, s32[8,8,34]{2,1,0:T(8,128)} %rows.3, s32[8,8,34]{2,1,0:T(8,128)} %cols.3, s32[8,8]{1,0:T(8,128)} %live.3, bf16[8,32,512]{2,1,0:T(8,128)(2,1)} %copy-done.8, bf16[8,32,512]{2,1,0:T(8,128)(2,1)} %collective-permute-done.21.a2b, ...), custom_call_target="tpu_custom_call" | custom-call | flops 1100000000 | bytes 18000000 | tf_op jit(solution)/shard_map/far_weight_grad/pallas_call | solution.py:314
  136.9 0.8 copy.10
  (47 shorter events, 0.8 us)
Async XLA Ops:
  7.2 98.2 %all-gather.2.cloned.1.call-start = ((), (), s32[]{:S(2)}) async-start(), calls=%async_computation.3 | async-start | bytes 8912896 | tf_op jit(solution)/shard_map/all_gather | solution.py:209
  7.9 24.2 %all-to-all-start = ((bf16[16,32,512]{2,1,0:T(8,128)(2,1)}), bf16[16,32,512]{2,1,0:T(8,128)(2,1)S(1)}, u32[]{:S(2)}, u32[]{:S(2)}) async-start(bf16[16,32,512]{2,1,0:T(8,128)(2,1)} %x_ref), calls=%async_computation | async-start | bytes 1048576 | tf_op jit(solution)/shard_map/all_to_all | solution.py:207
  32.1 5.9 %copy-start.1 = (bf16[16,32,512]{2,1,0:T(8,128)(2,1)}, bf16[16,32,512]{2,1,0:T(8,128)(2,1)S(1)}, u32[]{:S(2)}) copy-start(bf16[16,32,512]{2,1,0:T(8,128)(2,1)S(1)} %all-to-all-done.a0) | copy-start | bytes 1572868
  32.1 3.5 %collective-permute-start = (f32[16,32,512]{2,1,0:T(8,128)}, f32[16,32,512]{2,1,0:T(8,128)S(1)}, u32[]{:S(2)}, u32[]{:S(2)}) collective-permute-start(f32[16,32,512]{2,1,0:T(8,128)} %get-tuple-element.40), channel_id=1, source_target_pairs={{0,1},{1,0},{2,3},{3,2},{4,5},{5,4},{6,7},{7,6},{8,9},{9,8},{10,11... | collective-permute-start | bytes 3145736 | tf_op jit(solution)/shard_map/ppermute | solution.py:204
  38.0 28.4 %collective-permute-start.1 = (f32[3,16,32,512]{3,2,1,0:T(8,128)}, f32[3,16,32,512]{3,2,1,0:T(8,128)S(1)}, u32[]{:S(2)}, u32[]{:S(2)}) collective-permute-start(f32[3,16,32,512]{3,2,1,0:T(8,128)} %get-tuple-element.43), channel_id=1, source_target_pairs={{0,1},{1,0},{2,3},{3,2},{4,5},{5,4},{6,7},{7,6},{8,9},{9,8},{10,11... | collective-permute-start | bytes 9437192 | tf_op jit(solution)/shard_map/ppermute | solution.py:204
  38.4 15.0 %collective-permute-start.4 = (bf16[16,32,512]{2,1,0:T(8,128)(2,1)}, bf16[16,32,512]{2,1,0:T(8,128)(2,1)}, u32[]{:S(2)}, u32[]{:S(2)}) collective-permute-start(bf16[16,32,512]{2,1,0:T(8,128)(2,1)} %copy-done.1), channel_id=1, source_target_pairs={{0,2},{1,3},{2,4},{3,5},{4,6},{5,7},{6,0},{7,1},{8,10},{9,11},{10,... | collective-permute-start | bytes 1572872 | tf_op jit(solution)/shard_map/ppermute | solution.py:201
  39.7 14.8 %collective-permute-start.5 = (bf16[16,32,512]{2,1,0:T(8,128)(2,1)}, bf16[16,32,512]{2,1,0:T(8,128)(2,1)}, u32[]{:S(2)}, u32[]{:S(2)}) collective-permute-start(bf16[16,32,512]{2,1,0:T(8,128)(2,1)} %copy-done.1), channel_id=1, source_target_pairs={{0,6},{1,7},{2,0},{3,1},{4,2},{5,3},{6,4},{7,5},{8,14},{9,15},{10,... | collective-permute-start | bytes 1572872 | tf_op jit(solution)/shard_map/ppermute | solution.py:201
  43.2 23.2 %all-to-all-start.1 = ((bf16[16,32,512]{2,1,0:T(8,128)(2,1)}), bf16[16,32,512]{2,1,0:T(8,128)(2,1)}, u32[]{:S(2)}, u32[]{:S(2)}) async-start(bf16[16,32,512]{2,1,0:T(8,128)(2,1)} %feature_rows.1), calls=%async_computation.1 | async-start | bytes 1048576 | tf_op jit(solution)/shard_map/all_to_all | solution.py:207
  54.4 8.3 %collective-permute-start.6 = (bf16[8,32,512]{2,1,0:T(8,128)(2,1)S(1)}, bf16[8,32,512]{2,1,0:T(8,128)(2,1)S(1)}, u32[]{:S(2)}, u32[]{:S(2)}) collective-permute-start(bf16[8,32,512]{2,1,0:T(8,128)(2,1)S(1)} %slice.77), channel_id=1, source_target_pairs={{0,2},{1,3},{2,4},{3,5},{4,6},{5,7},{6,0},{7,1},{8,10},{9,11},{10,... | collective-permute-start | bytes 786440 | tf_op jit(solution)/shard_map/ppermute | solution.py:201
  55.5 10.3 %collective-permute-start.7 = (bf16[8,32,512]{2,1,0:T(8,128)(2,1)S(1)}, bf16[8,32,512]{2,1,0:T(8,128)(2,1)}, u32[]{:S(2)}, u32[]{:S(2)}) collective-permute-start(bf16[8,32,512]{2,1,0:T(8,128)(2,1)S(1)} %slice.78), channel_id=1, source_target_pairs={{0,6},{1,7},{2,0},{3,1},{4,2},{5,3},{6,4},{7,5},{8,14},{9,15},{10,... | collective-permute-start | bytes 786440 | tf_op jit(solution)/shard_map/ppermute | solution.py:201
  58.2 15.8 %collective-permute-start.2 = (f32[8,32,512]{2,1,0:T(8,128)}, f32[8,32,512]{2,1,0:T(8,128)}, u32[]{:S(2)}, u32[]{:S(2)}) collective-permute-start(f32[8,32,512]{2,1,0:T(8,128)} %get-tuple-element.45), channel_id=1, source_target_pairs={{0,2},{1,3},{2,4},{3,5},{4,6},{5,7},{6,0},{7,1},{8,10},{9,11},{10,... | collective-permute-start | bytes 1572872 | tf_op jit(solution)/shard_map/ppermute | solution.py:201
  58.2 17.6 %collective-permute-start.3 = (f32[8,32,512]{2,1,0:T(8,128)}, f32[8,32,512]{2,1,0:T(8,128)}, u32[]{:S(2)}, u32[]{:S(2)}) collective-permute-start(f32[8,32,512]{2,1,0:T(8,128)} %get-tuple-element.47), channel_id=1, source_target_pairs={{0,6},{1,7},{2,0},{3,1},{4,2},{5,3},{6,4},{7,5},{8,14},{9,15},{10,... | collective-permute-start | bytes 1572872 | tf_op jit(solution)/shard_map/ppermute | solution.py:201
  62.7 23.8 %copy-start.6 = (bf16[8,32,512]{2,1,0:T(8,128)(2,1)}, bf16[8,32,512]{2,1,0:T(8,128)(2,1)S(1)}, u32[]{:S(2)}) copy-start(bf16[8,32,512]{2,1,0:T(8,128)(2,1)S(1)} %collective-permute-done.6.a2a) | copy-start | bytes 786436
  62.7 15.9 %collective-permute-start.8 = (bf16[16,32,512]{2,1,0:T(8,128)(2,1)}, bf16[16,32,512]{2,1,0:T(8,128)(2,1)}, u32[]{:S(2)}, u32[]{:S(2)}) collective-permute-start(bf16[16,32,512]{2,1,0:T(8,128)(2,1)} %copy-done.1), channel_id=1, source_target_pairs={{0,1},{1,0},{2,3},{3,2},{4,5},{5,4},{6,7},{7,6},{8,9},{9,8},{10,11... | collective-permute-start | bytes 1572872 | tf_op jit(solution)/shard_map/ppermute | solution.py:204
  65.8 17.7 %collective-permute-start.9 = (bf16[16,32,512]{2,1,0:T(8,128)(2,1)}, bf16[16,32,512]{2,1,0:T(8,128)(2,1)}, u32[]{:S(2)}, u32[]{:S(2)}) collective-permute-start(bf16[16,32,512]{2,1,0:T(8,128)(2,1)} %collective-permute-done.4.am), channel_id=1, source_target_pairs={{0,1},{1,0},{2,3},{3,2},{4,5},{5,4},{6,7},{7,6},{8,9},{9,8},{10,11... | collective-permute-start | bytes 1572872 | tf_op jit(solution)/shard_map/ppermute | solution.py:204
  66.4 1.6 %copy-start = (f32[3,16,32,512]{3,2,1,0:T(8,128)}, f32[3,16,32,512]{3,2,1,0:T(8,128)S(1)}, u32[]{:S(2)}) copy-start(f32[3,16,32,512]{3,2,1,0:T(8,128)S(1)} %collective-permute-done.1) | copy-start | bytes 9437188
  68.0 15.8 %collective-permute-start.10 = (bf16[16,32,512]{2,1,0:T(8,128)(2,1)}, bf16[16,32,512]{2,1,0:T(8,128)(2,1)S(1)}, u32[]{:S(2)}, u32[]{:S(2)}) collective-permute-start(bf16[16,32,512]{2,1,0:T(8,128)(2,1)} %collective-permute-done.5.ap), channel_id=1, source_target_pairs={{0,1},{1,0},{2,3},{3,2},{4,5},{5,4},{6,7},{7,6},{8,9},{9,8},{10,11... | collective-permute-start | bytes 1572872 | tf_op jit(solution)/shard_map/ppermute | solution.py:204
  74.0 5.5 %collective-permute-start.11 = (bf16[8,32,512]{2,1,0:T(8,128)(2,1)S(1)}, bf16[8,32,512]{2,1,0:T(8,128)(2,1)}, u32[]{:S(2)}, u32[]{:S(2)}) collective-permute-start(bf16[8,32,512]{2,1,0:T(8,128)(2,1)S(1)} %collective-permute-done.6.a2a), channel_id=1, source_target_pairs={{0,1},{1,0},{2,3},{3,2},{4,5},{5,4},{6,7},{7,6},{8,9},{9,8},{10,11... | collective-permute-start | bytes 786440 | tf_op jit(solution)/shard_map/ppermute | solution.py:204
  75.8 7.4 %collective-permute-start.12 = (bf16[8,32,512]{2,1,0:T(8,128)(2,1)}, bf16[8,32,512]{2,1,0:T(8,128)(2,1)S(1)}, u32[]{:S(2)}, u32[]{:S(2)}) collective-permute-start(bf16[8,32,512]{2,1,0:T(8,128)(2,1)} %collective-permute-done.7.a2b), channel_id=1, source_target_pairs={{0,1},{1,0},{2,3},{3,2},{4,5},{5,4},{6,7},{7,6},{8,9},{9,8},{10,11... | collective-permute-start | bytes 786440 | tf_op jit(solution)/shard_map/ppermute | solution.py:204
  78.7 20.6 %collective-permute-start.13 = (bf16[16,32,512]{2,1,0:T(8,128)(2,1)}, bf16[16,32,512]{2,1,0:T(8,128)(2,1)S(1)}, u32[]{:S(2)}, u32[]{:S(2)}) collective-permute-start(bf16[16,32,512]{2,1,0:T(8,128)(2,1)} %all-to-all-done.1.a0), channel_id=1, source_target_pairs={{0,2},{1,3},{2,4},{3,5},{4,6},{5,7},{6,0},{7,1},{8,10},{9,11},{10,... | collective-permute-start | bytes 1572872 | tf_op jit(solution)/shard_map/ppermute | solution.py:201
  79.5 19.9 %collective-permute-start.14 = (bf16[16,32,512]{2,1,0:T(8,128)(2,1)}, bf16[16,32,512]{2,1,0:T(8,128)(2,1)S(1)}, u32[]{:S(2)}, u32[]{:S(2)}) collective-permute-start(bf16[16,32,512]{2,1,0:T(8,128)(2,1)} %all-to-all-done.1.a0), channel_id=1, source_target_pairs={{0,6},{1,7},{2,0},{3,1},{4,2},{5,3},{6,4},{7,5},{8,14},{9,15},{10,... | collective-permute-start | bytes 1572872 | tf_op jit(solution)/shard_map/ppermute | solution.py:201
  83.2 0.7 copy-start.7
  83.2 18.7 %collective-permute-start.17 = (bf16[16,32,512]{2,1,0:T(8,128)(2,1)}, bf16[16,32,512]{2,1,0:T(8,128)(2,1)}, u32[]{:S(2)}, u32[]{:S(2)}) collective-permute-start(bf16[16,32,512]{2,1,0:T(8,128)(2,1)} %all-to-all-done.1.a0), channel_id=1, source_target_pairs={{0,1},{1,0},{2,3},{3,2},{4,5},{5,4},{6,7},{7,6},{8,9},{9,8},{10,11... | collective-permute-start | bytes 1572872 | tf_op jit(solution)/shard_map/ppermute | solution.py:204
  83.9 2.7 %copy-start.4 = (bf16[16,32,512]{2,1,0:T(8,128)(2,1)}, bf16[16,32,512]{2,1,0:T(8,128)(2,1)S(1)}, u32[]{:S(2)}) copy-start(bf16[16,32,512]{2,1,0:T(8,128)(2,1)S(1)} %collective-permute-done.10.bp) | copy-start | bytes 1572868
  83.9 33.1 %collective-permute-start.15 = (f32[16,32,512]{2,1,0:T(8,128)}, f32[16,32,512]{2,1,0:T(8,128)S(1)}, u32[]{:S(2)}, u32[]{:S(2)}) collective-permute-start(f32[16,32,512]{2,1,0:T(8,128)} %pad_maximum_fusion), channel_id=1, source_target_pairs={{0,2},{1,3},{2,4},{3,5},{4,6},{5,7},{6,0},{7,1},{8,10},{9,11},{10,... | collective-permute-start | bytes 3145736 | tf_op jit(solution)/shard_map/ppermute | solution.py:201
  83.9 33.1 %collective-permute-start.16 = (f32[16,32,512]{2,1,0:T(8,128)}, f32[16,32,512]{2,1,0:T(8,128)}, u32[]{:S(2)}, u32[]{:S(2)}) collective-permute-start(f32[16,32,512]{2,1,0:T(8,128)} %pad_maximum_fusion.1), channel_id=1, source_target_pairs={{0,6},{1,7},{2,0},{3,1},{4,2},{5,3},{6,4},{7,5},{8,14},{9,15},{10,... | collective-permute-start | bytes 3145736 | tf_op jit(solution)/shard_map/ppermute | solution.py:201
  99.3 6.0 %copy-start.2 = (bf16[16,32,512]{2,1,0:T(8,128)(2,1)}, bf16[16,32,512]{2,1,0:T(8,128)(2,1)S(1)}, u32[]{:S(2)}) copy-start(bf16[16,32,512]{2,1,0:T(8,128)(2,1)S(1)} %collective-permute-done.13.am) | copy-start | bytes 1572868
  99.4 6.0 %copy-start.3 = (bf16[16,32,512]{2,1,0:T(8,128)(2,1)}, bf16[16,32,512]{2,1,0:T(8,128)(2,1)S(1)}, u32[]{:S(2)}) copy-start(bf16[16,32,512]{2,1,0:T(8,128)(2,1)S(1)} %collective-permute-done.14.ap) | copy-start | bytes 1572868
  99.4 2.5 %collective-permute-start.18 = (bf16[16,32,512]{2,1,0:T(8,128)(2,1)S(1)}, bf16[16,32,512]{2,1,0:T(8,128)(2,1)S(1)}, u32[]{:S(2)}, u32[]{:S(2)}) collective-permute-start(bf16[16,32,512]{2,1,0:T(8,128)(2,1)S(1)} %collective-permute-done.13.am), channel_id=1, source_target_pairs={{0,1},{1,0},{2,3},{3,2},{4,5},{5,4},{6,7},{7,6},{8,9},{9,8},{10,11... | collective-permute-start | bytes 1572872 | tf_op jit(solution)/shard_map/ppermute | solution.py:204
  100.3 5.0 %collective-permute-start.19 = (bf16[16,32,512]{2,1,0:T(8,128)(2,1)S(1)}, bf16[16,32,512]{2,1,0:T(8,128)(2,1)}, u32[]{:S(2)}, u32[]{:S(2)}) collective-permute-start(bf16[16,32,512]{2,1,0:T(8,128)(2,1)S(1)} %collective-permute-done.14.ap), channel_id=1, source_target_pairs={{0,1},{1,0},{2,3},{3,2},{4,5},{5,4},{6,7},{7,6},{8,9},{9,8},{10,11... | collective-permute-start | bytes 1572872 | tf_op jit(solution)/shard_map/ppermute | solution.py:204
  101.9 24.4 %collective-permute-start.20 = (bf16[8,32,512]{2,1,0:T(8,128)(2,1)}, bf16[8,32,512]{2,1,0:T(8,128)(2,1)S(1)}, u32[]{:S(2)}, u32[]{:S(2)}) collective-permute-start(bf16[8,32,512]{2,1,0:T(8,128)(2,1)} %slice.70), channel_id=1, source_target_pairs={{0,2},{1,3},{2,4},{3,5},{4,6},{5,7},{6,0},{7,1},{8,10},{9,11},{10,... | collective-permute-start | bytes 786440 | tf_op jit(solution)/shard_map/ppermute | solution.py:201
  101.9 0.8 copy-start.5
  102.7 24.7 %collective-permute-start.21 = (bf16[8,32,512]{2,1,0:T(8,128)(2,1)}, bf16[8,32,512]{2,1,0:T(8,128)(2,1)}, u32[]{:S(2)}, u32[]{:S(2)}) collective-permute-start(bf16[8,32,512]{2,1,0:T(8,128)(2,1)} %slice.71), channel_id=1, source_target_pairs={{0,6},{1,7},{2,0},{3,1},{4,2},{5,3},{6,4},{7,5},{8,14},{9,15},{10,... | collective-permute-start | bytes 786440 | tf_op jit(solution)/shard_map/ppermute | solution.py:201
  119.3 17.6 %all-to-all-start.2 = ((bf16[16,32,512]{2,1,0:T(8,128)(2,1)}), bf16[16,32,512]{2,1,0:T(8,128)(2,1)S(1)}, u32[]{:S(2)}, u32[]{:S(2)}) async-start(bf16[16,32,512]{2,1,0:T(8,128)(2,1)} %add_convert_fusion), calls=%async_computation.2 | async-start | bytes 1048576 | tf_op jit(solution)/shard_map/all_to_all | solution.py:207
  126.3 2.8 %copy-start.8 = (bf16[8,32,512]{2,1,0:T(8,128)(2,1)}, bf16[8,32,512]{2,1,0:T(8,128)(2,1)S(1)}, u32[]{:S(2)}) copy-start(bf16[8,32,512]{2,1,0:T(8,128)(2,1)S(1)} %collective-permute-done.20.a2a) | copy-start | bytes 786436
  126.3 2.2 %collective-permute-start.22 = (bf16[8,32,512]{2,1,0:T(8,128)(2,1)S(1)}, bf16[8,32,512]{2,1,0:T(8,128)(2,1)S(1)}, u32[]{:S(2)}, u32[]{:S(2)}) collective-permute-start(bf16[8,32,512]{2,1,0:T(8,128)(2,1)S(1)} %collective-permute-done.20.a2a), channel_id=1, source_target_pairs={{0,1},{1,0},{2,3},{3,2},{4,5},{5,4},{6,7},{7,6},{8,9},{9,8},{10,11... | collective-permute-start | bytes 786440 | tf_op jit(solution)/shard_map/ppermute | solution.py:204
  127.4 1.7 %collective-permute-start.23 = (bf16[8,32,512]{2,1,0:T(8,128)(2,1)}, bf16[8,32,512]{2,1,0:T(8,128)(2,1)S(1)}, u32[]{:S(2)}, u32[]{:S(2)}) collective-permute-start(bf16[8,32,512]{2,1,0:T(8,128)(2,1)} %collective-permute-done.21.a2b), channel_id=1, source_target_pairs={{0,1},{1,0},{2,3},{3,2},{4,5},{5,4},{6,7},{7,6},{8,9},{9,8},{10,11... | collective-permute-start | bytes 786440 | tf_op jit(solution)/shard_map/ppermute | solution.py:204
  128.5 0.7 copy-start.9
  129.3 0.7 copy-start.10
Sparse Core Ops, SparseCore 0:
  10.1 79.6 all-gather.1
